TPU v7x, 32 devices: a whole 2x2x4 slice. The times are simulated.
32 devices in a mesh: dp: 16 (over z, x, core), tensor: 2 (over y).
Axes of the slice: x: 2, y: 2, z: 4, core: 2. Of those that a mesh axis runs over, the one named last changes fastest.
Arguments:
- tokens: bfloat16 [8192, 1024], P(('dp', 'tensor')), may hold values from -6 to 6
- time_index: int32 [64], P(('dp', 'tensor')), may hold values from 0 to 255
- time_table: float32 [256, 1024], replicated, may hold values from -1 to 1
- norm_gain: float32 [2, 2, 1024], replicated, may hold values from 0.5 to 1.5
- norm_bias: float32 [2, 2, 1024], replicated, may hold values from -1 to 1
- w_qkv: bfloat16 [2, 1024, 3, 1024], P(None, None, None, 'tensor'), may hold values from -0.1875 to 0.1875
- w_out: bfloat16 [2, 1024, 1024], P(None, 'tensor'), may hold values from -1 to 1
- w_up: bfloat16 [2, 1024, 4096], P(None, None, 'tensor'), may hold values from -0.1875 to 0.1875
- w_down: bfloat16 [2, 4096, 1024], P(None, 'tensor'), may hold values from -0.09375 to 0.09375
- time_weight: float32 [2, 1024], replicated, may hold values from -0.5 to 0.5
- cotangent: bfloat16 [8192, 1024], P(('dp', 'tensor')), may hold values from -6 to 6
Outputs:
- result: float32 [8192, 1024], P(('dp', 'tensor'))
- grad_tokens: float32 [8192, 1024], P(('dp', 'tensor'))
- grad_norm_gain: float32 [2, 2, 1024], replicated
- grad_norm_bias: float32 [2, 2, 1024], replicated
- grad_w_qkv: float32 [2, 1024, 3, 1024], P(None, None, None, 'tensor')
- grad_w_out: float32 [2, 1024, 1024], P(None, 'tensor')
- grad_w_up: float32 [2, 1024, 4096], P(None, None, 'tensor')
- grad_w_down: float32 [2, 4096, 1024], P(None, 'tensor')
- grad_time_weight: float32 [2, 1024], replicated
- grad_mlp_norm: float32 [2, 1024], replicated
All inputs are finite; a program needn't handle non-finite values.
Results may differ from a plain program's by a relative error of at most 0.028.
Values may be sent and summed in bfloat16 or wider, within the bound.
No kernel may reach another device: no remote copies, remote signals or barrier semaphores. Data moves between devices by JAX's collectives and lax.ppermute only.
A program may use at most 192 MiB of HBM per device.

v0:
```python
import math

import jax
import jax.numpy as jnp
from jax import lax
from jax.sharding import PartitionSpec as P

HD = 64


epsilon = 1e-05


def gelu_tanh(u):
    return 0.5 * u * (1.0 + jnp.tanh(0.7978845608 * (u + 0.044715 * u * u * u)))


def layer_norm_statistics(v):
    centered = v - jnp.mean(v, axis=-1, keepdims=True)
    inverse_deviation = lax.rsqrt(jnp.mean(centered * centered, axis=-1, keepdims=True) + epsilon)
    return (centered * inverse_deviation, inverse_deviation)


def layer_norm_backward(
    normalized_gradient, standardized_input, inverse_deviation, norm_scale_factor
):
    scaled_rows = normalized_gradient * norm_scale_factor
    return inverse_deviation * (
        scaled_rows
        - jnp.mean(scaled_rows, axis=-1, keepdims=True)
        - standardized_input * jnp.mean(scaled_rows * standardized_input, axis=-1, keepdims=True)
    )


def rope_tables(length, head_size):
    half = head_size // 2
    freqs = jnp.exp(-math.log(10000.0) * jnp.arange(half, dtype=jnp.float32) * 2.0 / head_size)
    angles = jnp.arange(length, dtype=jnp.float32)[:, None] * freqs[None, :]
    angles = jnp.concatenate([angles, angles], axis=1)
    return (jnp.cos(angles)[None, :, None, :], jnp.sin(angles)[None, :, None, :])


def rotate_half(v):
    half = v.shape[-1] // 2
    return jnp.concatenate([-v[..., half:], v[..., :half]], axis=-1)


def rotate(v, cos_table, sin_table):
    return v * cos_table + rotate_half(v) * sin_table


def unrotate(incoming_gradient, cos_table, sin_table):
    return incoming_gradient * cos_table - rotate_half(incoming_gradient * sin_table)


def attend(q_rot, k_rot, values, scale):
    scores = jnp.einsum("sqhd,skhd->shqk", q_rot, k_rot, preferred_element_type=jnp.float32) * scale
    top = jnp.max(scores, axis=-1, keepdims=True)
    total = jnp.sum(jnp.exp(scores - top), axis=-1, keepdims=True)
    logsum = top + jnp.log(total)
    probs = jnp.exp(scores - logsum).astype(jnp.bfloat16)
    attended = jnp.einsum("shqk,skhd->sqhd", probs, values, preferred_element_type=jnp.float32)
    return (attended, logsum)


def attend_back(q_rot, k_rot, values, logsum, grad_att, scale):
    scores = jnp.einsum("sqhd,skhd->shqk", q_rot, k_rot, preferred_element_type=jnp.float32) * scale
    probs = jnp.exp(scores - logsum)
    grad_values = jnp.einsum(
        "shqk,sqhd->skhd", probs.astype(jnp.bfloat16), grad_att, preferred_element_type=jnp.float32
    )
    grad_probs = jnp.einsum("sqhd,skhd->shqk", grad_att, values, preferred_element_type=jnp.float32)
    grad_scores = probs * (grad_probs - jnp.sum(probs * grad_probs, axis=-1, keepdims=True))
    grad_scores = grad_scores.astype(jnp.bfloat16)
    grad_query = (
        jnp.einsum("shqk,skhd->sqhd", grad_scores, k_rot, preferred_element_type=jnp.float32)
        * scale
    )
    grad_keys = (
        jnp.einsum("shqk,sqhd->skhd", grad_scores, q_rot, preferred_element_type=jnp.float32)
        * scale
    )
    return (grad_query, grad_keys, grad_values)


def local(
    tokens,
    time_index,
    time_table,
    norm_gain,
    norm_bias,
    w_qkv,
    w_out,
    w_up,
    w_down,
    time_weight,
    cotangent,
):
    rows, width = tokens.shape
    seq_here = time_index.shape[0]
    length = rows // seq_here
    layers = norm_gain.shape[0]
    local_width = w_out.shape[1]
    local_heads = local_width // HD
    scale = HD ** (-0.5)
    cos_table, sin_table = rope_tables(length, HD)
    table_rows = time_table.shape[0]
    onehot = (time_index[:, None] == jnp.arange(table_rows, dtype=jnp.int32)[None, :]).astype(
        jnp.float32
    )
    time_seq = jnp.dot(onehot, time_table, precision=lax.Precision.HIGHEST)
    time_rows = jnp.broadcast_to(time_seq[:, None, :], (seq_here, length, width)).reshape(
        rows, width
    )
    hidden_state = tokens.astype(jnp.float32)
    kept = []
    for layer in range(layers):
        norm_scale_factor = norm_gain[layer]
        shift_bias = norm_bias[layer]
        first_standardized_input, first_inverse_deviation = layer_norm_statistics(hidden_state)
        first_normalized_rows = (
            first_standardized_input * norm_scale_factor[0] + shift_bias[0]
        ).astype(jnp.bfloat16)
        normed_all = lax.all_gather(first_normalized_rows, "tensor", axis=0, tiled=True)
        group_rows = normed_all.shape[0]
        group_seqs = group_rows // length
        weights_qkv = w_qkv[layer].reshape(width, 3 * local_width)
        projected = jnp.dot(normed_all, weights_qkv, preferred_element_type=jnp.float32)
        projected = projected.reshape(group_seqs, length, 3, local_heads, HD)
        q_rot = rotate(projected[:, :, 0], cos_table, sin_table).astype(jnp.bfloat16)
        k_rot = rotate(projected[:, :, 1], cos_table, sin_table).astype(jnp.bfloat16)
        values = projected[:, :, 2].astype(jnp.bfloat16)
        attended, logsum = attend(q_rot, k_rot, values, scale)
        attended = attended.astype(jnp.bfloat16).reshape(group_rows, local_width)
        out_local = w_out[layer]
        out_full = None
        attended_rows = None
        branch = lax.psum_scatter(
            jnp.dot(attended, out_local, preferred_element_type=jnp.float32).astype(jnp.bfloat16),
            "tensor",
            scatter_dimension=0,
            tiled=True,
        ).astype(jnp.float32)
        after_attention_rows = hidden_state + branch
        second_standardized_input, second_inverse_deviation = layer_norm_statistics(
            after_attention_rows
        )
        second_normalized_rows = (
            second_standardized_input * norm_scale_factor[1] + shift_bias[1]
        ).astype(jnp.bfloat16)
        normed_two_all = lax.all_gather(second_normalized_rows, "tensor", axis=0, tiled=True)
        upper = jnp.dot(normed_two_all, w_up[layer], preferred_element_type=jnp.float32)
        hidden = gelu_tanh(upper).astype(jnp.bfloat16)
        down_local = w_down[layer]
        after_mlp = after_attention_rows + lax.psum_scatter(
            jnp.dot(hidden, down_local, preferred_element_type=jnp.float32).astype(jnp.bfloat16),
            "tensor",
            scatter_dimension=0,
            tiled=True,
        ).astype(jnp.float32)
        kept.append(
            (
                first_standardized_input,
                first_inverse_deviation,
                normed_all,
                q_rot,
                k_rot,
                values,
                logsum,
                attended,
                attended_rows,
                out_full,
                second_standardized_input,
                second_inverse_deviation,
                normed_two_all,
                upper,
                hidden,
                after_mlp,
            )
        )
        hidden_state = after_mlp * (1.0 + time_rows * time_weight[layer])
    incoming_gradient = cotangent.astype(jnp.float32)
    gain_grads = [None] * layers
    bias_grads = [None] * layers
    time_grads = [None] * layers
    qkv_grads = [None] * layers
    out_grads = [None] * layers
    up_grads = [None] * layers
    down_grads = [None] * layers
    for layer in reversed(range(layers)):
        (
            first_standardized_input,
            first_inverse_deviation,
            normed_all,
            q_rot,
            k_rot,
            values,
            logsum,
            attended,
            attended_rows,
            out_full,
            second_standardized_input,
            second_inverse_deviation,
            normed_two_all,
            upper,
            hidden,
            after_mlp,
        ) = kept[layer]
        norm_scale_factor = norm_gain[layer]
        time_grads[layer] = jnp.sum(incoming_gradient * after_mlp * time_rows, axis=0)
        incoming_gradient = incoming_gradient * (1.0 + time_rows * time_weight[layer])
        grad_low = incoming_gradient.astype(jnp.bfloat16)
        grad_all = lax.all_gather(grad_low, "tensor", axis=0, tiled=True)
        grad_down = jnp.einsum("rf,rd->fd", hidden, grad_all, preferred_element_type=jnp.float32)
        grad_hidden = jnp.einsum(
            "rd,fd->rf", grad_all, w_down[layer], preferred_element_type=jnp.float32
        )
        unused, gelu_pull = jax.vjp(gelu_tanh, upper)
        grad_upper = gelu_pull(grad_hidden)[0].astype(jnp.bfloat16)
        grad_up = jnp.einsum(
            "rd,rf->df", normed_two_all, grad_upper, preferred_element_type=jnp.float32
        )
        up_local = w_up[layer]
        second_normalized_gradient = lax.psum_scatter(
            jnp.einsum(
                "rf,df->rd", grad_upper, up_local, preferred_element_type=jnp.float32
            ).astype(jnp.bfloat16),
            "tensor",
            scatter_dimension=0,
            tiled=True,
        ).astype(jnp.float32)
        second_norm_scale = jnp.sum(second_normalized_gradient * second_standardized_input, axis=0)
        bias_two = jnp.sum(second_normalized_gradient, axis=0)
        incoming_gradient = incoming_gradient + layer_norm_backward(
            second_normalized_gradient,
            second_standardized_input,
            second_inverse_deviation,
            norm_scale_factor[1],
        )
        grad_low = incoming_gradient.astype(jnp.bfloat16)
        grad_branch = lax.all_gather(grad_low, "tensor", axis=0, tiled=True)
        grad_out = jnp.einsum(
            "rh,rd->hd", attended, grad_branch, preferred_element_type=jnp.float32
        )
        grad_attended = jnp.einsum(
            "rd,hd->rh", grad_branch, w_out[layer], preferred_element_type=jnp.float32
        ).astype(jnp.bfloat16)
        group_rows = normed_all.shape[0]
        group_seqs = group_rows // length
        grad_att = grad_attended.reshape(group_seqs, length, local_heads, HD)
        grad_query, grad_keys, grad_values = attend_back(
            q_rot, k_rot, values, logsum, grad_att, scale
        )
        grad_query = unrotate(grad_query, cos_table, sin_table)
        grad_keys = unrotate(grad_keys, cos_table, sin_table)
        grad_proj = jnp.stack([grad_query, grad_keys, grad_values], axis=2).astype(jnp.bfloat16)
        grad_proj = grad_proj.reshape(group_rows, 3 * local_width)
        weights_qkv = w_qkv[layer].reshape(width, 3 * local_width)
        grad_qkv = jnp.einsum(
            "rd,re->de", normed_all, grad_proj, preferred_element_type=jnp.float32
        )
        grad_qkv = grad_qkv.reshape(width, 3, local_width)
        first_normalized_gradient = lax.psum_scatter(
            jnp.einsum(
                "re,de->rd", grad_proj, weights_qkv, preferred_element_type=jnp.float32
            ).astype(jnp.bfloat16),
            "tensor",
            scatter_dimension=0,
            tiled=True,
        ).astype(jnp.float32)
        first_norm_scale = jnp.sum(first_normalized_gradient * first_standardized_input, axis=0)
        bias_one = jnp.sum(first_normalized_gradient, axis=0)
        incoming_gradient = incoming_gradient + layer_norm_backward(
            first_normalized_gradient,
            first_standardized_input,
            first_inverse_deviation,
            norm_scale_factor[0],
        )
        gain_grads[layer] = jnp.stack([first_norm_scale, second_norm_scale], axis=0)
        bias_grads[layer] = jnp.stack([bias_one, bias_two], axis=0)
        summed = (
            lax.psum(grad_qkv.astype(jnp.bfloat16), "dp").astype(jnp.float32),
            lax.psum(grad_out.astype(jnp.bfloat16), "dp").astype(jnp.float32),
            lax.psum(grad_up.astype(jnp.bfloat16), "dp").astype(jnp.float32),
            lax.psum(grad_down.astype(jnp.bfloat16), "dp").astype(jnp.float32),
        )
        qkv_grads[layer], out_grads[layer], up_grads[layer], down_grads[layer] = summed
    small = lax.psum(
        (
            jnp.stack(gain_grads, axis=0),
            jnp.stack(bias_grads, axis=0),
            jnp.stack(time_grads, axis=0),
        ),
        ("dp", "tensor"),
    )
    mlp_norm = jnp.stack([small[0][layers - 1, 1], small[1][layers - 1, 1]], axis=0)
    return (
        hidden_state,
        incoming_gradient,
        small[0],
        small[1],
        jnp.stack(qkv_grads, axis=0),
        jnp.stack(out_grads, axis=0),
        jnp.stack(up_grads, axis=0),
        jnp.stack(down_grads, axis=0),
        small[2],
        mlp_norm,
    )


def solution(mesh):
    placed = (
        P(("dp", "tensor"), None),
        P(("dp", "tensor")),
        P(),
        P(),
        P(),
        P(None, None, None, "tensor"),
        P(None, "tensor", None),
        P(None, None, "tensor"),
        P(None, "tensor", None),
        P(),
        P(("dp", "tensor"), None),
    )
    return jax.shard_map(
        local,
        mesh=mesh,
        in_specs=placed,
        out_specs=(
            P(("dp", "tensor"), None),
            P(("dp", "tensor"), None),
            P(),
            P(),
            P(None, None, None, "tensor"),
            P(None, "tensor", None),
            P(None, None, "tensor"),
            P(None, "tensor", None),
            P(),
            P(),
        ),
        check_vma=False,
    )
```

profile of v0, /device:TPU:0, one launch (start us, length us, event | category | flops | bytes accessed | tf_op | source)
XLA Modules:
  0.0 973.6 jit_solution(17000092381548821399)
XLA Ops:
  11.5 2.1 fusion.75
  13.6 6.3 fusion.167
  20.0 4.7 copy.81
  24.9 12.9 %all-gather.9.cloned.1.call-done = bf16[512,1024]{1,0:T(8,128)(2,1)} async-done(((bf16[256,1024]{1,0:T(8,128)(2,1)}), bf16[512,1024]{1,0:T(8,128)(2,1)}) %all-gather.9.cloned.1.call-update) | async-done | bytes 1048592 | tf_op jit(solution)/shard_map/all_gather | solution.py:124
  37.7 4.1 fusion.171
  45.5 1.7 convolution_convert_fusion.5
  47.3 20.4 %reduce-scatter.9.cloned.1.call-done = bf16[256,1024]{1,0:T(8,128)(2,1)} async-done(((bf16[512,1024]{1,0:T(8,128)(2,1)}), bf16[256,1024]{1,0:T(8,128)(2,1)}) %reduce-scatter.9.cloned.1.call-update) | async-done | bytes 524304 | tf_op jit(solution)/shard_map/reduce_scatter | solution.py:138
  70.6 2.3 add_convert_fusion.2
  73.0 21.4 %all-gather.11.cloned.1.call-done = bf16[512,1024]{1,0:T(8,128)(2,1)} async-done(((bf16[256,1024]{1,0:T(8,128)(2,1)}), bf16[512,1024]{1,0:T(8,128)(2,1)}) %all-gather.11.cloned.1.call-update) | async-done | bytes 1048592 | tf_op jit(solution)/shard_map/all_gather | solution.py:151
  94.4 4.8 fusion.26
  99.2 2.0 copy-done.54
  101.2 5.8 fusion.43
  107.8 19.7 %reduce-scatter.11.cloned.1.call-done = bf16[256,1024]{1,0:T(8,128)(2,1)} async-done(((bf16[512,1024]{1,0:T(8,128)(2,1)}), bf16[256,1024]{1,0:T(8,128)(2,1)}) %reduce-scatter.11.cloned.1.call-update) | async-done | bytes 524304 | tf_op jit(solution)/shard_map/reduce_scatter | solution.py:155
  127.5 2.7 fusion.165
  131.6 4.6 copy.83
  136.3 16.8 %all-gather.13.cloned.1.call-done = bf16[512,1024]{1,0:T(8,128)(2,1)} async-done(((bf16[256,1024]{1,0:T(8,128)(2,1)}), bf16[512,1024]{1,0:T(8,128)(2,1)}) %all-gather.13.cloned.1.call-update) | async-done | bytes 1048592 | tf_op jit(solution)/shard_map/all_gather | solution.py:124
  153.0 4.1 fusion.172
  160.8 1.7 convolution_convert_fusion.4
  162.6 20.4 %reduce-scatter.13.cloned.1.call-done = bf16[256,1024]{1,0:T(8,128)(2,1)} async-done(((bf16[512,1024]{1,0:T(8,128)(2,1)}), bf16[256,1024]{1,0:T(8,128)(2,1)}) %reduce-scatter.13.cloned.1.call-update) | async-done | bytes 524304 | tf_op jit(solution)/shard_map/reduce_scatter | solution.py:138
  187.5 20.3 %all-gather.15.cloned.1.call-done = bf16[512,1024]{1,0:T(8,128)(2,1)} async-done(((bf16[256,1024]{1,0:T(8,128)(2,1)}), bf16[512,1024]{1,0:T(8,128)(2,1)}) %all-gather.15.cloned.1.call-update) | async-done | bytes 1048592 | tf_op jit(solution)/shard_map/all_gather | solution.py:151
  207.8 6.9 fusion.18
  214.6 16.7 %all-gather.17.cloned.1.call-done = bf16[512,1024]{1,0:T(8,128)(2,1)} async-done(((bf16[256,1024]{1,0:T(8,128)(2,1)}), bf16[512,1024]{1,0:T(8,128)(2,1)}) %all-gather.17.cloned.1.call-update) | async-done | bytes 1048592 | tf_op jit(solution)/shard_map/all_gather | solution.py:213
  231.3 7.9 fusion.7
  240.6 5.5 fusion.46
  246.2 7.1 fusion.49
  253.4 13.3 %reduce-scatter.17.cloned.1.call-done = bf16[256,1024]{1,0:T(8,128)(2,1)} async-done(((bf16[512,1024]{1,0:T(8,128)(2,1)}), bf16[256,1024]{1,0:T(8,128)(2,1)}) %reduce-scatter.17.cloned.1.call-update) | async-done | bytes 524304 | tf_op jit(solution)/shard_map/reduce_scatter | solution.py:224
  266.6 23.0 %reduce-scatter.15.cloned.1.call-done = bf16[256,1024]{1,0:T(8,128)(2,1)} async-done(((bf16[512,1024]{1,0:T(8,128)(2,1)}), bf16[256,1024]{1,0:T(8,128)(2,1)}) %reduce-scatter.15.cloned.1.call-update) | async-done | bytes 524304 | tf_op jit(solution)/shard_map/reduce_scatter | solution.py:155
  289.6 3.5 fusion.93
  293.2 1.6 fusion.162
  295.1 21.2 %all-gather.19.cloned.1.call-done = bf16[512,1024]{1,0:T(8,128)(2,1)} async-done(((bf16[256,1024]{1,0:T(8,128)(2,1)}), bf16[512,1024]{1,0:T(8,128)(2,1)}) %all-gather.19.cloned.1.call-update) | async-done | bytes 1048592 | tf_op jit(solution)/shard_map/all_gather | solution.py:241
  316.3 3.1 convolution_convert_fusion.9
  319.4 2.4 reshape.240
  321.7 2.5 copy.48
  324.2 2.9 multiply_reduce_fusion.1
  333.7 2.8 convolution_convert_fusion.1
  336.6 20.4 %reduce-scatter.19.cloned.1.call-done = bf16[256,1024]{1,0:T(8,128)(2,1)} async-done(((bf16[512,1024]{1,0:T(8,128)(2,1)}), bf16[256,1024]{1,0:T(8,128)(2,1)}) %reduce-scatter.19.cloned.1.call-update) | async-done | bytes 524304 | tf_op jit(solution)/shard_map/reduce_scatter | solution.py:263
  358.6 3.0 fusion.127
  361.7 21.4 %all-gather.21.cloned.1.call-done = bf16[512,1024]{1,0:T(8,128)(2,1)} async-done(((bf16[256,1024]{1,0:T(8,128)(2,1)}), bf16[512,1024]{1,0:T(8,128)(2,1)}) %all-gather.21.cloned.1.call-update) | async-done | bytes 1048592 | tf_op jit(solution)/shard_map/all_gather | solution.py:213
  383.1 7.9 fusion.3
  392.4 5.6 fusion.40
  398.1 20.4 %reduce-scatter.21.cloned.1.call-done = bf16[256,1024]{1,0:T(8,128)(2,1)} async-done(((bf16[512,1024]{1,0:T(8,128)(2,1)}), bf16[256,1024]{1,0:T(8,128)(2,1)}) %reduce-scatter.21.cloned.1.call-update) | async-done | bytes 524304 | tf_op jit(solution)/shard_map/reduce_scatter | solution.py:224
  418.6 2.4 fusion.95
  421.0 1.7 fusion.159
  423.2 6.5 convert_bitcast_fusion.2
  429.7 5.0 convert_bitcast_fusion
  436.1 8.1 all-gather.23.cloned.1.call-done
  444.2 2.3 convolution_convert_fusion.8
  448.0 1.7 copy.55
  449.8 1.9 multiply_reduce_fusion
  457.4 3.1 convolution_convert_fusion
  460.6 5.4 convert_bitcast_fusion.4
  466.0 1.7 fusion.65
  467.7 4.4 convert_bitcast_fusion.3
  472.1 5.0 convert_bitcast_fusion.1
  478.5 1.7 fusion.64
  480.2 3.5 convert_bitcast_fusion.5
  484.4 1.6 fusion.96
  486.1 42.1 %all-reduce = (f32[2,2,1024]{2,1,0:T(2,128)S(1)}, f32[2,2,1024]{2,1,0:T(2,128)S(1)}, f32[2,1024]{1,0:T(2,128)}) all-reduce(f32[2,2,1024]{2,1,0:T(2,128)S(1)} %pad_maximum_fusion.1, f32[2,2,1024]{2,1,0:T(2,128)S(1)} %pad_maximum_fusion.2, f32[2,1024]{1,0:T(2,128)S(1)} %pad_maximum_fusion.3), channel_id=1, replica_groups=mesh['dp'=16,'tensor'=2] {'dp','tensor'}, use_global_device_ids=true, to_apply=%region_34.0 | all-reduce | flops 10240 | bytes 81920 | tf_op jit(solution)/shard_map/psum | solution.py:288
  528.8 2.4 fusion.78
  531.2 404.1 %all-reduce.4.cloned.1.call-done = (bf16[1,1024,3,512]{3,1,2,0:T(8,128)(2,1)}, bf16[1,1024,3,512]{3,1,2,0:T(8,128)(2,1)}, bf16[1,512,1024]{2,1,0:T(8,128)(2,1)},...) async-done(((bf16[1,1024,3,512]{3,1,2,0:T(8,128)(2,1)}, ...) | async-done | bytes 25165840 | tf_op jit(solution)/shard_map/psum | solution.py:282
  935.3 10.7 %maximum_convert_fusion.1 = f32[2,2048,1024]{2,1,0:T(8,128)} fusion(bf16[1,2048,1024]{2,1,0:T(8,128)(2,1)} %get-tuple-element.37, bf16[1,2048,1024]{2,1,0:T(8,128)(2,1)} %get-tuple-element.38), kind=kLoop, calls=%fused_computation.1 | loop fusion | flops 8388608 | bytes 25165824 | tf_op jit(solution)/shard_map/stack | solution.py:305
  946.1 10.8 %maximum_convert_fusion = f32[2,1024,2048]{2,1,0:T(8,128)} fusion(bf16[1,1024,2048]{2,1,0:T(8,128)(2,1)} %get-tuple-element.35, bf16[1,1024,2048]{2,1,0:T(8,128)(2,1)} %get-tuple-element.36), kind=kLoop, calls=%fused_computation | loop fusion | flops 8388608 | bytes 25165824 | tf_op jit(solution)/shard_map/stack | solution.py:304
  956.9 2.4 maximum_convert_fusion.5
  961.3 5.6 maximum_convert_fusion.2
  (235 shorter events, 46.4 us)
Async XLA Ops:
  7.2 100.2 %copy-start = (f32[256,1024]{1,0:T(8,128)S(1)}, f32[256,1024]{1,0:T(8,128)}, u32[]{:S(2)}) copy-start(f32[256,1024]{1,0:T(8,128)} %param.13) | copy-start | bytes 3145732
  7.2 30.6 %all-gather.9.cloned.1.call-start = ((), (), s32[]{:S(2)}) async-start(), calls=%async_computation.8 | async-start | bytes 1572864 | tf_op jit(solution)/shard_map/all_gather | solution.py:124
  8.1 11.9 %copy-start.36 = (f32[1,1,1024]{2,1,0:T(1,128)}, f32[1,1,1024]{2,1,0:T(1,128)S(1)}, u32[]{:S(2)}) copy-start(f32[1,1,1024]{2,1,0:T(1,128)S(1)} %get-tuple-element.90) | copy-start | bytes 12292
  9.3 10.7 %copy-start.38 = (f32[256]{0:T(256)}, f32[256]{0:T(256)S(1)}, u32[]{:S(2)}) copy-start(f32[256]{0:T(256)S(1)} %broadcast_multiply_fusion.17) | copy-start | bytes 3076
  10.6 9.3 copy-start.40
  13.6 54.1 %reduce-scatter.9.cloned.1.call-start = ((), (), s32[]{:S(2)}) async-start(), calls=%async_computation.9 | async-start | bytes 1572864 | tf_op jit(solution)/shard_map/reduce_scatter | solution.py:138
  41.8 1.9 copy-start.8
  42.7 1.5 copy-start.14
  42.8 1.5 copy-start.19
  43.3 2.2 copy-start.46
  47.2 47.2 %all-gather.11.cloned.1.call-start = ((), (), s32[]{:S(2)}) async-start(), calls=%async_computation.10 | async-start | bytes 1572864 | tf_op jit(solution)/shard_map/all_gather | solution.py:151
  72.9 54.6 %reduce-scatter.11.cloned.1.call-start = ((), (), s32[]{:S(2)}) async-start(), calls=%async_computation.11 | async-start | bytes 1572864 | tf_op jit(solution)/shard_map/reduce_scatter | solution.py:155
  99.2 2.0 copy-start.54
  101.2 6.1 copy-start.42
  101.2 6.1 copy-start.45
  107.1 46.0 %all-gather.13.cloned.1.call-start = ((), (), s32[]{:S(2)}) async-start(), calls=%async_computation.12 | async-start | bytes 1572864 | tf_op jit(solution)/shard_map/all_gather | solution.py:124
  131.6 51.5 %reduce-scatter.13.cloned.1.call-start = ((), (), s32[]{:S(2)}) async-start(), calls=%async_computation.13 | async-start | bytes 1572864 | tf_op jit(solution)/shard_map/reduce_scatter | solution.py:138
  157.1 1.8 copy-start.9
  158.0 1.5 copy-start.16
  158.0 1.5 copy-start.21
  158.5 1.4 copy-start.2
  158.5 2.3 copy-start.47
  162.6 45.2 %all-gather.15.cloned.1.call-start = ((), (), s32[]{:S(2)}) async-start(), calls=%async_computation.14 | async-start | bytes 1572864 | tf_op jit(solution)/shard_map/all_gather | solution.py:151
  186.3 45.0 %all-gather.17.cloned.1.call-start = ((), (), s32[]{:S(2)}) async-start(), calls=%async_computation.16 | async-start | bytes 1572864 | tf_op jit(solution)/shard_map/all_gather | solution.py:213
  187.1 79.6 %reduce-scatter.17.cloned.1.call-start = ((), (), s32[]{:S(2)}) async-start(), calls=%async_computation.17 | async-start | bytes 1572864 | tf_op jit(solution)/shard_map/reduce_scatter | solution.py:224
  246.1 43.5 %reduce-scatter.15.cloned.1.call-start = ((), (), s32[]{:S(2)}) async-start(), calls=%async_computation.15 | async-start | bytes 1572864 | tf_op jit(solution)/shard_map/reduce_scatter | solution.py:155
  253.3 63.0 %all-gather.19.cloned.1.call-start = ((), (), s32[]{:S(2)}) async-start(), calls=%async_computation.18 | async-start | bytes 1572864 | tf_op jit(solution)/shard_map/all_gather | solution.py:241
  289.6 3.5 copy-start.6
  289.6 3.5 copy-start.13
  289.6 3.5 copy-start.29
  294.8 62.2 %reduce-scatter.19.cloned.1.call-start = ((), (), s32[]{:S(2)}) async-start(), calls=%async_computation.19 | async-start | bytes 1572864 | tf_op jit(solution)/shard_map/reduce_scatter | solution.py:263
  324.2 2.9 copy-start.3
  324.2 2.9 copy-start.18
  328.0 1.9 copy-start.22
  331.0 2.8 copy-start.27
  336.6 46.5 %all-gather.21.cloned.1.call-start = ((), (), s32[]{:S(2)}) async-start(), calls=%async_computation.20 | async-start | bytes 1572864 | tf_op jit(solution)/shard_map/all_gather | solution.py:213
  361.7 56.9 %reduce-scatter.21.cloned.1.call-start = ((), (), s32[]{:S(2)}) async-start(), calls=%async_computation.21 | async-start | bytes 1572864 | tf_op jit(solution)/shard_map/reduce_scatter | solution.py:224
  392.4 26.1 %copy-start.4 = (bf16[256,1024]{1,0:T(8,128)(2,1)S(1)}, bf16[256,1024]{1,0:T(8,128)(2,1)}, u32[]{:S(2)}) copy-start(bf16[256,1024]{1,0:T(8,128)(2,1)} %param.11) | copy-start | bytes 1572868
  392.4 26.1 %copy-start.7 = (bf16[256,1024]{1,0:T(8,128)(2,1)S(1)}, bf16[256,1024]{1,0:T(8,128)(2,1)}, u32[]{:S(2)}) copy-start(bf16[256,1024]{1,0:T(8,128)(2,1)} %reduce-scatter.9.cloned.1.call-done) | copy-start | bytes 1572868
  398.1 46.1 %all-gather.23.cloned.1.call-start = ((), (), s32[]{:S(2)}) async-start(), calls=%async_computation.22 | async-start | bytes 1572864 | tf_op jit(solution)/shard_map/all_gather | solution.py:241
  418.5 2.4 copy-start.10
  418.5 2.4 copy-start.28
  422.7 61.1 %reduce-scatter.23.cloned.1.call-start = ((), (), s32[]{:S(2)}) async-start(), calls=%async_computation.23 | async-start | bytes 1572864 | tf_op jit(solution)/shard_map/reduce_scatter | solution.py:263
  423.2 6.5 copy-start.51
  423.2 6.5 copy-start.56
  429.7 5.0 copy-start.12
  452.5 1.8 copy-start.20
  455.5 1.9 copy-start.26
  460.5 474.8 %all-reduce.4.cloned.1.call-start = ((), (), s32[]{:S(2)}) async-start(), calls=%async_computation.24 | async-start | bytes 50331648 | tf_op jit(solution)/shard_map/psum | solution.py:282
  460.5 5.4 copy-start.35
  460.6 5.4 copy-start.50
  460.6 7.1 copy-start.49
  460.6 7.1 copy-start.59
  467.7 4.4 copy-start.52
  467.7 4.4 copy-start.55
  477.1 3.1 copy-start.48
  483.7 45.1 %copy-start.23 = (f32[256,1024]{1,0:T(8,128)S(1)}, f32[256,1024]{1,0:T(8,128)}, u32[]{:S(2)}) copy-start(f32[256,1024]{1,0:T(8,128)} %get-tuple-element.40) | copy-start | bytes 3145732
  528.2 417.9 %copy-start.43 = (f32[2,2,1024]{2,1,0:T(2,128)}, f32[2,2,1024]{2,1,0:T(2,128)S(1)}, u32[]{:S(2)}) copy-start(f32[2,2,1024]{2,1,0:T(2,128)S(1)} %get-tuple-element.28) | copy-start | bytes 49156
  528.2 417.9 %copy-start.44 = (f32[2,2,1024]{2,1,0:T(2,128)}, f32[2,2,1024]{2,1,0:T(2,128)S(1)}, u32[]{:S(2)}) copy-start(f32[2,2,1024]{2,1,0:T(2,128)S(1)} %get-tuple-element.29) | copy-start | bytes 49156
  946.1 10.9 %copy-start.30 = (bf16[1,512,1024]{2,1,0:T(8,128)(2,1)S(1)}, bf16[1,512,1024]{2,1,0:T(8,128)(2,1)}, u32[]{:S(2)}) copy-start(bf16[1,512,1024]{2,1,0:T(8,128)(2,1)} %get-tuple-element.33) | copy-start | bytes 3145732
  946.1 10.9 %copy-start.31 = (bf16[1,512,1024]{2,1,0:T(8,128)(2,1)S(1)}, bf16[1,512,1024]{2,1,0:T(8,128)(2,1)}, u32[]{:S(2)}) copy-start(bf16[1,512,1024]{2,1,0:T(8,128)(2,1)} %get-tuple-element.34) | copy-start | bytes 3145732
  956.9 3.4 copy-start.24
  956.9 4.4 copy-start.25
  961.3 5.6 copy-start.1
  (13 other events, 13.1 us)
Sparse Core Ops, SparseCore 0:
  13.7 23.9 all-gather.8
  47.3 20.3 reduce-scatter.8
  73.0 21.2 all-gather.10
  107.2 20.3 reduce-scatter.10
  131.7 21.2 all-gather.12
  162.7 20.3 reduce-scatter.12
  186.4 21.2 all-gather.14
  210.0 21.2 all-gather.16
  246.3 20.3 reduce-scatter.16
  269.3 20.3 reduce-scatter.14
  294.9 21.2 all-gather.18
  336.7 20.3 reduce-scatter.18
  361.8 21.2 all-gather.20
  398.2 20.3 reduce-scatter.20
  422.9 21.2 all-gather.22
  460.6 20.3 reduce-scatter.22
  487.1 448.1 all-reduce.3
where the time goes:
time: 983 us; the launch traced here: 974 us
  waiting for transfers between devices  682 us (69%)
  matrix products  119 us (12%)
  other arithmetic  69.8 us (7%)
  local copies, waits for them, and re-layouts  44.3 us (5%)
  blocking collectives  42.1 us (4%)
  between operations  15.1 us (2%)
    psum x1, waiting for transfers between devices, local(): lax.psum(grad_qkv.astype(jnp.bfloat16), 'dp').astype(jnp.float32)  404 us
    reduce_scatter x2, waiting for transfers between devices, local(): lax.psum_scatter(jnp.dot(hidden, down_local, preferred_element_type=jnp.f...  42.7 us
    psum x1, blocking collectives, local(): lax.psum((jnp.stack(gain_grads, axis=0), jnp.stack(bias_grads, axis=0), j...  42.1 us
    all_gather x2, waiting for transfers between devices, local(): lax.all_gather(second_normalized_rows, 'tensor', axis=0, tiled=True)  41.7 us
    reduce_scatter x2, waiting for transfers between devices, local(): lax.psum_scatter(jnp.dot(attended, out_local, preferred_element_type=jnp....  40.9 us
    all_gather x2, waiting for transfers between devices, local(): grad_all = lax.all_gather(grad_low, 'tensor', axis=0, tiled=True)  38.1 us
    reduce_scatter x2, waiting for transfers between devices, local(): lax.psum_scatter(jnp.einsum('rf,df->rd', grad_upper, up_local, preferred_...  33.7 us
    all_gather x2, waiting for transfers between devices, local(): lax.all_gather(first_normalized_rows, 'tensor', axis=0, tiled=True)  29.7 us
  transfers between devices with their start and end apart: 17, of which 16 were waited for; matrix products, arithmetic and copies ran while one was open for 7% of the time, Pallas kernels for 0%

commit v1 on v0

v1 whole, which is shorter than its diff:
```python
import math

import jax
import jax.numpy as jnp
from jax import lax
from jax.experimental import pallas as pl
from jax.experimental.pallas import tpu as pltpu
from jax.sharding import PartitionSpec as P

HD = 64
bf16 = jnp.bfloat16
f32 = jnp.float32
epsilon = 1e-05


def mm(a, b):
    return jnp.dot(a, b, preferred_element_type=f32)


def mm_t(a, b):
    return lax.dot_general(a, b, (((1,), (1,)), ((), ())), preferred_element_type=f32)


def across(a, b):
    return lax.dot_general(a, b, (((0,), (0,)), ((), ())), preferred_element_type=f32)


def ein(spec, a, b):
    return jnp.einsum(spec, a, b, preferred_element_type=f32)


def gelu_parts(u):
    inner = 0.7978845608 * (u + 0.044715 * u * u * u)
    th = jnp.tanh(inner)
    half = 0.5 * (1.0 + th)
    slope = half + 0.5 * u * (1.0 - th * th) * (0.7978845608 + 3.0 * 0.7978845608 * 0.044715 * u * u)
    return u * half, slope


def standardize(v):
    centered = v - jnp.mean(v, axis=-1, keepdims=True)
    inverse = lax.rsqrt(jnp.mean(centered * centered, axis=-1, keepdims=True) + epsilon)
    return centered * inverse, inverse


def norm_backward(grad, xhat, inverse, gain):
    e = grad * gain
    return inverse * (
        e
        - jnp.mean(e, axis=-1, keepdims=True)
        - xhat * jnp.mean(e * xhat, axis=-1, keepdims=True)
    )


CHUNK = 32
BLOCK = 256


def rope_tables(length, width):
    half = HD // 2
    freqs = jnp.exp(-math.log(10000.0) * jnp.arange(half, dtype=f32) * 2.0 / HD)
    angles = jnp.arange(length, dtype=f32)[:, None] * freqs[None, :]
    heads = width // HD
    cos = jnp.tile(jnp.cos(angles), (1, 2 * heads))
    sin = jnp.tile(jnp.concatenate([-jnp.sin(angles), jnp.sin(angles)], axis=1), (1, heads))
    return cos, sin


def partner(u):
    width = u.shape[1]
    lane = lax.broadcasted_iota(jnp.int32, u.shape, 1)
    low = (lane & (HD - 1)) < HD // 2
    return jnp.where(low, pltpu.roll(u, width - HD // 2, 1), pltpu.roll(u, HD // 2, 1))


def chunks(rows, body, start=0):
    def step(i, carry):
        body(pl.multiple_of(i * CHUNK, CHUNK))
        return carry

    lax.fori_loop(start // CHUNK, rows // CHUNK, step, 0)


def rows_at(at):
    return pl.ds(at, CHUNK)


def other_rows(at, rows, swapped):
    if not swapped:
        return rows_at(at)
    half = rows // 2
    return rows_at(pl.multiple_of(jnp.where(at < half, at + half, at - half), CHUNK))


def fold(v):
    return jnp.sum(v.reshape(-1, 8, v.shape[-1]), axis=0)


LIMIT = 18 * 2**20


def call(kernel, ins, outs, scratch, flops, name, aliases={}):
    vmem = pl.BlockSpec(memory_space=pltpu.VMEM)
    far = pl.BlockSpec(memory_space=pltpu.HBM)
    smem = pl.BlockSpec(memory_space=pltpu.SMEM)
    spec = lambda a, away: smem if a.dtype == jnp.int32 else far if away else vmem
    return pl.pallas_call(
        kernel,
        out_shape=[jax.ShapeDtypeStruct(s, d) for s, d, _ in outs],
        in_specs=[spec(a, away) for a, away in ins],
        out_specs=[far if away else vmem for _, _, away in outs],
        scratch_shapes=scratch,
        input_output_aliases=aliases,
        compiler_params=pltpu.CompilerParams(vmem_limit_bytes=LIMIT),
        cost_estimate=pl.CostEstimate(flops=flops, bytes_accessed=2**20, transcendentals=0),
        name=name,
    )(*[a for a, _ in ins])


def masks():
    lane = lax.broadcasted_iota(jnp.int32, (1, 2 * HD), 1)
    return lane < HD


def both_heads(v, low):
    zero = jnp.zeros_like(v)
    return jnp.concatenate([jnp.where(low, v, zero), jnp.where(low, zero, v)], axis=0)


def softmax(scores):
    top = jnp.max(scores, axis=-1, keepdims=True)
    e = jnp.exp(scores - top)
    return e / jnp.sum(e, axis=-1, keepdims=True)


def forward_attention(layer, part_index, length, swapped, head, tau, time_weight, gain, bias, w_qkv, w_out, tables):
    first = layer == 0
    rows = sum(n for _, _, n in head) if first else head[0].shape[0]
    width = w_out.shape[2]
    local = w_out.shape[1]
    block = min(BLOCK, local)
    scale = HD ** (-0.5)
    seqs = rows // length
    parts = tau.shape[0] // seqs

    def kernel(*refs):
        it = iter(refs)
        take = lambda n: [next(it) for _ in range(n)]
        head_refs = take(len(head))
        tau_ref, tw_ref, gain_ref, bias_ref, wq_any, wo_any, cos_ref, sin_ref = take(8)
        if not first:
            x2_ref, = take(1)
        x_ref, n_ref, q_ref, k_ref, v_ref, att_ref, part_ref = take(7)
        wq, wo, sems = take(3)
        copies = [pltpu.make_async_copy(wq_any.at[layer, j], wq.at[j], sems.at[j]) for j in range(3)]
        copies.append(pltpu.make_async_copy(wo_any.at[layer], wo, sems.at[3]))
        for c in copies:
            c.start()

        def norm(at, x):
            x_ref[rows_at(at), :] = x
            xhat, _ = standardize(x)
            n_ref[rows_at(at), :] = (xhat * gain_ref[layer, 0:1, :] + bias_ref[layer, 0:1, :]).astype(bf16)

        if first:
            low = 0
            for ref, (_, begin, count) in zip(head_refs, head):
                chunks(
                    low + count,
                    lambda at, ref=ref, shift=begin - low: norm(
                        at, ref[rows_at(pl.multiple_of(at + shift, CHUNK)), :].astype(f32)
                    ),
                    low,
                )
                low += count
        else:
            x1, own, got = head_refs

            def scaled(at):
                here = rows_at(at)
                there = other_rows(at, rows, swapped)
                x2 = x1[here, :] + own[here, :].astype(f32) + got[there, :].astype(f32)
                x2_ref[here, :] = x2
                t = tau_ref[pl.ds(at // length * parts + part_index, 1), :]
                norm(at, x2 * (1.0 + t * tw_ref[layer - 1 : layer, :]))

            chunks(rows, scaled)
        for j, out in enumerate((q_ref, k_ref, v_ref)):
            copies[j].wait()
            for b in range(0, local, block):
                u = mm(n_ref[...], wq[j, :, b : b + block])
                if j < 2:
                    for s in range(0, rows, length):
                        us = u[s : s + length]
                        us = us * cos_ref[:, b : b + block] + partner(us) * sin_ref[:, b : b + block]
                        out[s : s + length, b : b + block] = us.astype(bf16)
                else:
                    out[:, b : b + block] = u.astype(bf16)
        low = masks()
        for s in range(0, rows, length):
            for b in range(0, local, 2 * HD):
                here = (slice(s, s + length), slice(b, b + 2 * HD))
                q2 = both_heads(q_ref[here], low)
                probs = softmax(mm_t(q2, k_ref[here]) * scale).astype(bf16)
                o = mm(probs, v_ref[here])
                att_ref[here] = jnp.where(low, o[:length], o[length:]).astype(bf16)
        copies[3].wait()
        for b in range(0, width, BLOCK):
            part_ref[:, b : b + BLOCK] = mm(att_ref[...], wo[:, b : b + BLOCK]).astype(bf16)

    ins = [(a[0] if first else a, False) for a in head]
    ins += [(a, False) for a in (tau, time_weight, gain, bias)] + [(w_qkv, True), (w_out, True)]
    ins += [(t, False) for t in tables]
    near = lambda n, d: ((rows, n), d, False)
    outs = [] if first else [near(width, f32)]
    outs += [near(width, f32), near(width, bf16)] + [near(local, bf16)] * 4 + [near(width, bf16)]
    scratch = [
        pltpu.VMEM((3, width, local), bf16),
        pltpu.VMEM((local, width), bf16),
        pltpu.SemaphoreType.DMA((4,)),
    ]
    return call(kernel, ins, outs, scratch, 4 * 10**9, "forward_attention")


def forward_mlp(layer, swapped, x, own, got, gain, bias, w_up, w_down):
    rows, width = x.shape
    hidden = w_up.shape[2]
    tiles = hidden // BLOCK

    def kernel(x_ref, own_ref, got_ref, gain_ref, bias_ref, wu_any, wd_any,
               x1_ref, n_ref, h_ref, slope_ref, part_ref, wu, wd, sems):
        ups = [
            pltpu.make_async_copy(
                wu_any.at[layer, :, pl.ds(t * BLOCK, BLOCK)], wu.at[t], sems.at[t]
            )
            for t in range(tiles)
        ]
        down = pltpu.make_async_copy(wd_any.at[layer], wd, sems.at[tiles])
        for c in ups:
            c.start()
        down.start()

        def norm(at):
            here = rows_at(at)
            there = other_rows(at, rows, swapped)
            x1 = x_ref[here, :] + own_ref[here, :].astype(f32) + got_ref[there, :].astype(f32)
            x1_ref[here, :] = x1
            xhat, _ = standardize(x1)
            n_ref[here, :] = (xhat * gain_ref[layer, 1:2, :] + bias_ref[layer, 1:2, :]).astype(bf16)

        chunks(rows, norm)
        for t in range(tiles):
            ups[t].wait()
            value, slope = gelu_parts(mm(n_ref[...], wu[t]))
            h_ref[:, t * BLOCK : (t + 1) * BLOCK] = value.astype(bf16)
            slope_ref[:, t * BLOCK : (t + 1) * BLOCK] = slope.astype(bf16)
        down.wait()
        for b in range(0, width, BLOCK):
            part_ref[:, b : b + BLOCK] = mm(h_ref[...], wd[:, b : b + BLOCK]).astype(bf16)

    ins = [(a, False) for a in (x, own, got, gain, bias)] + [(w_up, True), (w_down, True)]
    near = lambda n, d: ((rows, n), d, False)
    outs = [near(width, f32), near(width, bf16), near(hidden, bf16), near(hidden, bf16), near(width, bf16)]
    scratch = [
        pltpu.VMEM((tiles, width, BLOCK), bf16),
        pltpu.VMEM((hidden, width), bf16),
        pltpu.SemaphoreType.DMA((tiles + 1,)),
    ]
    return call(kernel, ins, outs, scratch, 6 * 10**9, "forward_mlp")


def backward_mlp(layer, part_index, length, swapped, head, x2, tau, time_weight, gain, slope, w_up, w_down):
    last = layer == gain.shape[0] - 1
    rows, width = x2.shape
    hidden = w_up.shape[2]
    tiles = hidden // BLOCK
    seqs = rows // length
    parts = tau.shape[0] // seqs

    def kernel(*refs):
        it = iter(refs)
        take = lambda n: [next(it) for _ in range(n)]
        head_refs = take(len(head))
        x2_ref, tau_ref, tw_ref, gain_ref, slope_ref, wu_any, wd_any = take(7)
        g2_ref, gm_ref, du_ref, part_ref, sums_ref = take(5)
        wu, wd, sems = take(3)
        downs = [
            pltpu.make_async_copy(
                wd_any.at[layer, pl.ds(t * BLOCK, BLOCK), :], wd.at[t], sems.at[t]
            )
            for t in range(tiles)
        ]
        up = pltpu.make_async_copy(wu_any.at[layer], wu, sems.at[tiles])
        for c in downs:
            c.start()
        up.start()
        sums_ref[...] = jnp.zeros_like(sums_ref)

        def begin(at, g):
            here = rows_at(at)
            t = tau_ref[pl.ds(at // length * parts + part_index, 1), :]
            sums_ref[16:24, :] += fold(g * x2_ref[here, :]) * t
            g2 = g * (1.0 + t * tw_ref[layer : layer + 1, :])
            g2_ref[here, :] = g2
            gm_ref[here, :] = g2.astype(bf16)

        if last:
            low = 0
            for ref, (_, start, count) in zip(head_refs, head):
                chunks(
                    low + count,
                    lambda at, ref=ref, shift=start - low: begin(
                        at, ref[rows_at(pl.multiple_of(at + shift, CHUNK)), :].astype(f32)
                    ),
                    low,
                )
                low += count
        else:
            g1, x, own, got = head_refs

            def through_norm(at):
                here = rows_at(at)
                dn = own[here, :].astype(f32) + got[other_rows(at, rows, swapped), :].astype(f32)
                xhat, inverse = standardize(x[here, :])
                sums_ref[0:8, :] += fold(dn * xhat)
                sums_ref[8:16, :] += fold(dn)
                begin(at, g1[here, :] + norm_backward(dn, xhat, inverse, gain_ref[layer + 1, 0:1, :]))

            chunks(rows, through_norm)
        for t in range(tiles):
            downs[t].wait()
            at = slice(t * BLOCK, (t + 1) * BLOCK)
            dh = mm_t(gm_ref[...], wd[t])
            du_ref[:, at] = (dh * slope_ref[:, at].astype(f32)).astype(bf16)
        up.wait()
        for b in range(0, width, BLOCK):
            part_ref[:, b : b + BLOCK] = mm_t(du_ref[...], wu[b : b + BLOCK, :]).astype(bf16)

    ins = [(a[0] if last else a, False) for a in head]
    ins += [(a, False) for a in (x2, tau, time_weight, gain, slope)]
    ins += [(w_up, True), (w_down, True)]
    near = lambda n, d: ((rows, n), d, False)
    outs = [near(width, f32), near(width, bf16), near(hidden, bf16), near(width, bf16)]
    outs += [((24, width), f32, False)]
    scratch = [
        pltpu.VMEM((width, hidden), bf16),
        pltpu.VMEM((tiles, BLOCK, width), bf16),
        pltpu.SemaphoreType.DMA((tiles + 1,)),
    ]
    return call(kernel, ins, outs, scratch, 6 * 10**9, "backward_mlp")


def backward_attention(layer, length, swapped, g2, x1, own, got, gain, q, k, v, w_qkv, w_out, tables):
    rows, width = x1.shape
    local = w_out.shape[1]
    block = min(BLOCK, local)
    scale = HD ** (-0.5)

    def kernel(g2_ref, x1_ref, own_ref, got_ref, gain_ref, q_ref, k_ref, v_ref, wq_any, wo_any, cos_ref, sin_ref,
               g1_ref, ga_ref, dq_ref, dk_ref, dv_ref, part_ref, sums_ref, wq, wo, do_ref, sems):
        copies = [pltpu.make_async_copy(wo_any.at[layer], wo, sems.at[3])]
        copies += [pltpu.make_async_copy(wq_any.at[layer, j], wq.at[j], sems.at[j]) for j in range(3)]
        for c in copies:
            c.start()
        sums_ref[...] = jnp.zeros_like(sums_ref)

        def begin(at):
            here = rows_at(at)
            dn = own_ref[here, :].astype(f32) + got_ref[other_rows(at, rows, swapped), :].astype(f32)
            xhat, inverse = standardize(x1_ref[here, :])
            sums_ref[0:8, :] += fold(dn * xhat)
            sums_ref[8:16, :] += fold(dn)
            g1 = g2_ref[here, :] + norm_backward(dn, xhat, inverse, gain_ref[layer, 1:2, :])
            g1_ref[here, :] = g1
            ga_ref[here, :] = g1.astype(bf16)

        chunks(rows, begin)
        copies[0].wait()
        for b in range(0, local, block):
            do_ref[:, b : b + block] = mm_t(ga_ref[...], wo[b : b + block, :]).astype(bf16)
        low = masks()
        for s in range(0, rows, length):
            for b in range(0, local, 2 * HD):
                here = (slice(s, s + length), slice(b, b + 2 * HD))
                lanes = slice(b, b + 2 * HD)
                keys = k_ref[here]
                q2 = both_heads(q_ref[here], low)
                do2 = both_heads(do_ref[here], low)
                probs = softmax(mm_t(q2, keys) * scale)
                dp = mm_t(do2, v_ref[here])
                ds = probs * (dp - jnp.sum(probs * dp, axis=-1, keepdims=True))
                ds = ds.astype(bf16)
                dv_ref[here] = across(probs.astype(bf16), do2).astype(bf16)
                dq = mm(ds, keys) * scale
                dq = jnp.where(low, dq[:length], dq[length:])
                dk = across(ds, q2) * scale
                for d, out in ((dq, dq_ref), (dk, dk_ref)):
                    out[here] = (d * cos_ref[:, lanes] + partner(d * sin_ref[:, lanes])).astype(bf16)
        for c in copies[1:]:
            c.wait()
        for b in range(0, width, BLOCK):
            at = slice(b, b + BLOCK)
            part = mm_t(dq_ref[...], wq[0, at, :]) + mm_t(dk_ref[...], wq[1, at, :])
            part_ref[:, at] = (part + mm_t(dv_ref[...], wq[2, at, :])).astype(bf16)

    ins = [(a, False) for a in (g2, x1, own, got, gain, q, k, v)] + [(w_qkv, True), (w_out, True)]
    ins += [(t, False) for t in tables]
    near = lambda n, d: ((rows, n), d, False)
    outs = [near(width, f32), near(width, bf16)] + [near(local, bf16)] * 3
    outs += [near(width, bf16), ((16, width), f32, False)]
    scratch = [
        pltpu.VMEM((3, width, local), bf16),
        pltpu.VMEM((local, width), bf16),
        pltpu.VMEM((rows, local), bf16),
        pltpu.SemaphoreType.DMA((4,)),
    ]
    return call(kernel, ins, outs, scratch, 7 * 10**9, "backward_attention")


class Links:
    def __init__(self, dp, tensor):
        self.dp, self.tensor = dp, tensor
        self.chips = dp // 2
        self.ring = dp == 16
        self.walk = [0, 2, 4, 6, 7, 5, 3, 1]
        place = [self.walk.index(i) for i in range(8)]
        self.place = place
        self.ring_pairs = []
        for k in range(8):
            here, there = self.walk[k], self.walk[(k + 1) % 8]
            self.ring_pairs.append((2 * here, 2 * there))
            self.ring_pairs.append((2 * there + 1, 2 * here + 1))
        self.core_pairs = [(i, i ^ 1) for i in range(dp)]

    def ring_place(self):
        i = lax.axis_index("dp")
        p = jnp.asarray(self.place, jnp.int32)[i >> 1]
        return jnp.where(i & 1 == 0, p, (8 - p) % 8)

    def swap_tensor(self, v):
        return lax.ppermute(v, "tensor", [(0, 1), (1, 0)])

    def gather_tensor(self, v):
        if self.tensor != 2:
            return lax.all_gather(v, "tensor", axis=0, tiled=True)
        other = self.swap_tensor(v)
        first = lax.axis_index("tensor") == 0
        return jnp.concatenate([jnp.where(first, v, other), jnp.where(first, other, v)])

    def start_sum(self, part):
        part = part.astype(bf16)
        if self.tensor != 2:
            summed = lax.psum(part, "tensor")
            return (summed, jnp.zeros_like(summed))
        return (part, self.swap_tensor(part))

    def sum_small(self, v):
        if self.dp & (self.dp - 1):
            return lax.psum(v, "dp")
        mask = 1
        while mask < self.dp:
            v = v + lax.ppermute(v, "dp", [(i, i ^ mask) for i in range(self.dp)])
            mask *= 2
        return v


def total(parts):
    out = parts[0].astype(f32)
    for p in parts[1:]:
        out = out + p.astype(f32)
    return out


def over_rows(lefts, rights):
    out = across(lefts[0], rights[0])
    for a, b in zip(lefts[1:], rights[1:]):
        out = out + across(a, b)
    return out


def mlp_gradients(h, gm, n2, du, core, place):
    n = len(h)
    hidden, width = h[0].shape[1], gm[0].shape[1]
    half_hidden = hidden // 2
    tall = half_hidden // 8
    wide = width // 8

    def kernel(s_ref, *refs):
        hs, gms, ns, dus = [refs[n * j : n * j + n] for j in range(4)]
        for target, half, p in (
            (refs[4 * n], 1 - s_ref[0], lax.rem(8 - s_ref[1], 8)),
            (refs[4 * n + 1], s_ref[0], s_ref[1]),
        ):
            for j in range(4):
                first = pl.multiple_of(half * half_hidden + j * 2 * tall, 2 * tall)
                down = over_rows([r[:, pl.ds(first, 2 * tall)] for r in hs], [r[...] for r in gms])
                columns = pl.ds(pl.multiple_of(half * half_hidden, half_hidden), half_hidden)
                up = over_rows(
                    [r[:, j * 2 * wide : (j + 1) * 2 * wide] for r in ns], [r[:, columns] for r in dus]
                )
                for i in range(2):
                    slot = lax.rem(p - (2 * j + i) + 8, 8)
                    target[slot, 0:tall, :] = down[i * tall : (i + 1) * tall].astype(bf16)
                    target[slot, tall : tall + wide, :] = up[i * wide : (i + 1) * wide].astype(bf16)

    ins = [(jnp.stack([core, place]).astype(jnp.int32), False)]
    ins += [(v, False) for group in (h, gm, n2, du) for v in group]
    out = ((8, tall + wide, width), bf16, False)
    return call(kernel, ins, [out, out], [], 9 * 10**9, "mlp_gradients")


def attention_gradients(att, ga, n1, dq, dk, dv, core, place):
    n = len(att)
    local, width = att[0].shape[1], ga[0].shape[1]
    heads, wide = local // 2, width // 2

    def kernel(s_ref, *refs):
        atts, gas, ns = [refs[n * j : n * j + n] for j in range(3)]
        dps = [refs[n * j : n * j + n] for j in range(3, 6)]
        for target, half, p in (
            (refs[6 * n], 1 - s_ref[0], lax.rem(8 - s_ref[1], 8)),
            (refs[6 * n + 1], s_ref[0], s_ref[1]),
        ):

            def put(value, low, size):
                for b in range(8):
                    slot = lax.rem(p - b + 8, 8)
                    target[slot, low : low + size, :] = value[b * size : (b + 1) * size].astype(bf16)

            lefts = [r[:, pl.ds(pl.multiple_of(half * heads, heads), heads)] for r in atts]
            for j in range(2):
                put(over_rows(lefts, [r[:, j * wide : (j + 1) * wide] for r in gas]), heads // 8 * j, heads // 8)
            lefts = [r[:, pl.ds(pl.multiple_of(half * wide, wide), wide)] for r in ns]
            for j in range(3):
                put(over_rows(lefts, [r[...] for r in dps[j]]), heads // 4 + wide // 8 * j, wide // 8)

    ins = [(jnp.stack([core, place]).astype(jnp.int32), False)]
    ins += [(v, False) for group in (att, ga, n1, dq, dk, dv) for v in group]
    out = ((8, heads // 4 + 3 * wide // 8, local), bf16, False)
    return call(kernel, ins, [out, out], [], 5 * 10**9, "attention_gradients")


def pack(blocks):
    def kernel(*refs):
        for i, r in enumerate(refs[:-1]):
            refs[-1][i] = r[...]

    out = ((len(blocks),) + blocks[0].shape, bf16, False)
    return call(kernel, [(v, False) for v in blocks], [out], [], 10**9, "pack")[0]


DEEP = 4


def spread(pieces, shapes, mine, peer, core, place, before):
    depth, width = mine.shape[1:]

    def kernel(s_ref, mine_ref, peer_ref, *refs):
        held, sems = refs[-2:]
        outs = refs[len(refs) - 2 - len(shapes) : -2]

        def copies(i):
            half, p = (s_ref[0], s_ref[1]) if i < 8 else (1 - s_ref[0], lax.rem(8 - s_ref[1], 8))
            b = lax.rem(p + 1 - i % 8 + 8, 8)
            return [
                pltpu.make_async_copy(
                    held.at[(i % DEEP,) + source], outs[o].at[place], sems.at[i % DEEP, j]
                )
                for j, (source, o, place) in enumerate(pieces(half, b))
            ]

        for i in range(16):
            if i >= DEEP:
                for c in copies(i - DEEP):
                    c.wait()
            held[i % DEEP] = (mine_ref if i < 8 else peer_ref)[i % 8].astype(f32)
            for c in copies(i):
                c.start()
        for i in range(16 - DEEP, 16):
            for c in copies(i):
                c.wait()

    ins = [(jnp.stack([core, place]).astype(jnp.int32), False), (mine, False), (peer, False)]
    aliases = {}
    if before is not None:
        for j, v in enumerate(before):
            aliases[len(ins)] = j
            ins.append((v, True))
    scratch = [
        pltpu.VMEM((DEEP, depth, width), f32),
        pltpu.SemaphoreType.DMA((DEEP, len(pieces(0, 0)))),
    ]
    outs = [(s, f32, True) for s in shapes]
    return call(kernel, ins, outs, scratch, 5 * 10**9, "spread", aliases)


def mlp_pieces(layer, layers, hidden, width):
    tall, wide = hidden // 16, width // 8

    def pieces(half, b):
        rows = pl.ds(pl.multiple_of(half * (hidden // 2) + b * tall, tall), tall)
        across_rows = pl.ds(pl.multiple_of(b * wide, wide), wide)
        columns = pl.ds(pl.multiple_of(half * (hidden // 2), hidden // 2), hidden // 2)
        return [
            ((slice(0, tall), slice(None)), 0, (layer, rows, slice(None))),
            ((slice(tall, tall + wide), slice(None)), 1, (layer, across_rows, columns)),
        ]

    return pieces, [(layers, hidden, width), (layers, width, hidden)]


def attention_pieces(layer, layers, local, width):
    tall, wide = local // 16, width // 16

    def pieces(half, b):
        rows = pl.ds(pl.multiple_of(half * (local // 2) + b * tall, tall), tall)
        deep = pl.ds(pl.multiple_of(half * (width // 2) + b * wide, wide), wide)
        out = []
        for j in range(2):
            columns = slice(j * width // 2, (j + 1) * width // 2)
            out.append(((slice(tall * j, tall * (j + 1)), slice(None)), 0, (layer, rows, columns)))
        for j in range(3):
            low = 2 * tall + wide * j
            out.append(((slice(low, low + wide), slice(None)), 1, (layer, j, deep, slice(None))))
        return out

    return pieces, [(layers, local, width), (layers, 3, width, local)]


class Stream:
    def __init__(self, links, kind, layer, layers, groups):
        self.links = links
        self.steps = 0
        self.core = lax.axis_index("dp") & 1
        self.p = links.ring_place()
        if kind == "mlp":
            send, self.keep = mlp_gradients(*groups, self.core, self.p)
            self.layout = mlp_pieces(layer, layers, groups[0][0].shape[1], groups[1][0].shape[1])
        else:
            send, self.keep = attention_gradients(*groups, self.core, self.p)
            self.layout = attention_pieces(layer, layers, groups[0][0].shape[1], groups[1][0].shape[1])
        self.got = lax.ppermute(send, "dp", links.core_pairs)
        self.cur = None
        self.done = []

    def step(self):
        if self.steps >= 14:
            return
        if self.cur is None:
            self.cur = (self.keep[0].astype(f32) + self.got[0].astype(f32)).astype(bf16)
        got = lax.ppermute(self.cur, "dp", self.links.ring_pairs)
        self.steps += 1
        if self.steps < 8:
            i = self.steps
            got = got.astype(f32) + self.keep[i].astype(f32) + self.got[i].astype(f32)
            got = got.astype(bf16)
        self.cur = got
        if self.steps >= 7:
            self.done.append(got)

    def state(self):
        return (self.keep, self.got) if self.cur is None else (self.cur,)

    def set_state(self, st):
        if self.cur is None:
            self.keep, self.got = st
        else:
            self.cur, = st
            if self.done:
                self.done[-1] = self.cur

    def finish(self, before):
        while self.steps < 14:
            self.step()
        mine = pack(self.done)
        peer = lax.ppermute(mine, "dp", self.links.core_pairs)
        return spread(*self.layout, mine, peer, self.core, self.p, before)


class Plain:
    def __init__(self, links, kind, layer, layers, groups):
        self.layer, self.layers, self.steps = layer, layers, 14
        left, right, deep, *dps = [jnp.concatenate(g) for g in groups]
        out = [ein("ra,rb->ab", left, right)]
        if kind == "mlp":
            out.append(ein("ra,rb->ab", deep, dps[0]))
        else:
            out.append(jnp.stack([ein("ra,rb->ab", deep, d) for d in dps]))
        self.out = [lax.psum(v.astype(bf16), "dp").astype(f32) for v in out]

    def step(self):
        pass

    def state(self):
        return ()

    def set_state(self, st):
        pass

    def finish(self, before):
        if before is None:
            before = [jnp.zeros((self.layers,) + v.shape, f32) for v in self.out]
        return [b.at[self.layer].set(v) for b, v in zip(before, self.out)]


def make_local(links):
    def local(
        tokens,
        time_index,
        time_table,
        norm_gain,
        norm_bias,
        w_qkv,
        w_out,
        w_up,
        w_down,
        time_weight,
        cotangent,
    ):
        rows, width = tokens.shape
        seq_here = time_index.shape[0]
        length = rows // seq_here
        layers = norm_gain.shape[0]
        local_width = w_out.shape[1]
        tables = rope_tables(length, local_width)
        parts = 2 if seq_here % 2 == 0 else 1
        own = rows // parts
        paired = links.tensor == 2
        wq = jnp.transpose(w_qkv, (0, 2, 1, 3))

        def group_rows(v, m):
            if paired:
                got = links.swap_tensor(v[m * own : (m + 1) * own])
                return [(v, m * own, own), (got, 0, own)]
            v = links.gather_tensor(v[m * own : (m + 1) * own])
            return [(v, 0, v.shape[0])]

        heads = [group_rows(tokens, m) for m in range(parts)]
        if paired:
            index = jnp.concatenate([time_index, links.swap_tensor(time_index)])
        else:
            index = links.gather_tensor(time_index)
        onehot = (index[:, None] == jnp.arange(time_table.shape[0], dtype=jnp.int32)[None, :]).astype(f32)
        tau = jnp.dot(onehot, time_table, precision=lax.Precision.HIGHEST)
        saved = [[None] * parts for _ in range(layers)]
        after = [[None] * parts for _ in range(layers)]
        for l in range(layers):
            for m in range(parts):
                out = forward_attention(
                    l, m, length, paired, heads[m], tau, time_weight, norm_gain, norm_bias, wq, w_out, tables
                )
                if l > 0:
                    after[l - 1][m], out = out[0], out[1:]
                x, n1, q, k, v, att, part = out
                saved[l][m] = [x, n1, q, k, v, att, links.start_sum(part)]
            for m in range(parts):
                x, n1, q, k, v, att, summed = saved[l][m]
                x1, n2, h, slope, part = forward_mlp(
                    l, paired, x, *summed, norm_gain, norm_bias, w_up, w_down
                )
                saved[l][m] = (x, n1, q, k, v, att, x1, n2, h, slope)
                heads[m] = (x1, *links.start_sum(part))
        gs = [group_rows(cotangent, m) for m in range(parts)]

        def meet(v):
            return jnp.roll(v, v.shape[0] // 2, axis=0) if paired else v

        result = []
        for m in range(parts):
            x1, mine_part, got = heads[m]
            x2 = x1 + mine_part.astype(f32) + meet(got).astype(f32)
            after[layers - 1][m] = x2
            t = tau.reshape(-1, parts, 1, width)[:, m]
            scaled = x2.reshape(-1, length, width) * (1.0 + t * time_weight[layers - 1])
            result.append(scaled.reshape(x2.shape))
        kind = Stream if links.ring else Plain
        small = [[0.0] * 5 for _ in range(layers)]
        streams = []

        def add_sums(l, first, sums):
            for j in range(sums.shape[0] // 8):
                small[l][first[j]] += jnp.sum(sums[8 * j : 8 * j + 8], axis=0)

        keep = lambda l, i: [s[i] for s in saved[l]]

        def sync(live):
            going = [s for s in streams if s.steps < 14]
            for s in going:
                s.step()
            leaves, tree = jax.tree.flatten(live)
            arrays = [i for i, v in enumerate(leaves) if not isinstance(v, int)]
            held, states = lax.optimization_barrier(([leaves[i] for i in arrays], [s.state() for s in going]))
            for s, st in zip(going, states):
                s.set_state(st)
            for i, v in zip(arrays, held):
                leaves[i] = v
            return jax.tree.unflatten(tree, leaves)

        for l in reversed(range(layers)):
            g2s, gms, dus, sums = [None] * parts, [None] * parts, [None] * parts, [None] * parts
            for m in range(parts):
                g2, gm, du, part, s = backward_mlp(
                    l, m, length, paired, gs[m], after[l][m], tau, time_weight, norm_gain, saved[l][m][9], w_up, w_down
                )
                if l < layers - 1:
                    add_sums(l + 1, (0, 2), s[0:16])
                add_sums(l, (4,), s[16:24])
                if m == 0:
                    part, gs[1:] = sync((part, gs[1:]))
                else:
                    part, sums[:m] = sync((part, sums[:m]))
                g2s[m], gms[m], dus[m], sums[m] = g2, gm, du, links.start_sum(part)
            groups = [keep(l, 8), gms, keep(l, 7), dus]
            stream = kind(links, "mlp", l, layers, groups)
            if links.ring:
                (sums, stream.keep) = sync((sums, stream.keep))
            streams.append(stream)
            gas, dps = [None] * parts, [None] * parts
            for m in range(parts):
                x, n1, q, k, v, att, x1 = saved[l][m][:7]
                g1, gas[m], dq, dk, dv, part, s = backward_attention(
                    l, length, paired, g2s[m], x1, *sums[m], norm_gain, q, k, v, wq, w_out, tables
                )
                add_sums(l, (1, 3), s)
                dps[m] = (dq, dk, dv)
                if m == 0:
                    part, sums[1:] = sync((part, sums[1:]))
                else:
                    part, gs[:m] = sync((part, gs[:m]))
                gs[m] = (g1, x, *links.start_sum(part))
            groups = [keep(l, 5), gas, keep(l, 1)] + [[d[j] for d in dps] for j in range(3)]
            stream = kind(links, "attention", l, layers, groups)
            if links.ring:
                (gs, stream.keep) = sync((gs, stream.keep))
            streams.append(stream)
        inputs = []
        for m in range(parts):
            g1, x, mine_part, got = gs[m]
            dn1 = mine_part.astype(f32) + meet(got).astype(f32)
            xhat, inverse = standardize(x)
            small[0][0] += jnp.sum(dn1 * xhat, axis=0)
            small[0][2] += jnp.sum(dn1, axis=0)
            inputs.append((g1 + norm_backward(dn1, xhat, inverse, norm_gain[0, 0])))
        tiny = jnp.stack([jnp.stack(a) for a in small])
        tiny = links.sum_small(tiny)
        written = {}
        for j, s in enumerate(streams):
            written[j % 2] = s.finish(written.get(j % 2))
        if paired:
            mine = lambda vs: jnp.concatenate([v[:own] for v in vs])
        else:
            t = lax.axis_index("tensor")
            mine = lambda vs: jnp.concatenate([lax.dynamic_slice_in_dim(v, t * own, own) for v in vs])
        gains, biases = tiny[:, 0:2], tiny[:, 2:4]
        return (
            mine(result),
            mine(inputs),
            gains,
            biases,
            jnp.transpose(written[1][1], (0, 2, 1, 3)),
            written[1][0],
            written[0][1],
            written[0][0],
            tiny[:, 4],
            jnp.stack([gains[layers - 1, 1], biases[layers - 1, 1]]),
        )

    return local


def solution(mesh):
    links = Links(mesh.shape["dp"], mesh.shape["tensor"])
    token_spec = P(("dp", "tensor"), None)
    in_specs = (
        token_spec,
        P(("dp", "tensor")),
        P(),
        P(),
        P(),
        P(None, None, None, "tensor"),
        P(None, "tensor", None),
        P(None, None, "tensor"),
        P(None, "tensor", None),
        P(),
        token_spec,
    )
    out_specs = (
        token_spec,
        token_spec,
        P(),
        P(),
        P(None, None, None, "tensor"),
        P(None, "tensor", None),
        P(None, None, "tensor"),
        P(None, "tensor", None),
        P(),
        P(),
    )
    return jax.shard_map(
        make_local(links), mesh=mesh, in_specs=in_specs, out_specs=out_specs, check_vma=False
    )
```

time: 983 us -> 591 us (0.60)
  waiting for transfers between devices: 682 us -> 185 us
  Pallas kernels: 0 us -> 171 us
  matrix products: 119 us -> 0.46 us
  starting transfers between devices: 1.9 us -> 113 us
  blocking collectives: 42.1 us -> 0 us
  other arithmetic: 69.8 us -> 46.5 us
  local copies, waits for them, and re-layouts: 44.3 us -> 60.4 us
  between operations: 15.1 us -> 4.85 us
    psum x1 -> x0, waiting for transfers between devices: 404 us -> none  [local(): lax.psum(grad_qkv.astype(jnp.bfloat16), 'dp').astype(jnp.float32)]
    ppermute x0 -> x89, waiting for transfers between devices: none -> 185 us  [the longest x56 117 us: step(): got = lax.ppermute(self.cur, 'dp', self.links.ring_pairs)]
    pallas_call x0 -> x28, Pallas kernels: none -> 171 us  [call(): pl.pallas_call(kernel, out_shape=[jax.ShapeDtypeStruct(s, d) for s, d, _...]
    all_gather x8 -> x0, waiting for transfers between devices: 139 us -> none  [the longest x2 41.7 us: local(): lax.all_gather(second_normalized_rows, 'tensor', axis=0, tiled=True)]
    reduce_scatter x8 -> x0, waiting for transfers between devices: 138 us -> none  [the longest x2 42.7 us: local(): lax.psum_scatter(jnp.dot(hidden, down_local, preferred_element_type=jnp.f...]
    dot_general x37 -> x1, matrix products: 119 us -> 0.46 us  [local(): tau = jnp.dot(onehot, time_table, precision=lax.Precision.HIGHEST)]
    ppermute x0 -> x89, starting transfers between devices: none -> 113 us  [the longest x56 80.7 us: step(): got = lax.ppermute(self.cur, 'dp', self.links.ring_pairs)]
    psum x1 -> x0, blocking collectives: 42.1 us -> none  [local(): lax.psum((jnp.stack(gain_grads, axis=0), jnp.stack(bias_grads, axis=0), j...]
  transfers between devices with their start and end apart: 17 -> 89, of which waited for: 16 -> 47; matrix products, arithmetic and copies ran while one was open for 7% -> 9% of each run, Pallas kernels for 0% -> 24%
where the time goes in v1:
time: 591 us; the launch traced here: 581 us
  waiting for transfers between devices  185 us (31%)
  Pallas kernels  171 us (29%)
  starting transfers between devices  113 us (19%)
  local copies, waits for them, and re-layouts  60.4 us (10%)
  other arithmetic  46.5 us (8%)
    pallas_call x28, Pallas kernels, call(): pl.pallas_call(kernel, out_shape=[jax.ShapeDtypeStruct(s, d) for s, d, _...  171 us
    ppermute x56, waiting for transfers between devices, step(): got = lax.ppermute(self.cur, 'dp', self.links.ring_pairs)  117 us
    ppermute x56, starting transfers between devices, step(): got = lax.ppermute(self.cur, 'dp', self.links.ring_pairs)  80.7 us
    ppermute x21, waiting for transfers between devices, swap_tensor(): return lax.ppermute(v, 'tensor', [(0, 1), (1, 0)])  63.7 us
    unnamed x370, local copies, waits for them, and re-layouts  52.6 us
    convert_element_type x28, other arithmetic, step(): got = got.astype(bf16)  33.3 us
    ppermute x21, starting transfers between devices, swap_tensor(): return lax.ppermute(v, 'tensor', [(0, 1), (1, 0)])  27.5 us
  transfers between devices with their start and end apart: 89, of which 47 were waited for; matrix products, arithmetic and copies ran while one was open for 9% of the time, Pallas kernels for 24%

profile of v1, /device:TPU:0, one launch (start us, length us, event | category | flops | bytes accessed | tf_op | source)
XLA Modules:
  0.0 581.1 jit_solution(6022921740545389068)
XLA Ops:
  0.7 3.0 collective-permute-start.1
  9.9 4.8 collective-permute-done.refs_1_
  18.8 2.8 copy-done.60
  24.9 5.0 forward_attention.4
  32.9 6.2 %forward_attention.6 = (f32[256,1024]{1,0:T(8,128)S(1)}, bf16[256,1024]{1,0:T(8,128)(2,1)S(1)}, bf16[256,512]{1,0:T(8,128)(2,1)S(1)}, bf16[256,512]{1,0:T(8,128)...) custom-call(bf16[256,1024]{1,0:T(8,128)(2,1)S(1)} %copy-done.24, ...), custom_call_target="tpu_custom_call" | custom-call | flops 4000000000 | bytes 1048576 | tf_op jit(solution)/shard_map/forward_attention/pallas_call | solution.py:107
  39.9 2.4 collective-permute-start.7
  42.3 4.9 collective-permute-done.2.got_ref
  47.2 8.0 %forward_mlp.4 = (f32[256,1024]{1,0:T(8,128)S(1)}, bf16[256,1024]{1,0:T(8,128)(2,1)S(1)}, bf16[256,2048]{1,0:T(8,128)(2,1)S(1)}, bf16[256,2048]{1,0:T(8,128)(2,1)S(1)}, bf16[256,1024]{1,0:T(8,128)(2,1)S(1)}) custom-call(f32[256,1024]{1,0:T(8,128)S(1)} %get-tuple-element.362.x_ref, bf16[256,1024]{1,0:T(8,128)(2,1)S(1)} %get-tuple-element.201.own_ref, ...), custom_call_target="tpu_custom_call" | custom-call | flops 6000000000 | bytes 1048576 | tf_op jit(solution)/shard_map/forward_mlp/pallas_call | solution.py:107
  58.2 9.0 %forward_mlp.6 = (f32[256,1024]{1,0:T(8,128)S(1)}, bf16[256,1024]{1,0:T(8,128)(2,1)S(1)}, bf16[256,2048]{1,0:T(8,128)(2,1)S(1)}, bf16[256,2048]{1,0:T(8,128)(2,1)S(1)}, bf16[256,1024]{1,0:T(8,128)(2,1)}) custom-call(f32[256,1024]{1,0:T(8,128)S(1)} %get-tuple-element.366.x_ref, bf16[256,1024]{1,0:T(8,128)(2,1)S(1)} %get-tuple-element.209.own_ref, ...), custom_call_target="tpu_custom_call" | custom-call | flops 6000000000 | bytes 1048576 | tf_op jit(solution)/shard_map/forward_mlp/pallas_call | solution.py:107
  69.3 6.0 %forward_attention.5 = (f32[256,1024]{1,0:T(8,128)S(1)}, f32[256,1024]{1,0:T(8,128)S(1)}, bf16[256,1024]{1,0:T(8,128)(2,1)S(1)}, bf16[256,512]{1,0:T(8,128)(2,1)...) custom-call(f32[256,1024]{1,0:T(8,128)S(1)} %get-tuple-element.202.r, ...), custom_call_target="tpu_custom_call" | custom-call | flops 4000000000 | bytes 1048576 | tf_op jit(solution)/shard_map/forward_attention/pallas_call | solution.py:107
  87.8 2.8 copy-done.61
  93.4 6.4 %forward_attention.7 = (f32[256,1024]{1,0:T(8,128)S(1)}, f32[256,1024]{1,0:T(8,128)S(1)}, bf16[256,1024]{1,0:T(8,128)(2,1)S(1)}, bf16[256,512]{1,0:T(8,128)(2,1)...) custom-call(f32[256,1024]{1,0:T(8,128)S(1)} %copy-done.93, ...), custom_call_target="tpu_custom_call" | custom-call | flops 4000000000 | bytes 1048576 | tf_op jit(solution)/shard_map/forward_attention/pallas_call | solution.py:107
  104.8 3.4 copy-done.57
  108.2 3.4 copy-done.58
  111.6 9.6 %forward_mlp.5 = (f32[256,1024]{1,0:T(8,128)S(1)}, bf16[256,1024]{1,0:T(8,128)(2,1)S(1)}, bf16[256,2048]{1,0:T(8,128)(2,1)S(1)}, bf16[256,2048]{1,0:T(8,128)(2,1)S(1)}, bf16[256,1024]{1,0:T(8,128)(2,1)S(1)}) custom-call(f32[256,1024]{1,0:T(8,128)S(1)} %copy-done.78, bf16[256,1024]{1,0:T(8,128)(2,1)} %get-tuple-element.205.own_ref, ...), custom_call_target="tpu_custom_call" | custom-call | flops 6000000000 | bytes 1048576 | tf_op jit(solution)/shard_map/forward_mlp/pallas_call | solution.py:107
  123.0 8.1 %forward_mlp.7 = (f32[256,1024]{1,0:T(8,128)S(1)}, bf16[256,1024]{1,0:T(8,128)(2,1)S(1)}, bf16[256,2048]{1,0:T(8,128)(2,1)S(1)}, bf16[256,2048]{1,0:T(8,128)(2,1)S(1)}, bf16[256,1024]{1,0:T(8,128)(2,1)S(1)}) custom-call(f32[256,1024]{1,0:T(8,128)S(1)} %get-tuple-element.291.x_ref.refs_1_, bf16[256,1024]{1,0:T(8,128)(2,1)S(1)} %get-tuple-element.213.own_ref, ...), custom_call_target="tpu_custom_call" | custom-call | flops 6000000000 | bytes 1048576 | tf_op jit(solution)/shard_map/forward_mlp/pallas_call | solution.py:107
  131.6 3.6 collective-permute-done.5
  135.6 6.9 %backward_mlp.4 = (f32[256,1024]{1,0:T(8,128)S(1)}, bf16[256,1024]{1,0:T(8,128)(2,1)S(1)}, bf16[256,2048]{1,0:T(8,128)(2,1)S(1)}, bf16[256,1024]{1,0:T(8,128)(2,1)S(1)}, f32[24,1024]{1,0:T(8,128)S(1)}) custom-call(bf16[256,1024]{1,0:T(8,128)(2,1)S(1)} %copy-done.26, bf16[128,1024]{1,0:T(8,128)(2,1)} %collective-permute-done.11.refs_1_, ...), custom_call_target="tpu_custom_call" | custom-call | flops 6000000000 | bytes 1048576 | tf_op jit(solution)/shard_map/backward_mlp/pallas_call | solution.py:107
  143.5 7.3 %backward_mlp.5 = (f32[256,1024]{1,0:T(8,128)S(1)}, bf16[256,1024]{1,0:T(8,128)(2,1)S(1)}, bf16[256,2048]{1,0:T(8,128)(2,1)S(1)}, bf16[256,1024]{1,0:T(8,128)(2,1)S(1)}, f32[24,1024]{1,0:T(8,128)S(1)}) custom-call(bf16[256,1024]{1,0:T(8,128)(2,1)S(1)} %copy-done.26, bf16[128,1024]{1,0:T(8,128)(2,1)} %collective-permute-done.12.refs_1_, ...), custom_call_target="tpu_custom_call" | custom-call | flops 6000000000 | bytes 1048576 | tf_op jit(solution)/shard_map/backward_mlp/pallas_call | solution.py:107
  154.3 5.5 mlp_gradients.2
  162.0 12.5 %collective-permute-done.13.got_ref = bf16[256,1024]{1,0:T(8,128)(2,1)S(1)} collective-permute-done((bf16[256,1024]{1,0:T(8,128)(2,1)S(1)}, bf16[256,1024]{1,0:T(8,128)(2,1)S(1)}, u32[]{:S(2)}, u32[]{:S(2)}) %collective-permute-start.13) | collective-permute-done | bytes 524320 | tf_op jit(solution)/shard_map/ppermute | solution.py:441
  176.2 11.9 %collective-permute-done.14.got_ref = bf16[256,1024]{1,0:T(8,128)(2,1)S(1)} collective-permute-done((bf16[256,1024]{1,0:T(8,128)(2,1)S(1)}, bf16[256,1024]{1,0:T(8,128)(2,1)S(1)}, u32[]{:S(2)}, u32[]{:S(2)}) %collective-permute-start.14) | collective-permute-done | bytes 524320 | tf_op jit(solution)/shard_map/ppermute | solution.py:441
  190.2 7.8 %backward_attention.4 = (f32[256,1024]{1,0:T(8,128)S(1)}, bf16[256,1024]{1,0:T(8,128)(2,1)S(1)}, bf16[256,512]{1,0:T(8,128)(2,1)S(1)}, bf16[256,512]{1,0:T(8,128...) custom-call(f32[256,1024]{1,0:T(8,128)S(1)} %copy-done.91, ...), custom_call_target="tpu_custom_call" | custom-call | flops 7000000000 | bytes 1048576 | tf_op jit(solution)/shard_map/backward_attention/pallas_call | solution.py:107
  201.5 8.1 %backward_attention.5 = (f32[256,1024]{1,0:T(8,128)S(1)}, bf16[256,1024]{1,0:T(8,128)(2,1)S(1)}, bf16[256,512]{1,0:T(8,128)(2,1)S(1)}, bf16[256,512]{1,0:T(8,128...) custom-call(f32[256,1024]{1,0:T(8,128)S(1)} %get-tuple-element.221.g2_ref, ...), custom_call_target="tpu_custom_call" | custom-call | flops 7000000000 | bytes 1048576 | tf_op jit(solution)/shard_map/backward_attention/pallas_call | solution.py:107
  209.6 2.9 attention_gradients.2
  215.9 11.1 %collective-permute-done.17.refs_3_ = bf16[256,1024]{1,0:T(8,128)(2,1)S(1)} collective-permute-done((bf16[256,1024]{1,0:T(8,128)(2,1)S(1)}, bf16[256,1024]{1,0:T(8,128)(2,1)S(1)}, u32[]{:S(2)}, u32[]{:S(2)}) %collective-permute-start.17) | collective-permute-done | bytes 524320 | tf_op jit(solution)/shard_map/ppermute | solution.py:441
  230.2 6.0 %collective-permute-done.20 = bf16[256,1024]{1,0:T(8,128)(2,1)S(1)} collective-permute-done((bf16[256,1024]{1,0:T(8,128)(2,1)S(1)}, bf16[256,1024]{1,0:T(8,128)(2,1)S(1)}, u32[]{:S(2)}, u32[]{:S(2)}) %collective-permute-start.20) | collective-permute-done | bytes 524320 | tf_op jit(solution)/shard_map/ppermute | solution.py:651
  237.5 3.2 collective-permute-done.19.refs_3_
  242.3 3.4 copy-done.59
  245.6 8.0 %backward_mlp.6 = (f32[256,1024]{1,0:T(8,128)S(1)}, bf16[256,1024]{1,0:T(8,128)(2,1)S(1)}, bf16[256,2048]{1,0:T(8,128)(2,1)S(1)}, bf16[256,1024]{1,0:T(8,128)(2,1)S(1)}, f32[24,1024]{1,0:T(8,128)S(1)}) custom-call(f32[256,1024]{1,0:T(8,128)S(1)} %copy-done.87, f32[256,1024]{1,0:T(8,128)S(1)} %copy-done.79, bf16[256,1024]{1,0:T(8,128)(2,1)S(1)} %get-tuple-element.278.refs_2_, ...), custom_call_target="tpu_custom_call" | custom-call | flops 6000000000 | bytes 1048576 | tf_op jit(solution)/shard_map/backward_mlp/pallas_call | solution.py:107
  258.7 2.7 collective-permute-done.23
  262.5 8.4 %backward_mlp.7 = (f32[256,1024]{1,0:T(8,128)S(1)}, bf16[256,1024]{1,0:T(8,128)(2,1)S(1)}, bf16[256,2048]{1,0:T(8,128)(2,1)S(1)}, bf16[256,1024]{1,0:T(8,128)(2,1)S(1)}, f32[24,1024]{1,0:T(8,128)S(1)}) custom-call(f32[256,1024]{1,0:T(8,128)S(1)} %get-tuple-element.290.refs_0_, f32[256,1024]{1,0:T(8,128)S(1)} %copy-done.83, ...), custom_call_target="tpu_custom_call" | custom-call | flops 6000000000 | bytes 1048576 | tf_op jit(solution)/shard_map/backward_mlp/pallas_call | solution.py:107
  271.0 5.5 mlp_gradients.3
  281.5 7.3 %collective-permute-done.26 = bf16[256,512]{1,0:T(8,128)(2,1)S(1)} collective-permute-done((bf16[256,512]{1,0:T(8,128)(2,1)S(1)}, bf16[256,512]{1,0:T(8,128)(2,1)S(1)}, u32[]{:S(2)}, u32[]{:S(2)}) %collective-permute-start.26) | collective-permute-done | bytes 262176 | tf_op jit(solution)/shard_map/ppermute | solution.py:651
  296.1 8.3 %collective-permute-done.29 = bf16[256,512]{1,0:T(8,128)(2,1)S(1)} collective-permute-done((bf16[256,512]{1,0:T(8,128)(2,1)S(1)}, bf16[256,512]{1,0:T(8,128)(2,1)S(1)}, u32[]{:S(2)}, u32[]{:S(2)}) %collective-permute-start.29) | collective-permute-done | bytes 262176 | tf_op jit(solution)/shard_map/ppermute | solution.py:651
  309.0 8.0 %backward_attention.6 = (f32[256,1024]{1,0:T(8,128)S(1)}, bf16[256,1024]{1,0:T(8,128)(2,1)S(1)}, bf16[256,512]{1,0:T(8,128)(2,1)S(1)}, bf16[256,512]{1,0:T(8,128...) custom-call(f32[256,1024]{1,0:T(8,128)S(1)} %copy-done.85, ...), custom_call_target="tpu_custom_call" | custom-call | flops 7000000000 | bytes 1048576 | tf_op jit(solution)/shard_map/backward_attention/pallas_call | solution.py:107
  322.2 4.4 collective-permute-done.33
  332.8 7.8 %backward_attention.7 = (f32[256,1024]{1,0:T(8,128)S(1)}, bf16[256,1024]{1,0:T(8,128)(2,1)S(1)}, bf16[256,512]{1,0:T(8,128)(2,1)S(1)}, bf16[256,512]{1,0:T(8,128...) custom-call(f32[256,1024]{1,0:T(8,128)S(1)} %get-tuple-element.296.g2_ref, ...), custom_call_target="tpu_custom_call" | custom-call | flops 7000000000 | bytes 1048576 | tf_op jit(solution)/shard_map/backward_attention/pallas_call | solution.py:107
  347.5 2.9 attention_gradients.3
  353.7 2.9 collective-permute-done.40
  358.6 6.3 %collective-permute-done.38 = bf16[256,1024]{1,0:T(8,128)(2,1)S(1)} collective-permute-done((bf16[256,1024]{1,0:T(8,128)(2,1)S(1)}, bf16[256,1024]{1,0:T(8,128)(2,1)S(1)}, u32[]{:S(2)}, u32[]{:S(2)}) %collective-permute-start.38) | collective-permute-done | bytes 524320 | tf_op jit(solution)/shard_map/ppermute | solution.py:441
  366.2 7.9 %collective-permute-done.71 = bf16[256,1024]{1,0:T(8,128)(2,1)S(1)} collective-permute-done((bf16[256,1024]{1,0:T(8,128)(2,1)S(1)}, bf16[256,1024]{1,0:T(8,128)(2,1)S(1)}, u32[]{:S(2)}, u32[]{:S(2)}) %collective-permute-start.71) | collective-permute-done | bytes 524320 | tf_op jit(solution)/shard_map/ppermute | solution.py:651
  375.7 7.9 %collective-permute-done.72 = bf16[256,1024]{1,0:T(8,128)(2,1)S(1)} collective-permute-done((bf16[256,1024]{1,0:T(8,128)(2,1)S(1)}, bf16[256,1024]{1,0:T(8,128)(2,1)S(1)}, u32[]{:S(2)}, u32[]{:S(2)}) %collective-permute-start.72) | collective-permute-done | bytes 524320 | tf_op jit(solution)/shard_map/ppermute | solution.py:651
  388.5 8.5 %collective-permute-done.47 = bf16[256,512]{1,0:T(8,128)(2,1)} collective-permute-done((bf16[256,512]{1,0:T(8,128)(2,1)S(1)}, bf16[256,512]{1,0:T(8,128)(2,1)}, u32[]{:S(2)}, u32[]{:S(2)}) %collective-permute-start.47) | collective-permute-done | bytes 262176 | tf_op jit(solution)/shard_map/ppermute | solution.py:651
  407.2 3.3 collective-permute-done.74
  413.7 5.2 collective-permute-done.49
  430.7 3.4 collective-permute-done.76.refs_2_
  437.1 2.7 collective-permute-done.84.refs_4_
  453.8 2.8 collective-permute-done.85.refs_5_
  462.5 2.5 collective-permute-done.78.refs_4_
  469.4 4.0 collective-permute-done.86.refs_6_
  480.3 4.3 collective-permute-done.64.refs_2_
  487.4 5.6 collective-permute-done.54.refs_1_
  499.7 3.8 pack.7.mine_ref
  507.1 3.6 fusion.14
  513.8 5.2 collective-permute-done.67.refs_5_
  530.2 3.3 collective-permute-done.69.refs_7_
  538.7 4.2 collective-permute-done.60.refs_7_
  545.5 2.7 collective-permute-done.44
  550.9 2.3 collective-permute-done.45
  555.7 4.5 spread.4
  560.2 4.5 spread.5
  564.7 9.4 %spread.6 = (f32[2,2048,1024]{2,1,0:T(8,128)}, f32[2,1024,2048]{2,1,0:T(8,128)}) custom-call(s32[2]{0:T(128)S(1)} %pad_add_fusion.1.s_ref, bf16[8,256,1024]{2,1,0:T(8,128)(2,1)} %pack.7.mine_ref, bf16[8,256,1024]{2,1,0:T(8,128)(2,1)} %collective-permute-done.88.peer_ref), custom_call_target="tpu_custom_call" | custom-call | flops 5000000000 | bytes 1048576 | tf_op jit(solution)/shard_map/spread/pallas_call | solution.py:107
  574.1 6.5 %spread.7 = (f32[2,2048,1024]{2,1,0:T(8,128)}, f32[2,1024,2048]{2,1,0:T(8,128)}) custom-call(s32[2]{0:T(128)S(1)} %pad_add_fusion.1.s_ref, bf16[8,256,1024]{2,1,0:T(8,128)(2,1)S(1)} %pack.6.mine_ref, bf16[8,256,1024]{2,1,0:T(8,128)(2,1)S(1)} %collective-permute-done.82.peer_ref, ...), custom_call_target="tpu_custom_call", output_to_operand_aliasing={{0}: (3, {}), {1}: (4, {})} | custom-call | flops 5000000000 | bytes 1048576 | tf_op jit(solution)/shard_map/spread/pallas_call | solution.py:107
  (626 shorter events, 219.6 us)
Async XLA Ops:
  5.5 27.3 %collective-permute-start.6 = (bf16[128,1024]{1,0:T(8,128)(2,1)}, bf16[128,1024]{1,0:T(8,128)(2,1)}, u32[]{:S(2)}, u32[]{:S(2)}) collective-permute-start(bf16[128,1024]{1,0:T(8,128)(2,1)} %get-tuple-element.445), channel_id=1, source_target_pairs={{0,1},{1,0},{2,3},{3,2},{4,5},{5,4},{6,7},{7,6},{8,9},{9,8},{10,11... | collective-permute-start | bytes 786440 | tf_op jit(solution)/shard_map/ppermute | solution.py:441
  32.8 14.4 %collective-permute-start.2 = (bf16[256,1024]{1,0:T(8,128)(2,1)S(1)}, bf16[256,1024]{1,0:T(8,128)(2,1)S(1)}, u32[]{:S(2)}, u32[]{:S(2)}) collective-permute-start(bf16[256,1024]{1,0:T(8,128)(2,1)S(1)} %get-tuple-element.201.own_ref), channel_id=1, source_target_pairs={{0,1},{1,0},{2,3},{3,2},{4,5},{5,4},{6,7},{7,6},{8,9},{9,8},{10,11... | collective-permute-start | bytes 1572872 | tf_op jit(solution)/shard_map/ppermute | solution.py:441
  39.9 18.3 %collective-permute-start.7 = (bf16[256,1024]{1,0:T(8,128)(2,1)S(1)}, bf16[256,1024]{1,0:T(8,128)(2,1)S(1)}, u32[]{:S(2)}, u32[]{:S(2)}) collective-permute-start(bf16[256,1024]{1,0:T(8,128)(2,1)S(1)} %get-tuple-element.209.own_ref), channel_id=1, source_target_pairs={{0,1},{1,0},{2,3},{3,2},{4,5},{5,4},{6,7},{7,6},{8,9},{9,8},{10,11... | collective-permute-start | bytes 1572872 | tf_op jit(solution)/shard_map/ppermute | solution.py:441
  56.3 13.1 %collective-permute-start.3 = (bf16[256,1024]{1,0:T(8,128)(2,1)S(1)}, bf16[256,1024]{1,0:T(8,128)(2,1)S(1)}, u32[]{:S(2)}, u32[]{:S(2)}) collective-permute-start(bf16[256,1024]{1,0:T(8,128)(2,1)S(1)} %get-tuple-element.203.refs_1_), channel_id=1, source_target_pairs={{0,1},{1,0},{2,3},{3,2},{4,5},{5,4},{6,7},{7,6},{8,9},{9,8},{10,11... | collective-permute-start | bytes 1572872 | tf_op jit(solution)/shard_map/ppermute | solution.py:441
  69.2 17.6 %collective-permute-start.8 = (bf16[256,1024]{1,0:T(8,128)(2,1)}, bf16[256,1024]{1,0:T(8,128)(2,1)}, u32[]{:S(2)}, u32[]{:S(2)}) collective-permute-start(bf16[256,1024]{1,0:T(8,128)(2,1)} %get-tuple-element.211.refs_1_), channel_id=1, source_target_pairs={{0,1},{1,0},{2,3},{3,2},{4,5},{5,4},{6,7},{7,6},{8,9},{9,8},{10,11... | collective-permute-start | bytes 1572872 | tf_op jit(solution)/shard_map/ppermute | solution.py:441
  80.0 24.8 %collective-permute-start.4 = (bf16[256,1024]{1,0:T(8,128)(2,1)}, bf16[256,1024]{1,0:T(8,128)(2,1)}, u32[]{:S(2)}, u32[]{:S(2)}) collective-permute-start(bf16[256,1024]{1,0:T(8,128)(2,1)} %get-tuple-element.205.own_ref), channel_id=1, source_target_pairs={{0,1},{1,0},{2,3},{3,2},{4,5},{5,4},{6,7},{7,6},{8,9},{9,8},{10,11... | collective-permute-start | bytes 1572872 | tf_op jit(solution)/shard_map/ppermute | solution.py:441
  82.8 52.7 %collective-permute-start.11 = (bf16[128,1024]{1,0:T(8,128)(2,1)}, bf16[128,1024]{1,0:T(8,128)(2,1)}, u32[]{:S(2)}, u32[]{:S(2)}) collective-permute-start(bf16[128,1024]{1,0:T(8,128)(2,1)} %get-tuple-element.441), channel_id=1, source_target_pairs={{0,1},{1,0},{2,3},{3,2},{4,5},{5,4},{6,7},{7,6},{8,9},{9,8},{10,11... | collective-permute-start | bytes 786440 | tf_op jit(solution)/shard_map/ppermute | solution.py:441
  83.1 59.4 %collective-permute-start.12 = (bf16[128,1024]{1,0:T(8,128)(2,1)}, bf16[128,1024]{1,0:T(8,128)(2,1)}, u32[]{:S(2)}, u32[]{:S(2)}) collective-permute-start(bf16[128,1024]{1,0:T(8,128)(2,1)} %get-tuple-element.440), channel_id=1, source_target_pairs={{0,1},{1,0},{2,3},{3,2},{4,5},{5,4},{6,7},{7,6},{8,9},{9,8},{10,11... | collective-permute-start | bytes 786440 | tf_op jit(solution)/shard_map/ppermute | solution.py:441
  104.5 18.5 %collective-permute-start.9 = (bf16[256,1024]{1,0:T(8,128)(2,1)S(1)}, bf16[256,1024]{1,0:T(8,128)(2,1)S(1)}, u32[]{:S(2)}, u32[]{:S(2)}) collective-permute-start(bf16[256,1024]{1,0:T(8,128)(2,1)S(1)} %get-tuple-element.213.own_ref), channel_id=1, source_target_pairs={{0,1},{1,0},{2,3},{3,2},{4,5},{5,4},{6,7},{7,6},{8,9},{9,8},{10,11... | collective-permute-start | bytes 1572872 | tf_op jit(solution)/shard_map/ppermute | solution.py:441
  121.3 13.9 %collective-permute-start.5 = (bf16[256,1024]{1,0:T(8,128)(2,1)S(1)}, bf16[256,1024]{1,0:T(8,128)(2,1)S(1)}, u32[]{:S(2)}, u32[]{:S(2)}) collective-permute-start(bf16[256,1024]{1,0:T(8,128)(2,1)S(1)} %get-tuple-element.207), channel_id=1, source_target_pairs={{0,1},{1,0},{2,3},{3,2},{4,5},{5,4},{6,7},{7,6},{8,9},{9,8},{10,11... | collective-permute-start | bytes 1572872 | tf_op jit(solution)/shard_map/ppermute | solution.py:441
  131.2 11.4 %collective-permute-start.10 = (bf16[256,1024]{1,0:T(8,128)(2,1)S(1)}, bf16[256,1024]{1,0:T(8,128)(2,1)S(1)}, u32[]{:S(2)}, u32[]{:S(2)}) collective-permute-start(bf16[256,1024]{1,0:T(8,128)(2,1)S(1)} %get-tuple-element.215), channel_id=1, source_target_pairs={{0,1},{1,0},{2,3},{3,2},{4,5},{5,4},{6,7},{7,6},{8,9},{9,8},{10,11... | collective-permute-start | bytes 1572872 | tf_op jit(solution)/shard_map/ppermute | solution.py:441
  159.8 28.3 %collective-permute-start.15 = (bf16[8,256,1024]{2,1,0:T(8,128)(2,1)S(1)}, bf16[8,256,1024]{2,1,0:T(8,128)(2,1)S(1)}, u32[]{:S(2)}, u32[]{:S(2)}) collective-permute-start(bf16[8,256,1024]{2,1,0:T(8,128)(2,1)S(1)} %get-tuple-element.246), channel_id=1, source_target_pairs={{0,2},{2,0},{4,6},{6,4},{8,10},{10,8},{12,14},{14,12},{16,18},{18,... | collective-permute-start | bytes 12582920 | tf_op jit(solution)/shard_map/ppermute | solution.py:642
  159.9 14.6 %collective-permute-start.13 = (bf16[256,1024]{1,0:T(8,128)(2,1)S(1)}, bf16[256,1024]{1,0:T(8,128)(2,1)S(1)}, u32[]{:S(2)}, u32[]{:S(2)}) collective-permute-start(bf16[256,1024]{1,0:T(8,128)(2,1)S(1)} %get-tuple-element.237.own_ref), channel_id=1, source_target_pairs={{0,1},{1,0},{2,3},{3,2},{4,5},{5,4},{6,7},{7,6},{8,9},{9,8},{10,11... | collective-permute-start | bytes 1572872 | tf_op jit(solution)/shard_map/ppermute | solution.py:441
  174.5 13.6 %collective-permute-start.14 = (bf16[256,1024]{1,0:T(8,128)(2,1)S(1)}, bf16[256,1024]{1,0:T(8,128)(2,1)S(1)}, u32[]{:S(2)}, u32[]{:S(2)}) collective-permute-start(bf16[256,1024]{1,0:T(8,128)(2,1)S(1)} %get-tuple-element.247.own_ref), channel_id=1, source_target_pairs={{0,1},{1,0},{2,3},{3,2},{4,5},{5,4},{6,7},{7,6},{8,9},{9,8},{10,11... | collective-permute-start | bytes 1572872 | tf_op jit(solution)/shard_map/ppermute | solution.py:441
  199.8 14.5 %collective-permute-start.18 = (bf16[256,1024]{1,0:T(8,128)(2,1)S(1)}, bf16[256,1024]{1,0:T(8,128)(2,1)S(1)}, u32[]{:S(2)}, u32[]{:S(2)}) collective-permute-start(bf16[256,1024]{1,0:T(8,128)(2,1)S(1)} %fusion.13), channel_id=1, source_target_pairs={{0,8},{10,2},{8,16},{18,10},{16,24},{26,18},{24,28},{30,26},{28,20... | collective-permute-start | bytes 1572872 | tf_op jit(solution)/shard_map/ppermute | solution.py:651
  212.6 41.1 %collective-permute-start.22 = (bf16[8,256,512]{2,1,0:T(8,128)(2,1)S(1)}, bf16[8,256,512]{2,1,0:T(8,128)(2,1)}, u32[]{:S(2)}, u32[]{:S(2)}) collective-permute-start(bf16[8,256,512]{2,1,0:T(8,128)(2,1)S(1)} %get-tuple-element.289), channel_id=1, source_target_pairs={{0,2},{2,0},{4,6},{6,4},{8,10},{10,8},{12,14},{14,12},{16,18},{18,... | collective-permute-start | bytes 6291464 | tf_op jit(solution)/shard_map/ppermute | solution.py:642
  212.7 14.3 %collective-permute-start.17 = (bf16[256,1024]{1,0:T(8,128)(2,1)S(1)}, bf16[256,1024]{1,0:T(8,128)(2,1)S(1)}, u32[]{:S(2)}, u32[]{:S(2)}) collective-permute-start(bf16[256,1024]{1,0:T(8,128)(2,1)S(1)} %get-tuple-element.278.refs_2_), channel_id=1, source_target_pairs={{0,1},{1,0},{2,3},{3,2},{4,5},{5,4},{6,7},{7,6},{8,9},{9,8},{10,11... | collective-permute-start | bytes 1572872 | tf_op jit(solution)/shard_map/ppermute | solution.py:441
  228.6 12.1 %collective-permute-start.19 = (bf16[256,1024]{1,0:T(8,128)(2,1)S(1)}, bf16[256,1024]{1,0:T(8,128)(2,1)S(1)}, u32[]{:S(2)}, u32[]{:S(2)}) collective-permute-start(bf16[256,1024]{1,0:T(8,128)(2,1)S(1)} %get-tuple-element.292.refs_2_), channel_id=1, source_target_pairs={{0,1},{1,0},{2,3},{3,2},{4,5},{5,4},{6,7},{7,6},{8,9},{9,8},{10,11... | collective-permute-start | bytes 1572872 | tf_op jit(solution)/shard_map/ppermute | solution.py:441
  240.7 15.9 %collective-permute-start.21 = (bf16[256,1024]{1,0:T(8,128)(2,1)S(1)}, bf16[256,1024]{1,0:T(8,128)(2,1)S(1)}, u32[]{:S(2)}, u32[]{:S(2)}) collective-permute-start(bf16[256,1024]{1,0:T(8,128)(2,1)S(1)} %fusion.11), channel_id=1, source_target_pairs={{0,8},{10,2},{8,16},{18,10},{16,24},{26,18},{24,28},{30,26},{28,20... | collective-permute-start | bytes 1572872 | tf_op jit(solution)/shard_map/ppermute | solution.py:651
  276.7 40.5 %collective-permute-start.32 = (bf16[8,256,1024]{2,1,0:T(8,128)(2,1)S(1)}, bf16[8,256,1024]{2,1,0:T(8,128)(2,1)S(1)}, u32[]{:S(2)}, u32[]{:S(2)}) collective-permute-start(bf16[8,256,1024]{2,1,0:T(8,128)(2,1)S(1)} %get-tuple-element.327), channel_id=1, source_target_pairs={{0,2},{2,0},{4,6},{6,4},{8,10},{10,8},{12,14},{14,12},{16,18},{18,... | collective-permute-start | bytes 12582920 | tf_op jit(solution)/shard_map/ppermute | solution.py:642
  276.7 13.1 %collective-permute-start.25 = (bf16[256,1024]{1,0:T(8,128)(2,1)S(1)}, bf16[256,1024]{1,0:T(8,128)(2,1)S(1)}, u32[]{:S(2)}, u32[]{:S(2)}) collective-permute-start(bf16[256,1024]{1,0:T(8,128)(2,1)S(1)} %copy-done.167), channel_id=1, source_target_pairs={{0,8},{10,2},{8,16},{18,10},{16,24},{26,18},{24,28},{30,26},{28,20... | collective-permute-start | bytes 1572872 | tf_op jit(solution)/shard_map/ppermute | solution.py:651
  278.4 10.4 %collective-permute-start.26 = (bf16[256,512]{1,0:T(8,128)(2,1)S(1)}, bf16[256,512]{1,0:T(8,128)(2,1)S(1)}, u32[]{:S(2)}, u32[]{:S(2)}) collective-permute-start(bf16[256,512]{1,0:T(8,128)(2,1)S(1)} %fusion.39), channel_id=1, source_target_pairs={{0,8},{10,2},{8,16},{18,10},{16,24},{26,18},{24,28},{30,26},{28,20... | collective-permute-start | bytes 786440 | tf_op jit(solution)/shard_map/ppermute | solution.py:651
  279.9 12.5 %collective-permute-start.24 = (bf16[256,1024]{1,0:T(8,128)(2,1)S(1)}, bf16[256,1024]{1,0:T(8,128)(2,1)S(1)}, u32[]{:S(2)}, u32[]{:S(2)}) collective-permute-start(bf16[256,1024]{1,0:T(8,128)(2,1)S(1)} %get-tuple-element.316.own_ref), channel_id=1, source_target_pairs={{0,1},{1,0},{2,3},{3,2},{4,5},{5,4},{6,7},{7,6},{8,9},{9,8},{10,11... | collective-permute-start | bytes 1572872 | tf_op jit(solution)/shard_map/ppermute | solution.py:441
  292.4 13.0 %collective-permute-start.28 = (bf16[256,1024]{1,0:T(8,128)(2,1)S(1)}, bf16[256,1024]{1,0:T(8,128)(2,1)S(1)}, u32[]{:S(2)}, u32[]{:S(2)}) collective-permute-start(bf16[256,1024]{1,0:T(8,128)(2,1)S(1)} %fusion.9), channel_id=1, source_target_pairs={{0,8},{10,2},{8,16},{18,10},{16,24},{26,18},{24,28},{30,26},{28,20... | collective-permute-start | bytes 1572872 | tf_op jit(solution)/shard_map/ppermute | solution.py:651
  293.0 11.4 %collective-permute-start.29 = (bf16[256,512]{1,0:T(8,128)(2,1)S(1)}, bf16[256,512]{1,0:T(8,128)(2,1)S(1)}, u32[]{:S(2)}, u32[]{:S(2)}) collective-permute-start(bf16[256,512]{1,0:T(8,128)(2,1)S(1)} %fusion.38), channel_id=1, source_target_pairs={{0,8},{10,2},{8,16},{18,10},{16,24},{26,18},{24,28},{30,26},{28,20... | collective-permute-start | bytes 786440 | tf_op jit(solution)/shard_map/ppermute | solution.py:651
  294.6 14.4 %collective-permute-start.27 = (bf16[256,1024]{1,0:T(8,128)(2,1)S(1)}, bf16[256,1024]{1,0:T(8,128)(2,1)S(1)}, u32[]{:S(2)}, u32[]{:S(2)}) collective-permute-start(bf16[256,1024]{1,0:T(8,128)(2,1)S(1)} %get-tuple-element.328.own_ref), channel_id=1, source_target_pairs={{0,1},{1,0},{2,3},{3,2},{4,5},{5,4},{6,7},{7,6},{8,9},{9,8},{10,11... | collective-permute-start | bytes 1572872 | tf_op jit(solution)/shard_map/ppermute | solution.py:441
  308.9 12.0 %collective-permute-start.30 = (bf16[256,1024]{1,0:T(8,128)(2,1)S(1)}, bf16[256,1024]{1,0:T(8,128)(2,1)S(1)}, u32[]{:S(2)}, u32[]{:S(2)}) collective-permute-start(bf16[256,1024]{1,0:T(8,128)(2,1)S(1)} %fusion.8), channel_id=1, source_target_pairs={{0,8},{10,2},{8,16},{18,10},{16,24},{26,18},{24,28},{30,26},{28,20... | collective-permute-start | bytes 1572872 | tf_op jit(solution)/shard_map/ppermute | solution.py:651
  326.9 15.1 %collective-permute-start.37 = (bf16[256,1024]{1,0:T(8,128)(2,1)S(1)}, bf16[256,1024]{1,0:T(8,128)(2,1)S(1)}, u32[]{:S(2)}, u32[]{:S(2)}) collective-permute-start(bf16[256,1024]{1,0:T(8,128)(2,1)S(1)} %fusion.6), channel_id=1, source_target_pairs={{0,8},{10,2},{8,16},{18,10},{16,24},{26,18},{24,28},{30,26},{28,20... | collective-permute-start | bytes 1572872 | tf_op jit(solution)/shard_map/ppermute | solution.py:651
  328.5 12.2 %collective-permute-start.36 = (bf16[256,512]{1,0:T(8,128)(2,1)S(1)}, bf16[256,512]{1,0:T(8,128)(2,1)S(1)}, u32[]{:S(2)}, u32[]{:S(2)}) collective-permute-start(bf16[256,512]{1,0:T(8,128)(2,1)S(1)} %fusion.36), channel_id=1, source_target_pairs={{0,8},{10,2},{8,16},{18,10},{16,24},{26,18},{24,28},{30,26},{28,20... | collective-permute-start | bytes 786440 | tf_op jit(solution)/shard_map/ppermute | solution.py:651
  329.9 12.4 %collective-permute-start.34 = (bf16[256,1024]{1,0:T(8,128)(2,1)S(1)}, bf16[256,1024]{1,0:T(8,128)(2,1)S(1)}, u32[]{:S(2)}, u32[]{:S(2)}) collective-permute-start(bf16[256,1024]{1,0:T(8,128)(2,1)S(1)} %get-tuple-element.363), channel_id=1, source_target_pairs={{0,1},{1,0},{2,3},{3,2},{4,5},{5,4},{6,7},{7,6},{8,9},{9,8},{10,11... | collective-permute-start | bytes 1572872 | tf_op jit(solution)/shard_map/ppermute | solution.py:441
  331.4 13.1 %collective-permute-start.35 = (bf16[256,1024]{1,0:T(8,128)(2,1)S(1)}, bf16[256,1024]{1,0:T(8,128)(2,1)S(1)}, u32[]{:S(2)}, u32[]{:S(2)}) collective-permute-start(bf16[256,1024]{1,0:T(8,128)(2,1)S(1)} %fusion.7.refs_0_), channel_id=1, source_target_pairs={{0,8},{10,2},{8,16},{18,10},{16,24},{26,18},{24,28},{30,26},{28,20... | collective-permute-start | bytes 1572872 | tf_op jit(solution)/shard_map/ppermute | solution.py:651
  344.5 13.8 %collective-permute-start.41 = (bf16[256,1024]{1,0:T(8,128)(2,1)S(1)}, bf16[256,1024]{1,0:T(8,128)(2,1)S(1)}, u32[]{:S(2)}, u32[]{:S(2)}) collective-permute-start(bf16[256,1024]{1,0:T(8,128)(2,1)S(1)} %fusion.5), channel_id=1, source_target_pairs={{0,8},{10,2},{8,16},{18,10},{16,24},{26,18},{24,28},{30,26},{28,20... | collective-permute-start | bytes 1572872 | tf_op jit(solution)/shard_map/ppermute | solution.py:651
  350.5 35.6 %collective-permute-start.46 = (bf16[8,256,512]{2,1,0:T(8,128)(2,1)S(1)}, bf16[8,256,512]{2,1,0:T(8,128)(2,1)S(1)}, u32[]{:S(2)}, u32[]{:S(2)}) collective-permute-start(bf16[8,256,512]{2,1,0:T(8,128)(2,1)S(1)} %get-tuple-element.378), channel_id=1, source_target_pairs={{0,2},{2,0},{4,6},{6,4},{8,10},{10,8},{12,14},{14,12},{16,18},{18,... | collective-permute-start | bytes 6291464 | tf_op jit(solution)/shard_map/ppermute | solution.py:642
  350.6 14.3 %collective-permute-start.38 = (bf16[256,1024]{1,0:T(8,128)(2,1)S(1)}, bf16[256,1024]{1,0:T(8,128)(2,1)S(1)}, u32[]{:S(2)}, u32[]{:S(2)}) collective-permute-start(bf16[256,1024]{1,0:T(8,128)(2,1)S(1)} %get-tuple-element.367), channel_id=1, source_target_pairs={{0,1},{1,0},{2,3},{3,2},{4,5},{5,4},{6,7},{7,6},{8,9},{9,8},{10,11... | collective-permute-start | bytes 1572872 | tf_op jit(solution)/shard_map/ppermute | solution.py:441
  352.2 12.7 %collective-permute-start.39 = (bf16[256,1024]{1,0:T(8,128)(2,1)S(1)}, bf16[256,1024]{1,0:T(8,128)(2,1)S(1)}, u32[]{:S(2)}, u32[]{:S(2)}) collective-permute-start(bf16[256,1024]{1,0:T(8,128)(2,1)S(1)} %collective-permute-done.35.refs_1_), channel_id=1, source_target_pairs={{0,8},{10,2},{8,16},{18,10},{16,24},{26,18},{24,28},{30,26},{28,20... | collective-permute-start | bytes 1572872 | tf_op jit(solution)/shard_map/ppermute | solution.py:651
  384.7 14.9 %collective-permute-start.73 = (bf16[256,1024]{1,0:T(8,128)(2,1)}, bf16[256,1024]{1,0:T(8,128)(2,1)}, u32[]{:S(2)}, u32[]{:S(2)}) collective-permute-start(bf16[256,1024]{1,0:T(8,128)(2,1)} %fusion.2), channel_id=1, source_target_pairs={{0,8},{10,2},{8,16},{18,10},{16,24},{26,18},{24,28},{30,26},{28,20... | collective-permute-start | bytes 1572872 | tf_op jit(solution)/shard_map/ppermute | solution.py:651
  386.1 10.9 %collective-permute-start.47 = (bf16[256,512]{1,0:T(8,128)(2,1)S(1)}, bf16[256,512]{1,0:T(8,128)(2,1)}, u32[]{:S(2)}, u32[]{:S(2)}) collective-permute-start(bf16[256,512]{1,0:T(8,128)(2,1)S(1)} %fusion.41), channel_id=1, source_target_pairs={{0,8},{10,2},{8,16},{18,10},{16,24},{26,18},{24,28},{30,26},{28,20... | collective-permute-start | bytes 786440 | tf_op jit(solution)/shard_map/ppermute | solution.py:651
  403.7 23.4 %collective-permute-start.83 = (bf16[256,1024]{1,0:T(8,128)(2,1)}, bf16[256,1024]{1,0:T(8,128)(2,1)}, u32[]{:S(2)}, u32[]{:S(2)}) collective-permute-start(bf16[256,1024]{1,0:T(8,128)(2,1)} %copy-done.19), channel_id=1, source_target_pairs={{0,8},{10,2},{8,16},{18,10},{16,24},{26,18},{24,28},{30,26},{28,20... | collective-permute-start | bytes 1572872 | tf_op jit(solution)/shard_map/ppermute | solution.py:651
  405.8 13.0 %collective-permute-start.49 = (bf16[256,512]{1,0:T(8,128)(2,1)S(1)}, bf16[256,512]{1,0:T(8,128)(2,1)S(1)}, u32[]{:S(2)}, u32[]{:S(2)}) collective-permute-start(bf16[256,512]{1,0:T(8,128)(2,1)S(1)} %fusion.32), channel_id=1, source_target_pairs={{0,8},{10,2},{8,16},{18,10},{16,24},{26,18},{24,28},{30,26},{28,20... | collective-permute-start | bytes 786440 | tf_op jit(solution)/shard_map/ppermute | solution.py:651
  411.9 12.7 %collective-permute-start.75 = (bf16[256,1024]{1,0:T(8,128)(2,1)S(1)}, bf16[256,1024]{1,0:T(8,128)(2,1)}, u32[]{:S(2)}, u32[]{:S(2)}) collective-permute-start(bf16[256,1024]{1,0:T(8,128)(2,1)S(1)} %fusion.refs_0_), channel_id=1, source_target_pairs={{0,8},{10,2},{8,16},{18,10},{16,24},{26,18},{24,28},{30,26},{28,20... | collective-permute-start | bytes 1572872 | tf_op jit(solution)/shard_map/ppermute | solution.py:651
  427.1 12.6 %collective-permute-start.84 = (bf16[256,1024]{1,0:T(8,128)(2,1)}, bf16[256,1024]{1,0:T(8,128)(2,1)}, u32[]{:S(2)}, u32[]{:S(2)}) collective-permute-start(bf16[256,1024]{1,0:T(8,128)(2,1)} %collective-permute-done.83.refs_3_), channel_id=1, source_target_pairs={{0,8},{10,2},{8,16},{18,10},{16,24},{26,18},{24,28},{30,26},{28,20... | collective-permute-start | bytes 1572872 | tf_op jit(solution)/shard_map/ppermute | solution.py:651
  429.5 13.0 %collective-permute-start.51 = (bf16[256,512]{1,0:T(8,128)(2,1)S(1)}, bf16[256,512]{1,0:T(8,128)(2,1)S(1)}, u32[]{:S(2)}, u32[]{:S(2)}) collective-permute-start(bf16[256,512]{1,0:T(8,128)(2,1)S(1)} %fusion.30), channel_id=1, source_target_pairs={{0,8},{10,2},{8,16},{18,10},{16,24},{26,18},{24,28},{30,26},{28,20... | collective-permute-start | bytes 786440 | tf_op jit(solution)/shard_map/ppermute | solution.py:651
  434.1 14.2 %collective-permute-start.77 = (bf16[256,1024]{1,0:T(8,128)(2,1)}, bf16[256,1024]{1,0:T(8,128)(2,1)}, u32[]{:S(2)}, u32[]{:S(2)}) collective-permute-start(bf16[256,1024]{1,0:T(8,128)(2,1)} %collective-permute-done.76.refs_2_), channel_id=1, source_target_pairs={{0,8},{10,2},{8,16},{18,10},{16,24},{26,18},{24,28},{30,26},{28,20... | collective-permute-start | bytes 1572872 | tf_op jit(solution)/shard_map/ppermute | solution.py:651
  435.9 15.0 %collective-permute-start.62 = (bf16[256,512]{1,0:T(8,128)(2,1)}, bf16[256,512]{1,0:T(8,128)(2,1)S(1)}, u32[]{:S(2)}, u32[]{:S(2)}) collective-permute-start(bf16[256,512]{1,0:T(8,128)(2,1)} %fusion.34), channel_id=1, source_target_pairs={{0,8},{10,2},{8,16},{18,10},{16,24},{26,18},{24,28},{30,26},{28,20... | collective-permute-start | bytes 786440 | tf_op jit(solution)/shard_map/ppermute | solution.py:651
  439.7 16.9 %collective-permute-start.85 = (bf16[256,1024]{1,0:T(8,128)(2,1)}, bf16[256,1024]{1,0:T(8,128)(2,1)}, u32[]{:S(2)}, u32[]{:S(2)}) collective-permute-start(bf16[256,1024]{1,0:T(8,128)(2,1)} %collective-permute-done.84.refs_4_), channel_id=1, source_target_pairs={{0,8},{10,2},{8,16},{18,10},{16,24},{26,18},{24,28},{30,26},{28,20... | collective-permute-start | bytes 1572872 | tf_op jit(solution)/shard_map/ppermute | solution.py:651
  444.3 15.1 %collective-permute-start.52 = (bf16[256,512]{1,0:T(8,128)(2,1)}, bf16[256,512]{1,0:T(8,128)(2,1)}, u32[]{:S(2)}, u32[]{:S(2)}) collective-permute-start(bf16[256,512]{1,0:T(8,128)(2,1)} %fusion.29), channel_id=1, source_target_pairs={{0,8},{10,2},{8,16},{18,10},{16,24},{26,18},{24,28},{30,26},{28,20... | collective-permute-start | bytes 786440 | tf_op jit(solution)/shard_map/ppermute | solution.py:651
  448.3 16.7 %collective-permute-start.78 = (bf16[256,1024]{1,0:T(8,128)(2,1)}, bf16[256,1024]{1,0:T(8,128)(2,1)}, u32[]{:S(2)}, u32[]{:S(2)}) collective-permute-start(bf16[256,1024]{1,0:T(8,128)(2,1)} %collective-permute-done.77.refs_3_), channel_id=1, source_target_pairs={{0,8},{10,2},{8,16},{18,10},{16,24},{26,18},{24,28},{30,26},{28,20... | collective-permute-start | bytes 1572872 | tf_op jit(solution)/shard_map/ppermute | solution.py:651
  452.0 15.7 %collective-permute-start.63 = (bf16[256,512]{1,0:T(8,128)(2,1)S(1)}, bf16[256,512]{1,0:T(8,128)(2,1)S(1)}, u32[]{:S(2)}, u32[]{:S(2)}) collective-permute-start(bf16[256,512]{1,0:T(8,128)(2,1)S(1)} %fusion.26.refs_0_), channel_id=1, source_target_pairs={{0,8},{10,2},{8,16},{18,10},{16,24},{26,18},{24,28},{30,26},{28,20... | collective-permute-start | bytes 786440 | tf_op jit(solution)/shard_map/ppermute | solution.py:651
  456.6 16.9 %collective-permute-start.86 = (bf16[256,1024]{1,0:T(8,128)(2,1)}, bf16[256,1024]{1,0:T(8,128)(2,1)}, u32[]{:S(2)}, u32[]{:S(2)}) collective-permute-start(bf16[256,1024]{1,0:T(8,128)(2,1)} %collective-permute-done.85.refs_5_), channel_id=1, source_target_pairs={{0,8},{10,2},{8,16},{18,10},{16,24},{26,18},{24,28},{30,26},{28,20... | collective-permute-start | bytes 1572872 | tf_op jit(solution)/shard_map/ppermute | solution.py:651
  460.6 15.6 %collective-permute-start.53 = (bf16[256,512]{1,0:T(8,128)(2,1)S(1)}, bf16[256,512]{1,0:T(8,128)(2,1)}, u32[]{:S(2)}, u32[]{:S(2)}) collective-permute-start(bf16[256,512]{1,0:T(8,128)(2,1)S(1)} %fusion.28), channel_id=1, source_target_pairs={{0,8},{10,2},{8,16},{18,10},{16,24},{26,18},{24,28},{30,26},{28,20... | collective-permute-start | bytes 786440 | tf_op jit(solution)/shard_map/ppermute | solution.py:651
  465.0 21.3 %collective-permute-start.79 = (bf16[256,1024]{1,0:T(8,128)(2,1)}, bf16[256,1024]{1,0:T(8,128)(2,1)S(1)}, u32[]{:S(2)}, u32[]{:S(2)}) collective-permute-start(bf16[256,1024]{1,0:T(8,128)(2,1)} %collective-permute-done.78.refs_4_), channel_id=1, source_target_pairs={{0,8},{10,2},{8,16},{18,10},{16,24},{26,18},{24,28},{30,26},{28,20... | collective-permute-start | bytes 1572872 | tf_op jit(solution)/shard_map/ppermute | solution.py:651
  467.7 16.9 %collective-permute-start.64 = (bf16[256,512]{1,0:T(8,128)(2,1)S(1)}, bf16[256,512]{1,0:T(8,128)(2,1)S(1)}, u32[]{:S(2)}, u32[]{:S(2)}) collective-permute-start(bf16[256,512]{1,0:T(8,128)(2,1)S(1)} %collective-permute-done.63.refs_1_), channel_id=1, source_target_pairs={{0,8},{10,2},{8,16},{18,10},{16,24},{26,18},{24,28},{30,26},{28,20... | collective-permute-start | bytes 786440 | tf_op jit(solution)/shard_map/ppermute | solution.py:651
  473.4 24.2 %collective-permute-start.87 = (bf16[256,1024]{1,0:T(8,128)(2,1)}, bf16[256,1024]{1,0:T(8,128)(2,1)S(1)}, u32[]{:S(2)}, u32[]{:S(2)}) collective-permute-start(bf16[256,1024]{1,0:T(8,128)(2,1)} %collective-permute-done.86.refs_6_), channel_id=1, source_target_pairs={{0,8},{10,2},{8,16},{18,10},{16,24},{26,18},{24,28},{30,26},{28,20... | collective-permute-start | bytes 1572872 | tf_op jit(solution)/shard_map/ppermute | solution.py:651
  477.4 15.5 %collective-permute-start.54 = (bf16[256,512]{1,0:T(8,128)(2,1)S(1)}, bf16[256,512]{1,0:T(8,128)(2,1)S(1)}, u32[]{:S(2)}, u32[]{:S(2)}) collective-permute-start(bf16[256,512]{1,0:T(8,128)(2,1)S(1)} %fusion.27.refs_0_), channel_id=1, source_target_pairs={{0,8},{10,2},{8,16},{18,10},{16,24},{26,18},{24,28},{30,26},{28,20... | collective-permute-start | bytes 786440 | tf_op jit(solution)/shard_map/ppermute | solution.py:651
  484.6 11.3 %collective-permute-start.65 = (bf16[256,512]{1,0:T(8,128)(2,1)S(1)}, bf16[256,512]{1,0:T(8,128)(2,1)}, u32[]{:S(2)}, u32[]{:S(2)}) collective-permute-start(bf16[256,512]{1,0:T(8,128)(2,1)S(1)} %collective-permute-done.64.refs_2_), channel_id=1, source_target_pairs={{0,8},{10,2},{8,16},{18,10},{16,24},{26,18},{24,28},{30,26},{28,20... | collective-permute-start | bytes 786440 | tf_op jit(solution)/shard_map/ppermute | solution.py:651
  486.3 19.7 %collective-permute-start.80 = (bf16[256,1024]{1,0:T(8,128)(2,1)S(1)}, bf16[256,1024]{1,0:T(8,128)(2,1)}, u32[]{:S(2)}, u32[]{:S(2)}) collective-permute-start(bf16[256,1024]{1,0:T(8,128)(2,1)S(1)} %collective-permute-done.79.refs_5_), channel_id=1, source_target_pairs={{0,8},{10,2},{8,16},{18,10},{16,24},{26,18},{24,28},{30,26},{28,20... | collective-permute-start | bytes 1572872 | tf_op jit(solution)/shard_map/ppermute | solution.py:651
  493.0 11.2 %collective-permute-start.55 = (bf16[256,512]{1,0:T(8,128)(2,1)S(1)}, bf16[256,512]{1,0:T(8,128)(2,1)S(1)}, u32[]{:S(2)}, u32[]{:S(2)}) collective-permute-start(bf16[256,512]{1,0:T(8,128)(2,1)S(1)} %collective-permute-done.54.refs_1_), channel_id=1, source_target_pairs={{0,8},{10,2},{8,16},{18,10},{16,24},{26,18},{24,28},{30,26},{28,20... | collective-permute-start | bytes 786440 | tf_op jit(solution)/shard_map/ppermute | solution.py:651
  495.9 14.9 %collective-permute-start.66 = (bf16[256,512]{1,0:T(8,128)(2,1)}, bf16[256,512]{1,0:T(8,128)(2,1)}, u32[]{:S(2)}, u32[]{:S(2)}) collective-permute-start(bf16[256,512]{1,0:T(8,128)(2,1)} %collective-permute-done.65.refs_3_), channel_id=1, source_target_pairs={{0,8},{10,2},{8,16},{18,10},{16,24},{26,18},{24,28},{30,26},{28,20... | collective-permute-start | bytes 786440 | tf_op jit(solution)/shard_map/ppermute | solution.py:651
  503.6 61.1 %collective-permute-start.88 = (bf16[8,256,1024]{2,1,0:T(8,128)(2,1)}, bf16[8,256,1024]{2,1,0:T(8,128)(2,1)}, u32[]{:S(2)}, u32[]{:S(2)}) collective-permute-start(bf16[8,256,1024]{2,1,0:T(8,128)(2,1)} %pack.7.mine_ref), channel_id=1, source_target_pairs={{0,2},{2,0},{4,6},{6,4},{8,10},{10,8},{12,14},{14,12},{16,18},{18,... | collective-permute-start | bytes 12582920 | tf_op jit(solution)/shard_map/ppermute | solution.py:676
  505.9 17.6 %collective-permute-start.81 = (bf16[256,1024]{1,0:T(8,128)(2,1)}, bf16[256,1024]{1,0:T(8,128)(2,1)}, u32[]{:S(2)}, u32[]{:S(2)}) collective-permute-start(bf16[256,1024]{1,0:T(8,128)(2,1)} %collective-permute-done.80.refs_6_), channel_id=1, source_target_pairs={{0,8},{10,2},{8,16},{18,10},{16,24},{26,18},{24,28},{30,26},{28,20... | collective-permute-start | bytes 1572872 | tf_op jit(solution)/shard_map/ppermute | solution.py:651
  513.0 24.6 %collective-permute-start.42 = (f32[2,5,1024]{2,0,1:T(2,128)S(1)}, f32[2,5,1024]{2,0,1:T(2,128)S(1)}, u32[]{:S(2)}, u32[]{:S(2)}) collective-permute-start(f32[2,5,1024]{2,0,1:T(2,128)S(1)} %pad_maximum_fusion.4), channel_id=1, source_target_pairs={{0,2},{2,0},{4,6},{6,4},{8,10},{10,8},{12,14},{14,12},{16,18},{18,... | collective-permute-start | bytes 122888 | tf_op jit(solution)/shard_map/ppermute | solution.py:462
  526.9 47.2 %collective-permute-start.82 = (bf16[8,256,1024]{2,1,0:T(8,128)(2,1)S(1)}, bf16[8,256,1024]{2,1,0:T(8,128)(2,1)S(1)}, u32[]{:S(2)}, u32[]{:S(2)}) collective-permute-start(bf16[8,256,1024]{2,1,0:T(8,128)(2,1)S(1)} %pack.6.mine_ref), channel_id=1, source_target_pairs={{0,2},{2,0},{4,6},{6,4},{8,10},{10,8},{12,14},{14,12},{16,18},{18,... | collective-permute-start | bytes 12582920 | tf_op jit(solution)/shard_map/ppermute | solution.py:676
  534.6 21.1 %collective-permute-start.70 = (bf16[8,256,512]{2,1,0:T(8,128)(2,1)S(1)}, bf16[8,256,512]{2,1,0:T(8,128)(2,1)S(1)}, u32[]{:S(2)}, u32[]{:S(2)}) collective-permute-start(bf16[8,256,512]{2,1,0:T(8,128)(2,1)S(1)} %pack.5.mine_ref), channel_id=1, source_target_pairs={{0,2},{2,0},{4,6},{6,4},{8,10},{10,8},{12,14},{14,12},{16,18},{18,... | collective-permute-start | bytes 6291464 | tf_op jit(solution)/shard_map/ppermute | solution.py:676
  544.0 16.2 %collective-permute-start.61 = (bf16[8,256,512]{2,1,0:T(8,128)(2,1)S(1)}, bf16[8,256,512]{2,1,0:T(8,128)(2,1)S(1)}, u32[]{:S(2)}, u32[]{:S(2)}) collective-permute-start(bf16[8,256,512]{2,1,0:T(8,128)(2,1)S(1)} %pack.4.mine_ref), channel_id=1, source_target_pairs={{0,2},{2,0},{4,6},{6,4},{8,10},{10,8},{12,14},{14,12},{16,18},{18,... | collective-permute-start | bytes 6291464 | tf_op jit(solution)/shard_map/ppermute | solution.py:676
  (211 other events, 2751.6 us)

commit v2 on v1

v2 whole, which is shorter than its diff:
```python
import functools
import math

import jax
import jax.numpy as jnp
import numpy as np
from jax import lax
from jax.experimental import pallas as pl
from jax.experimental.pallas import tpu as pltpu
from jax.sharding import PartitionSpec as P

HD = 64
bf16 = jnp.bfloat16
f32 = jnp.float32
epsilon = 1e-05


def mm(a, b):
    return jnp.dot(a, b, preferred_element_type=f32)


def mm_t(a, b):
    return lax.dot_general(a, b, (((1,), (1,)), ((), ())), preferred_element_type=f32)


def across(a, b):
    return lax.dot_general(a, b, (((0,), (0,)), ((), ())), preferred_element_type=f32)


def ein(spec, a, b):
    return jnp.einsum(spec, a, b, preferred_element_type=f32)


def gelu_parts(u):
    square = u * u
    s = 0.5 + 0.5 * jnp.tanh(u * (0.7978845608 + 0.7978845608 * 0.044715 * square))
    value = u * s
    slope = s + value * (1.0 - s) * (2.0 * 0.7978845608 + 6.0 * 0.7978845608 * 0.044715 * square)
    return value, slope


def standardize(v):
    centered = v - jnp.mean(v, axis=-1, keepdims=True)
    inverse = lax.rsqrt(jnp.mean(centered * centered, axis=-1, keepdims=True) + epsilon)
    return centered * inverse, inverse


def norm_backward(grad, xhat, inverse, gain):
    e = grad * gain
    return inverse * (
        e
        - jnp.mean(e, axis=-1, keepdims=True)
        - xhat * jnp.mean(e * xhat, axis=-1, keepdims=True)
    )


CHUNK = 32
BLOCK = 256


def rope_tables(length, width):
    half = HD // 2
    freqs = np.exp(-math.log(10000.0) * np.arange(half) * 2.0 / HD)
    angles = np.arange(length)[:, None] * freqs[None, :]
    heads = width // HD
    cos = np.tile(np.cos(angles), (1, 2 * heads))
    sin = np.tile(np.concatenate([-np.sin(angles), np.sin(angles)], axis=1), (1, heads))
    return jnp.asarray(cos, f32), jnp.asarray(sin, f32)


def partner(u):
    width = u.shape[1]
    lane = lax.broadcasted_iota(jnp.int32, u.shape, 1)
    low = (lane & (HD - 1)) < HD // 2
    return jnp.where(low, pltpu.roll(u, width - HD // 2, 1), pltpu.roll(u, HD // 2, 1))


GAIN, BIAS, TIME = 0, 1, 2


def vector(ref, group, row):
    at = group * (ref.shape[0] // 3) + row
    return ref[at : at + 1, :]


def chunks(rows, body, start=0):
    def step(i, carry):
        body(pl.multiple_of(i * CHUNK, CHUNK))
        return carry

    lax.fori_loop(start // CHUNK, rows // CHUNK, step, 0, unroll=4)


def rows_at(at):
    return pl.ds(at, CHUNK)


def other_rows(at, rows, swapped):
    if not swapped:
        return rows_at(at)
    half = rows // 2
    return rows_at(pl.multiple_of(jnp.where(at < half, at + half, at - half), CHUNK))


def fold(v):
    return jnp.sum(v.reshape(-1, 8, v.shape[-1]), axis=0)


LIMIT = 17 * 2**20
SMALL = 12 * 2**20


def call(kernel, ins, outs, scratch, flops, name, aliases={}, after=(), limit=LIMIT):
    count, late = len(ins), len(after)
    specs, args = [], []
    for a, away in ins:
        space = pltpu.SMEM if a.dtype == jnp.int32 else pltpu.HBM if away else pltpu.VMEM
        specs.append(pl.BlockSpec(memory_space=space))
        args.append(a if space == pltpu.SMEM else pltpu.with_memory_space_constraint(a, space))

    def run(*refs):
        kernel(*refs[:count], *refs[count + late :])

    return pl.pallas_call(
        run,
        out_shape=[(pltpu.HBM if away else pltpu.VMEM)(s, d) for s, d, away in outs],
        in_specs=specs + [pl.BlockSpec(memory_space=pl.ANY)] * late,
        out_specs=[pl.BlockSpec(memory_space=pltpu.HBM if away else pltpu.VMEM) for _, _, away in outs],
        scratch_shapes=scratch,
        input_output_aliases=aliases,
        compiler_params=pltpu.CompilerParams(vmem_limit_bytes=limit),
        cost_estimate=pl.CostEstimate(flops=20 * flops, bytes_accessed=2**20, transcendentals=0),
        name=name,
    )(*args, *after)


class Saver:
    def __init__(self, sems):
        self.sems, self.copies = sems, []

    def save(self, held, out):
        c = pltpu.make_async_copy(held, out, self.sems.at[len(self.copies)])
        c.start()
        self.copies.append(c)

    def wait(self):
        for c in self.copies:
            c.wait()


def masks():
    lane = lax.broadcasted_iota(jnp.int32, (1, 2 * HD), 1)
    return lane < HD


def both_heads(v, low):
    zero = jnp.zeros_like(v)
    return jnp.concatenate([jnp.where(low, v, zero), jnp.where(low, zero, v)], axis=0)


def halves(v):
    n = v.shape[1] // 2
    return v[:, :n], v[:, n:]


def softmax(scores):
    out = []
    for s in halves(scores):
        e = jnp.exp(s - jnp.max(s, axis=-1, keepdims=True))
        out.append(e * (1.0 / jnp.sum(e, axis=-1, keepdims=True)))
    return out


def beside(a, b):
    return jnp.concatenate([a, b], axis=1)


def forward_attention(layer, part_index, length, swapped, head, tau, vectors, w_qkv, w_out, tables):
    first = layer == 0
    rows = sum(n for _, _, n in head) if first else head[0].shape[0]
    width = w_out.shape[2]
    local = w_out.shape[1]
    block = min(BLOCK, local)
    scale = HD ** (-0.5)
    seqs = rows // length
    parts = tau.shape[0] // seqs

    def kernel(*refs):
        it = iter(refs)
        take = lambda n: [next(it) for _ in range(n)]
        head_refs = take(len(head))
        tau_ref, vec_ref, wq_any, wo_any, cos_any, sin_any = take(6)
        x_ref, part_ref = take(2)
        outs = take(6 if first else 7)
        wq, wo, cos_ref, sin_ref, sems, out_sems = take(6)
        n_ref, q_ref, k_ref, v_ref, att_ref = take(5)
        if first:
            held, = take(1)
        else:
            x2_ref, = take(1)
        saver = Saver(out_sems)
        if first:
            own = head_refs[0].at[pl.ds(head[0][1], head[0][2]), :]
            fetch = pltpu.make_async_copy(own, held, sems.at[4])
            fetch.start()
        ropes = [pltpu.make_async_copy(a, b, sems.at[5 + j]) for j, (a, b) in
                 enumerate(((cos_any, cos_ref), (sin_any, sin_ref)))]
        copies = [pltpu.make_async_copy(wq_any.at[layer, j], wq.at[j], sems.at[j]) for j in range(3)]
        copies.append(pltpu.make_async_copy(wo_any.at[layer], wo, sems.at[3]))
        for c in copies[:1] + ropes + copies[1:]:
            c.start()
        gain, bias = vector(vec_ref, GAIN, 2 * layer), vector(vec_ref, BIAS, 2 * layer)

        def norm(at, x):
            x_ref[rows_at(at), :] = x
            xhat, _ = standardize(x)
            n_ref[rows_at(at), :] = (xhat * gain + bias).astype(bf16)

        if first:
            count = head[0][2]
            if len(head) > 1:
                ref = head_refs[1]
                chunks(rows, lambda at: norm(at, ref[rows_at(at - count), :].astype(f32)), count)
            fetch.wait()
            chunks(count, lambda at: norm(at, held[rows_at(at), :].astype(f32)))
        else:
            x1, own, got = head_refs

            def scaled(at):
                here = rows_at(at)
                there = other_rows(at, rows, swapped)
                x2 = x1[here, :] + own[here, :].astype(f32) + got[there, :].astype(f32)
                x2_ref[here, :] = x2
                t = tau_ref[pl.ds(at // length * parts + part_index, 1), :]
                norm(at, x2 * (1.0 + t * vector(vec_ref, TIME, layer - 1)))

            chunks(rows, scaled)
            saver.save(x2_ref, outs[6])
        saver.save(x_ref, outs[0])
        saver.save(n_ref, outs[1])
        for c in ropes:
            c.wait()
        for j, out in enumerate((q_ref, k_ref, v_ref)):
            copies[j].wait()
            for b in range(0, local, block):
                u = mm(n_ref[...], wq[j, :, b : b + block])
                if j < 2:
                    for s in range(0, rows, length):
                        us = u[s : s + length]
                        us = us * cos_ref[:, b : b + block] + partner(us) * sin_ref[:, b : b + block]
                        out[s : s + length, b : b + block] = us.astype(bf16)
                else:
                    out[:, b : b + block] = u.astype(bf16)
            saver.save(out, outs[2 + j])
        low = masks()
        for s in range(0, rows, length):
            for b in range(0, local, 2 * HD):
                here = (slice(s, s + length), slice(b, b + 2 * HD))
                keys = both_heads(k_ref[here], low)
                probs = beside(*softmax(mm_t(q_ref[here], keys) * scale)).astype(bf16)
                att_ref[here] = mm(probs, both_heads(v_ref[here], low)).astype(bf16)
        saver.save(att_ref, outs[5])
        copies[3].wait()
        for b in range(0, width, BLOCK):
            part_ref[:, b : b + BLOCK] = mm(att_ref[...], wo[:, b : b + BLOCK]).astype(bf16)
        saver.wait()

    ins = [(a[0], j == 0) for j, a in enumerate(head)] if first else [(a, False) for a in head]
    ins += [(a, False) for a in (tau, vectors)] + [(w_qkv, True), (w_out, True)]
    ins += [(t, True) for t in tables]
    near = lambda n, d: ((rows, n), d, False)
    far = lambda n, d: ((rows, n), d, True)
    outs = [near(width, f32), near(width, bf16)]
    outs += [far(width, f32), far(width, bf16)] + [far(local, bf16)] * 4
    outs += [] if first else [far(width, f32)]
    scratch = [
        pltpu.VMEM((3, width, local), bf16),
        pltpu.VMEM((local, width), bf16),
        pltpu.VMEM((length, local), f32),
        pltpu.VMEM((length, local), f32),
        pltpu.SemaphoreType.DMA((7,)),
        pltpu.SemaphoreType.DMA((7,)),
        pltpu.VMEM((rows, width), bf16),
    ]
    scratch += [pltpu.VMEM((rows, local), bf16)] * 4
    scratch.append(pltpu.VMEM((head[0][2], width), bf16) if first else pltpu.VMEM((rows, width), f32))
    return call(kernel, ins, outs, scratch, 4 * 10**9, "forward_attention")


def forward_mlp(layer, swapped, split, x, own, got, vectors, w_up, w_down, after):
    rows, width = x.shape
    hidden = w_up.shape[2]
    tiles = hidden // BLOCK

    def kernel(x_ref, own_ref, got_ref, vec_ref, wu_any, wd_any, x1_ref, *refs):
        part_refs, refs = refs[: 1 + split], refs[1 + split :]
        x1_out, n_out, h_out, slope_out, n_ref, h_ref, slope_ref, wu, wd, sems, out_sems = refs
        saver = Saver(out_sems)
        gain, bias = vector(vec_ref, GAIN, 2 * layer + 1), vector(vec_ref, BIAS, 2 * layer + 1)
        ups = [
            pltpu.make_async_copy(
                wu_any.at[layer, :, pl.ds(t * BLOCK, BLOCK)], wu.at[t], sems.at[t]
            )
            for t in range(tiles)
        ]
        down = pltpu.make_async_copy(wd_any.at[layer], wd, sems.at[tiles])
        for c in ups:
            c.start()
        down.start()

        def norm(at):
            here = rows_at(at)
            there = other_rows(at, rows, swapped)
            x1 = x_ref[here, :] + own_ref[here, :].astype(f32) + got_ref[there, :].astype(f32)
            x1_ref[here, :] = x1
            xhat, _ = standardize(x1)
            n_ref[here, :] = (xhat * gain + bias).astype(bf16)

        chunks(rows, norm)
        saver.save(x1_ref, x1_out)
        saver.save(n_ref, n_out)
        for t in range(tiles):
            ups[t].wait()
            value, slope = gelu_parts(mm(n_ref[...], wu[t]))
            h_ref[:, t * BLOCK : (t + 1) * BLOCK] = value.astype(bf16)
            slope_ref[:, t * BLOCK : (t + 1) * BLOCK] = slope.astype(bf16)
        saver.save(h_ref, h_out)
        saver.save(slope_ref, slope_out)
        down.wait()
        for b in range(0, width, BLOCK):
            part = mm(h_ref[...], wd[:, b : b + BLOCK]).astype(bf16)
            for j, ref in enumerate(part_refs):
                ref[:, b : b + BLOCK] = part[j * ref.shape[0] : (j + 1) * ref.shape[0]]
        saver.wait()

    ins = [(a, False) for a in (x, own, got, vectors)] + [(w_up, True), (w_down, True)]
    near = lambda n, d: ((rows, n), d, False)
    far = lambda n, d: ((rows, n), d, True)
    outs = [near(width, f32)] + [((rows // (1 + split), width), bf16, False)] * (1 + split)
    outs += [far(width, f32), far(width, bf16), far(hidden, bf16), far(hidden, bf16)]
    scratch = [
        pltpu.VMEM((rows, width), bf16),
        pltpu.VMEM((rows, hidden), bf16),
        pltpu.VMEM((rows, hidden), bf16),
        pltpu.VMEM((tiles, width, BLOCK), bf16),
        pltpu.VMEM((hidden, width), bf16),
        pltpu.SemaphoreType.DMA((tiles + 1,)),
        pltpu.SemaphoreType.DMA((4,)),
    ]
    return call(kernel, ins, outs, scratch, 6 * 10**9, "forward_mlp", after=after)


def last_layer(layer, length, parts, tau, vectors, cotangent, rows_of, after):
    rows = cotangent.shape[0] // parts
    width = cotangent.shape[1]
    seqs = rows // length

    def kernel(tau_ref, vec_ref, cot_ref, *refs):
        result_ref, sums_ref = refs[-2:]
        sums_ref[...] = jnp.zeros_like(sums_ref)
        for m in range(parts):
            x1_ref, own_ref, got_ref = refs[3 * m : 3 * m + 3]

            def body(at):
                here, there = rows_at(at), rows_at(pl.multiple_of(at + m * rows, CHUNK))
                x2 = x1_ref[here, :] + own_ref[here, :].astype(f32) + got_ref[here, :].astype(f32)
                t = tau_ref[pl.ds(at // length * parts + m, 1), :]
                sums_ref[...] += fold(cot_ref[there, :].astype(f32) * x2) * t
                result_ref[there, :] = x2 * (1.0 + t * vector(vec_ref, TIME, layer))

            chunks(rows, body)

    ins = [(tau, False), (vectors, False), (cotangent, False)] + [(v, False) for part in rows_of for v in part]
    outs = [(cotangent.shape, f32, False), ((8, width), f32, False)]
    return call(kernel, ins, outs, [], 10**8, "last_layer", after=after)


def backward_mlp(layer, last, part_index, length, swapped, head, x2, tau, vectors, slope, w_up, w_down, after):
    rows = slope.shape[0]
    width = vectors.shape[1]
    hidden = w_up.shape[2]
    tiles = hidden // BLOCK
    seqs = rows // length
    parts = tau.shape[0] // seqs

    def kernel(*refs):
        it = iter(refs)
        take = lambda n: [next(it) for _ in range(n)]
        head_refs = take(len(head))
        x2_ref = None if last else take(1)[0]
        tau_ref, vec_ref, slope_ref, wu_any, wd_any = take(5)
        g2_ref, gm_ref, du_ref, part_ref, sums_ref = take(5)
        wu, wd, sems = take(3)
        downs = [
            pltpu.make_async_copy(
                wd_any.at[layer, pl.ds(t * BLOCK, BLOCK), :], wd.at[t], sems.at[t]
            )
            for t in range(tiles)
        ]
        up = pltpu.make_async_copy(wu_any.at[layer], wu, sems.at[tiles])
        for c in downs:
            c.start()
        up.start()
        sums_ref[...] = jnp.zeros_like(sums_ref)

        def begin(at, g):
            here = rows_at(at)
            t = tau_ref[pl.ds(at // length * parts + part_index, 1), :]
            if not last:
                sums_ref[16:24, :] += fold(g * x2_ref[here, :]) * t
            g2 = g * (1.0 + t * vector(vec_ref, TIME, layer))
            g2_ref[here, :] = g2
            gm_ref[here, :] = g2.astype(bf16)

        if last:
            low = 0
            for ref, (_, start, count) in zip(head_refs, head):
                chunks(
                    low + count,
                    lambda at, ref=ref, shift=start - low: begin(
                        at, ref[rows_at(pl.multiple_of(at + shift, CHUNK)), :].astype(f32)
                    ),
                    low,
                )
                low += count
        else:
            g1, x, own, got = head_refs

            def through_norm(at):
                here = rows_at(at)
                dn = own[here, :].astype(f32) + got[other_rows(at, rows, swapped), :].astype(f32)
                xhat, inverse = standardize(x[here, :])
                sums_ref[0:8, :] += fold(dn * xhat)
                sums_ref[8:16, :] += fold(dn)
                begin(at, g1[here, :] + norm_backward(dn, xhat, inverse, vector(vec_ref, GAIN, 2 * layer + 2)))

            chunks(rows, through_norm)
        for t in range(tiles):
            downs[t].wait()
            at = slice(t * BLOCK, (t + 1) * BLOCK)
            dh = mm_t(gm_ref[...], wd[t])
            du_ref[:, at] = (dh * slope_ref[:, at].astype(f32)).astype(bf16)
        up.wait()
        for b in range(0, width, BLOCK):
            part_ref[:, b : b + BLOCK] = mm_t(du_ref[...], wu[b : b + BLOCK, :]).astype(bf16)

    ins = [(a[0] if last else a, False) for a in head]
    ins += [] if last else [(x2, False)]
    ins += [(a, False) for a in (tau, vectors, slope)]
    ins += [(w_up, True), (w_down, True)]
    near = lambda n, d: ((rows, n), d, False)
    outs = [near(width, f32), near(width, bf16), near(hidden, bf16), near(width, bf16)]
    outs += [((24, width), f32, False)]
    scratch = [
        pltpu.VMEM((width, hidden), bf16),
        pltpu.VMEM((tiles, BLOCK, width), bf16),
        pltpu.SemaphoreType.DMA((tiles + 1,)),
    ]
    return call(kernel, ins, outs, scratch, 6 * 10**9, "backward_mlp", after=after)


def input_gradient(layer, swapped, own_rows, vectors, rows_of, after):
    rows, width = rows_of[0][1].shape

    def kernel(vec_ref, *refs):
        out_ref, sums_ref = refs[-2:]
        sums_ref[...] = jnp.zeros_like(sums_ref)
        for m in range(len(rows_of)):
            g1_ref, x_ref, own_ref, got_ref = refs[4 * m : 4 * m + 4]

            def body(at, mine):
                here = rows_at(at)
                dn = own_ref[here, :].astype(f32) + got_ref[other_rows(at, rows, swapped), :].astype(f32)
                xhat, inverse = standardize(x_ref[here, :])
                sums_ref[0:8, :] += fold(dn * xhat)
                sums_ref[8:16, :] += fold(dn)
                if mine:
                    out_ref[rows_at(pl.multiple_of(at + m * own_rows, CHUNK)), :] = g1_ref[here, :] + norm_backward(
                        dn, xhat, inverse, vector(vec_ref, GAIN, 2 * layer)
                    )

            chunks(own_rows, lambda at: body(at, True))
            chunks(rows, lambda at: body(at, False), own_rows)

    ins = [(vectors, False)] + [(v, False) for part in rows_of for v in part]
    outs = [((own_rows * len(rows_of), width), f32, False), ((16, width), f32, False)]
    return call(kernel, ins, outs, [], 10**8, "input_gradient", after=after)


def totals(sums, layers, width, after):
    def kernel(*refs):
        out = refs[-1]
        out[...] = jnp.zeros_like(out)
        for ref, (layer, rows, factor, _) in zip(refs, sums):
            for j, row in enumerate(rows):
                if row is not None:
                    out[layer, row : row + 1, :] += factor * jnp.sum(ref[8 * j : 8 * j + 8, :], axis=0, keepdims=True)

    ins = [(v, False) for _, _, _, v in sums]
    return call(kernel, ins, [((layers, 8, width), f32, False)], [], 10**8, "totals", after=after)[0]


def backward_attention(layer, length, swapped, g2, x1, own, got, vectors, q, k, v, w_qkv, w_out, tables, after):
    rows, width = x1.shape
    local = w_out.shape[1]
    block = min(BLOCK, local)
    scale = HD ** (-0.5)

    def kernel(g2_ref, x1_ref, own_ref, got_ref, vec_ref, q_ref, k_ref, v_ref, wq_any, wo_any, cos_any, sin_any,
               g1_ref, ga_ref, dq_ref, dk_ref, dv_ref, part_ref, sums_ref, wq, wo, do_ref, cos_ref, sin_ref, sems):
        copies = [pltpu.make_async_copy(wo_any.at[layer], wo, sems.at[3])]
        copies += [pltpu.make_async_copy(cos_any, cos_ref, sems.at[4])]
        copies += [pltpu.make_async_copy(sin_any, sin_ref, sems.at[5])]
        copies += [pltpu.make_async_copy(wq_any.at[layer, j], wq.at[j], sems.at[j]) for j in range(3)]
        for c in copies:
            c.start()
        sums_ref[...] = jnp.zeros_like(sums_ref)

        def begin(at):
            here = rows_at(at)
            dn = own_ref[here, :].astype(f32) + got_ref[other_rows(at, rows, swapped), :].astype(f32)
            xhat, inverse = standardize(x1_ref[here, :])
            sums_ref[0:8, :] += fold(dn * xhat)
            sums_ref[8:16, :] += fold(dn)
            g1 = g2_ref[here, :] + norm_backward(dn, xhat, inverse, vector(vec_ref, GAIN, 2 * layer + 1))
            g1_ref[here, :] = g1
            ga_ref[here, :] = g1.astype(bf16)

        chunks(rows, begin)
        for c in copies[:3]:
            c.wait()
        for b in range(0, local, block):
            do_ref[:, b : b + block] = mm_t(ga_ref[...], wo[b : b + block, :]).astype(bf16)
        low = masks()
        for s in range(0, rows, length):
            for b in range(0, local, 2 * HD):
                here = (slice(s, s + length), slice(b, b + 2 * HD))
                lanes = slice(b, b + 2 * HD)
                keys = both_heads(k_ref[here], low)
                grad = do_ref[here]
                probs = softmax(mm_t(q_ref[here], keys) * scale)
                dps = halves(mm_t(grad, both_heads(v_ref[here], low)))
                ds = [p * (d - jnp.sum(p * d, axis=-1, keepdims=True)) for p, d in zip(probs, dps)]
                across_heads = lambda v, w: mm(beside(v[0].T, v[1].T).astype(bf16), both_heads(w, low))
                dv_ref[here] = across_heads(probs, grad).astype(bf16)
                dq = mm(beside(*ds).astype(bf16), keys) * scale
                dk = across_heads(ds, q_ref[here]) * scale
                for d, out in ((dq, dq_ref), (dk, dk_ref)):
                    out[here] = (d * cos_ref[:, lanes] + partner(d * sin_ref[:, lanes])).astype(bf16)
        for c in copies[3:]:
            c.wait()
        for b in range(0, width, BLOCK):
            at = slice(b, b + BLOCK)
            part = mm_t(dq_ref[...], wq[0, at, :]) + mm_t(dk_ref[...], wq[1, at, :])
            part_ref[:, at] = (part + mm_t(dv_ref[...], wq[2, at, :])).astype(bf16)

    ins = [(a, False) for a in (g2, x1, own, got, vectors, q, k, v)] + [(w_qkv, True), (w_out, True)]
    ins += [(t, True) for t in tables]
    near = lambda n, d: ((rows, n), d, False)
    outs = [near(width, f32), near(width, bf16)] + [near(local, bf16)] * 3
    outs += [near(width, bf16), ((16, width), f32, False)]
    scratch = [
        pltpu.VMEM((3, width, local), bf16),
        pltpu.VMEM((local, width), bf16),
        pltpu.VMEM((rows, local), bf16),
        pltpu.VMEM((length, local), f32),
        pltpu.VMEM((length, local), f32),
        pltpu.SemaphoreType.DMA((6,)),
    ]
    return call(kernel, ins, outs, scratch, 7 * 10**9, "backward_attention", after=after)


class Links:
    def __init__(self, dp, tensor):
        self.dp, self.tensor = dp, tensor
        self.chips = dp // 2
        self.ring = dp == 16
        self.walk = [0, 2, 4, 6, 7, 5, 3, 1]
        place = [self.walk.index(i) for i in range(8)]
        self.place = place
        self.ring_pairs = []
        for k in range(8):
            here, there = self.walk[k], self.walk[(k + 1) % 8]
            self.ring_pairs.append((2 * here, 2 * there))
            self.ring_pairs.append((2 * there + 1, 2 * here + 1))
        self.core_pairs = [(i, i ^ 1) for i in range(dp)]

    def ring_place(self):
        i = lax.axis_index("dp")
        p = jnp.asarray(self.place, jnp.int32)[i >> 1]
        return jnp.where(i & 1 == 0, p, (8 - p) % 8)

    def swap_tensor(self, v):
        return lax.ppermute(v, "tensor", [(0, 1), (1, 0)])

    def gather_tensor(self, v):
        if self.tensor != 2:
            return lax.all_gather(v, "tensor", axis=0, tiled=True)
        other = self.swap_tensor(v)
        first = lax.axis_index("tensor") == 0
        return jnp.concatenate([jnp.where(first, v, other), jnp.where(first, other, v)])

    def start_sum(self, part):
        part = part.astype(bf16)
        if self.tensor != 2:
            summed = lax.psum(part, "tensor")
            return (summed, jnp.zeros_like(summed))
        return (part, self.swap_tensor(part))

def total(parts):
    out = parts[0].astype(f32)
    for p in parts[1:]:
        out = out + p.astype(f32)
    return out


def over_rows(lefts, rights):
    return across(jnp.concatenate(lefts), jnp.concatenate(rights))


def mlp_gradients(h, gm, n2, du, core, place, after):
    n = len(h)
    hidden, width = h[0].shape[1], gm[0].shape[1]
    half_hidden = hidden // 2
    tall = half_hidden // 8
    wide = width // 8

    def kernel(s_ref, *refs):
        hs, gms, ns, dus = [refs[n * j : n * j + n] for j in range(4)]

        def make(target, half, p):
            gm_all = jnp.concatenate([r[...] for r in gms])
            columns = slice(half * half_hidden, (half + 1) * half_hidden)
            du_all = jnp.concatenate([r[:, columns] for r in dus])
            for j in range(4):
                first = half * half_hidden + j * 2 * tall
                down = across(jnp.concatenate([r[:, first : first + 2 * tall] for r in hs]), gm_all)
                up = across(jnp.concatenate([r[:, j * 2 * wide : (j + 1) * 2 * wide] for r in ns]), du_all)
                for i in range(2):
                    slot = lax.rem(p - (2 * j + i) + 8, 8)
                    target[slot, 0:tall, :] = down[i * tall : (i + 1) * tall].astype(bf16)
                    target[slot, tall : tall + wide, :] = up[i * wide : (i + 1) * wide].astype(bf16)

        for c in range(2):

            @pl.when(s_ref[0] == c)
            def _():
                make(refs[4 * n], 1 - c, lax.rem(8 - s_ref[1], 8))
                make(refs[4 * n + 1], c, s_ref[1])

    ins = [(jnp.stack([core, place]).astype(jnp.int32), False)]
    ins += [(v, False) for group in (h, gm, n2, du) for v in group]
    out = ((8, tall + wide, width), bf16, False)
    return call(kernel, ins, [out, out], [], 9 * 10**9, "mlp_gradients", after=after, limit=SMALL)


def attention_gradients(att, ga, n1, dq, dk, dv, core, place, after):
    n = len(att)
    local, width = att[0].shape[1], ga[0].shape[1]
    heads, wide = local // 2, width // 2

    def kernel(s_ref, *refs):
        atts, gas, ns = [refs[n * j : n * j + n] for j in range(3)]
        dps = [refs[n * j : n * j + n] for j in range(3, 6)]

        def make(target, half, p):
            def put(value, low, size):
                for b in range(8):
                    slot = lax.rem(p - b + 8, 8)
                    target[slot, low : low + size, :] = value[b * size : (b + 1) * size].astype(bf16)

            lefts = [r[:, half * heads : (half + 1) * heads] for r in atts]
            for j in range(2):
                put(over_rows(lefts, [r[:, j * wide : (j + 1) * wide] for r in gas]), heads // 8 * j, heads // 8)
            lefts = [r[:, half * wide : (half + 1) * wide] for r in ns]
            for j in range(3):
                put(over_rows(lefts, [r[...] for r in dps[j]]), heads // 4 + wide // 8 * j, wide // 8)

        for c in range(2):

            @pl.when(s_ref[0] == c)
            def _():
                make(refs[6 * n], 1 - c, lax.rem(8 - s_ref[1], 8))
                make(refs[6 * n + 1], c, s_ref[1])

    ins = [(jnp.stack([core, place]).astype(jnp.int32), False)]
    ins += [(v, False) for group in (att, ga, n1, dq, dk, dv) for v in group]
    out = ((8, heads // 4 + 3 * wide // 8, local), bf16, False)
    return call(kernel, ins, [out, out], [], 5 * 10**9, "attention_gradients", after=after, limit=SMALL)


def pack(lanes, after):
    depths = [lane[0].shape[0] for lane in lanes]
    count, width = len(lanes[0]), lanes[0][0].shape[1]

    def kernel(*refs):
        low = 0
        for j, depth in enumerate(depths):
            for i in range(count):
                refs[-1][i, low : low + depth, :] = refs[j * count + i][...]
            low += depth

    out = ((count, sum(depths), width), bf16, False)
    ins = [(v, False) for lane in lanes for v in lane]
    return call(kernel, ins, [out], [], 10**8, "pack", after=after, limit=SMALL)[0]


def merge(a, b, lanes, after):
    count, depth, width = a.shape
    depth //= lanes

    def kernel(a_ref, b_ref, *outs):
        def total(i, j):
            at = slice(j * depth, (j + 1) * depth)
            return (a_ref[i, at, :].astype(f32) + b_ref[i, at, :].astype(f32)).astype(bf16)

        for j in range(lanes):
            outs[2 * j][...] = total(0, j)

        def body(i, carry):
            for j in range(lanes):
                outs[2 * j + 1][i] = total(i, j)
            return carry

        lax.fori_loop(1, count, body, 0)

    outs = [((depth, width), bf16, False), ((count, depth, width), bf16, False)] * lanes
    out = call(kernel, [(a, False), (b, False)], outs, [], 10**8, "merge", after=after, limit=SMALL)
    return out[0::2], out[1::2]


def add(a, blocks, i, after):
    def kernel(a_ref, b_ref, out_ref):
        out_ref[...] = (a_ref[...].astype(f32) + b_ref[i].astype(f32)).astype(bf16)

    outs = [(a.shape, bf16, False)]
    return call(kernel, [(a, False), (blocks, False)], outs, [], 10**8, "add", after=after, limit=SMALL)[0]


def hold(a, after):
    def kernel(a_ref, out_ref):
        out_ref[...] = a_ref[...]

    return call(kernel, [(a, False)], [(a.shape, bf16, False)], [], 10**8, "hold", after=after, limit=SMALL)[0]


DEEP = 4


def spread(pieces, shapes, mine, peer, core, place, before, after):
    depth, width = mine.shape[1:]

    def kernel(s_ref, mine_ref, peer_ref, *refs):
        token_ref, held, sems = refs[-3:]
        outs = refs[len(refs) - 3 - len(shapes) : -3]
        token_ref[...] = jnp.zeros_like(token_ref)

        def copies(i):
            half, p = (s_ref[0], s_ref[1]) if i < 8 else (1 - s_ref[0], lax.rem(8 - s_ref[1], 8))
            b = lax.rem(p + 1 - i % 8 + 8, 8)
            return [
                pltpu.make_async_copy(
                    held.at[(i % DEEP,) + source], outs[o].at[place], sems.at[i % DEEP, j]
                )
                for j, (source, o, place) in enumerate(pieces(half, b))
            ]

        for i in range(16):
            if i >= DEEP:
                for c in copies(i - DEEP):
                    c.wait()
            held[i % DEEP] = (mine_ref if i < 8 else peer_ref)[i % 8].astype(f32)
            for c in copies(i):
                c.start()
        for i in range(16 - DEEP, 16):
            for c in copies(i):
                c.wait()

    ins = [(jnp.stack([core, place]).astype(jnp.int32), False), (mine, False), (peer, False)]
    aliases = {}
    if before is not None:
        for j, v in enumerate(before):
            aliases[len(ins)] = j
            ins.append((v, True))
    scratch = [
        pltpu.VMEM((DEEP, depth, width), f32),
        pltpu.SemaphoreType.DMA((DEEP, len(pieces(0, 0)))),
    ]
    outs = [(s, f32, True) for s in shapes] + [((8, 128), f32, False)]
    *outs, token = call(kernel, ins, outs, scratch, 10**8, "spread", aliases, after=after, limit=SMALL)
    return outs, token


def mlp_pieces(layer, layers, hidden, width):
    tall, wide = hidden // 16, width // 8

    def pieces(half, b):
        rows = pl.ds(pl.multiple_of(half * (hidden // 2) + b * tall, tall), tall)
        across_rows = pl.ds(pl.multiple_of(b * wide, wide), wide)
        columns = pl.ds(pl.multiple_of(half * (hidden // 2), hidden // 2), hidden // 2)
        return [
            ((slice(0, tall), slice(None)), 0, (layer, rows, slice(None))),
            ((slice(tall, tall + wide), slice(None)), 1, (layer, across_rows, columns)),
        ]

    return pieces, [(layers, hidden, width), (layers, width, hidden)]


def attention_pieces(layer, layers, local, width):
    tall, wide = local // 16, width // 16

    def pieces(half, b):
        rows = pl.ds(pl.multiple_of(half * (local // 2) + b * tall, tall), tall)
        deep = pl.ds(pl.multiple_of(half * (width // 2) + b * wide, wide), wide)
        out = []
        for j in range(2):
            columns = slice(j * width // 2, (j + 1) * width // 2)
            out.append(((slice(tall * j, tall * (j + 1)), slice(None)), 0, (layer, rows, columns)))
        for j in range(3):
            low = 2 * tall + wide * j
            out.append(((slice(low, low + wide), slice(None)), 1, (layer, j, deep, slice(None))))
        return out

    return pieces, [(layers, local, width), (layers, 3, width, local)]


class Stream:
    def __init__(self, links, kind, layer, layers, groups, after, written):
        self.links, self.kind, self.written = links, kind, written
        self.steps = -2
        self.lanes = LANES[kind][min(layer, 1)]
        self.core = lax.axis_index("dp") & 1
        self.p = links.ring_place()
        if kind == "mlp":
            send, self.blocks = mlp_gradients(*groups, self.core, self.p, after)
            self.layout = mlp_pieces(layer, layers, groups[0][0].shape[1], groups[1][0].shape[1])
        else:
            send, self.blocks = attention_gradients(*groups, self.core, self.p, after)
            self.layout = attention_pieces(layer, layers, groups[0][0].shape[1], groups[1][0].shape[1])
        self.raw = lax.ppermute(send, "dp", links.core_pairs)
        self.done = [[] for _ in range(self.lanes)]
        self.token = self.blocks

    def step(self, after):
        self.steps += 1
        if self.steps < 0:
            return []
        if self.steps == 15:
            before = self.written.get(self.kind)
            self.written[self.kind], token = spread(
                *self.layout, self.mine, self.raw, self.core, self.p, before, after
            )
            return [token]
        if self.steps == 14:
            for lane, v in zip(self.done, self.raw):
                lane.append(v)
            self.mine = pack(self.done, after)
            self.raw = lax.ppermute(self.mine, "dp", self.links.core_pairs)
            return [self.mine]
        if self.steps == 0:
            now, self.blocks = merge(self.blocks, self.raw, self.lanes, after)
        elif self.steps < 8:
            now = [add(r, b, self.steps, after) for r, b in zip(self.raw, self.blocks)]
        else:
            now = [hold(r, after) for r in self.raw]
        if self.steps >= 7:
            for lane, v in zip(self.done, now):
                lane.append(v)
        self.raw = [lax.ppermute(v, "dp", self.links.ring_pairs) for v in now]
        return list(now)

    def going(self):
        return self.steps < 15


LANES = {"mlp": (2, 1), "attention": (1, 1)}


class Plain:
    def __init__(self, links, kind, layer, layers, groups, after, written):
        left, right, deep, *dps = [jnp.concatenate(g) for g in groups]
        out = [ein("ra,rb->ab", left, right)]
        if kind == "mlp":
            out.append(ein("ra,rb->ab", deep, dps[0]))
        else:
            out.append(jnp.stack([ein("ra,rb->ab", deep, d) for d in dps]))
        out = [lax.psum(v.astype(bf16), "dp").astype(f32) for v in out]
        if kind not in written:
            written[kind] = [jnp.zeros((layers,) + v.shape, f32) for v in out]
        written[kind] = [b.at[layer].set(v) for b, v in zip(written[kind], out)]
        self.token = after[0]

    def going(self):
        return False

def make_local(links):
    def local(
        tokens,
        time_index,
        time_table,
        norm_gain,
        norm_bias,
        w_qkv,
        w_out,
        w_up,
        w_down,
        time_weight,
        cotangent,
    ):
        rows, width = tokens.shape
        seq_here = time_index.shape[0]
        length = rows // seq_here
        layers = norm_gain.shape[0]
        local_width = w_out.shape[1]
        tables = rope_tables(length, local_width)
        parts = 2 if seq_here % 2 == 0 else 1
        own = rows // parts
        paired = links.tensor == 2
        wq = jnp.transpose(w_qkv, (0, 2, 1, 3))

        def group_rows(v, m):
            if paired:
                got = links.swap_tensor(v[m * own : (m + 1) * own])
                return [(v, m * own, own), (got, 0, own)]
            v = links.gather_tensor(v[m * own : (m + 1) * own])
            return [(v, 0, v.shape[0])]

        heads = [group_rows(tokens, m) for m in range(parts)]
        gs = [group_rows(cotangent, m) for m in range(parts)]
        arrived = [g[-1][0] for g in gs]
        vectors = [norm_gain.reshape(2 * layers, width), norm_bias.reshape(2 * layers, width)]
        vectors += [time_weight, jnp.zeros((layers, width), f32)]
        vectors = jnp.concatenate(vectors)
        if paired:
            index = jnp.concatenate([time_index, links.swap_tensor(time_index)])
        else:
            index = links.gather_tensor(time_index)
        onehot = (index[:, None] == jnp.arange(time_table.shape[0], dtype=jnp.int32)[None, :]).astype(f32)
        tau = jnp.dot(onehot, time_table, precision=lax.Precision.HIGHEST)
        saved = [[None] * parts for _ in range(layers)]
        after = [[None] * parts for _ in range(layers)]
        for l in range(layers):
            for m in range(parts):
                x_near, part, *out = forward_attention(
                    l, m, length, paired, heads[m], tau, vectors, wq, w_out, tables
                )
                if l > 0:
                    after[l - 1][m] = out.pop()
                saved[l][m] = out
                heads[m] = (x_near, *links.start_sum(part))
            for m in range(parts):
                split = paired and l == layers - 1
                x1, *out = forward_mlp(l, paired, split, *heads[m], vectors, w_up, w_down, arrived)
                if split:
                    heads[m] = (x1, *out[:2])
                else:
                    heads[m] = (x1, *links.start_sum(out[0]))
                saved[l][m] += out[1 + split :]
                arrived = []

        kind = Stream if links.ring else Plain
        streams = []
        small = []
        share = 0.5 if paired else 1.0
        keep = lambda l, i: [s[i] for s in saved[l]]

        last, written = [], {}

        def step(also=()):
            before = list(also)
            for s in streams:
                if s.going():
                    before += s.step(list(last))
            return before

        def ran(out):
            last[:] = [out]

        gs_first = gs
        gs = list(gs)
        for l in reversed(range(layers)):
            g2s, gms, dus, sums = [None] * parts, [None] * parts, [None] * parts, [None] * parts
            for m in range(parts):
                g2s[m], gms[m], dus[m], part, s = backward_mlp(
                    l, l == layers - 1, m, length, paired, gs[m], after[l][m], tau, vectors, saved[l][m][9],
                    w_up, w_down, step(),
                )
                ran(s)
                if l < layers - 1:
                    small.append((l + 1, (0, 2), share, s))
                    small.append((l, (None, None, 4), share, s))
                sums[m] = links.start_sum(part)
            groups = [keep(l, 8), gms, keep(l, 7), dus]
            streams.append(kind(links, "mlp", l, layers, groups, step([sums[0][1]]), written))
            ran(streams[-1].token)
            gas, dps = [None] * parts, [None] * parts
            for m in range(parts):
                x, n1, q, k, v, att, x1 = saved[l][m][:7]
                g1, gas[m], dq, dk, dv, part, s = backward_attention(
                    l, length, paired, g2s[m], x1, *sums[m], vectors, q, k, v, wq, w_out, tables, step()
                )
                ran(s)
                small.append((l, (1, 3), share, s))
                dps[m] = (dq, dk, dv)
                gs[m] = (g1, x, *links.start_sum(part))
            groups = [keep(l, 5), gas, keep(l, 1)] + [[d[j] for d in dps] for j in range(3)]
            streams.append(kind(links, "attention", l, layers, groups, step([gs[0][3]]), written))
            ran(streams[-1].token)
        tiny, ends, due = [], {}, {}

        def by(round_number, array):
            due.setdefault(round_number, []).append(array)

        def send_last(r):
            if paired:
                for m in range(parts):
                    x1, mine_part, theirs = heads[m]
                    heads[m] = (x1, mine_part, links.swap_tensor(hold(theirs, list(last))))
                    by(r + 2 + m, heads[m][2])

        def end_layers(r):
            cot = cotangent if paired else jnp.concatenate([g[0][0] for g in gs_first])
            ends["result"], s = last_layer(layers - 1, length, parts, tau, vectors, cot, heads, list(last))
            small.append((layers - 1, (4,), 1.0, s))
            by(r + 1, s)

        def end_input(r):
            rows_here = own if paired else gs[0][1].shape[0]
            ends["inputs"], s = input_gradient(0, paired, rows_here, vectors, gs, list(last))
            small.append((0, (0, 2), share, s))
            by(r + 1, s)

        def add_up(r):
            tiny.append(totals(small, layers, width, list(last)))
            by(r + 1, tiny[-1])

        def exchange(axis, pairs, r):
            got = lax.ppermute(tiny[-1], axis, pairs)
            by(r + 2, got)
            tiny.append((tiny[-1], got))

        def take(r):
            tiny.append(tiny[-1][0] + tiny[-1][1])

        nothing = lambda r: None
        errands = [nothing, nothing, end_input, send_last, nothing, nothing, end_layers, add_up]
        for j in range(links.dp.bit_length() - 1):
            pairs = [(i, i ^ (1 << j)) for i in range(links.dp)]
            errands += [functools.partial(exchange, "dp", pairs), take]
        if paired:
            errands += [functools.partial(exchange, "tensor", [(0, 1), (1, 0)]), take]
        for m in range(parts):
            by(1 + m, gs[m][3])
        r = 0
        while errands or any(s.going() for s in streams):
            last[:] = step(due.pop(r, []))
            if errands:
                errands.pop(0)(r)
            r += 1
        tiny = tiny[-1]
        result, inputs = ends["result"], ends["inputs"]
        if not paired:
            t = lax.axis_index("tensor")
            cut = lambda v: jnp.concatenate(
                [
                    lax.dynamic_slice_in_dim(v, m * v.shape[0] // parts + t * own, own)
                    for m in range(parts)
                ]
            )
            result, inputs = cut(result), cut(inputs)
        gains, biases = tiny[:, 0:2], tiny[:, 2:4]
        return (
            result,
            inputs,
            gains,
            biases,
            jnp.transpose(written["attention"][1], (0, 2, 1, 3)),
            written["attention"][0],
            written["mlp"][1],
            written["mlp"][0],
            tiny[:, 4],
            jnp.stack([gains[layers - 1, 1], biases[layers - 1, 1]]),
        )

    return local


def solution(mesh):
    links = Links(mesh.shape["dp"], mesh.shape["tensor"])
    token_spec = P(("dp", "tensor"), None)
    in_specs = (
        token_spec,
        P(("dp", "tensor")),
        P(),
        P(),
        P(),
        P(None, None, None, "tensor"),
        P(None, "tensor", None),
        P(None, None, "tensor"),
        P(None, "tensor", None),
        P(),
        token_spec,
    )
    out_specs = (
        token_spec,
        token_spec,
        P(),
        P(),
        P(None, None, None, "tensor"),
        P(None, "tensor", None),
        P(None, None, "tensor"),
        P(None, "tensor", None),
        P(),
        P(),
    )
    return jax.shard_map(
        make_local(links), mesh=mesh, in_specs=in_specs, out_specs=out_specs, check_vma=False
    )
```

time: 591 us -> 465 us (0.79)
  local copies, waits for them, and re-layouts: 60.4 us -> 11.7 us
  other arithmetic: 46.5 us -> 2.26 us
  starting transfers between devices: 113 us -> 82.2 us
    unnamed x370 -> x147, local copies, waits for them, and re-layouts: 52.6 us -> 5.3 us
    convert_element_type x32 -> x0, other arithmetic: 35 us -> none  [the longest x28 33.3 us: step(): got = got.astype(bf16)]
    ppermute x68 -> x83, waiting for transfers between devices: 122 us -> 153 us  [the longest x70 139 us: step(): self.raw = [lax.ppermute(v, 'dp', self.links.ring_pairs) for v in now]]
    ppermute x21, waiting for transfers between devices: 63.7 us -> 36.3 us  [swap_tensor(): return lax.ppermute(v, 'tensor', [(0, 1), (1, 0)])]
    ppermute x68 -> x83, starting transfers between devices: 85.1 us -> 62.4 us  [the longest x70 55.7 us: step(): self.raw = [lax.ppermute(v, 'dp', self.links.ring_pairs) for v in now]]
    ppermute x21, starting transfers between devices: 27.5 us -> 19.8 us  [swap_tensor(): return lax.ppermute(v, 'tensor', [(0, 1), (1, 0)])]
    pallas_call x28 -> x102, Pallas kernels: 171 us -> 170 us  [call(): pl.pallas_call(run, out_shape=[(pltpu.HBM if away else pltpu.VMEM)(s, d)...]
  transfers between devices with their start and end apart: 89 -> 104, of which waited for: 47 -> 56; matrix products, arithmetic and copies ran while one was open for 9% -> 3% of each run, Pallas kernels for 24% -> 35%
where the time goes in v2:
time: 465 us; the launch traced here: 459 us
  waiting for transfers between devices  189 us (41%)
  Pallas kernels  170 us (37%)
  starting transfers between devices  82.2 us (18%)
  local copies, waits for them, and re-layouts  11.7 us (3%)
    pallas_call x102, Pallas kernels, call(): pl.pallas_call(run, out_shape=[(pltpu.HBM if away else pltpu.VMEM)(s, d)...  170 us
    ppermute x70, waiting for transfers between devices, step(): self.raw = [lax.ppermute(v, 'dp', self.links.ring_pairs) for v in now]  139 us
    ppermute x70, starting transfers between devices, step(): self.raw = [lax.ppermute(v, 'dp', self.links.ring_pairs) for v in now]  55.7 us
    ppermute x21, waiting for transfers between devices, swap_tensor(): return lax.ppermute(v, 'tensor', [(0, 1), (1, 0)])  36.3 us
    ppermute x21, starting transfers between devices, swap_tensor(): return lax.ppermute(v, 'tensor', [(0, 1), (1, 0)])  19.8 us
    ppermute x5, waiting for transfers between devices, exchange(): got = lax.ppermute(tiny[-1], axis, pairs)  13.7 us
  transfers between devices with their start and end apart: 104, of which 56 were waited for; matrix products, arithmetic and copies ran while one was open for 3% of the time, Pallas kernels for 35%

profile of v2, /device:TPU:0, one launch (start us, length us, event | category | flops | bytes accessed | tf_op | source)
XLA Modules:
  0.0 459.4 jit_solution(17200923733125614540)
XLA Ops:
  0.7 3.0 collective-permute-start
  16.9 8.3 %collective-permute-done.1.refs_1_ = bf16[128,1024]{1,0:T(8,128)(2,1)S(1)} collective-permute-done((bf16[128,1024]{1,0:T(8,128)(2,1)S(1)}, bf16[128,1024]{1,0:T(8,128)(2,1)S(1)}, u32[]{:S(2)}, u32[]{:S(2)}) %collective-permute-start.1) | collective-permute-done | bytes 262176 | tf_op jit(solution)/shard_map/ppermute | solution.py:594
  25.3 5.1 %forward_attention.4 = (f32[256,1024]{1,0:T(8,128)S(1)}, bf16[256,1024]{1,0:T(8,128)(2,1)S(1)}, f32[256,1024]{1,0:T(8,128)}, bf16[256,1024]{1,0:T(8,128)(2,1)}, ...) custom-call(bf16[256,1024]{1,0:T(8,128)(2,1)} %refs_0_.6, ...), custom_call_target="tpu_custom_call" | custom-call | flops 80000000000 | bytes 1048576 | tf_op jit(solution)/shard_map/forward_attention/pallas_call | solution.py:124
  30.5 5.1 %forward_attention.6 = (f32[256,1024]{1,0:T(8,128)S(1)}, bf16[256,1024]{1,0:T(8,128)(2,1)S(1)}, f32[256,1024]{1,0:T(8,128)}, bf16[256,1024]{1,0:T(8,128)(2,1)}, ...) custom-call(bf16[256,1024]{1,0:T(8,128)(2,1)} %refs_0_.6, ...), custom_call_target="tpu_custom_call" | custom-call | flops 80000000000 | bytes 1048576 | tf_op jit(solution)/shard_map/forward_attention/pallas_call | solution.py:124
  37.6 7.7 %collective-permute-done.2.refs_2_ = bf16[256,1024]{1,0:T(8,128)(2,1)S(1)} collective-permute-done((bf16[256,1024]{1,0:T(8,128)(2,1)S(1)}, bf16[256,1024]{1,0:T(8,128)(2,1)S(1)}, u32[]{:S(2)}, u32[]{:S(2)}) %collective-permute-start.2) | collective-permute-done | bytes 524320 | tf_op jit(solution)/shard_map/ppermute | solution.py:594
  45.3 6.4 %forward_mlp.4 = (f32[256,1024]{1,0:T(8,128)S(1)}, bf16[256,1024]{1,0:T(8,128)(2,1)S(1)}, f32[256,1024]{1,0:T(8,128)}, bf16[256,1024]{1,0:T(8,128)(2,1)}, bf16[2...) custom-call(f32[256,1024]{1,0:T(8,128)S(1)} %get-tuple-element.149.refs_0_, ...), custom_call_target="tpu_custom_call" | custom-call | flops 120000004096 | bytes 1048576 | tf_op jit(solution)/shard_map/forward_mlp/pallas_call | solution.py:124
  51.8 4.7 %collective-permute-done.10.refs_2_ = bf16[256,1024]{1,0:T(8,128)(2,1)S(1)} collective-permute-done((bf16[256,1024]{1,0:T(8,128)(2,1)S(1)}, bf16[256,1024]{1,0:T(8,128)(2,1)S(1)}, u32[]{:S(2)}, u32[]{:S(2)}) %collective-permute-start.10) | collective-permute-done | bytes 524320 | tf_op jit(solution)/shard_map/ppermute | solution.py:594
  56.5 6.4 %forward_mlp.6 = (f32[256,1024]{1,0:T(8,128)S(1)}, bf16[256,1024]{1,0:T(8,128)(2,1)S(1)}, f32[256,1024]{1,0:T(8,128)}, bf16[256,1024]{1,0:T(8,128)(2,1)}, bf16[2...) custom-call(f32[256,1024]{1,0:T(8,128)S(1)} %get-tuple-element.171.refs_0_, ...), custom_call_target="tpu_custom_call" | custom-call | flops 120000004096 | bytes 1048576 | tf_op jit(solution)/shard_map/forward_mlp/pallas_call | solution.py:124
  63.1 4.7 %collective-permute-done.5.refs_2_ = bf16[256,1024]{1,0:T(8,128)(2,1)S(1)} collective-permute-done((bf16[256,1024]{1,0:T(8,128)(2,1)S(1)}, bf16[256,1024]{1,0:T(8,128)(2,1)S(1)}, u32[]{:S(2)}, u32[]{:S(2)}) %collective-permute-start.5) | collective-permute-done | bytes 524320 | tf_op jit(solution)/shard_map/ppermute | solution.py:594
  67.8 5.3 %forward_attention.5 = (f32[256,1024]{1,0:T(8,128)S(1)}, bf16[256,1024]{1,0:T(8,128)(2,1)S(1)}, f32[256,1024]{1,0:T(8,128)}, bf16[256,1024]{1,0:T(8,128)(2,1)}, ...) custom-call(f32[256,1024]{1,0:T(8,128)S(1)} %get-tuple-element.151.r, ...), custom_call_target="tpu_custom_call" | custom-call | flops 80000000000 | bytes 1048576 | tf_op jit(solution)/shard_map/forward_attention/pallas_call | solution.py:124
  73.2 5.8 %collective-permute-done.11.refs_2_ = bf16[256,1024]{1,0:T(8,128)(2,1)S(1)} collective-permute-done((bf16[256,1024]{1,0:T(8,128)(2,1)S(1)}, bf16[256,1024]{1,0:T(8,128)(2,1)S(1)}, u32[]{:S(2)}, u32[]{:S(2)}) %collective-permute-start.11) | collective-permute-done | bytes 524320 | tf_op jit(solution)/shard_map/ppermute | solution.py:594
  79.0 6.1 %forward_attention.7 = (f32[256,1024]{1,0:T(8,128)S(1)}, bf16[256,1024]{1,0:T(8,128)(2,1)}, f32[256,1024]{1,0:T(8,128)}, bf16[256,1024]{1,0:T(8,128)(2,1)}, bf16...) custom-call(f32[256,1024]{1,0:T(8,128)S(1)} %get-tuple-element.173.r, ...), custom_call_target="tpu_custom_call" | custom-call | flops 80000000000 | bytes 1048576 | tf_op jit(solution)/shard_map/forward_attention/pallas_call | solution.py:124
  85.2 5.0 %collective-permute-done.6.refs_2_ = bf16[256,1024]{1,0:T(8,128)(2,1)S(1)} collective-permute-done((bf16[256,1024]{1,0:T(8,128)(2,1)S(1)}, bf16[256,1024]{1,0:T(8,128)(2,1)S(1)}, u32[]{:S(2)}, u32[]{:S(2)}) %collective-permute-start.6) | collective-permute-done | bytes 524320 | tf_op jit(solution)/shard_map/ppermute | solution.py:594
  90.2 6.5 %forward_mlp.5 = (f32[256,1024]{1,0:T(8,128)S(1)}, bf16[128,1024]{1,0:T(8,128)(2,1)S(1)}, bf16[128,1024]{1,0:T(8,128)(2,1)S(1)}, f32[256,1024]{1,0:T(8,128)}, bf...) custom-call(f32[256,1024]{1,0:T(8,128)S(1)} %get-tuple-element.153.refs_0_, ...), custom_call_target="tpu_custom_call" | custom-call | flops 120000004096 | bytes 1048576 | tf_op jit(solution)/shard_map/forward_mlp/pallas_call | solution.py:124
  97.9 7.8 %backward_mlp.4 = (f32[256,1024]{1,0:T(8,128)S(1)}, bf16[256,1024]{1,0:T(8,128)(2,1)S(1)}, bf16[256,2048]{1,0:T(8,128)(2,1)S(1)}, bf16[256,1024]{1,0:T(8,128)(2,1)}, f32[24,1024]{1,0:T(8,128)}) custom-call(bf16[256,1024]{1,0:T(8,128)(2,1)S(1)} %copy-done.4, bf16[128,1024]{1,0:T(8,128)(2,1)} %collective-permute-done.3.refs_6_.refs_1_, ...), custom_call_target="tpu_custom_call" | custom-call | flops 120000004096 | bytes 1048576 | tf_op jit(solution)/shard_map/backward_mlp/pallas_call | solution.py:124
  105.9 7.6 %forward_mlp.7 = (f32[256,1024]{1,0:T(8,128)S(1)}, bf16[128,1024]{1,0:T(8,128)(2,1)S(1)}, bf16[128,1024]{1,0:T(8,128)(2,1)S(1)}, f32[256,1024]{1,0:T(8,128)}, bf...) custom-call(f32[256,1024]{1,0:T(8,128)S(1)} %get-tuple-element.175.refs_0_, ...), custom_call_target="tpu_custom_call" | custom-call | flops 120000004096 | bytes 1048576 | tf_op jit(solution)/shard_map/forward_mlp/pallas_call | solution.py:124
  114.7 8.0 %backward_mlp.5 = (f32[256,1024]{1,0:T(8,128)S(1)}, bf16[256,1024]{1,0:T(8,128)(2,1)S(1)}, bf16[256,2048]{1,0:T(8,128)(2,1)S(1)}, bf16[256,1024]{1,0:T(8,128)(2,1)}, f32[24,1024]{1,0:T(8,128)}) custom-call(bf16[256,1024]{1,0:T(8,128)(2,1)S(1)} %copy-done.4, bf16[128,1024]{1,0:T(8,128)(2,1)} %collective-permute-done.4.refs_7_.refs_1_, ...), custom_call_target="tpu_custom_call" | custom-call | flops 120000004096 | bytes 1048576 | tf_op jit(solution)/shard_map/backward_mlp/pallas_call | solution.py:124
  124.8 5.7 %mlp_gradients.2 = (bf16[8,256,1024]{2,1,0:T(8,128)(2,1)S(1)}, bf16[8,256,1024]{2,1,0:T(8,128)(2,1)S(1)}) custom-call(s32[2]{0:T(128)S(1)} %pad_add_fusion.1.refs_0_, bf16[256,2048]{1,0:T(8,128)(2,1)S(1)} %copy-done.48, bf16[256,2048]{1,0:T(8,128)(2,1)S(1)} %copy-done.49, bf16[256,1024]{1,0:T(8,128)(2,1)S(1)} %get-tuple-element.178.refs_3_, ...), custom_call_target="tpu_custom_call" | custom-call | flops 179999997952 | bytes 1048576 | tf_op jit(solution)/shard_map/mlp_gradients/pallas_call | solution.py:124
  130.7 7.6 %backward_attention.4 = (f32[256,1024]{1,0:T(8,128)S(1)}, bf16[256,1024]{1,0:T(8,128)(2,1)S(1)}, bf16[256,512]{1,0:T(8,128)(2,1)S(1)}, bf16[256,512]{1,0:T(8,128...) custom-call(f32[256,1024]{1,0:T(8,128)S(1)} %get-tuple-element.159.refs_0_, ...), custom_call_target="tpu_custom_call" | custom-call | flops 140000002048 | bytes 1048576 | tf_op jit(solution)/shard_map/backward_attention/pallas_call | solution.py:124
  141.5 8.4 %backward_attention.5 = (f32[256,1024]{1,0:T(8,128)S(1)}, bf16[256,1024]{1,0:T(8,128)(2,1)S(1)}, bf16[256,512]{1,0:T(8,128)(2,1)S(1)}, bf16[256,512]{1,0:T(8,128...) custom-call(f32[256,1024]{1,0:T(8,128)S(1)} %get-tuple-element.190.refs_0_, ...), custom_call_target="tpu_custom_call" | custom-call | flops 140000002048 | bytes 1048576 | tf_op jit(solution)/shard_map/backward_attention/pallas_call | solution.py:124
  153.4 3.3 attention_gradients.2
  156.9 4.1 collective-permute-done.16.refs_0_
  162.7 6.2 %backward_mlp.6 = (f32[256,1024]{1,0:T(8,128)S(1)}, bf16[256,1024]{1,0:T(8,128)(2,1)S(1)}, bf16[256,2048]{1,0:T(8,128)(2,1)S(1)}, bf16[256,1024]{1,0:T(8,128)(2,1)S(1)}, f32[24,1024]{1,0:T(8,128)S(1)}) custom-call(f32[256,1024]{1,0:T(8,128)S(1)} %get-tuple-element.165.refs_0_, f32[256,1024]{1,0:T(8,128)S(1)} %copy-done.34, ...), custom_call_target="tpu_custom_call" | custom-call | flops 120000004096 | bytes 1048576 | tf_op jit(solution)/shard_map/backward_mlp/pallas_call | solution.py:124
  174.3 8.1 %backward_mlp.7 = (f32[256,1024]{1,0:T(8,128)S(1)}, bf16[256,1024]{1,0:T(8,128)(2,1)S(1)}, bf16[256,2048]{1,0:T(8,128)(2,1)S(1)}, bf16[256,1024]{1,0:T(8,128)(2,1)}, f32[24,1024]{1,0:T(8,128)S(1)}) custom-call(f32[256,1024]{1,0:T(8,128)S(1)} %get-tuple-element.217.refs_0_, f32[256,1024]{1,0:T(8,128)S(1)} %copy-done.32, ...), custom_call_target="tpu_custom_call" | custom-call | flops 120000004096 | bytes 1048576 | tf_op jit(solution)/shard_map/backward_mlp/pallas_call | solution.py:124
  187.5 7.7 %mlp_gradients.3 = (bf16[8,256,1024]{2,1,0:T(8,128)(2,1)}, bf16[8,256,1024]{2,1,0:T(8,128)(2,1)S(1)}) custom-call(s32[2]{0:T(128)S(1)} %copy-done.20, bf16[256,2048]{1,0:T(8,128)(2,1)S(1)} %copy-done.43, bf16[256,2048]{1,0:T(8,128)(2,1)S(1)} %copy-done.45, bf16[256,1024]{1,0:T(8,128)(2,1)S(1)} %get-tuple-element.227.refs_3_, ...), custom_call_target="tpu_custom_call" | custom-call | flops 179999997952 | bytes 1048576 | tf_op jit(solution)/shard_map/mlp_gradients/pallas_call | solution.py:124
  201.1 7.2 %backward_attention.6 = (f32[256,1024]{1,0:T(8,128)S(1)}, bf16[256,1024]{1,0:T(8,128)(2,1)S(1)}, bf16[256,512]{1,0:T(8,128)(2,1)S(1)}, bf16[256,512]{1,0:T(8,128...) custom-call(f32[256,1024]{1,0:T(8,128)S(1)} %get-tuple-element.210.refs_0_, ...), custom_call_target="tpu_custom_call" | custom-call | flops 140000002048 | bytes 1048576 | tf_op jit(solution)/shard_map/backward_attention/pallas_call | solution.py:124
  210.6 3.9 merge.6
  216.4 7.7 %backward_attention.7 = (f32[256,1024]{1,0:T(8,128)S(1)}, bf16[256,1024]{1,0:T(8,128)(2,1)S(1)}, bf16[256,512]{1,0:T(8,128)(2,1)S(1)}, bf16[256,512]{1,0:T(8,128...) custom-call(f32[256,1024]{1,0:T(8,128)S(1)} %get-tuple-element.238.refs_0_, ...), custom_call_target="tpu_custom_call" | custom-call | flops 140000002048 | bytes 1048576 | tf_op jit(solution)/shard_map/backward_attention/pallas_call | solution.py:124
  224.5 2.3 collective-permute-done.34.refs_0_
  227.9 3.3 attention_gradients.3
  234.7 3.1 collective-permute-done.37.refs_0_
  238.3 2.3 collective-permute-done.39.refs_0_
  241.1 7.9 %collective-permute-done.38.refs_0_ = bf16[128,1024]{1,0:T(8,128)(2,1)S(1)} collective-permute-done((bf16[128,1024]{1,0:T(8,128)(2,1)S(1)}, bf16[128,1024]{1,0:T(8,128)(2,1)S(1)}, u32[]{:S(2)}, u32[]{:S(2)}) %collective-permute-start.38) | collective-permute-done | bytes 262176 | tf_op jit(solution)/shard_map/ppermute | solution.py:869
  252.3 3.0 collective-permute-done.43.refs_0_
  255.9 2.3 collective-permute-done.42.refs_0_
  258.7 5.1 %collective-permute-done.36.refs_0_ = bf16[256,1024]{1,0:T(8,128)(2,1)S(1)} collective-permute-done((bf16[256,1024]{1,0:T(8,128)(2,1)S(1)}, bf16[256,1024]{1,0:T(8,128)(2,1)S(1)}, u32[]{:S(2)}, u32[]{:S(2)}) %collective-permute-start.36) | collective-permute-done | bytes 524320 | tf_op jit(solution)/shard_map/ppermute | solution.py:869
  265.5 4.0 collective-permute-done.47.refs_0_
  270.0 2.3 collective-permute-done.46.refs_0_
  273.5 4.4 collective-permute-done.40.refs_0_
  278.4 2.3 collective-permute-done.48.refs_0_
  289.6 2.5 input_gradient.1
  292.1 5.4 %collective-permute-done.53.refs_0_ = bf16[256,512]{1,0:T(8,128)(2,1)S(1)} collective-permute-done((bf16[256,512]{1,0:T(8,128)(2,1)S(1)}, bf16[256,512]{1,0:T(8,128)(2,1)S(1)}, u32[]{:S(2)}, u32[]{:S(2)}) %collective-permute-start.53) | collective-permute-done | bytes 262176 | tf_op jit(solution)/shard_map/ppermute | solution.py:869
  303.7 5.0 %collective-permute-done.61.refs_0_ = bf16[256,512]{1,0:T(8,128)(2,1)S(1)} collective-permute-done((bf16[256,512]{1,0:T(8,128)(2,1)S(1)}, bf16[256,512]{1,0:T(8,128)(2,1)S(1)}, u32[]{:S(2)}, u32[]{:S(2)}) %collective-permute-start.61) | collective-permute-done | bytes 262176 | tf_op jit(solution)/shard_map/ppermute | solution.py:869
  309.3 5.0 %collective-permute-done.56.refs_0_ = bf16[256,1024]{1,0:T(8,128)(2,1)S(1)} collective-permute-done((bf16[256,1024]{1,0:T(8,128)(2,1)S(1)}, bf16[256,1024]{1,0:T(8,128)(2,1)S(1)}, u32[]{:S(2)}, u32[]{:S(2)}) %collective-permute-start.56) | collective-permute-done | bytes 524320 | tf_op jit(solution)/shard_map/ppermute | solution.py:869
  315.6 7.2 %collective-permute-done.66.refs_0_ = bf16[256,512]{1,0:T(8,128)(2,1)S(1)} collective-permute-done((bf16[256,512]{1,0:T(8,128)(2,1)S(1)}, bf16[256,512]{1,0:T(8,128)(2,1)S(1)}, u32[]{:S(2)}, u32[]{:S(2)}) %collective-permute-start.66) | collective-permute-done | bytes 262176 | tf_op jit(solution)/shard_map/ppermute | solution.py:869
  324.2 4.2 collective-permute-done.57.refs_0_
  331.2 6.4 %collective-permute-done.62.refs_7_ = bf16[256,1024]{1,0:T(8,128)(2,1)S(1)} collective-permute-done((bf16[256,1024]{1,0:T(8,128)(2,1)S(1)}, bf16[256,1024]{1,0:T(8,128)(2,1)S(1)}, u32[]{:S(2)}, u32[]{:S(2)}) %collective-permute-start.62) | collective-permute-done | bytes 524320 | tf_op jit(solution)/shard_map/ppermute | solution.py:869
  341.5 3.0 collective-permute-done.70.refs_0_
  345.0 2.3 collective-permute-done.69.refs_0_
  347.8 2.3 collective-permute-done.68.refs_0_
  350.6 2.3 collective-permute-done.67.refs_0_
  354.0 4.5 collective-permute-done.74.refs_0_
  366.0 6.5 %spread.4 = (f32[2,2048,1024]{2,1,0:T(8,128)}, f32[2,1024,2048]{2,1,0:T(8,128)}, f32[8,128]{1,0:T(8,128)S(1)}) custom-call(s32[2]{0:T(128)S(1)} %copy-done.21, bf16[8,256,1024]{2,1,0:T(8,128)(2,1)S(1)} %pack.4.refs_10_.refs_1_.refs_4_.refs_2_.refs_3_, bf16[8,256,1024]{2,1,0:T(8,128)(2,1)S(1)} %collective-permute-done.71.refs_2_, ...), custom_call_target="tpu_custom_call" | custom-call | flops 2000000000 | bytes 1048576 | tf_op jit(solution)/shard_map/spread/pallas_call | solution.py:124
  375.4 3.8 collective-permute-done.87.refs_7_
  383.0 2.8 collective-permute-done.89.refs_0_
  400.7 4.5 spread.5
  408.3 3.4 collective-permute-done.99.refs_15_
  411.7 2.8 collective-permute-done.98.refs_7_
  416.2 5.1 %collective-permute-done.94.refs_0_ = bf16[256,512]{1,0:T(8,128)(2,1)S(1)} collective-permute-done((bf16[256,512]{1,0:T(8,128)(2,1)S(1)}, bf16[256,512]{1,0:T(8,128)(2,1)S(1)}, u32[]{:S(2)}, u32[]{:S(2)}) %collective-permute-start.94) | collective-permute-done | bytes 262176 | tf_op jit(solution)/shard_map/ppermute | solution.py:869
  423.4 5.3 %collective-permute-done.77.refs_1_.refs_5_ = f32[2,8,1024]{2,1,0:T(8,128)S(1)} collective-permute-done((f32[2,8,1024]{2,1,0:T(8,128)S(1)}, f32[2,8,1024]{2,1,0:T(8,128)S(1)}, u32[]{:S(2)}, u32[]{:S(2)}) %collective-permute-start.77) | collective-permute-done | bytes 65568 | tf_op jit(solution)/shard_map/ppermute | solution.py:1038
  429.1 6.5 %spread.6 = (f32[2,2048,1024]{2,1,0:T(8,128)}, f32[2,1024,2048]{2,1,0:T(8,128)}, f32[8,128]{1,0:T(8,128)S(1)}) custom-call(s32[2]{0:T(128)S(1)} %copy-done.21, bf16[8,256,1024]{2,1,0:T(8,128)(2,1)S(1)} %pack.6.refs_2_.refs_1_.refs_6_, bf16[8,256,1024]{2,1,0:T(8,128)(2,1)S(1)} %collective-permute-done.101.refs_2_, ...), custom_call_target="tpu_custom_call", output_to_operand_aliasing={{0}: (3, {}), {1}: (4, {})} | custom-call | flops 2000000000 | bytes 1048576 | tf_op jit(solution)/shard_map/spread/pallas_call | solution.py:124
  438.5 3.8 collective-permute-done.78.refs_8_
  444.6 3.4 collective-permute-done.79
  454.2 5.1 %spread.7 = (f32[2,512,1024]{2,1,0:T(8,128)}, f32[2,3,1024,512]{3,2,1,0:T(8,128)}, f32[8,128]{1,0:T(8,128)}) custom-call(s32[2]{0:T(128)S(1)} %copy-done.21, bf16[8,256,512]{2,1,0:T(8,128)(2,1)S(1)} %pack.7.refs_1_.refs_5_, bf16[8,256,512]{2,1,0:T(8,128)(2,1)S(1)} %collective-permute-done.103.refs_2_, ...), custom_call_target="tpu_custom_call", output_to_operand_aliasing={{0}: (3, {}), {1}: (4, {})} | custom-call | flops 2000000000 | bytes 1048576 | tf_op jit(solution)/shard_map/spread/pallas_call | solution.py:124
  (413 shorter events, 137.3 us)
Async XLA Ops:
  0.7 15.1 %collective-permute-start = (s32[2]{0:T(128)}, s32[2]{0:T(128)S(1)}, u32[]{:S(2)}, u32[]{:S(2)}) collective-permute-start(s32[2]{0:T(128)} %param.18), channel_id=1, source_target_pairs={{0,1},{1,0},{2,3},{3,2},{4,5},{5,4},{6,7},{7,6},{8,9},{9,8},{10,11... | collective-permute-start | bytes 32 | tf_op jit(solution)/shard_map/ppermute | solution.py:594
  4.8 25.7 %collective-permute-start.9 = (bf16[128,1024]{1,0:T(8,128)(2,1)S(1)}, bf16[128,1024]{1,0:T(8,128)(2,1)S(1)}, u32[]{:S(2)}, u32[]{:S(2)}) collective-permute-start(bf16[128,1024]{1,0:T(8,128)(2,1)S(1)} %get-tuple-element.288), channel_id=1, source_target_pairs={{0,1},{1,0},{2,3},{3,2},{4,5},{5,4},{6,7},{7,6},{8,9},{9,8},{10,11... | collective-permute-start | bytes 786440 | tf_op jit(solution)/shard_map/ppermute | solution.py:594
  6.8 30.8 %collective-permute-start.4 = (bf16[128,1024]{1,0:T(8,128)(2,1)}, bf16[128,1024]{1,0:T(8,128)(2,1)}, u32[]{:S(2)}, u32[]{:S(2)}) collective-permute-start(bf16[128,1024]{1,0:T(8,128)(2,1)} %get-tuple-element.290), channel_id=1, source_target_pairs={{0,1},{1,0},{2,3},{3,2},{4,5},{5,4},{6,7},{7,6},{8,9},{9,8},{10,11... | collective-permute-start | bytes 786440 | tf_op jit(solution)/shard_map/ppermute | solution.py:594
  8.7 16.6 %collective-permute-start.1 = (bf16[128,1024]{1,0:T(8,128)(2,1)S(1)}, bf16[128,1024]{1,0:T(8,128)(2,1)S(1)}, u32[]{:S(2)}, u32[]{:S(2)}) collective-permute-start(bf16[128,1024]{1,0:T(8,128)(2,1)S(1)} %get-tuple-element.289), channel_id=1, source_target_pairs={{0,1},{1,0},{2,3},{3,2},{4,5},{5,4},{6,7},{7,6},{8,9},{9,8},{10,11... | collective-permute-start | bytes 786440 | tf_op jit(solution)/shard_map/ppermute | solution.py:594
  8.8 28.8 %collective-permute-start.3 = (bf16[128,1024]{1,0:T(8,128)(2,1)}, bf16[128,1024]{1,0:T(8,128)(2,1)}, u32[]{:S(2)}, u32[]{:S(2)}) collective-permute-start(bf16[128,1024]{1,0:T(8,128)(2,1)} %get-tuple-element.291), channel_id=1, source_target_pairs={{0,1},{1,0},{2,3},{3,2},{4,5},{5,4},{6,7},{7,6},{8,9},{9,8},{10,11... | collective-permute-start | bytes 786440 | tf_op jit(solution)/shard_map/ppermute | solution.py:594
  30.3 14.9 %collective-permute-start.2 = (bf16[256,1024]{1,0:T(8,128)(2,1)S(1)}, bf16[256,1024]{1,0:T(8,128)(2,1)S(1)}, u32[]{:S(2)}, u32[]{:S(2)}) collective-permute-start(bf16[256,1024]{1,0:T(8,128)(2,1)S(1)} %get-tuple-element.150.refs_1_), channel_id=1, source_target_pairs={{0,1},{1,0},{2,3},{3,2},{4,5},{5,4},{6,7},{7,6},{8,9},{9,8},{10,11... | collective-permute-start | bytes 1572872 | tf_op jit(solution)/shard_map/ppermute | solution.py:594
  35.5 21.0 %collective-permute-start.10 = (bf16[256,1024]{1,0:T(8,128)(2,1)S(1)}, bf16[256,1024]{1,0:T(8,128)(2,1)S(1)}, u32[]{:S(2)}, u32[]{:S(2)}) collective-permute-start(bf16[256,1024]{1,0:T(8,128)(2,1)S(1)} %get-tuple-element.172.refs_1_), channel_id=1, source_target_pairs={{0,1},{1,0},{2,3},{3,2},{4,5},{5,4},{6,7},{7,6},{8,9},{9,8},{10,11... | collective-permute-start | bytes 1572872 | tf_op jit(solution)/shard_map/ppermute | solution.py:594
  51.7 16.1 %collective-permute-start.5 = (bf16[256,1024]{1,0:T(8,128)(2,1)S(1)}, bf16[256,1024]{1,0:T(8,128)(2,1)S(1)}, u32[]{:S(2)}, u32[]{:S(2)}) collective-permute-start(bf16[256,1024]{1,0:T(8,128)(2,1)S(1)} %get-tuple-element.152.refs_1_), channel_id=1, source_target_pairs={{0,1},{1,0},{2,3},{3,2},{4,5},{5,4},{6,7},{7,6},{8,9},{9,8},{10,11... | collective-permute-start | bytes 1572872 | tf_op jit(solution)/shard_map/ppermute | solution.py:594
  62.9 16.0 %collective-permute-start.11 = (bf16[256,1024]{1,0:T(8,128)(2,1)S(1)}, bf16[256,1024]{1,0:T(8,128)(2,1)S(1)}, u32[]{:S(2)}, u32[]{:S(2)}) collective-permute-start(bf16[256,1024]{1,0:T(8,128)(2,1)S(1)} %get-tuple-element.174.refs_1_), channel_id=1, source_target_pairs={{0,1},{1,0},{2,3},{3,2},{4,5},{5,4},{6,7},{7,6},{8,9},{9,8},{10,11... | collective-permute-start | bytes 1572872 | tf_op jit(solution)/shard_map/ppermute | solution.py:594
  73.1 17.1 %collective-permute-start.6 = (bf16[256,1024]{1,0:T(8,128)(2,1)S(1)}, bf16[256,1024]{1,0:T(8,128)(2,1)S(1)}, u32[]{:S(2)}, u32[]{:S(2)}) collective-permute-start(bf16[256,1024]{1,0:T(8,128)(2,1)S(1)} %get-tuple-element.154.refs_1_), channel_id=1, source_target_pairs={{0,1},{1,0},{2,3},{3,2},{4,5},{5,4},{6,7},{7,6},{8,9},{9,8},{10,11... | collective-permute-start | bytes 1572872 | tf_op jit(solution)/shard_map/ppermute | solution.py:594
  85.1 20.7 %collective-permute-start.12 = (bf16[256,1024]{1,0:T(8,128)(2,1)}, bf16[256,1024]{1,0:T(8,128)(2,1)}, u32[]{:S(2)}, u32[]{:S(2)}) collective-permute-start(bf16[256,1024]{1,0:T(8,128)(2,1)} %get-tuple-element.176.refs_1_), channel_id=1, source_target_pairs={{0,1},{1,0},{2,3},{3,2},{4,5},{5,4},{6,7},{7,6},{8,9},{9,8},{10,11... | collective-permute-start | bytes 1572872 | tf_op jit(solution)/shard_map/ppermute | solution.py:594
  105.7 19.0 %collective-permute-start.7 = (bf16[256,1024]{1,0:T(8,128)(2,1)}, bf16[256,1024]{1,0:T(8,128)(2,1)}, u32[]{:S(2)}, u32[]{:S(2)}) collective-permute-start(bf16[256,1024]{1,0:T(8,128)(2,1)} %get-tuple-element.161.refs_2_), channel_id=1, source_target_pairs={{0,1},{1,0},{2,3},{3,2},{4,5},{5,4},{6,7},{7,6},{8,9},{9,8},{10,11... | collective-permute-start | bytes 1572872 | tf_op jit(solution)/shard_map/ppermute | solution.py:594
  122.7 18.8 %collective-permute-start.15 = (bf16[256,1024]{1,0:T(8,128)(2,1)}, bf16[256,1024]{1,0:T(8,128)(2,1)}, u32[]{:S(2)}, u32[]{:S(2)}) collective-permute-start(bf16[256,1024]{1,0:T(8,128)(2,1)} %get-tuple-element.192.refs_2_), channel_id=1, source_target_pairs={{0,1},{1,0},{2,3},{3,2},{4,5},{5,4},{6,7},{7,6},{8,9},{9,8},{10,11... | collective-permute-start | bytes 1572872 | tf_op jit(solution)/shard_map/ppermute | solution.py:594
  138.3 15.1 %collective-permute-start.8 = (bf16[256,1024]{1,0:T(8,128)(2,1)S(1)}, bf16[256,1024]{1,0:T(8,128)(2,1)S(1)}, u32[]{:S(2)}, u32[]{:S(2)}) collective-permute-start(bf16[256,1024]{1,0:T(8,128)(2,1)S(1)} %get-tuple-element.167.refs_2_), channel_id=1, source_target_pairs={{0,1},{1,0},{2,3},{3,2},{4,5},{5,4},{6,7},{7,6},{8,9},{9,8},{10,11... | collective-permute-start | bytes 1572872 | tf_op jit(solution)/shard_map/ppermute | solution.py:594
  139.4 12.2 %collective-permute-start.14 = (bf16[256,1024]{1,0:T(8,128)(2,1)S(1)}, bf16[256,1024]{1,0:T(8,128)(2,1)S(1)}, u32[]{:S(2)}, u32[]{:S(2)}) collective-permute-start(bf16[256,1024]{1,0:T(8,128)(2,1)S(1)} %get-tuple-element.188.refs_12_), channel_id=1, source_target_pairs={{0,8},{10,2},{8,16},{18,10},{16,24},{26,18},{24,28},{30,26},{28,20... | collective-permute-start | bytes 1572872 | tf_op jit(solution)/shard_map/ppermute | solution.py:869
  150.0 24.3 %collective-permute-start.20 = (bf16[256,1024]{1,0:T(8,128)(2,1)}, bf16[256,1024]{1,0:T(8,128)(2,1)}, u32[]{:S(2)}, u32[]{:S(2)}) collective-permute-start(bf16[256,1024]{1,0:T(8,128)(2,1)} %get-tuple-element.219.refs_2_), channel_id=1, source_target_pairs={{0,1},{1,0},{2,3},{3,2},{4,5},{5,4},{6,7},{7,6},{8,9},{9,8},{10,11... | collective-permute-start | bytes 1572872 | tf_op jit(solution)/shard_map/ppermute | solution.py:594
  156.8 15.3 %collective-permute-start.21 = (bf16[8,256,512]{2,1,0:T(8,128)(2,1)S(1)}, bf16[8,256,512]{2,1,0:T(8,128)(2,1)S(1)}, u32[]{:S(2)}, u32[]{:S(2)}) collective-permute-start(bf16[8,256,512]{2,1,0:T(8,128)(2,1)S(1)} %get-tuple-element.222), channel_id=1, source_target_pairs={{0,2},{2,0},{4,6},{6,4},{8,10},{10,8},{12,14},{14,12},{16,18},{18,... | collective-permute-start | bytes 6291464 | tf_op jit(solution)/shard_map/ppermute | solution.py:840
  168.9 18.6 %collective-permute-start.17 = (bf16[256,1024]{1,0:T(8,128)(2,1)S(1)}, bf16[256,1024]{1,0:T(8,128)(2,1)S(1)}, u32[]{:S(2)}, u32[]{:S(2)}) collective-permute-start(bf16[256,1024]{1,0:T(8,128)(2,1)S(1)} %get-tuple-element.212.refs_2_), channel_id=1, source_target_pairs={{0,1},{1,0},{2,3},{3,2},{4,5},{5,4},{6,7},{7,6},{8,9},{9,8},{10,11... | collective-permute-start | bytes 1572872 | tf_op jit(solution)/shard_map/ppermute | solution.py:594
  170.5 12.0 %collective-permute-start.19 = (bf16[256,1024]{1,0:T(8,128)(2,1)S(1)}, bf16[256,1024]{1,0:T(8,128)(2,1)S(1)}, u32[]{:S(2)}, u32[]{:S(2)}) collective-permute-start(bf16[256,1024]{1,0:T(8,128)(2,1)S(1)} %add.85.refs_10_), channel_id=1, source_target_pairs={{0,8},{10,2},{8,16},{18,10},{16,24},{26,18},{24,28},{30,26},{28,20... | collective-permute-start | bytes 1572872 | tf_op jit(solution)/shard_map/ppermute | solution.py:869
  172.6 12.8 %collective-permute-start.23 = (bf16[256,512]{1,0:T(8,128)(2,1)S(1)}, bf16[256,512]{1,0:T(8,128)(2,1)S(1)}, u32[]{:S(2)}, u32[]{:S(2)}) collective-permute-start(bf16[256,512]{1,0:T(8,128)(2,1)S(1)} %get-tuple-element.223.refs_11_), channel_id=1, source_target_pairs={{0,8},{10,2},{8,16},{18,10},{16,24},{26,18},{24,28},{30,26},{28,20... | collective-permute-start | bytes 786440 | tf_op jit(solution)/shard_map/ppermute | solution.py:869
  183.4 15.0 %collective-permute-start.22 = (bf16[256,1024]{1,0:T(8,128)(2,1)}, bf16[256,1024]{1,0:T(8,128)(2,1)}, u32[]{:S(2)}, u32[]{:S(2)}) collective-permute-start(bf16[256,1024]{1,0:T(8,128)(2,1)} %add.86.refs_10_), channel_id=1, source_target_pairs={{0,8},{10,2},{8,16},{18,10},{16,24},{26,18},{24,28},{30,26},{28,20... | collective-permute-start | bytes 1572872 | tf_op jit(solution)/shard_map/ppermute | solution.py:869
  185.0 30.7 %collective-permute-start.26 = (bf16[256,1024]{1,0:T(8,128)(2,1)}, bf16[256,1024]{1,0:T(8,128)(2,1)}, u32[]{:S(2)}, u32[]{:S(2)}) collective-permute-start(bf16[256,1024]{1,0:T(8,128)(2,1)} %get-tuple-element.240.refs_2_), channel_id=1, source_target_pairs={{0,1},{1,0},{2,3},{3,2},{4,5},{5,4},{6,7},{7,6},{8,9},{9,8},{10,11... | collective-permute-start | bytes 1572872 | tf_op jit(solution)/shard_map/ppermute | solution.py:594
  195.2 15.4 %collective-permute-start.29 = (bf16[8,256,1024]{2,1,0:T(8,128)(2,1)}, bf16[8,256,1024]{2,1,0:T(8,128)(2,1)}, u32[]{:S(2)}, u32[]{:S(2)}) collective-permute-start(bf16[8,256,1024]{2,1,0:T(8,128)(2,1)} %get-tuple-element.245), channel_id=1, source_target_pairs={{0,2},{2,0},{4,6},{6,4},{8,10},{10,8},{12,14},{14,12},{16,18},{18,... | collective-permute-start | bytes 12582920 | tf_op jit(solution)/shard_map/ppermute | solution.py:840
  197.1 11.9 %collective-permute-start.28 = (bf16[256,512]{1,0:T(8,128)(2,1)S(1)}, bf16[256,512]{1,0:T(8,128)(2,1)S(1)}, u32[]{:S(2)}, u32[]{:S(2)}) collective-permute-start(bf16[256,512]{1,0:T(8,128)(2,1)S(1)} %add.89.refs_13_), channel_id=1, source_target_pairs={{0,8},{10,2},{8,16},{18,10},{16,24},{26,18},{24,28},{30,26},{28,20... | collective-permute-start | bytes 786440 | tf_op jit(solution)/shard_map/ppermute | solution.py:869
  208.3 19.6 %collective-permute-start.25 = (bf16[256,1024]{1,0:T(8,128)(2,1)}, bf16[256,1024]{1,0:T(8,128)(2,1)}, u32[]{:S(2)}, u32[]{:S(2)}) collective-permute-start(bf16[256,1024]{1,0:T(8,128)(2,1)} %get-tuple-element.237.refs_3_), channel_id=1, source_target_pairs={{0,1},{1,0},{2,3},{3,2},{4,5},{5,4},{6,7},{7,6},{8,9},{9,8},{10,11... | collective-permute-start | bytes 1572872 | tf_op jit(solution)/shard_map/ppermute | solution.py:594
  209.1 15.1 %collective-permute-start.33 = (bf16[256,512]{1,0:T(8,128)(2,1)S(1)}, bf16[256,512]{1,0:T(8,128)(2,1)S(1)}, u32[]{:S(2)}, u32[]{:S(2)}) collective-permute-start(bf16[256,512]{1,0:T(8,128)(2,1)S(1)} %add.91.refs_13_), channel_id=1, source_target_pairs={{0,8},{10,2},{8,16},{18,10},{16,24},{26,18},{24,28},{30,26},{28,20... | collective-permute-start | bytes 786440 | tf_op jit(solution)/shard_map/ppermute | solution.py:869
  209.8 14.5 %collective-permute-start.31 = (bf16[256,1024]{1,0:T(8,128)(2,1)S(1)}, bf16[256,1024]{1,0:T(8,128)(2,1)S(1)}, u32[]{:S(2)}, u32[]{:S(2)}) collective-permute-start(bf16[256,1024]{1,0:T(8,128)(2,1)S(1)} %add.90.refs_12_), channel_id=1, source_target_pairs={{0,8},{10,2},{8,16},{18,10},{16,24},{26,18},{24,28},{30,26},{28,20... | collective-permute-start | bytes 1572872 | tf_op jit(solution)/shard_map/ppermute | solution.py:869
  215.7 11.1 %collective-permute-start.34 = (bf16[128,1024]{1,0:T(8,128)(2,1)}, bf16[128,1024]{1,0:T(8,128)(2,1)}, u32[]{:S(2)}, u32[]{:S(2)}) collective-permute-start(bf16[128,1024]{1,0:T(8,128)(2,1)} %get-tuple-element.246.refs_14_), channel_id=1, source_target_pairs={{0,8},{10,2},{8,16},{18,10},{16,24},{26,18},{24,28},{30,26},{28,20... | collective-permute-start | bytes 786440 | tf_op jit(solution)/shard_map/ppermute | solution.py:869
  231.3 33.1 %collective-permute-start.44 = (bf16[8,256,512]{2,1,0:T(8,128)(2,1)S(1)}, bf16[8,256,512]{2,1,0:T(8,128)(2,1)S(1)}, u32[]{:S(2)}, u32[]{:S(2)}) collective-permute-start(bf16[8,256,512]{2,1,0:T(8,128)(2,1)S(1)} %get-tuple-element.267), channel_id=1, source_target_pairs={{0,2},{2,0},{4,6},{6,4},{8,10},{10,8},{12,14},{14,12},{16,18},{18,... | collective-permute-start | bytes 6291464 | tf_op jit(solution)/shard_map/ppermute | solution.py:840
  232.4 17.1 %collective-permute-start.32 = (bf16[256,1024]{1,0:T(8,128)(2,1)S(1)}, bf16[256,1024]{1,0:T(8,128)(2,1)S(1)}, u32[]{:S(2)}, u32[]{:S(2)}) collective-permute-start(bf16[256,1024]{1,0:T(8,128)(2,1)S(1)} %add.92.refs_14_.refs_0_), channel_id=1, source_target_pairs={{0,8},{10,2},{8,16},{18,10},{16,24},{26,18},{24,28},{30,26},{28,20... | collective-permute-start | bytes 1572872 | tf_op jit(solution)/shard_map/ppermute | solution.py:869
  233.2 48.0 %collective-permute-start.30 = (bf16[256,1024]{1,0:T(8,128)(2,1)S(1)}, bf16[256,1024]{1,0:T(8,128)(2,1)S(1)}, u32[]{:S(2)}, u32[]{:S(2)}) collective-permute-start(bf16[256,1024]{1,0:T(8,128)(2,1)S(1)} %get-tuple-element.250.refs_7_), channel_id=1, source_target_pairs={{0,1},{1,0},{2,3},{3,2},{4,5},{5,4},{6,7},{7,6},{8,9},{9,8},{10,11... | collective-permute-start | bytes 1572872 | tf_op jit(solution)/shard_map/ppermute | solution.py:594
  237.8 11.2 %collective-permute-start.38 = (bf16[128,1024]{1,0:T(8,128)(2,1)S(1)}, bf16[128,1024]{1,0:T(8,128)(2,1)S(1)}, u32[]{:S(2)}, u32[]{:S(2)}) collective-permute-start(bf16[128,1024]{1,0:T(8,128)(2,1)S(1)} %add.94.refs_16_), channel_id=1, source_target_pairs={{0,8},{10,2},{8,16},{18,10},{16,24},{26,18},{24,28},{30,26},{28,20... | collective-permute-start | bytes 786440 | tf_op jit(solution)/shard_map/ppermute | solution.py:869
  240.6 11.2 %collective-permute-start.41 = (bf16[256,512]{1,0:T(8,128)(2,1)S(1)}, bf16[256,512]{1,0:T(8,128)(2,1)S(1)}, u32[]{:S(2)}, u32[]{:S(2)}) collective-permute-start(bf16[256,512]{1,0:T(8,128)(2,1)S(1)} %add.96.refs_2_.refs_3_), channel_id=1, source_target_pairs={{0,8},{10,2},{8,16},{18,10},{16,24},{26,18},{24,28},{30,26},{28,20... | collective-permute-start | bytes 786440 | tf_op jit(solution)/shard_map/ppermute | solution.py:869
  251.8 12.0 %collective-permute-start.36 = (bf16[256,1024]{1,0:T(8,128)(2,1)S(1)}, bf16[256,1024]{1,0:T(8,128)(2,1)S(1)}, u32[]{:S(2)}, u32[]{:S(2)}) collective-permute-start(bf16[256,1024]{1,0:T(8,128)(2,1)S(1)} %hold.32.refs_1_.refs_2_), channel_id=1, source_target_pairs={{0,8},{10,2},{8,16},{18,10},{16,24},{26,18},{24,28},{30,26},{28,20... | collective-permute-start | bytes 1572872 | tf_op jit(solution)/shard_map/ppermute | solution.py:869
  255.4 17.4 %collective-permute-start.45 = (bf16[256,512]{1,0:T(8,128)(2,1)S(1)}, bf16[256,512]{1,0:T(8,128)(2,1)S(1)}, u32[]{:S(2)}, u32[]{:S(2)}) collective-permute-start(bf16[256,512]{1,0:T(8,128)(2,1)S(1)} %add.99.refs_3_.refs_4_), channel_id=1, source_target_pairs={{0,8},{10,2},{8,16},{18,10},{16,24},{26,18},{24,28},{30,26},{28,20... | collective-permute-start | bytes 786440 | tf_op jit(solution)/shard_map/ppermute | solution.py:869
  258.2 11.2 %collective-permute-start.47 = (bf16[128,1024]{1,0:T(8,128)(2,1)S(1)}, bf16[128,1024]{1,0:T(8,128)(2,1)S(1)}, u32[]{:S(2)}, u32[]{:S(2)}) collective-permute-start(bf16[128,1024]{1,0:T(8,128)(2,1)S(1)} %add.101.refs_5_.refs_6_), channel_id=1, source_target_pairs={{0,8},{10,2},{8,16},{18,10},{16,24},{26,18},{24,28},{30,26},{28,20... | collective-permute-start | bytes 786440 | tf_op jit(solution)/shard_map/ppermute | solution.py:869
  264.3 13.5 %collective-permute-start.40 = (bf16[256,1024]{1,0:T(8,128)(2,1)S(1)}, bf16[256,1024]{1,0:T(8,128)(2,1)S(1)}, u32[]{:S(2)}, u32[]{:S(2)}) collective-permute-start(bf16[256,1024]{1,0:T(8,128)(2,1)S(1)} %hold.33.refs_2_.refs_3_), channel_id=1, source_target_pairs={{0,8},{10,2},{8,16},{18,10},{16,24},{26,18},{24,28},{30,26},{28,20... | collective-permute-start | bytes 1572872 | tf_op jit(solution)/shard_map/ppermute | solution.py:869
  269.4 11.2 %collective-permute-start.48 = (bf16[256,512]{1,0:T(8,128)(2,1)S(1)}, bf16[256,512]{1,0:T(8,128)(2,1)S(1)}, u32[]{:S(2)}, u32[]{:S(2)}) collective-permute-start(bf16[256,512]{1,0:T(8,128)(2,1)S(1)} %get-tuple-element.268.refs_6_.refs_7_), channel_id=1, source_target_pairs={{0,8},{10,2},{8,16},{18,10},{16,24},{26,18},{24,28},{30,26},{28,20... | collective-permute-start | bytes 786440 | tf_op jit(solution)/shard_map/ppermute | solution.py:869
  272.2 11.2 %collective-permute-start.52 = (bf16[128,1024]{1,0:T(8,128)(2,1)S(1)}, bf16[128,1024]{1,0:T(8,128)(2,1)S(1)}, u32[]{:S(2)}, u32[]{:S(2)}) collective-permute-start(bf16[128,1024]{1,0:T(8,128)(2,1)S(1)} %add.104.refs_13_.refs_5_.refs_6_), channel_id=1, source_target_pairs={{0,8},{10,2},{8,16},{18,10},{16,24},{26,18},{24,28},{30,26},{28,20... | collective-permute-start | bytes 786440 | tf_op jit(solution)/shard_map/ppermute | solution.py:869
  272.8 13.5 %collective-permute-start.51 = (bf16[128,1024]{1,0:T(8,128)(2,1)S(1)}, bf16[128,1024]{1,0:T(8,128)(2,1)S(1)}, u32[]{:S(2)}, u32[]{:S(2)}) collective-permute-start(bf16[128,1024]{1,0:T(8,128)(2,1)S(1)} %add.103.refs_12_.refs_4_.refs_5_), channel_id=1, source_target_pairs={{0,8},{10,2},{8,16},{18,10},{16,24},{26,18},{24,28},{30,26},{28,20... | collective-permute-start | bytes 786440 | tf_op jit(solution)/shard_map/ppermute | solution.py:869
  277.8 11.2 %collective-permute-start.50 = (bf16[256,512]{1,0:T(8,128)(2,1)S(1)}, bf16[256,512]{1,0:T(8,128)(2,1)S(1)}, u32[]{:S(2)}, u32[]{:S(2)}) collective-permute-start(bf16[256,512]{1,0:T(8,128)(2,1)S(1)} %add.102.refs_11_.refs_3_.refs_4_.refs_0_), channel_id=1, source_target_pairs={{0,8},{10,2},{8,16},{18,10},{16,24},{26,18},{24,28},{30,26},{28,20... | collective-permute-start | bytes 786440 | tf_op jit(solution)/shard_map/ppermute | solution.py:869
  280.6 17.4 %collective-permute-start.49 = (bf16[256,1024]{1,0:T(8,128)(2,1)S(1)}, bf16[256,1024]{1,0:T(8,128)(2,1)S(1)}, u32[]{:S(2)}, u32[]{:S(2)}) collective-permute-start(bf16[256,1024]{1,0:T(8,128)(2,1)S(1)} %hold.34.refs_10_.refs_2_.refs_3_), channel_id=1, source_target_pairs={{0,8},{10,2},{8,16},{18,10},{16,24},{26,18},{24,28},{30,26},{28,20... | collective-permute-start | bytes 1572872 | tf_op jit(solution)/shard_map/ppermute | solution.py:869
  281.2 16.3 %collective-permute-start.53 = (bf16[256,512]{1,0:T(8,128)(2,1)S(1)}, bf16[256,512]{1,0:T(8,128)(2,1)S(1)}, u32[]{:S(2)}, u32[]{:S(2)}) collective-permute-start(bf16[256,512]{1,0:T(8,128)(2,1)S(1)} %add.105.refs_14_.refs_6_.refs_7_), channel_id=1, source_target_pairs={{0,8},{10,2},{8,16},{18,10},{16,24},{26,18},{24,28},{30,26},{28,20... | collective-permute-start | bytes 786440 | tf_op jit(solution)/shard_map/ppermute | solution.py:869
  283.5 16.8 %collective-permute-start.60 = (bf16[128,1024]{1,0:T(8,128)(2,1)S(1)}, bf16[128,1024]{1,0:T(8,128)(2,1)S(1)}, u32[]{:S(2)}, u32[]{:S(2)}) collective-permute-start(bf16[128,1024]{1,0:T(8,128)(2,1)S(1)} %add.107.refs_5_.refs_6_), channel_id=1, source_target_pairs={{0,8},{10,2},{8,16},{18,10},{16,24},{26,18},{24,28},{30,26},{28,20... | collective-permute-start | bytes 786440 | tf_op jit(solution)/shard_map/ppermute | solution.py:869
  286.4 16.8 %collective-permute-start.59 = (bf16[128,1024]{1,0:T(8,128)(2,1)S(1)}, bf16[128,1024]{1,0:T(8,128)(2,1)S(1)}, u32[]{:S(2)}, u32[]{:S(2)}) collective-permute-start(bf16[128,1024]{1,0:T(8,128)(2,1)S(1)} %add.106.refs_4_.refs_5_), channel_id=1, source_target_pairs={{0,8},{10,2},{8,16},{18,10},{16,24},{26,18},{24,28},{30,26},{28,20... | collective-permute-start | bytes 786440 | tf_op jit(solution)/shard_map/ppermute | solution.py:869
  289.1 25.8 %collective-permute-start.58 = (bf16[256,512]{1,0:T(8,128)(2,1)S(1)}, bf16[256,512]{1,0:T(8,128)(2,1)S(1)}, u32[]{:S(2)}, u32[]{:S(2)}) collective-permute-start(bf16[256,512]{1,0:T(8,128)(2,1)S(1)} %hold.36.refs_3_.refs_4_.refs_1_), channel_id=1, source_target_pairs={{0,8},{10,2},{8,16},{18,10},{16,24},{26,18},{24,28},{30,26},{28,20... | collective-permute-start | bytes 786440 | tf_op jit(solution)/shard_map/ppermute | solution.py:869
  297.6 11.2 %collective-permute-start.61 = (bf16[256,512]{1,0:T(8,128)(2,1)S(1)}, bf16[256,512]{1,0:T(8,128)(2,1)S(1)}, u32[]{:S(2)}, u32[]{:S(2)}) collective-permute-start(bf16[256,512]{1,0:T(8,128)(2,1)S(1)} %add.108.refs_6_.refs_7_), channel_id=1, source_target_pairs={{0,8},{10,2},{8,16},{18,10},{16,24},{26,18},{24,28},{30,26},{28,20... | collective-permute-start | bytes 786440 | tf_op jit(solution)/shard_map/ppermute | solution.py:869
  298.1 16.2 %collective-permute-start.56 = (bf16[256,1024]{1,0:T(8,128)(2,1)S(1)}, bf16[256,1024]{1,0:T(8,128)(2,1)S(1)}, u32[]{:S(2)}, u32[]{:S(2)}) collective-permute-start(bf16[256,1024]{1,0:T(8,128)(2,1)S(1)} %hold.35.refs_2_.refs_3_.refs_4_), channel_id=1, source_target_pairs={{0,8},{10,2},{8,16},{18,10},{16,24},{26,18},{24,28},{30,26},{28,20... | collective-permute-start | bytes 1572872 | tf_op jit(solution)/shard_map/ppermute | solution.py:869
  300.4 28.6 %collective-permute-start.65 = (bf16[128,1024]{1,0:T(8,128)(2,1)S(1)}, bf16[128,1024]{1,0:T(8,128)(2,1)S(1)}, u32[]{:S(2)}, u32[]{:S(2)}) collective-permute-start(bf16[128,1024]{1,0:T(8,128)(2,1)S(1)} %add.110.refs_4_.refs_5_), channel_id=1, source_target_pairs={{0,8},{10,2},{8,16},{18,10},{16,24},{26,18},{24,28},{30,26},{28,20... | collective-permute-start | bytes 786440 | tf_op jit(solution)/shard_map/ppermute | solution.py:869
  303.2 25.9 %collective-permute-start.64 = (bf16[128,1024]{1,0:T(8,128)(2,1)S(1)}, bf16[128,1024]{1,0:T(8,128)(2,1)S(1)}, u32[]{:S(2)}, u32[]{:S(2)}) collective-permute-start(bf16[128,1024]{1,0:T(8,128)(2,1)S(1)} %add.109.refs_3_.refs_4_), channel_id=1, source_target_pairs={{0,8},{10,2},{8,16},{18,10},{16,24},{26,18},{24,28},{30,26},{28,20... | collective-permute-start | bytes 786440 | tf_op jit(solution)/shard_map/ppermute | solution.py:869
  308.8 14.0 %collective-permute-start.66 = (bf16[256,512]{1,0:T(8,128)(2,1)S(1)}, bf16[256,512]{1,0:T(8,128)(2,1)S(1)}, u32[]{:S(2)}, u32[]{:S(2)}) collective-permute-start(bf16[256,512]{1,0:T(8,128)(2,1)S(1)} %add.111.refs_5_.refs_6_), channel_id=1, source_target_pairs={{0,8},{10,2},{8,16},{18,10},{16,24},{26,18},{24,28},{30,26},{28,20... | collective-permute-start | bytes 786440 | tf_op jit(solution)/shard_map/ppermute | solution.py:869
  314.4 14.0 %collective-permute-start.57 = (bf16[256,1024]{1,0:T(8,128)(2,1)S(1)}, bf16[256,1024]{1,0:T(8,128)(2,1)S(1)}, u32[]{:S(2)}, u32[]{:S(2)}) collective-permute-start(bf16[256,1024]{1,0:T(8,128)(2,1)S(1)} %hold.39.refs_1_.refs_2_.refs_5_), channel_id=1, source_target_pairs={{0,8},{10,2},{8,16},{18,10},{16,24},{26,18},{24,28},{30,26},{28,20... | collective-permute-start | bytes 1572872 | tf_op jit(solution)/shard_map/ppermute | solution.py:869
  314.9 16.3 %collective-permute-start.63 = (bf16[256,512]{1,0:T(8,128)(2,1)S(1)}, bf16[256,512]{1,0:T(8,128)(2,1)S(1)}, u32[]{:S(2)}, u32[]{:S(2)}) collective-permute-start(bf16[256,512]{1,0:T(8,128)(2,1)S(1)} %hold.40.refs_2_.refs_3_), channel_id=1, source_target_pairs={{0,8},{10,2},{8,16},{18,10},{16,24},{26,18},{24,28},{30,26},{28,20... | collective-permute-start | bytes 786440 | tf_op jit(solution)/shard_map/ppermute | solution.py:869
  337.9 28.0 %collective-permute-start.71 = (bf16[8,256,1024]{2,1,0:T(8,128)(2,1)S(1)}, bf16[8,256,1024]{2,1,0:T(8,128)(2,1)S(1)}, u32[]{:S(2)}, u32[]{:S(2)}) collective-permute-start(bf16[8,256,1024]{2,1,0:T(8,128)(2,1)S(1)} %pack.4.refs_10_.refs_1_.refs_4_.refs_2_.refs_3_), channel_id=1, source_target_pairs={{0,2},{2,0},{4,6},{6,4},{8,10},{10,8},{12,14},{14,12},{16,18},{18,... | collective-permute-start | bytes 12582920 | tf_op jit(solution)/shard_map/ppermute | solution.py:858
  339.2 14.2 %collective-permute-start.55 = (bf16[128,1024]{1,0:T(8,128)(2,1)S(1)}, bf16[128,1024]{1,0:T(8,128)(2,1)S(1)}, u32[]{:S(2)}, u32[]{:S(2)}) collective-permute-start(bf16[128,1024]{1,0:T(8,128)(2,1)S(1)} %hold.38), channel_id=1, source_target_pairs={{0,1},{1,0},{2,3},{3,2},{4,5},{5,4},{6,7},{7,6},{8,9},{9,8},{10,11... | collective-permute-start | bytes 786440 | tf_op jit(solution)/shard_map/ppermute | solution.py:594
  347.3 17.4 %collective-permute-start.75 = (bf16[256,512]{1,0:T(8,128)(2,1)S(1)}, bf16[256,512]{1,0:T(8,128)(2,1)S(1)}, u32[]{:S(2)}, u32[]{:S(2)}) collective-permute-start(bf16[256,512]{1,0:T(8,128)(2,1)S(1)} %add.115.refs_14_.refs_8_.refs_6_.refs_7_), channel_id=1, source_target_pairs={{0,8},{10,2},{8,16},{18,10},{16,24},{26,18},{24,28},{30,26},{28,20... | collective-permute-start | bytes 786440 | tf_op jit(solution)/shard_map/ppermute | solution.py:869
  353.4 10.7 %collective-permute-start.72 = (bf16[256,512]{1,0:T(8,128)(2,1)S(1)}, bf16[256,512]{1,0:T(8,128)(2,1)S(1)}, u32[]{:S(2)}, u32[]{:S(2)}) collective-permute-start(bf16[256,512]{1,0:T(8,128)(2,1)S(1)} %hold.43.refs_11_.refs_5_.refs_3_.refs_4_), channel_id=1, source_target_pairs={{0,8},{10,2},{8,16},{18,10},{16,24},{26,18},{24,28},{30,26},{28,20... | collective-permute-start | bytes 786440 | tf_op jit(solution)/shard_map/ppermute | solution.py:869
  358.5 15.1 %collective-permute-start.85 = (bf16[128,1024]{1,0:T(8,128)(2,1)S(1)}, bf16[128,1024]{1,0:T(8,128)(2,1)S(1)}, u32[]{:S(2)}, u32[]{:S(2)}) collective-permute-start(bf16[128,1024]{1,0:T(8,128)(2,1)S(1)} %hold.48.refs_14_.refs_6_.refs_5_.refs_10_), channel_id=1, source_target_pairs={{0,8},{10,2},{8,16},{18,10},{16,24},{26,18},{24,28},{30,26},{28,20... | collective-permute-start | bytes 786440 | tf_op jit(solution)/shard_map/ppermute | solution.py:869
  361.3 12.3 %collective-permute-start.84 = (bf16[128,1024]{1,0:T(8,128)(2,1)S(1)}, bf16[128,1024]{1,0:T(8,128)(2,1)S(1)}, u32[]{:S(2)}, u32[]{:S(2)}) collective-permute-start(bf16[128,1024]{1,0:T(8,128)(2,1)S(1)} %hold.47.refs_13_.refs_5_.refs_4_.refs_2_), channel_id=1, source_target_pairs={{0,8},{10,2},{8,16},{18,10},{16,24},{26,18},{24,28},{30,26},{28,20... | collective-permute-start | bytes 786440 | tf_op jit(solution)/shard_map/ppermute | solution.py:869
  379.3 21.4 %collective-permute-start.91 = (bf16[8,256,512]{2,1,0:T(8,128)(2,1)S(1)}, bf16[8,256,512]{2,1,0:T(8,128)(2,1)S(1)}, u32[]{:S(2)}, u32[]{:S(2)}) collective-permute-start(bf16[8,256,512]{2,1,0:T(8,128)(2,1)S(1)} %pack.5.refs_1_.refs_3_), channel_id=1, source_target_pairs={{0,2},{2,0},{4,6},{6,4},{8,10},{10,8},{12,14},{14,12},{16,18},{18,... | collective-permute-start | bytes 6291464 | tf_op jit(solution)/shard_map/ppermute | solution.py:858
  381.5 23.7 %collective-permute-start.76 = (f32[2,8,1024]{2,1,0:T(8,128)S(1)}, f32[2,8,1024]{2,1,0:T(8,128)S(1)}, u32[]{:S(2)}, u32[]{:S(2)}) collective-permute-start(f32[2,8,1024]{2,1,0:T(8,128)S(1)} %totals.1.refs_1_.refs_8_), channel_id=1, source_target_pairs={{0,2},{2,0},{4,6},{6,4},{8,10},{10,8},{12,14},{14,12},{16,18},{18,... | collective-permute-start | bytes 196616 | tf_op jit(solution)/shard_map/ppermute | solution.py:1038
  394.3 10.9 %collective-permute-start.96 = (bf16[128,1024]{1,0:T(8,128)(2,1)S(1)}, bf16[128,1024]{1,0:T(8,128)(2,1)S(1)}, u32[]{:S(2)}, u32[]{:S(2)}) collective-permute-start(bf16[128,1024]{1,0:T(8,128)(2,1)S(1)} %hold.57.refs_4_.refs_13_), channel_id=1, source_target_pairs={{0,8},{10,2},{8,16},{18,10},{16,24},{26,18},{24,28},{30,26},{28,20... | collective-permute-start | bytes 786440 | tf_op jit(solution)/shard_map/ppermute | solution.py:869
  414.8 14.3 %collective-permute-start.101 = (bf16[8,256,1024]{2,1,0:T(8,128)(2,1)S(1)}, bf16[8,256,1024]{2,1,0:T(8,128)(2,1)S(1)}, u32[]{:S(2)}, u32[]{:S(2)}) collective-permute-start(bf16[8,256,1024]{2,1,0:T(8,128)(2,1)S(1)} %pack.6.refs_2_.refs_1_.refs_6_), channel_id=1, source_target_pairs={{0,2},{2,0},{4,6},{6,4},{8,10},{10,8},{12,14},{14,12},{16,18},{18,... | collective-permute-start | bytes 12582920 | tf_op jit(solution)/shard_map/ppermute | solution.py:858
  442.4 11.8 %collective-permute-start.103 = (bf16[8,256,512]{2,1,0:T(8,128)(2,1)S(1)}, bf16[8,256,512]{2,1,0:T(8,128)(2,1)S(1)}, u32[]{:S(2)}, u32[]{:S(2)}) collective-permute-start(bf16[8,256,512]{2,1,0:T(8,128)(2,1)S(1)} %pack.7.refs_1_.refs_5_), channel_id=1, source_target_pairs={{0,2},{2,0},{4,6},{6,4},{8,10},{10,8},{12,14},{14,12},{16,18},{18,... | collective-permute-start | bytes 6291464 | tf_op jit(solution)/shard_map/ppermute | solution.py:858
  (112 other events, 952.8 us)

commit v3 on v2

--- a/solution.py
+++ b/solution.py
@@ -183,13 +183,13 @@
     block = min(BLOCK, local)
     scale = HD ** (-0.5)
     seqs = rows // length
-    parts = tau.shape[0] // seqs
 
     def kernel(*refs):
         it = iter(refs)
         take = lambda n: [next(it) for _ in range(n)]
         head_refs = take(len(head))
-        tau_ref, vec_ref, wq_any, wo_any, cos_any, sin_any = take(6)
+        tau_ref = None if first else take(1)[0]
+        vec_ref, wq_any, wo_any, cos_any, sin_any = take(5)
         x_ref, part_ref = take(2)
         outs = take(6 if first else 7)
         wq, wo, cos_ref, sin_ref, sems, out_sems = take(6)
@@ -231,7 +231,7 @@
                 there = other_rows(at, rows, swapped)
                 x2 = x1[here, :] + own[here, :].astype(f32) + got[there, :].astype(f32)
                 x2_ref[here, :] = x2
-                t = tau_ref[pl.ds(at // length * parts + part_index, 1), :]
+                t = tau_ref[pl.ds(at // length * (tau.shape[0] // seqs) + part_index, 1), :]
                 norm(at, x2 * (1.0 + t * vector(vec_ref, TIME, layer - 1)))
 
             chunks(rows, scaled)
@@ -266,8 +266,8 @@
         saver.wait()
 
     ins = [(a[0], j == 0) for j, a in enumerate(head)] if first else [(a, False) for a in head]
-    ins += [(a, False) for a in (tau, vectors)] + [(w_qkv, True), (w_out, True)]
-    ins += [(t, True) for t in tables]
+    ins += [] if first else [(tau, False)]
+    ins += [(vectors, False), (w_qkv, True), (w_out, True)] + [(t, True) for t in tables]
     near = lambda n, d: ((rows, n), d, False)
     far = lambda n, d: ((rows, n), d, True)
     outs = [near(width, f32), near(width, bf16)]
@@ -287,14 +287,13 @@
     return call(kernel, ins, outs, scratch, 4 * 10**9, "forward_attention")
 
 
-def forward_mlp(layer, swapped, split, x, own, got, vectors, w_up, w_down, after):
+def forward_mlp(layer, swapped, x, own, got, vectors, w_up, w_down, after):
     rows, width = x.shape
     hidden = w_up.shape[2]
     tiles = hidden // BLOCK
 
     def kernel(x_ref, own_ref, got_ref, vec_ref, wu_any, wd_any, x1_ref, *refs):
-        part_refs, refs = refs[: 1 + split], refs[1 + split :]
-        x1_out, n_out, h_out, slope_out, n_ref, h_ref, slope_ref, wu, wd, sems, out_sems = refs
+        part_ref, x1_out, n_out, h_out, slope_out, n_ref, h_ref, slope_ref, wu, wd, sems, out_sems = refs
         saver = Saver(out_sems)
         gain, bias = vector(vec_ref, GAIN, 2 * layer + 1), vector(vec_ref, BIAS, 2 * layer + 1)
         ups = [
@@ -328,15 +327,13 @@
         saver.save(slope_ref, slope_out)
         down.wait()
         for b in range(0, width, BLOCK):
-            part = mm(h_ref[...], wd[:, b : b + BLOCK]).astype(bf16)
-            for j, ref in enumerate(part_refs):
-                ref[:, b : b + BLOCK] = part[j * ref.shape[0] : (j + 1) * ref.shape[0]]
+            part_ref[:, b : b + BLOCK] = mm(h_ref[...], wd[:, b : b + BLOCK]).astype(bf16)
         saver.wait()
 
     ins = [(a, False) for a in (x, own, got, vectors)] + [(w_up, True), (w_down, True)]
     near = lambda n, d: ((rows, n), d, False)
     far = lambda n, d: ((rows, n), d, True)
-    outs = [near(width, f32)] + [((rows // (1 + split), width), bf16, False)] * (1 + split)
+    outs = [near(width, f32), near(width, bf16)]
     outs += [far(width, f32), far(width, bf16), far(hidden, bf16), far(hidden, bf16)]
     scratch = [
         pltpu.VMEM((rows, width), bf16),
@@ -350,29 +347,45 @@
     return call(kernel, ins, outs, scratch, 6 * 10**9, "forward_mlp", after=after)
 
 
-def last_layer(layer, length, parts, tau, vectors, cotangent, rows_of, after):
-    rows = cotangent.shape[0] // parts
-    width = cotangent.shape[1]
-    seqs = rows // length
-
-    def kernel(tau_ref, vec_ref, cot_ref, *refs):
-        result_ref, sums_ref = refs[-2:]
+def last_layer(layer, length, swapped, own_rows, tau, vectors, rows_of, after):
+    rows, width = rows_of[0][0].shape
+    parts = len(rows_of)
+    pieces = rows_of[0][3]
+
+    def kernel(tau_ref, vec_ref, *refs):
+        result_out, sums_ref, result_ref, sem = refs[-4:]
         sums_ref[...] = jnp.zeros_like(sums_ref)
         for m in range(parts):
-            x1_ref, own_ref, got_ref = refs[3 * m : 3 * m + 3]
-
-            def body(at):
-                here, there = rows_at(at), rows_at(pl.multiple_of(at + m * rows, CHUNK))
-                x2 = x1_ref[here, :] + own_ref[here, :].astype(f32) + got_ref[here, :].astype(f32)
-                t = tau_ref[pl.ds(at // length * parts + m, 1), :]
-                sums_ref[...] += fold(cot_ref[there, :].astype(f32) * x2) * t
-                result_ref[there, :] = x2 * (1.0 + t * vector(vec_ref, TIME, layer))
-
-            chunks(rows, body)
-
-    ins = [(tau, False), (vectors, False), (cotangent, False)] + [(v, False) for part in rows_of for v in part]
-    outs = [(cotangent.shape, f32, False), ((8, width), f32, False)]
-    return call(kernel, ins, outs, [], 10**8, "last_layer", after=after)
+            n = 3 + len(pieces)
+            x1_ref, own_ref, got_ref, *cot_refs = refs[n * m : n * m + n]
+            low = 0
+            for ref, (_, start, count) in zip(cot_refs, rows_of[m][3]):
+
+                def body(at, ref=ref, shift=start - low, mine=low < own_rows):
+                    here = rows_at(at)
+                    x2 = x1_ref[here, :] + own_ref[here, :].astype(f32)
+                    x2 = x2 + got_ref[other_rows(at, rows, swapped), :].astype(f32)
+                    t = tau_ref[pl.ds(at // length * parts + m, 1), :]
+                    g = ref[rows_at(pl.multiple_of(at + shift, CHUNK)), :].astype(f32)
+                    sums_ref[...] += fold(g * x2) * t
+                    if mine:
+                        result_ref[rows_at(pl.multiple_of(at + m * own_rows, CHUNK)), :] = x2 * (
+                            1.0 + t * vector(vec_ref, TIME, layer)
+                        )
+
+                chunks(low + count, body, low)
+                low += count
+        c = pltpu.make_async_copy(result_ref, result_out, sem)
+        c.start()
+        c.wait()
+
+    ins = [(tau, False), (vectors, False)]
+    for x1, mine, got, cot in rows_of:
+        ins += [(v, False) for v in (x1, mine, got)] + [(v, False) for v, _, _ in cot]
+    shape = (own_rows * parts, width)
+    outs = [(shape, f32, True), ((8, width), f32, False)]
+    scratch = [pltpu.VMEM(shape, f32), pltpu.SemaphoreType.DMA]
+    return call(kernel, ins, outs, scratch, 10**8, "last_layer", after=after, limit=SMALL)
 
 
 def backward_mlp(layer, last, part_index, length, swapped, head, x2, tau, vectors, slope, w_up, w_down, after):
@@ -463,7 +476,7 @@
     rows, width = rows_of[0][1].shape
 
     def kernel(vec_ref, *refs):
-        out_ref, sums_ref = refs[-2:]
+        out_far, sums_ref, out_ref, sem = refs[-4:]
         sums_ref[...] = jnp.zeros_like(sums_ref)
         for m in range(len(rows_of)):
             g1_ref, x_ref, own_ref, got_ref = refs[4 * m : 4 * m + 4]
@@ -481,23 +494,42 @@
 
             chunks(own_rows, lambda at: body(at, True))
             chunks(rows, lambda at: body(at, False), own_rows)
+        c = pltpu.make_async_copy(out_ref, out_far, sem)
+        c.start()
+        c.wait()
 
     ins = [(vectors, False)] + [(v, False) for part in rows_of for v in part]
-    outs = [((own_rows * len(rows_of), width), f32, False), ((16, width), f32, False)]
-    return call(kernel, ins, outs, [], 10**8, "input_gradient", after=after)
-
-
-def totals(sums, layers, width, after):
-    def kernel(*refs):
-        out = refs[-1]
-        out[...] = jnp.zeros_like(out)
-        for ref, (layer, rows, factor, _) in zip(refs, sums):
+    shape = (own_rows * len(rows_of), width)
+    outs = [(shape, f32, True), ((16, width), f32, False)]
+    scratch = [pltpu.VMEM(shape, f32), pltpu.SemaphoreType.DMA]
+    return call(kernel, ins, outs, scratch, 10**8, "input_gradient", after=after, limit=SMALL)
+
+
+def totals(sums, layers, width, core, place, after):
+    half_width = width // 2
+    shape = (8, 16, half_width)
+
+    def kernel(s_ref, *refs):
+        send_ref, keep_ref, all_ref = refs[-3:]
+        all_ref[...] = jnp.zeros_like(all_ref)
+        for ref, (layer, rows, _) in zip(refs, sums):
             for j, row in enumerate(rows):
                 if row is not None:
-                    out[layer, row : row + 1, :] += factor * jnp.sum(ref[8 * j : 8 * j + 8, :], axis=0, keepdims=True)
-
-    ins = [(v, False) for _, _, _, v in sums]
-    return call(kernel, ins, [((layers, 8, width), f32, False)], [], 10**8, "totals", after=after)[0]
+                    all_ref[layer, row : row + 1, :] += jnp.sum(ref[8 * j : 8 * j + 8, :], axis=0, keepdims=True)
+        rows = lax.broadcasted_iota(jnp.int32, (16, half_width), 0)
+        for target, half, p in (
+            (send_ref, 1 - s_ref[0], lax.rem(8 - s_ref[1], 8)),
+            (keep_ref, s_ref[0], s_ref[1]),
+        ):
+            for b in range(8):
+                v = all_ref[half, b : b + 1, :]
+                block = jnp.where(rows == 0, v[:, :half_width], jnp.where(rows == 1, v[:, half_width:], 0.0))
+                target[lax.rem(p - b + 8, 8)] = block.astype(bf16)
+
+    ins = [(jnp.stack([core, place]).astype(jnp.int32), False)] + [(v, False) for _, _, v in sums]
+    outs = [(shape, bf16, False)] * 2
+    scratch = [pltpu.VMEM((2, 8, width), f32)]
+    return call(kernel, ins, outs, scratch, 10**8, "totals", after=after, limit=SMALL)
 
 
 def backward_attention(layer, length, swapped, g2, x1, own, got, vectors, q, k, v, w_qkv, w_out, tables, after):
@@ -576,8 +608,6 @@
         self.chips = dp // 2
         self.ring = dp == 16
         self.walk = [0, 2, 4, 6, 7, 5, 3, 1]
-        place = [self.walk.index(i) for i in range(8)]
-        self.place = place
         self.ring_pairs = []
         for k in range(8):
             here, there = self.walk[k], self.walk[(k + 1) % 8]
@@ -587,8 +617,9 @@
 
     def ring_place(self):
         i = lax.axis_index("dp")
-        p = jnp.asarray(self.place, jnp.int32)[i >> 1]
-        return jnp.where(i & 1 == 0, p, (8 - p) % 8)
+        z, x = i >> 2, (i >> 1) & 1
+        p = jnp.where(x == 0, z, 7 - z)
+        return jnp.where(i & 1 == 0, p, (8 - p) & 7)
 
     def swap_tensor(self, v):
         return lax.ppermute(v, "tensor", [(0, 1), (1, 0)])
@@ -627,8 +658,9 @@
 
     def kernel(s_ref, *refs):
         hs, gms, ns, dus = [refs[n * j : n * j + n] for j in range(4)]
-
-        def make(target, half, p):
+        send_out, keep_ref, send_ref, sems = refs[4 * n :]
+
+        def make(target, half, p, ended):
             gm_all = jnp.concatenate([r[...] for r in gms])
             columns = slice(half * half_hidden, (half + 1) * half_hidden)
             du_all = jnp.concatenate([r[:, columns] for r in dus])
@@ -640,18 +672,28 @@
                     slot = lax.rem(p - (2 * j + i) + 8, 8)
                     target[slot, 0:tall, :] = down[i * tall : (i + 1) * tall].astype(bf16)
                     target[slot, tall : tall + wide, :] = up[i * wide : (i + 1) * wide].astype(bf16)
+                    ended(slot, 2 * j + i)
+
+        def away(slot, i):
+            pltpu.make_async_copy(send_ref.at[slot], send_out.at[slot], sems.at[i]).start()
 
         for c in range(2):
 
             @pl.when(s_ref[0] == c)
             def _():
-                make(refs[4 * n], 1 - c, lax.rem(8 - s_ref[1], 8))
-                make(refs[4 * n + 1], c, s_ref[1])
+                make(send_ref, 1 - c, lax.rem(8 - s_ref[1], 8), away)
+                make(keep_ref, c, s_ref[1], lambda slot, i: None)
+
+        for i in range(8):
+            slot = lax.rem(lax.rem(8 - s_ref[1], 8) - i + 8, 8)
+            pltpu.make_async_copy(send_ref.at[slot], send_out.at[slot], sems.at[i]).wait()
 
     ins = [(jnp.stack([core, place]).astype(jnp.int32), False)]
     ins += [(v, False) for group in (h, gm, n2, du) for v in group]
-    out = ((8, tall + wide, width), bf16, False)
-    return call(kernel, ins, [out, out], [], 9 * 10**9, "mlp_gradients", after=after, limit=SMALL)
+    shape = (8, tall + wide, width)
+    scratch = [pltpu.VMEM(shape, bf16), pltpu.SemaphoreType.DMA((8,))]
+    outs = [(shape, bf16, True), (shape, bf16, False)]
+    return call(kernel, ins, outs, scratch, 9 * 10**9, "mlp_gradients", after=after, limit=SMALL)
 
 
 def attention_gradients(att, ga, n1, dq, dk, dv, core, place, after):
@@ -705,14 +747,24 @@
     return call(kernel, ins, [out], [], 10**8, "pack", after=after, limit=SMALL)[0]
 
 
-def merge(a, b, lanes, after):
-    count, depth, width = a.shape
-    depth //= lanes
-
-    def kernel(a_ref, b_ref, *outs):
+def merge(pairs, lanes, after):
+    count, _, width = pairs[0][0].shape
+    depths = [a.shape[1] for a, _ in pairs]
+    depth = sum(depths) // lanes
+
+    def kernel(*refs):
+        ins, outs = refs[: 2 * len(pairs)], refs[2 * len(pairs) :]
+
         def total(i, j):
+            if lanes == 1:
+                return jnp.concatenate(
+                    [
+                        (ins[2 * n][i].astype(f32) + ins[2 * n + 1][i].astype(f32)).astype(bf16)
+                        for n in range(len(pairs))
+                    ]
+                )
             at = slice(j * depth, (j + 1) * depth)
-            return (a_ref[i, at, :].astype(f32) + b_ref[i, at, :].astype(f32)).astype(bf16)
+            return (ins[0][i, at, :].astype(f32) + ins[1][i, at, :].astype(f32)).astype(bf16)
 
         for j in range(lanes):
             outs[2 * j][...] = total(0, j)
@@ -725,7 +777,8 @@
         lax.fori_loop(1, count, body, 0)
 
     outs = [((depth, width), bf16, False), ((count, depth, width), bf16, False)] * lanes
-    out = call(kernel, [(a, False), (b, False)], outs, [], 10**8, "merge", after=after, limit=SMALL)
+    ins = [(v, False) for pair in pairs for v in pair]
+    out = call(kernel, ins, outs, [], 10**8, "merge", after=after, limit=SMALL)
     return out[0::2], out[1::2]
 
 
@@ -741,50 +794,50 @@
     def kernel(a_ref, out_ref):
         out_ref[...] = a_ref[...]
 
-    return call(kernel, [(a, False)], [(a.shape, bf16, False)], [], 10**8, "hold", after=after, limit=SMALL)[0]
+    return call(kernel, [(a, False)], [(a.shape, a.dtype, False)], [], 10**8, "hold", after=after, limit=SMALL)[0]
 
 
 DEEP = 4
 
 
-def spread(pieces, shapes, mine, peer, core, place, before, after):
-    depth, width = mine.shape[1:]
-
-    def kernel(s_ref, mine_ref, peer_ref, *refs):
+def spread(pieces, shapes, blocks, begin, own, core, place, before, after):
+    count, depth, width = blocks.shape
+    deep = min(DEEP, count)
+
+    def kernel(s_ref, block_ref, *refs):
         token_ref, held, sems = refs[-3:]
         outs = refs[len(refs) - 3 - len(shapes) : -3]
         token_ref[...] = jnp.zeros_like(token_ref)
 
         def copies(i):
-            half, p = (s_ref[0], s_ref[1]) if i < 8 else (1 - s_ref[0], lax.rem(8 - s_ref[1], 8))
-            b = lax.rem(p + 1 - i % 8 + 8, 8)
+            half, p = (s_ref[0], s_ref[1]) if own else (1 - s_ref[0], lax.rem(8 - s_ref[1], 8))
+            b = lax.rem(p + 1 - begin - i + 16, 8)
             return [
                 pltpu.make_async_copy(
-                    held.at[(i % DEEP,) + source], outs[o].at[place], sems.at[i % DEEP, j]
+                    held.at[(i % deep,) + source], outs[o].at[place], sems.at[i % deep, j]
                 )
                 for j, (source, o, place) in enumerate(pieces(half, b))
             ]
 
-        for i in range(16):
-            if i >= DEEP:
-                for c in copies(i - DEEP):
+        for i in range(count):
+            if i >= deep:
+                for c in copies(i - deep):
                     c.wait()
-            held[i % DEEP] = (mine_ref if i < 8 else peer_ref)[i % 8].astype(f32)
+            held[i % deep] = block_ref[i].astype(f32)
             for c in copies(i):
                 c.start()
-        for i in range(16 - DEEP, 16):
+        for i in range(count - deep, count):
             for c in copies(i):
                 c.wait()
 
-    ins = [(jnp.stack([core, place]).astype(jnp.int32), False), (mine, False), (peer, False)]
+    ins = [(jnp.stack([core, place]).astype(jnp.int32), False), (blocks, False)]
     aliases = {}
-    if before is not None:
-        for j, v in enumerate(before):
-            aliases[len(ins)] = j
-            ins.append((v, True))
+    for j, v in enumerate(before):
+        aliases[len(ins)] = j
+        ins.append((v, True))
     scratch = [
-        pltpu.VMEM((DEEP, depth, width), f32),
-        pltpu.SemaphoreType.DMA((DEEP, len(pieces(0, 0)))),
+        pltpu.VMEM((deep, depth, width), f32),
+        pltpu.SemaphoreType.DMA((deep, len(pieces(0, 0)))),
     ]
     outs = [(s, f32, True) for s in shapes] + [((8, 128), f32, False)]
     *outs, token = call(kernel, ins, outs, scratch, 10**8, "spread", aliases, after=after, limit=SMALL)
@@ -824,10 +877,58 @@
     return pieces, [(layers, local, width), (layers, 3, width, local)]
 
 
+def small_outputs(ends, begins, layers, width, core, place):
+    row = ends[0][0].shape[1] - 16
+    half_width = width // 2
+
+    def kernel(s_ref, *refs):
+        outs, held = refs[2 * len(ends) : 2 * len(ends) + 4], refs[2 * len(ends) + 4 : -1]
+        gains, biases, times, norms = held
+
+        def put(source, half, p):
+            for b in range(5):
+                slot = lax.rem(p + 1 - b + 16, 8)
+                for n, begin in enumerate(begins):
+                    ref = refs[2 * n + source]
+
+                    @pl.when((slot >= begin) & (slot < begin + ref.shape[0]))
+                    def _():
+                        for j in range(2):
+                            v = ref[slot - begin, row : row + 16, :].astype(f32)[j : j + 1, :]
+                            at = slice(j * half_width, (j + 1) * half_width)
+                            if b == 4:
+                                times[half : half + 1, at] = v
+                            else:
+                                (gains, biases)[b // 2][half, b % 2 : b % 2 + 1, at] = v
+
+        for c in range(2):
+
+            @pl.when(s_ref[0] == c)
+            def _():
+                put(0, c, s_ref[1])
+                put(1, 1 - c, 8 - s_ref[1])
+
+        norms[0:1, :] = gains[layers - 1, 1:2, :]
+        norms[1:2, :] = biases[layers - 1, 1:2, :]
+        copies = [pltpu.make_async_copy(a, b, refs[-1].at[j]) for j, (a, b) in enumerate(zip(held, outs))]
+        for c in copies:
+            c.start()
+        for c in copies:
+            c.wait()
+
+    shapes = [(layers, 2, width), (layers, 2, width), (layers, width), (2, width)]
+    ins = [(jnp.stack([core, place]).astype(jnp.int32), False)] + [(v, False) for pair in ends for v in pair]
+    scratch = [pltpu.VMEM(s, f32) for s in shapes] + [pltpu.SemaphoreType.DMA((4,))]
+    return call(kernel, ins, [(s, f32, True) for s in shapes], scratch, 10**8, "small_outputs", limit=SMALL)
+
+
 class Stream:
     def __init__(self, links, kind, layer, layers, groups, after, written):
         self.links, self.kind, self.written = links, kind, written
         self.steps = -2
+        self.extra = []
+        self.cuts = [(0, 5), (5, 8)] if kind == "attention" and layer == 0 else [(0, 8)]
+        self.packed = []
         self.lanes = LANES[kind][min(layer, 1)]
         self.core = lax.axis_index("dp") & 1
         self.p = links.ring_place()
@@ -845,20 +946,26 @@
         self.steps += 1
         if self.steps < 0:
             return []
-        if self.steps == 15:
-            before = self.written.get(self.kind)
-            self.written[self.kind], token = spread(
-                *self.layout, self.mine, self.raw, self.core, self.p, before, after
-            )
-            return [token]
+        out = []
         if self.steps == 14:
             for lane, v in zip(self.done, self.raw):
                 lane.append(v)
-            self.mine = pack(self.done, after)
-            self.raw = lax.ppermute(self.mine, "dp", self.links.core_pairs)
-            return [self.mine]
+        if self.packed and len(self.packed[-1]) == 2 and not self.packed[-1][-1][1]:
+            (_, peer), state = self.packed[-1][0], self.packed[-1][-1]
+            state[1] = True
+            out.append(self.write(peer, state[0], False, after))
+        if self.steps == 15:
+            return out
+        for low, high in self.cuts:
+            if self.steps == min(high + 7, 14):
+                mine = pack([lane[low:high] for lane in self.done], after)
+                peer = lax.ppermute(mine, "dp", self.links.core_pairs)
+                out.append(self.write(mine, low, True, []))
+                self.packed.append(((mine, peer), [low, False]))
+        if self.steps == 14:
+            return out
         if self.steps == 0:
-            now, self.blocks = merge(self.blocks, self.raw, self.lanes, after)
+            now, self.blocks = merge([(self.blocks, self.raw)] + self.extra, self.lanes, after)
         elif self.steps < 8:
             now = [add(r, b, self.steps, after) for r, b in zip(self.raw, self.blocks)]
         else:
@@ -867,7 +974,14 @@
             for lane, v in zip(self.done, now):
                 lane.append(v)
         self.raw = [lax.ppermute(v, "dp", self.links.ring_pairs) for v in now]
-        return list(now)
+        return out + list(now)
+
+    def write(self, blocks, begin, own, after):
+        before = self.written.get(self.kind, [])
+        self.written[self.kind], token = spread(
+            *self.layout, blocks, begin, own, self.core, self.p, before, after
+        )
+        return token
 
     def going(self):
         return self.steps < 15
@@ -918,15 +1032,17 @@
         paired = links.tensor == 2
         wq = jnp.transpose(w_qkv, (0, 2, 1, 3))
 
-        def group_rows(v, m):
+        def group_rows(v, m, after=()):
             if paired:
-                got = links.swap_tensor(v[m * own : (m + 1) * own])
+                mine = v[m * own : (m + 1) * own]
+                got = links.swap_tensor(hold(mine, after) if after else mine)
                 return [(v, m * own, own), (got, 0, own)]
             v = links.gather_tensor(v[m * own : (m + 1) * own])
             return [(v, 0, v.shape[0])]
 
-        heads = [group_rows(tokens, m) for m in range(parts)]
-        gs = [group_rows(cotangent, m) for m in range(parts)]
+        heads = [group_rows(tokens, 0)]
+        heads += [group_rows(tokens, m, [heads[-1][-1][0]]) for m in range(1, parts)]
+        gs = [group_rows(cotangent, m, [heads[-1][-1][0]]) for m in range(parts)]
         arrived = [g[-1][0] for g in gs]
         vectors = [norm_gain.reshape(2 * layers, width), norm_bias.reshape(2 * layers, width)]
         vectors += [time_weight, jnp.zeros((layers, width), f32)]
@@ -949,19 +1065,14 @@
                 saved[l][m] = out
                 heads[m] = (x_near, *links.start_sum(part))
             for m in range(parts):
-                split = paired and l == layers - 1
-                x1, *out = forward_mlp(l, paired, split, *heads[m], vectors, w_up, w_down, arrived)
-                if split:
-                    heads[m] = (x1, *out[:2])
-                else:
-                    heads[m] = (x1, *links.start_sum(out[0]))
-                saved[l][m] += out[1 + split :]
+                x1, part, *out = forward_mlp(l, paired, *heads[m], vectors, w_up, w_down, arrived)
+                heads[m] = (x1, part) if l == layers - 1 else (x1, *links.start_sum(part))
+                saved[l][m] += out
                 arrived = []
 
         kind = Stream if links.ring else Plain
         streams = []
         small = []
-        share = 0.5 if paired else 1.0
         keep = lambda l, i: [s[i] for s in saved[l]]
 
         last, written = [], {}
@@ -980,6 +1091,7 @@
         gs = list(gs)
         for l in reversed(range(layers)):
             g2s, gms, dus, sums = [None] * parts, [None] * parts, [None] * parts, [None] * parts
+            gas, dps = [None] * parts, [None] * parts
             for m in range(parts):
                 g2s[m], gms[m], dus[m], part, s = backward_mlp(
                     l, l == layers - 1, m, length, paired, gs[m], after[l][m], tau, vectors, saved[l][m][9],
@@ -987,78 +1099,70 @@
                 )
                 ran(s)
                 if l < layers - 1:
-                    small.append((l + 1, (0, 2), share, s))
-                    small.append((l, (None, None, 4), share, s))
+                    small.append((l + 1, (0, 2), s))
+                    small.append((l, (None, None, 4), s))
                 sums[m] = links.start_sum(part)
-            groups = [keep(l, 8), gms, keep(l, 7), dus]
-            streams.append(kind(links, "mlp", l, layers, groups, step([sums[0][1]]), written))
-            ran(streams[-1].token)
-            gas, dps = [None] * parts, [None] * parts
+
+            def mlp_stream(also):
+                groups = [keep(l, 8), gms, keep(l, 7), dus]
+                streams.append(kind(links, "mlp", l, layers, groups, step(also), written))
+                ran(streams[-1].token)
+
+            if l > 0:
+                mlp_stream([sums[0][1]])
             for m in range(parts):
                 x, n1, q, k, v, att, x1 = saved[l][m][:7]
                 g1, gas[m], dq, dk, dv, part, s = backward_attention(
                     l, length, paired, g2s[m], x1, *sums[m], vectors, q, k, v, wq, w_out, tables, step()
                 )
                 ran(s)
-                small.append((l, (1, 3), share, s))
+                small.append((l, (1, 3), s))
                 dps[m] = (dq, dk, dv)
                 gs[m] = (g1, x, *links.start_sum(part))
+                if m == 0 and l == 0:
+                    mlp_stream([sums[-1][1]])
             groups = [keep(l, 5), gas, keep(l, 1)] + [[d[j] for d in dps] for j in range(3)]
             streams.append(kind(links, "attention", l, layers, groups, step([gs[0][3]]), written))
             ran(streams[-1].token)
-        tiny, ends, due = [], {}, {}
-
-        def by(round_number, array):
-            due.setdefault(round_number, []).append(array)
-
-        def send_last(r):
-            if paired:
-                for m in range(parts):
-                    x1, mine_part, theirs = heads[m]
-                    heads[m] = (x1, mine_part, links.swap_tensor(hold(theirs, list(last))))
-                    by(r + 2 + m, heads[m][2])
-
-        def end_layers(r):
-            cot = cotangent if paired else jnp.concatenate([g[0][0] for g in gs_first])
-            ends["result"], s = last_layer(layers - 1, length, parts, tau, vectors, cot, heads, list(last))
-            small.append((layers - 1, (4,), 1.0, s))
-            by(r + 1, s)
-
-        def end_input(r):
-            rows_here = own if paired else gs[0][1].shape[0]
-            ends["inputs"], s = input_gradient(0, paired, rows_here, vectors, gs, list(last))
-            small.append((0, (0, 2), share, s))
-            by(r + 1, s)
-
-        def add_up(r):
-            tiny.append(totals(small, layers, width, list(last)))
-            by(r + 1, tiny[-1])
-
-        def exchange(axis, pairs, r):
-            got = lax.ppermute(tiny[-1], axis, pairs)
-            by(r + 2, got)
-            tiny.append((tiny[-1], got))
-
-        def take(r):
-            tiny.append(tiny[-1][0] + tiny[-1][1])
-
-        nothing = lambda r: None
-        errands = [nothing, nothing, end_input, send_last, nothing, nothing, end_layers, add_up]
-        for j in range(links.dp.bit_length() - 1):
-            pairs = [(i, i ^ (1 << j)) for i in range(links.dp)]
-            errands += [functools.partial(exchange, "dp", pairs), take]
-        if paired:
-            errands += [functools.partial(exchange, "tensor", [(0, 1), (1, 0)]), take]
-        for m in range(parts):
-            by(1 + m, gs[m][3])
-        r = 0
-        while errands or any(s.going() for s in streams):
-            last[:] = step(due.pop(r, []))
-            if errands:
-                errands.pop(0)(r)
-            r += 1
-        tiny = tiny[-1]
-        result, inputs = ends["result"], ends["inputs"]
+        final = streams[-1]
+        own_here = own if paired else gs[0][1].shape[0]
+
+        def send_last():
+            for m in range(parts):
+                x1, part = heads[m]
+                held = hold(part, list(last)) if links.ring else part
+                heads[m] = (x1, *links.start_sum(held), gs_first[m])
+                heads[m] = (x1, part, heads[m][2], gs_first[m]) if paired else heads[m]
+
+        def end_layers():
+            inputs, s = input_gradient(0, paired, own_here, vectors, gs, list(last))
+            small.append((0, (0, 2), s))
+            result, s = last_layer(layers - 1, length, paired, own_here, tau, vectors, heads, list(last) + [s])
+            small.append((layers - 1, (4,), s))
+            return inputs, result
+
+        send_last()
+        if links.ring:
+            last[:] = step()
+            inputs, result = end_layers()
+            send, kept = totals(small, layers, width, final.core, final.p, list(last))
+            final.extra = [(kept, lax.ppermute(send, "dp", links.core_pairs))]
+            final.steps -= 1
+            while any(s.going() for s in streams):
+                last[:] = step()
+            ends = [pair for pair, _ in final.packed]
+            begins = [low for low, _ in final.cuts]
+            gains, biases, times, norms = small_outputs(ends, begins, layers, width, final.core, final.p)
+        else:
+            inputs, result = end_layers()
+            tiny = jnp.zeros((layers, 8, width), f32)
+            for l, rows_of, s in small:
+                for j, row in enumerate(rows_of):
+                    if row is not None:
+                        tiny = tiny.at[l, row].add(jnp.sum(s[8 * j : 8 * j + 8], axis=0))
+            tiny = lax.psum(tiny, "dp")
+            gains, biases, times = tiny[:, 0:2], tiny[:, 2:4], tiny[:, 4]
+            norms = jnp.stack([gains[layers - 1, 1], biases[layers - 1, 1]])
         if not paired:
             t = lax.axis_index("tensor")
             cut = lambda v: jnp.concatenate(
@@ -1068,7 +1172,6 @@
                 ]
             )
             result, inputs = cut(result), cut(inputs)
-        gains, biases = tiny[:, 0:2], tiny[:, 2:4]
         return (
             result,
             inputs,
@@ -1078,8 +1181,8 @@
             written["attention"][0],
             written["mlp"][1],
             written["mlp"][0],
-            tiny[:, 4],
-            jnp.stack([gains[layers - 1, 1], biases[layers - 1, 1]]),
+            times,
+            norms,
         )
 
     return local

time: 465 us -> 449 us (0.966)
  waiting for transfers between devices: 189 us -> 157 us
  starting transfers between devices: 82.2 us -> 98.8 us
  Pallas kernels: 170 us -> 176 us
  local copies, waits for them, and re-layouts: 11.7 us -> 6.54 us
    ppermute x70, waiting for transfers between devices: 139 us -> 111 us  [step(): self.raw = [lax.ppermute(v, 'dp', self.links.ring_pairs) for v in now]]
    ppermute x70, starting transfers between devices: 55.7 us -> 79.1 us  [step(): self.raw = [lax.ppermute(v, 'dp', self.links.ring_pairs) for v in now]]
    ppermute x9 -> x6, waiting for transfers between devices: 13.7 us -> 0.51 us  [the longest x5 0.51 us: step(): peer = lax.ppermute(mine, 'dp', self.links.core_pairs)]
    ppermute x21, waiting for transfers between devices: 36.3 us -> 44.9 us  [swap_tensor(): return lax.ppermute(v, 'tensor', [(0, 1), (1, 0)])]
    pallas_call x102 -> x113, Pallas kernels: 170 us -> 176 us  [call(): pl.pallas_call(run, out_shape=[(pltpu.HBM if away else pltpu.VMEM)(s, d)...]
    ppermute x9 -> x6, starting transfers between devices: 6.52 us -> 0.43 us  [the longest x5 0.36 us: step(): peer = lax.ppermute(mine, 'dp', self.links.core_pairs)]
  transfers between devices with their start and end apart: 104 -> 101, of which waited for: 56 -> 58; matrix products, arithmetic and copies ran while one was open for 3% -> 1% of each run, Pallas kernels for 35% -> 39%
where the time goes in v3:
time: 449 us; the launch traced here: 443 us
  Pallas kernels  176 us (39%)
  waiting for transfers between devices  157 us (35%)
  starting transfers between devices  98.8 us (22%)
  local copies, waits for them, and re-layouts  6.54 us (1%)
    pallas_call x113, Pallas kernels, call(): pl.pallas_call(run, out_shape=[(pltpu.HBM if away else pltpu.VMEM)(s, d)...  176 us
    ppermute x70, waiting for transfers between devices, step(): self.raw = [lax.ppermute(v, 'dp', self.links.ring_pairs) for v in now]  111 us
    ppermute x70, starting transfers between devices, step(): self.raw = [lax.ppermute(v, 'dp', self.links.ring_pairs) for v in now]  79.1 us
    ppermute x21, waiting for transfers between devices, swap_tensor(): return lax.ppermute(v, 'tensor', [(0, 1), (1, 0)])  44.9 us
    ppermute x21, starting transfers between devices, swap_tensor(): return lax.ppermute(v, 'tensor', [(0, 1), (1, 0)])  19 us
  transfers between devices with their start and end apart: 101, of which 58 were waited for; matrix products, arithmetic and copies ran while one was open for 1% of the time, Pallas kernels for 39%

profile of v3, /device:TPU:0, one launch (start us, length us, event | category | flops | bytes accessed | tf_op | source)
XLA Modules:
  0.0 443.0 jit_solution(15965973522538364321)
XLA Ops:
  1.8 3.0 collective-permute-start.1
  8.4 2.8 collective-permute-done
  12.4 1.8 collective-permute-start.3
  14.3 5.1 %forward_attention.4 = (f32[256,1024]{1,0:T(8,128)S(1)}, bf16[256,1024]{1,0:T(8,128)(2,1)S(1)}, f32[256,1024]{1,0:T(8,128)}, bf16[256,1024]{1,0:T(8,128)(2,1)}, ...) custom-call(bf16[256,1024]{1,0:T(8,128)(2,1)} %refs_0_.5, ...), custom_call_target="tpu_custom_call" | custom-call | flops 80000000000 | bytes 1048576 | tf_op jit(solution)/shard_map/forward_attention/pallas_call | solution.py:124
  22.1 5.1 %forward_attention.6 = (f32[256,1024]{1,0:T(8,128)S(1)}, bf16[256,1024]{1,0:T(8,128)(2,1)S(1)}, f32[256,1024]{1,0:T(8,128)}, bf16[256,1024]{1,0:T(8,128)(2,1)}, ...) custom-call(bf16[256,1024]{1,0:T(8,128)(2,1)} %refs_0_.5, ...), custom_call_target="tpu_custom_call" | custom-call | flops 80000000000 | bytes 1048576 | tf_op jit(solution)/shard_map/forward_attention/pallas_call | solution.py:124
  28.8 11.1 %collective-permute-done.5.refs_7_.refs_1_.refs_11_ = bf16[128,1024]{1,0:T(8,128)(2,1)S(1)} collective-permute-done((bf16[128,1024]{1,0:T(8,128)(2,1)S(1)}, bf16[128,1024]{1,0:T(8,128)(2,1)S(1)}, u32[]{:S(2)}, u32[]{:S(2)}) %collective-permute-start.5) | collective-permute-done | bytes 262176 | tf_op jit(solution)/shard_map/ppermute | solution.py:625
  39.9 5.6 %collective-permute-done.4.refs_6_.refs_1_ = bf16[128,1024]{1,0:T(8,128)(2,1)S(1)} collective-permute-done((bf16[128,1024]{1,0:T(8,128)(2,1)S(1)}, bf16[128,1024]{1,0:T(8,128)(2,1)S(1)}, u32[]{:S(2)}, u32[]{:S(2)}) %collective-permute-start.4) | collective-permute-done | bytes 262176 | tf_op jit(solution)/shard_map/ppermute | solution.py:625
  45.5 6.5 %forward_mlp.4 = (f32[256,1024]{1,0:T(8,128)S(1)}, bf16[256,1024]{1,0:T(8,128)(2,1)S(1)}, f32[256,1024]{1,0:T(8,128)}, bf16[256,1024]{1,0:T(8,128)(2,1)}, bf16[2...) custom-call(f32[256,1024]{1,0:T(8,128)S(1)} %get-tuple-element.171.refs_0_, ...), custom_call_target="tpu_custom_call" | custom-call | flops 120000004096 | bytes 1048576 | tf_op jit(solution)/shard_map/forward_mlp/pallas_call | solution.py:124
  52.3 4.4 collective-permute-done.10.refs_2_
  56.7 6.4 %forward_mlp.6 = (f32[256,1024]{1,0:T(8,128)S(1)}, bf16[256,1024]{1,0:T(8,128)(2,1)S(1)}, f32[256,1024]{1,0:T(8,128)}, bf16[256,1024]{1,0:T(8,128)(2,1)}, bf16[2...) custom-call(f32[256,1024]{1,0:T(8,128)S(1)} %get-tuple-element.194.refs_0_, ...), custom_call_target="tpu_custom_call" | custom-call | flops 120000004096 | bytes 1048576 | tf_op jit(solution)/shard_map/forward_mlp/pallas_call | solution.py:124
  63.5 4.5 %collective-permute-done.6.refs_2_ = bf16[256,1024]{1,0:T(8,128)(2,1)S(1)} collective-permute-done((bf16[256,1024]{1,0:T(8,128)(2,1)S(1)}, bf16[256,1024]{1,0:T(8,128)(2,1)S(1)}, u32[]{:S(2)}, u32[]{:S(2)}) %collective-permute-start.6) | collective-permute-done | bytes 524320 | tf_op jit(solution)/shard_map/ppermute | solution.py:625
  68.0 5.3 %forward_attention.5 = (f32[256,1024]{1,0:T(8,128)S(1)}, bf16[256,1024]{1,0:T(8,128)(2,1)S(1)}, f32[256,1024]{1,0:T(8,128)}, bf16[256,1024]{1,0:T(8,128)(2,1)}, ...) custom-call(f32[256,1024]{1,0:T(8,128)S(1)} %get-tuple-element.173.r, ...), custom_call_target="tpu_custom_call" | custom-call | flops 80000000000 | bytes 1048576 | tf_op jit(solution)/shard_map/forward_attention/pallas_call | solution.py:124
  73.6 5.6 %collective-permute-done.11.refs_2_ = bf16[256,1024]{1,0:T(8,128)(2,1)S(1)} collective-permute-done((bf16[256,1024]{1,0:T(8,128)(2,1)S(1)}, bf16[256,1024]{1,0:T(8,128)(2,1)S(1)}, u32[]{:S(2)}, u32[]{:S(2)}) %collective-permute-start.11) | collective-permute-done | bytes 524320 | tf_op jit(solution)/shard_map/ppermute | solution.py:625
  79.2 6.1 %forward_attention.7 = (f32[256,1024]{1,0:T(8,128)S(1)}, bf16[256,1024]{1,0:T(8,128)(2,1)}, f32[256,1024]{1,0:T(8,128)}, bf16[256,1024]{1,0:T(8,128)(2,1)}, bf16...) custom-call(f32[256,1024]{1,0:T(8,128)S(1)} %get-tuple-element.196.r, ...), custom_call_target="tpu_custom_call" | custom-call | flops 80000000000 | bytes 1048576 | tf_op jit(solution)/shard_map/forward_attention/pallas_call | solution.py:124
  85.7 4.7 %collective-permute-done.7.refs_2_ = bf16[256,1024]{1,0:T(8,128)(2,1)S(1)} collective-permute-done((bf16[256,1024]{1,0:T(8,128)(2,1)S(1)}, bf16[256,1024]{1,0:T(8,128)(2,1)S(1)}, u32[]{:S(2)}, u32[]{:S(2)}) %collective-permute-start.7) | collective-permute-done | bytes 524320 | tf_op jit(solution)/shard_map/ppermute | solution.py:625
  90.4 6.5 %forward_mlp.5 = (f32[256,1024]{1,0:T(8,128)S(1)}, bf16[256,1024]{1,0:T(8,128)(2,1)S(1)}, f32[256,1024]{1,0:T(8,128)}, bf16[256,1024]{1,0:T(8,128)(2,1)}, bf16[2...) custom-call(f32[256,1024]{1,0:T(8,128)S(1)} %get-tuple-element.175.refs_0_, ...), custom_call_target="tpu_custom_call" | custom-call | flops 120000004096 | bytes 1048576 | tf_op jit(solution)/shard_map/forward_mlp/pallas_call | solution.py:124
  98.2 6.9 %backward_mlp.4 = (f32[256,1024]{1,0:T(8,128)S(1)}, bf16[256,1024]{1,0:T(8,128)(2,1)S(1)}, bf16[256,2048]{1,0:T(8,128)(2,1)S(1)}, bf16[256,1024]{1,0:T(8,128)(2,1)}, f32[24,1024]{1,0:T(8,128)}) custom-call(bf16[256,1024]{1,0:T(8,128)(2,1)S(1)} %copy-done.6, bf16[128,1024]{1,0:T(8,128)(2,1)S(1)} %copy-done.23, ...), custom_call_target="tpu_custom_call" | custom-call | flops 120000004096 | bytes 1048576 | tf_op jit(solution)/shard_map/backward_mlp/pallas_call | solution.py:124
  105.4 7.6 %forward_mlp.7 = (f32[256,1024]{1,0:T(8,128)S(1)}, bf16[256,1024]{1,0:T(8,128)(2,1)S(1)}, f32[256,1024]{1,0:T(8,128)}, bf16[256,1024]{1,0:T(8,128)(2,1)}, bf16[2...) custom-call(f32[256,1024]{1,0:T(8,128)S(1)} %get-tuple-element.198.refs_0_, bf16[256,1024]{1,0:T(8,128)(2,1)} %get-tuple-element.199.refs_1_, ...), custom_call_target="tpu_custom_call" | custom-call | flops 120000004096 | bytes 1048576 | tf_op jit(solution)/shard_map/forward_mlp/pallas_call | solution.py:124
  114.3 7.0 %backward_mlp.5 = (f32[256,1024]{1,0:T(8,128)S(1)}, bf16[256,1024]{1,0:T(8,128)(2,1)S(1)}, bf16[256,2048]{1,0:T(8,128)(2,1)S(1)}, bf16[256,1024]{1,0:T(8,128)(2,1)}, f32[24,1024]{1,0:T(8,128)}) custom-call(bf16[256,1024]{1,0:T(8,128)(2,1)S(1)} %copy-done.6, bf16[128,1024]{1,0:T(8,128)(2,1)S(1)} %copy-done.20, ...), custom_call_target="tpu_custom_call" | custom-call | flops 120000004096 | bytes 1048576 | tf_op jit(solution)/shard_map/backward_mlp/pallas_call | solution.py:124
  121.3 1.8 collective-permute-start.15
  123.2 5.8 %mlp_gradients.2 = (bf16[8,256,1024]{2,1,0:T(8,128)(2,1)}, bf16[8,256,1024]{2,1,0:T(8,128)(2,1)S(1)}) custom-call(s32[2]{0:T(128)S(1)} %pad_add_fusion.1.refs_0_, bf16[256,2048]{1,0:T(8,128)(2,1)S(1)} %copy-done.49, bf16[256,2048]{1,0:T(8,128)(2,1)S(1)} %copy-done.50, bf16[256,1024]{1,0:T(8,128)(2,1)S(1)} %get-tuple-element.201.refs_3_, ...), custom_call_target="tpu_custom_call" | custom-call | flops 179999997952 | bytes 1048576 | tf_op jit(solution)/shard_map/mlp_gradients/pallas_call | solution.py:124
  129.2 7.6 %backward_attention.4 = (f32[256,1024]{1,0:T(8,128)S(1)}, bf16[256,1024]{1,0:T(8,128)(2,1)S(1)}, bf16[256,512]{1,0:T(8,128)(2,1)S(1)}, bf16[256,512]{1,0:T(8,128...) custom-call(f32[256,1024]{1,0:T(8,128)S(1)} %get-tuple-element.182.refs_0_, ...), custom_call_target="tpu_custom_call" | custom-call | flops 140000002048 | bytes 1048576 | tf_op jit(solution)/shard_map/backward_attention/pallas_call | solution.py:124
  138.2 1.8 collective-permute-start.14
  140.1 8.4 %backward_attention.5 = (f32[256,1024]{1,0:T(8,128)S(1)}, bf16[256,1024]{1,0:T(8,128)(2,1)S(1)}, bf16[256,512]{1,0:T(8,128)(2,1)S(1)}, bf16[256,512]{1,0:T(8,128...) custom-call(f32[256,1024]{1,0:T(8,128)S(1)} %get-tuple-element.213.refs_0_, ...), custom_call_target="tpu_custom_call" | custom-call | flops 140000002048 | bytes 1048576 | tf_op jit(solution)/shard_map/backward_attention/pallas_call | solution.py:124
  151.9 3.3 attention_gradients.2
  155.4 4.1 collective-permute-done.16.refs_0_
  161.3 6.1 %backward_mlp.6 = (f32[256,1024]{1,0:T(8,128)S(1)}, bf16[256,1024]{1,0:T(8,128)(2,1)S(1)}, bf16[256,2048]{1,0:T(8,128)(2,1)S(1)}, bf16[256,1024]{1,0:T(8,128)(2,1)S(1)}, f32[24,1024]{1,0:T(8,128)S(1)}) custom-call(f32[256,1024]{1,0:T(8,128)S(1)} %get-tuple-element.188.refs_0_, f32[256,1024]{1,0:T(8,128)S(1)} %copy-done.35, ...), custom_call_target="tpu_custom_call" | custom-call | flops 120000004096 | bytes 1048576 | tf_op jit(solution)/shard_map/backward_mlp/pallas_call | solution.py:124
  172.8 8.1 %backward_mlp.7 = (f32[256,1024]{1,0:T(8,128)S(1)}, bf16[256,1024]{1,0:T(8,128)(2,1)S(1)}, bf16[256,2048]{1,0:T(8,128)(2,1)S(1)}, bf16[256,1024]{1,0:T(8,128)(2,1)}, f32[24,1024]{1,0:T(8,128)S(1)}) custom-call(f32[256,1024]{1,0:T(8,128)S(1)} %get-tuple-element.240.refs_0_, f32[256,1024]{1,0:T(8,128)S(1)} %copy-done.33, ...), custom_call_target="tpu_custom_call" | custom-call | flops 120000004096 | bytes 1048576 | tf_op jit(solution)/shard_map/backward_mlp/pallas_call | solution.py:124
  184.8 7.2 %backward_attention.6 = (f32[256,1024]{1,0:T(8,128)S(1)}, bf16[256,1024]{1,0:T(8,128)(2,1)S(1)}, bf16[256,512]{1,0:T(8,128)(2,1)S(1)}, bf16[256,512]{1,0:T(8,128...) custom-call(f32[256,1024]{1,0:T(8,128)S(1)} %get-tuple-element.233.refs_0_, ...), custom_call_target="tpu_custom_call" | custom-call | flops 140000002048 | bytes 1048576 | tf_op jit(solution)/shard_map/backward_attention/pallas_call | solution.py:124
  197.7 5.8 %mlp_gradients.3 = (bf16[8,256,1024]{2,1,0:T(8,128)(2,1)}, bf16[8,256,1024]{2,1,0:T(8,128)(2,1)S(1)}) custom-call(s32[2]{0:T(128)S(1)} %copy-done.14, bf16[256,2048]{1,0:T(8,128)(2,1)S(1)} %copy-done.43, bf16[256,2048]{1,0:T(8,128)(2,1)S(1)} %copy-done.46, bf16[256,1024]{1,0:T(8,128)(2,1)S(1)} %get-tuple-element.259.refs_3_, ...), custom_call_target="tpu_custom_call" | custom-call | flops 179999997952 | bytes 1048576 | tf_op jit(solution)/shard_map/mlp_gradients/pallas_call | solution.py:124
  209.1 7.6 %backward_attention.7 = (f32[256,1024]{1,0:T(8,128)S(1)}, bf16[256,1024]{1,0:T(8,128)(2,1)S(1)}, bf16[256,512]{1,0:T(8,128)(2,1)S(1)}, bf16[256,512]{1,0:T(8,128...) custom-call(f32[256,1024]{1,0:T(8,128)S(1)} %get-tuple-element.250.refs_0_, ...), custom_call_target="tpu_custom_call" | custom-call | flops 140000002048 | bytes 1048576 | tf_op jit(solution)/shard_map/backward_attention/pallas_call | solution.py:124
  219.2 3.2 merge.6
  223.7 3.3 attention_gradients.3
  232.4 2.1 collective-permute-done.36.refs_0_
  234.5 2.7 collective-permute-done.42.refs_0_
  239.1 3.5 input_gradient.1
  242.5 3.1 collective-permute-done.44.refs_0_
  246.4 2.1 collective-permute-done.43.refs_0_
  251.2 5.9 %collective-permute-done.32.refs_4_ = bf16[256,1024]{1,0:T(8,128)(2,1)S(1)} collective-permute-done((bf16[256,1024]{1,0:T(8,128)(2,1)S(1)}, bf16[256,1024]{1,0:T(8,128)(2,1)S(1)}, u32[]{:S(2)}, u32[]{:S(2)}) %collective-permute-start.32) | collective-permute-done | bytes 524320 | tf_op jit(solution)/shard_map/ppermute | solution.py:625
  262.7 3.6 collective-permute-done.46.refs_0_
  269.8 2.1 collective-permute-done.54.refs_0_
  277.3 3.1 collective-permute-done.51.refs_0_
  290.2 7.2 %collective-permute-done.56.refs_0_ = bf16[256,1024]{1,0:T(8,128)(2,1)S(1)} collective-permute-done((bf16[256,1024]{1,0:T(8,128)(2,1)S(1)}, bf16[256,1024]{1,0:T(8,128)(2,1)S(1)}, u32[]{:S(2)}, u32[]{:S(2)}) %collective-permute-start.56) | collective-permute-done | bytes 524320 | tf_op jit(solution)/shard_map/ppermute | solution.py:976
  303.3 8.4 %collective-permute-done.61.refs_0_ = bf16[256,1024]{1,0:T(8,128)(2,1)S(1)} collective-permute-done((bf16[256,1024]{1,0:T(8,128)(2,1)S(1)}, bf16[256,1024]{1,0:T(8,128)(2,1)S(1)}, u32[]{:S(2)}, u32[]{:S(2)}) %collective-permute-start.61) | collective-permute-done | bytes 524320 | tf_op jit(solution)/shard_map/ppermute | solution.py:976
  314.4 3.0 collective-permute-done.55.refs_0_
  317.5 5.5 %collective-permute-done.66.refs_7_ = bf16[256,1024]{1,0:T(8,128)(2,1)S(1)} collective-permute-done((bf16[256,1024]{1,0:T(8,128)(2,1)S(1)}, bf16[256,1024]{1,0:T(8,128)(2,1)S(1)}, u32[]{:S(2)}, u32[]{:S(2)}) %collective-permute-start.66) | collective-permute-done | bytes 524320 | tf_op jit(solution)/shard_map/ppermute | solution.py:976
  327.0 2.8 collective-permute-done.69.refs_0_
  339.7 3.9 spread.10
  351.2 4.0 spread.11
  355.2 3.0 collective-permute-done.76.refs_0_
  361.3 3.4 collective-permute-done.80.refs_7_
  367.8 2.9 spread.12
  386.9 2.9 spread.13
  392.5 1.8 collective-permute-done.83.refs_0_
  403.0 2.8 collective-permute-done.94.refs_15_
  405.7 2.8 collective-permute-done.93.refs_7_
  410.1 3.9 spread.14
  416.9 5.4 %collective-permute-done.96.refs_0_ = bf16[272,512]{1,0:T(8,128)(2,1)S(1)} collective-permute-done((bf16[272,512]{1,0:T(8,128)(2,1)S(1)}, bf16[272,512]{1,0:T(8,128)(2,1)S(1)}, u32[]{:S(2)}, u32[]{:S(2)}) %collective-permute-start.96) | collective-permute-done | bytes 278560 | tf_op jit(solution)/shard_map/ppermute | solution.py:976
  423.5 2.4 spread.16
  425.9 4.0 spread.15
  431.2 2.4 spread.17
  433.5 2.9 collective-permute-done.99.refs_2_
  436.6 1.8 spread.18
  440.4 2.4 spread.19
  (407 shorter events, 152.6 us)
Async XLA Ops:
  1.8 10.6 %collective-permute-start.1 = (bf16[128,1024]{1,0:T(8,128)(2,1)S(1)}, bf16[128,1024]{1,0:T(8,128)(2,1)S(1)}, u32[]{:S(2)}, u32[]{:S(2)}) collective-permute-start(bf16[128,1024]{1,0:T(8,128)(2,1)S(1)} %get-tuple-element.335), channel_id=1, source_target_pairs={{0,1},{1,0},{2,3},{3,2},{4,5},{5,4},{6,7},{7,6},{8,9},{9,8},{10,11... | collective-permute-start | bytes 786440 | tf_op jit(solution)/shard_map/ppermute | solution.py:625
  19.3 20.5 %collective-permute-start.2 = (bf16[256,1024]{1,0:T(8,128)(2,1)S(1)}, bf16[256,1024]{1,0:T(8,128)(2,1)S(1)}, u32[]{:S(2)}, u32[]{:S(2)}) collective-permute-start(bf16[256,1024]{1,0:T(8,128)(2,1)S(1)} %get-tuple-element.172.refs_1_), channel_id=1, source_target_pairs={{0,1},{1,0},{2,3},{3,2},{4,5},{5,4},{6,7},{7,6},{8,9},{9,8},{10,11... | collective-permute-start | bytes 1572872 | tf_op jit(solution)/shard_map/ppermute | solution.py:625
  20.0 19.9 %collective-permute-start.5 = (bf16[128,1024]{1,0:T(8,128)(2,1)S(1)}, bf16[128,1024]{1,0:T(8,128)(2,1)S(1)}, u32[]{:S(2)}, u32[]{:S(2)}) collective-permute-start(bf16[128,1024]{1,0:T(8,128)(2,1)S(1)} %hold.37), channel_id=1, source_target_pairs={{0,1},{1,0},{2,3},{3,2},{4,5},{5,4},{6,7},{7,6},{8,9},{9,8},{10,11... | collective-permute-start | bytes 786440 | tf_op jit(solution)/shard_map/ppermute | solution.py:625
  21.5 23.9 %collective-permute-start.4 = (bf16[128,1024]{1,0:T(8,128)(2,1)S(1)}, bf16[128,1024]{1,0:T(8,128)(2,1)S(1)}, u32[]{:S(2)}, u32[]{:S(2)}) collective-permute-start(bf16[128,1024]{1,0:T(8,128)(2,1)S(1)} %hold.36), channel_id=1, source_target_pairs={{0,1},{1,0},{2,3},{3,2},{4,5},{5,4},{6,7},{7,6},{8,9},{9,8},{10,11... | collective-permute-start | bytes 786440 | tf_op jit(solution)/shard_map/ppermute | solution.py:625
  27.2 29.5 %collective-permute-start.10 = (bf16[256,1024]{1,0:T(8,128)(2,1)S(1)}, bf16[256,1024]{1,0:T(8,128)(2,1)S(1)}, u32[]{:S(2)}, u32[]{:S(2)}) collective-permute-start(bf16[256,1024]{1,0:T(8,128)(2,1)S(1)} %get-tuple-element.195.refs_1_), channel_id=1, source_target_pairs={{0,1},{1,0},{2,3},{3,2},{4,5},{5,4},{6,7},{7,6},{8,9},{9,8},{10,11... | collective-permute-start | bytes 1572872 | tf_op jit(solution)/shard_map/ppermute | solution.py:625
  52.0 16.0 %collective-permute-start.6 = (bf16[256,1024]{1,0:T(8,128)(2,1)S(1)}, bf16[256,1024]{1,0:T(8,128)(2,1)S(1)}, u32[]{:S(2)}, u32[]{:S(2)}) collective-permute-start(bf16[256,1024]{1,0:T(8,128)(2,1)S(1)} %get-tuple-element.174.refs_1_), channel_id=1, source_target_pairs={{0,1},{1,0},{2,3},{3,2},{4,5},{5,4},{6,7},{7,6},{8,9},{9,8},{10,11... | collective-permute-start | bytes 1572872 | tf_op jit(solution)/shard_map/ppermute | solution.py:625
  63.1 16.0 %collective-permute-start.11 = (bf16[256,1024]{1,0:T(8,128)(2,1)S(1)}, bf16[256,1024]{1,0:T(8,128)(2,1)S(1)}, u32[]{:S(2)}, u32[]{:S(2)}) collective-permute-start(bf16[256,1024]{1,0:T(8,128)(2,1)S(1)} %get-tuple-element.197.refs_1_), channel_id=1, source_target_pairs={{0,1},{1,0},{2,3},{3,2},{4,5},{5,4},{6,7},{7,6},{8,9},{9,8},{10,11... | collective-permute-start | bytes 1572872 | tf_op jit(solution)/shard_map/ppermute | solution.py:625
  73.3 17.2 %collective-permute-start.7 = (bf16[256,1024]{1,0:T(8,128)(2,1)S(1)}, bf16[256,1024]{1,0:T(8,128)(2,1)S(1)}, u32[]{:S(2)}, u32[]{:S(2)}) collective-permute-start(bf16[256,1024]{1,0:T(8,128)(2,1)S(1)} %get-tuple-element.176.refs_1_), channel_id=1, source_target_pairs={{0,1},{1,0},{2,3},{3,2},{4,5},{5,4},{6,7},{7,6},{8,9},{9,8},{10,11... | collective-permute-start | bytes 1572872 | tf_op jit(solution)/shard_map/ppermute | solution.py:625
  85.3 20.0 %collective-permute-start.12 = (bf16[256,1024]{1,0:T(8,128)(2,1)}, bf16[256,1024]{1,0:T(8,128)(2,1)}, u32[]{:S(2)}, u32[]{:S(2)}) collective-permute-start(bf16[256,1024]{1,0:T(8,128)(2,1)} %get-tuple-element.199.refs_1_), channel_id=1, source_target_pairs={{0,1},{1,0},{2,3},{3,2},{4,5},{5,4},{6,7},{7,6},{8,9},{9,8},{10,11... | collective-permute-start | bytes 1572872 | tf_op jit(solution)/shard_map/ppermute | solution.py:625
  105.0 18.1 %collective-permute-start.8 = (bf16[256,1024]{1,0:T(8,128)(2,1)}, bf16[256,1024]{1,0:T(8,128)(2,1)}, u32[]{:S(2)}, u32[]{:S(2)}) collective-permute-start(bf16[256,1024]{1,0:T(8,128)(2,1)} %get-tuple-element.184.refs_2_), channel_id=1, source_target_pairs={{0,1},{1,0},{2,3},{3,2},{4,5},{5,4},{6,7},{7,6},{8,9},{9,8},{10,11... | collective-permute-start | bytes 1572872 | tf_op jit(solution)/shard_map/ppermute | solution.py:625
  121.3 18.7 %collective-permute-start.15 = (bf16[256,1024]{1,0:T(8,128)(2,1)}, bf16[256,1024]{1,0:T(8,128)(2,1)}, u32[]{:S(2)}, u32[]{:S(2)}) collective-permute-start(bf16[256,1024]{1,0:T(8,128)(2,1)} %get-tuple-element.215.refs_2_), channel_id=1, source_target_pairs={{0,1},{1,0},{2,3},{3,2},{4,5},{5,4},{6,7},{7,6},{8,9},{9,8},{10,11... | collective-permute-start | bytes 1572872 | tf_op jit(solution)/shard_map/ppermute | solution.py:625
  136.8 15.1 %collective-permute-start.9 = (bf16[256,1024]{1,0:T(8,128)(2,1)S(1)}, bf16[256,1024]{1,0:T(8,128)(2,1)S(1)}, u32[]{:S(2)}, u32[]{:S(2)}) collective-permute-start(bf16[256,1024]{1,0:T(8,128)(2,1)S(1)} %get-tuple-element.190.refs_2_), channel_id=1, source_target_pairs={{0,1},{1,0},{2,3},{3,2},{4,5},{5,4},{6,7},{7,6},{8,9},{9,8},{10,11... | collective-permute-start | bytes 1572872 | tf_op jit(solution)/shard_map/ppermute | solution.py:625
  138.2 12.0 %collective-permute-start.14 = (bf16[256,1024]{1,0:T(8,128)(2,1)S(1)}, bf16[256,1024]{1,0:T(8,128)(2,1)S(1)}, u32[]{:S(2)}, u32[]{:S(2)}) collective-permute-start(bf16[256,1024]{1,0:T(8,128)(2,1)S(1)} %get-tuple-element.211.refs_12_), channel_id=1, source_target_pairs={{0,8},{10,2},{8,16},{18,10},{16,24},{26,18},{24,28},{30,26},{28,20... | collective-permute-start | bytes 1572872 | tf_op jit(solution)/shard_map/ppermute | solution.py:976
  148.5 24.3 %collective-permute-start.20 = (bf16[256,1024]{1,0:T(8,128)(2,1)}, bf16[256,1024]{1,0:T(8,128)(2,1)}, u32[]{:S(2)}, u32[]{:S(2)}) collective-permute-start(bf16[256,1024]{1,0:T(8,128)(2,1)} %get-tuple-element.242.refs_2_), channel_id=1, source_target_pairs={{0,1},{1,0},{2,3},{3,2},{4,5},{5,4},{6,7},{7,6},{8,9},{9,8},{10,11... | collective-permute-start | bytes 1572872 | tf_op jit(solution)/shard_map/ppermute | solution.py:625
  155.3 15.3 %collective-permute-start.21 = (bf16[8,256,512]{2,1,0:T(8,128)(2,1)S(1)}, bf16[8,256,512]{2,1,0:T(8,128)(2,1)S(1)}, u32[]{:S(2)}, u32[]{:S(2)}) collective-permute-start(bf16[8,256,512]{2,1,0:T(8,128)(2,1)S(1)} %get-tuple-element.245), channel_id=1, source_target_pairs={{0,2},{2,0},{4,6},{6,4},{8,10},{10,8},{12,14},{14,12},{16,18},{18,... | collective-permute-start | bytes 6291464 | tf_op jit(solution)/shard_map/ppermute | solution.py:941
  167.4 17.3 %collective-permute-start.17 = (bf16[256,1024]{1,0:T(8,128)(2,1)S(1)}, bf16[256,1024]{1,0:T(8,128)(2,1)S(1)}, u32[]{:S(2)}, u32[]{:S(2)}) collective-permute-start(bf16[256,1024]{1,0:T(8,128)(2,1)S(1)} %get-tuple-element.235.refs_2_), channel_id=1, source_target_pairs={{0,1},{1,0},{2,3},{3,2},{4,5},{5,4},{6,7},{7,6},{8,9},{9,8},{10,11... | collective-permute-start | bytes 1572872 | tf_op jit(solution)/shard_map/ppermute | solution.py:625
  169.0 12.0 %collective-permute-start.19 = (bf16[256,1024]{1,0:T(8,128)(2,1)S(1)}, bf16[256,1024]{1,0:T(8,128)(2,1)S(1)}, u32[]{:S(2)}, u32[]{:S(2)}) collective-permute-start(bf16[256,1024]{1,0:T(8,128)(2,1)S(1)} %add.41.refs_10_), channel_id=1, source_target_pairs={{0,8},{10,2},{8,16},{18,10},{16,24},{26,18},{24,28},{30,26},{28,20... | collective-permute-start | bytes 1572872 | tf_op jit(solution)/shard_map/ppermute | solution.py:976
  171.2 12.0 %collective-permute-start.22 = (bf16[256,512]{1,0:T(8,128)(2,1)S(1)}, bf16[256,512]{1,0:T(8,128)(2,1)S(1)}, u32[]{:S(2)}, u32[]{:S(2)}) collective-permute-start(bf16[256,512]{1,0:T(8,128)(2,1)S(1)} %get-tuple-element.246.refs_11_), channel_id=1, source_target_pairs={{0,8},{10,2},{8,16},{18,10},{16,24},{26,18},{24,28},{30,26},{28,20... | collective-permute-start | bytes 786440 | tf_op jit(solution)/shard_map/ppermute | solution.py:976
  181.2 14.4 %collective-permute-start.24 = (bf16[256,1024]{1,0:T(8,128)(2,1)S(1)}, bf16[256,1024]{1,0:T(8,128)(2,1)S(1)}, u32[]{:S(2)}, u32[]{:S(2)}) collective-permute-start(bf16[256,1024]{1,0:T(8,128)(2,1)S(1)} %add.42.refs_12_), channel_id=1, source_target_pairs={{0,8},{10,2},{8,16},{18,10},{16,24},{26,18},{24,28},{30,26},{28,20... | collective-permute-start | bytes 1572872 | tf_op jit(solution)/shard_map/ppermute | solution.py:976
  182.7 15.0 %collective-permute-start.23 = (bf16[256,1024]{1,0:T(8,128)(2,1)}, bf16[256,1024]{1,0:T(8,128)(2,1)}, u32[]{:S(2)}, u32[]{:S(2)}) collective-permute-start(bf16[256,1024]{1,0:T(8,128)(2,1)} %get-tuple-element.252.refs_2_), channel_id=1, source_target_pairs={{0,1},{1,0},{2,3},{3,2},{4,5},{5,4},{6,7},{7,6},{8,9},{9,8},{10,11... | collective-permute-start | bytes 1572872 | tf_op jit(solution)/shard_map/ppermute | solution.py:625
  183.3 10.3 %collective-permute-start.26 = (bf16[256,512]{1,0:T(8,128)(2,1)S(1)}, bf16[256,512]{1,0:T(8,128)(2,1)S(1)}, u32[]{:S(2)}, u32[]{:S(2)}) collective-permute-start(bf16[256,512]{1,0:T(8,128)(2,1)S(1)} %add.43.refs_13_), channel_id=1, source_target_pairs={{0,8},{10,2},{8,16},{18,10},{16,24},{26,18},{24,28},{30,26},{28,20... | collective-permute-start | bytes 786440 | tf_op jit(solution)/shard_map/ppermute | solution.py:976
  192.0 31.2 %collective-permute-start.28 = (bf16[256,1024]{1,0:T(8,128)(2,1)}, bf16[256,1024]{1,0:T(8,128)(2,1)}, u32[]{:S(2)}, u32[]{:S(2)}) collective-permute-start(bf16[256,1024]{1,0:T(8,128)(2,1)} %get-tuple-element.275.refs_3_), channel_id=1, source_target_pairs={{0,1},{1,0},{2,3},{3,2},{4,5},{5,4},{6,7},{7,6},{8,9},{9,8},{10,11... | collective-permute-start | bytes 1572872 | tf_op jit(solution)/shard_map/ppermute | solution.py:625
  196.4 10.3 %collective-permute-start.25 = (bf16[256,1024]{1,0:T(8,128)(2,1)}, bf16[256,1024]{1,0:T(8,128)(2,1)}, u32[]{:S(2)}, u32[]{:S(2)}) collective-permute-start(bf16[256,1024]{1,0:T(8,128)(2,1)} %add.44.refs_10_), channel_id=1, source_target_pairs={{0,8},{10,2},{8,16},{18,10},{16,24},{26,18},{24,28},{30,26},{28,20... | collective-permute-start | bytes 1572872 | tf_op jit(solution)/shard_map/ppermute | solution.py:976
  203.5 15.7 %collective-permute-start.31 = (bf16[8,256,1024]{2,1,0:T(8,128)(2,1)}, bf16[8,256,1024]{2,1,0:T(8,128)(2,1)}, u32[]{:S(2)}, u32[]{:S(2)}) collective-permute-start(bf16[8,256,1024]{2,1,0:T(8,128)(2,1)} %get-tuple-element.277), channel_id=1, source_target_pairs={{0,2},{2,0},{4,6},{6,4},{8,10},{10,8},{12,14},{14,12},{16,18},{18,... | collective-permute-start | bytes 12582920 | tf_op jit(solution)/shard_map/ppermute | solution.py:941
  204.8 11.9 %collective-permute-start.30 = (bf16[256,512]{1,0:T(8,128)(2,1)S(1)}, bf16[256,512]{1,0:T(8,128)(2,1)S(1)}, u32[]{:S(2)}, u32[]{:S(2)}) collective-permute-start(bf16[256,512]{1,0:T(8,128)(2,1)S(1)} %add.47.refs_13_), channel_id=1, source_target_pairs={{0,8},{10,2},{8,16},{18,10},{16,24},{26,18},{24,28},{30,26},{28,20... | collective-permute-start | bytes 786440 | tf_op jit(solution)/shard_map/ppermute | solution.py:976
  207.9 10.7 %collective-permute-start.29 = (bf16[256,1024]{1,0:T(8,128)(2,1)S(1)}, bf16[256,1024]{1,0:T(8,128)(2,1)S(1)}, u32[]{:S(2)}, u32[]{:S(2)}) collective-permute-start(bf16[256,1024]{1,0:T(8,128)(2,1)S(1)} %add.46.refs_12_), channel_id=1, source_target_pairs={{0,8},{10,2},{8,16},{18,10},{16,24},{26,18},{24,28},{30,26},{28,20... | collective-permute-start | bytes 1572872 | tf_op jit(solution)/shard_map/ppermute | solution.py:976
  216.8 10.2 %collective-permute-start.35 = (bf16[256,512]{1,0:T(8,128)(2,1)S(1)}, bf16[256,512]{1,0:T(8,128)(2,1)S(1)}, u32[]{:S(2)}, u32[]{:S(2)}) collective-permute-start(bf16[256,512]{1,0:T(8,128)(2,1)S(1)} %add.49.refs_15_), channel_id=1, source_target_pairs={{0,8},{10,2},{8,16},{18,10},{16,24},{26,18},{24,28},{30,26},{28,20... | collective-permute-start | bytes 786440 | tf_op jit(solution)/shard_map/ppermute | solution.py:976
  218.0 20.5 %collective-permute-start.38 = (bf16[256,1024]{1,0:T(8,128)(2,1)S(1)}, bf16[256,1024]{1,0:T(8,128)(2,1)S(1)}, u32[]{:S(2)}, u32[]{:S(2)}) collective-permute-start(bf16[256,1024]{1,0:T(8,128)(2,1)S(1)} %get-tuple-element.289.refs_7_), channel_id=1, source_target_pairs={{0,1},{1,0},{2,3},{3,2},{4,5},{5,4},{6,7},{7,6},{8,9},{9,8},{10,11... | collective-permute-start | bytes 1572872 | tf_op jit(solution)/shard_map/ppermute | solution.py:625
  223.2 11.2 %collective-permute-start.36 = (bf16[128,1024]{1,0:T(8,128)(2,1)S(1)}, bf16[128,1024]{1,0:T(8,128)(2,1)S(1)}, u32[]{:S(2)}, u32[]{:S(2)}) collective-permute-start(bf16[128,1024]{1,0:T(8,128)(2,1)S(1)} %get-tuple-element.278.refs_16_), channel_id=1, source_target_pairs={{0,8},{10,2},{8,16},{18,10},{16,24},{26,18},{24,28},{30,26},{28,20... | collective-permute-start | bytes 786440 | tf_op jit(solution)/shard_map/ppermute | solution.py:976
  227.1 10.1 %collective-permute-start.42 = (bf16[256,512]{1,0:T(8,128)(2,1)S(1)}, bf16[256,512]{1,0:T(8,128)(2,1)S(1)}, u32[]{:S(2)}, u32[]{:S(2)}) collective-permute-start(bf16[256,512]{1,0:T(8,128)(2,1)S(1)} %add.50.refs_10_.refs_13_.refs_12_.refs_2_.refs_3_), channel_id=1, source_target_pairs={{0,8},{10,2},{8,16},{18,10},{16,24},{26,18},{24,28},{30,26},{28,20... | collective-permute-start | bytes 786440 | tf_op jit(solution)/shard_map/ppermute | solution.py:976
  228.8 21.0 %collective-permute-start.41 = (bf16[256,1024]{1,0:T(8,128)(2,1)S(1)}, bf16[256,1024]{1,0:T(8,128)(2,1)S(1)}, u32[]{:S(2)}, u32[]{:S(2)}) collective-permute-start(bf16[256,1024]{1,0:T(8,128)(2,1)S(1)} %hold.40.refs_9_.refs_12_.refs_11_.refs_1_.refs_2_), channel_id=1, source_target_pairs={{0,8},{10,2},{8,16},{18,10},{16,24},{26,18},{24,28},{30,26},{28,20... | collective-permute-start | bytes 1572872 | tf_op jit(solution)/shard_map/ppermute | solution.py:976
  231.6 18.8 %collective-permute-start.33 = (bf16[256,1024]{1,0:T(8,128)(2,1)S(1)}, bf16[256,1024]{1,0:T(8,128)(2,1)S(1)}, u32[]{:S(2)}, u32[]{:S(2)}) collective-permute-start(bf16[256,1024]{1,0:T(8,128)(2,1)S(1)} %hold.39), channel_id=1, source_target_pairs={{0,1},{1,0},{2,3},{3,2},{4,5},{5,4},{6,7},{7,6},{8,9},{9,8},{10,11... | collective-permute-start | bytes 1572872 | tf_op jit(solution)/shard_map/ppermute | solution.py:625
  234.4 34.4 %collective-permute-start.39 = (bf16[8,256,512]{2,1,0:T(8,128)(2,1)S(1)}, bf16[8,256,512]{2,1,0:T(8,128)(2,1)S(1)}, u32[]{:S(2)}, u32[]{:S(2)}) collective-permute-start(bf16[8,256,512]{2,1,0:T(8,128)(2,1)S(1)} %get-tuple-element.293), channel_id=1, source_target_pairs={{0,2},{2,0},{4,6},{6,4},{8,10},{10,8},{12,14},{14,12},{16,18},{18,... | collective-permute-start | bytes 6291464 | tf_op jit(solution)/shard_map/ppermute | solution.py:941
  245.6 11.5 %collective-permute-start.32 = (bf16[256,1024]{1,0:T(8,128)(2,1)S(1)}, bf16[256,1024]{1,0:T(8,128)(2,1)S(1)}, u32[]{:S(2)}, u32[]{:S(2)}) collective-permute-start(bf16[256,1024]{1,0:T(8,128)(2,1)S(1)} %hold.38), channel_id=1, source_target_pairs={{0,1},{1,0},{2,3},{3,2},{4,5},{5,4},{6,7},{7,6},{8,9},{9,8},{10,11... | collective-permute-start | bytes 1572872 | tf_op jit(solution)/shard_map/ppermute | solution.py:625
  248.5 12.1 %collective-permute-start.47 = (bf16[256,512]{1,0:T(8,128)(2,1)S(1)}, bf16[256,512]{1,0:T(8,128)(2,1)S(1)}, u32[]{:S(2)}, u32[]{:S(2)}) collective-permute-start(bf16[256,512]{1,0:T(8,128)(2,1)S(1)} %add.53.refs_5_.refs_2_.refs_3_), channel_id=1, source_target_pairs={{0,8},{10,2},{8,16},{18,10},{16,24},{26,18},{24,28},{30,26},{28,20... | collective-permute-start | bytes 786440 | tf_op jit(solution)/shard_map/ppermute | solution.py:976
  249.8 10.9 %collective-permute-start.49 = (bf16[128,1024]{1,0:T(8,128)(2,1)S(1)}, bf16[128,1024]{1,0:T(8,128)(2,1)S(1)}, u32[]{:S(2)}, u32[]{:S(2)}) collective-permute-start(bf16[128,1024]{1,0:T(8,128)(2,1)S(1)} %add.55.refs_7_.refs_4_.refs_5_), channel_id=1, source_target_pairs={{0,8},{10,2},{8,16},{18,10},{16,24},{26,18},{24,28},{30,26},{28,20... | collective-permute-start | bytes 786440 | tf_op jit(solution)/shard_map/ppermute | solution.py:976
  250.4 11.7 %collective-permute-start.48 = (bf16[128,1024]{1,0:T(8,128)(2,1)S(1)}, bf16[128,1024]{1,0:T(8,128)(2,1)S(1)}, u32[]{:S(2)}, u32[]{:S(2)}) collective-permute-start(bf16[128,1024]{1,0:T(8,128)(2,1)S(1)} %add.54.refs_6_.refs_3_.refs_4_), channel_id=1, source_target_pairs={{0,8},{10,2},{8,16},{18,10},{16,24},{26,18},{24,28},{30,26},{28,20... | collective-permute-start | bytes 786440 | tf_op jit(solution)/shard_map/ppermute | solution.py:976
  260.7 15.3 %collective-permute-start.52 = (bf16[256,512]{1,0:T(8,128)(2,1)S(1)}, bf16[256,512]{1,0:T(8,128)(2,1)S(1)}, u32[]{:S(2)}, u32[]{:S(2)}) collective-permute-start(bf16[256,512]{1,0:T(8,128)(2,1)S(1)} %add.56.refs_3_.refs_2_.refs_0_), channel_id=1, source_target_pairs={{0,8},{10,2},{8,16},{18,10},{16,24},{26,18},{24,28},{30,26},{28,20... | collective-permute-start | bytes 786440 | tf_op jit(solution)/shard_map/ppermute | solution.py:976
  267.5 12.9 %collective-permute-start.51 = (bf16[256,1024]{1,0:T(8,128)(2,1)S(1)}, bf16[256,1024]{1,0:T(8,128)(2,1)S(1)}, u32[]{:S(2)}, u32[]{:S(2)}) collective-permute-start(bf16[256,1024]{1,0:T(8,128)(2,1)S(1)} %hold.42.refs_2_.refs_1_.refs_3_), channel_id=1, source_target_pairs={{0,8},{10,2},{8,16},{18,10},{16,24},{26,18},{24,28},{30,26},{28,20... | collective-permute-start | bytes 1572872 | tf_op jit(solution)/shard_map/ppermute | solution.py:976
  269.3 14.0 %collective-permute-start.45 = (bf16[272,512]{1,0:T(8,128)(2,1)S(1)}, bf16[272,512]{1,0:T(8,128)(2,1)S(1)}, u32[]{:S(2)}, u32[]{:S(2)}) collective-permute-start(bf16[272,512]{1,0:T(8,128)(2,1)S(1)} %get-tuple-element.297.refs_6_.refs_5_), channel_id=1, source_target_pairs={{0,8},{10,2},{8,16},{18,10},{16,24},{26,18},{24,28},{30,26},{28,20... | collective-permute-start | bytes 835592 | tf_op jit(solution)/shard_map/ppermute | solution.py:976
  272.0 14.2 %collective-permute-start.59 = (bf16[128,1024]{1,0:T(8,128)(2,1)S(1)}, bf16[128,1024]{1,0:T(8,128)(2,1)S(1)}, u32[]{:S(2)}, u32[]{:S(2)}) collective-permute-start(bf16[128,1024]{1,0:T(8,128)(2,1)S(1)} %add.61.refs_5_.refs_4_), channel_id=1, source_target_pairs={{0,8},{10,2},{8,16},{18,10},{16,24},{26,18},{24,28},{30,26},{28,20... | collective-permute-start | bytes 786440 | tf_op jit(solution)/shard_map/ppermute | solution.py:976
  274.8 14.2 %collective-permute-start.58 = (bf16[128,1024]{1,0:T(8,128)(2,1)S(1)}, bf16[128,1024]{1,0:T(8,128)(2,1)S(1)}, u32[]{:S(2)}, u32[]{:S(2)}) collective-permute-start(bf16[128,1024]{1,0:T(8,128)(2,1)S(1)} %add.60.refs_4_.refs_3_), channel_id=1, source_target_pairs={{0,8},{10,2},{8,16},{18,10},{16,24},{26,18},{24,28},{30,26},{28,20... | collective-permute-start | bytes 786440 | tf_op jit(solution)/shard_map/ppermute | solution.py:976
  276.0 22.6 %collective-permute-start.57 = (bf16[256,512]{1,0:T(8,128)(2,1)S(1)}, bf16[256,512]{1,0:T(8,128)(2,1)S(1)}, u32[]{:S(2)}, u32[]{:S(2)}) collective-permute-start(bf16[256,512]{1,0:T(8,128)(2,1)S(1)} %hold.44.refs_3_.refs_2_.refs_1_), channel_id=1, source_target_pairs={{0,8},{10,2},{8,16},{18,10},{16,24},{26,18},{24,28},{30,26},{28,20... | collective-permute-start | bytes 786440 | tf_op jit(solution)/shard_map/ppermute | solution.py:976
  280.4 17.0 %collective-permute-start.56 = (bf16[256,1024]{1,0:T(8,128)(2,1)S(1)}, bf16[256,1024]{1,0:T(8,128)(2,1)S(1)}, u32[]{:S(2)}, u32[]{:S(2)}) collective-permute-start(bf16[256,1024]{1,0:T(8,128)(2,1)S(1)} %hold.43.refs_2_.refs_1_.refs_4_), channel_id=1, source_target_pairs={{0,8},{10,2},{8,16},{18,10},{16,24},{26,18},{24,28},{30,26},{28,20... | collective-permute-start | bytes 1572872 | tf_op jit(solution)/shard_map/ppermute | solution.py:976
  283.4 17.0 %collective-permute-start.50 = (bf16[272,512]{1,0:T(8,128)(2,1)S(1)}, bf16[272,512]{1,0:T(8,128)(2,1)S(1)}, u32[]{:S(2)}, u32[]{:S(2)}) collective-permute-start(bf16[272,512]{1,0:T(8,128)(2,1)S(1)} %add.59.refs_6_.refs_5_), channel_id=1, source_target_pairs={{0,8},{10,2},{8,16},{18,10},{16,24},{26,18},{24,28},{30,26},{28,20... | collective-permute-start | bytes 835592 | tf_op jit(solution)/shard_map/ppermute | solution.py:976
  286.2 17.0 %collective-permute-start.64 = (bf16[128,1024]{1,0:T(8,128)(2,1)S(1)}, bf16[128,1024]{1,0:T(8,128)(2,1)S(1)}, u32[]{:S(2)}, u32[]{:S(2)}) collective-permute-start(bf16[128,1024]{1,0:T(8,128)(2,1)S(1)} %add.64.refs_5_.refs_4_), channel_id=1, source_target_pairs={{0,8},{10,2},{8,16},{18,10},{16,24},{26,18},{24,28},{30,26},{28,20... | collective-permute-start | bytes 786440 | tf_op jit(solution)/shard_map/ppermute | solution.py:976
  289.0 23.8 %collective-permute-start.63 = (bf16[128,1024]{1,0:T(8,128)(2,1)S(1)}, bf16[128,1024]{1,0:T(8,128)(2,1)S(1)}, u32[]{:S(2)}, u32[]{:S(2)}) collective-permute-start(bf16[128,1024]{1,0:T(8,128)(2,1)S(1)} %add.63.refs_4_.refs_3_), channel_id=1, source_target_pairs={{0,8},{10,2},{8,16},{18,10},{16,24},{26,18},{24,28},{30,26},{28,20... | collective-permute-start | bytes 786440 | tf_op jit(solution)/shard_map/ppermute | solution.py:976
  297.4 14.2 %collective-permute-start.61 = (bf16[256,1024]{1,0:T(8,128)(2,1)S(1)}, bf16[256,1024]{1,0:T(8,128)(2,1)S(1)}, u32[]{:S(2)}, u32[]{:S(2)}) collective-permute-start(bf16[256,1024]{1,0:T(8,128)(2,1)S(1)} %hold.45.refs_2_.refs_1_.refs_5_), channel_id=1, source_target_pairs={{0,8},{10,2},{8,16},{18,10},{16,24},{26,18},{24,28},{30,26},{28,20... | collective-permute-start | bytes 1572872 | tf_op jit(solution)/shard_map/ppermute | solution.py:976
  298.6 15.8 %collective-permute-start.62 = (bf16[256,512]{1,0:T(8,128)(2,1)S(1)}, bf16[256,512]{1,0:T(8,128)(2,1)S(1)}, u32[]{:S(2)}, u32[]{:S(2)}) collective-permute-start(bf16[256,512]{1,0:T(8,128)(2,1)S(1)} %hold.46.refs_3_.refs_2_), channel_id=1, source_target_pairs={{0,8},{10,2},{8,16},{18,10},{16,24},{26,18},{24,28},{30,26},{28,20... | collective-permute-start | bytes 786440 | tf_op jit(solution)/shard_map/ppermute | solution.py:976
  300.5 17.0 %collective-permute-start.55 = (bf16[272,512]{1,0:T(8,128)(2,1)S(1)}, bf16[272,512]{1,0:T(8,128)(2,1)S(1)}, u32[]{:S(2)}, u32[]{:S(2)}) collective-permute-start(bf16[272,512]{1,0:T(8,128)(2,1)S(1)} %add.62.refs_6_.refs_5_), channel_id=1, source_target_pairs={{0,8},{10,2},{8,16},{18,10},{16,24},{26,18},{24,28},{30,26},{28,20... | collective-permute-start | bytes 835592 | tf_op jit(solution)/shard_map/ppermute | solution.py:976
  311.7 11.4 %collective-permute-start.66 = (bf16[256,1024]{1,0:T(8,128)(2,1)S(1)}, bf16[256,1024]{1,0:T(8,128)(2,1)S(1)}, u32[]{:S(2)}, u32[]{:S(2)}) collective-permute-start(bf16[256,1024]{1,0:T(8,128)(2,1)S(1)} %hold.47.refs_2_.refs_6_.refs_8_.refs_1_), channel_id=1, source_target_pairs={{0,8},{10,2},{8,16},{18,10},{16,24},{26,18},{24,28},{30,26},{28,20... | collective-permute-start | bytes 1572872 | tf_op jit(solution)/shard_map/ppermute | solution.py:976
  323.3 27.9 %collective-permute-start.71 = (bf16[8,256,1024]{2,1,0:T(8,128)(2,1)S(1)}, bf16[8,256,1024]{2,1,0:T(8,128)(2,1)S(1)}, u32[]{:S(2)}, u32[]{:S(2)}) collective-permute-start(bf16[8,256,1024]{2,1,0:T(8,128)(2,1)S(1)} %pack.5.refs_1_), channel_id=1, source_target_pairs={{0,2},{2,0},{4,6},{6,4},{8,10},{10,8},{12,14},{14,12},{16,18},{18,... | collective-permute-start | bytes 12582920 | tf_op jit(solution)/shard_map/ppermute | solution.py:962
  326.3 12.2 %collective-permute-start.60 = (bf16[272,512]{1,0:T(8,128)(2,1)S(1)}, bf16[272,512]{1,0:T(8,128)(2,1)S(1)}, u32[]{:S(2)}, u32[]{:S(2)}) collective-permute-start(bf16[272,512]{1,0:T(8,128)(2,1)S(1)} %add.65.refs_6_.refs_12_.refs_5_), channel_id=1, source_target_pairs={{0,8},{10,2},{8,16},{18,10},{16,24},{26,18},{24,28},{30,26},{28,20... | collective-permute-start | bytes 835592 | tf_op jit(solution)/shard_map/ppermute | solution.py:976
  329.9 13.7 %collective-permute-start.74 = (bf16[128,1024]{1,0:T(8,128)(2,1)S(1)}, bf16[128,1024]{1,0:T(8,128)(2,1)S(1)}, u32[]{:S(2)}, u32[]{:S(2)}) collective-permute-start(bf16[128,1024]{1,0:T(8,128)(2,1)S(1)} %add.70.refs_5_.refs_7_.refs_4_.refs_8_), channel_id=1, source_target_pairs={{0,8},{10,2},{8,16},{18,10},{16,24},{26,18},{24,28},{30,26},{28,20... | collective-permute-start | bytes 786440 | tf_op jit(solution)/shard_map/ppermute | solution.py:976
  332.7 12.3 %collective-permute-start.73 = (bf16[128,1024]{1,0:T(8,128)(2,1)S(1)}, bf16[128,1024]{1,0:T(8,128)(2,1)S(1)}, u32[]{:S(2)}, u32[]{:S(2)}) collective-permute-start(bf16[128,1024]{1,0:T(8,128)(2,1)S(1)} %add.69.refs_4_.refs_6_.refs_3_.refs_0_), channel_id=1, source_target_pairs={{0,8},{10,2},{8,16},{18,10},{16,24},{26,18},{24,28},{30,26},{28,20... | collective-permute-start | bytes 786440 | tf_op jit(solution)/shard_map/ppermute | solution.py:976
  335.4 11.4 %collective-permute-start.72 = (bf16[256,512]{1,0:T(8,128)(2,1)S(1)}, bf16[256,512]{1,0:T(8,128)(2,1)S(1)}, u32[]{:S(2)}, u32[]{:S(2)}) collective-permute-start(bf16[256,512]{1,0:T(8,128)(2,1)S(1)} %hold.49.refs_3_.refs_5_.refs_2_.refs_4_), channel_id=1, source_target_pairs={{0,8},{10,2},{8,16},{18,10},{16,24},{26,18},{24,28},{30,26},{28,20... | collective-permute-start | bytes 786440 | tf_op jit(solution)/shard_map/ppermute | solution.py:976
  338.5 11.3 %collective-permute-start.65 = (bf16[272,512]{1,0:T(8,128)(2,1)S(1)}, bf16[272,512]{1,0:T(8,128)(2,1)S(1)}, u32[]{:S(2)}, u32[]{:S(2)}) collective-permute-start(bf16[272,512]{1,0:T(8,128)(2,1)S(1)} %add.68.refs_6_.refs_8_.refs_5_), channel_id=1, source_target_pairs={{0,8},{10,2},{8,16},{18,10},{16,24},{26,18},{24,28},{30,26},{28,20... | collective-permute-start | bytes 835592 | tf_op jit(solution)/shard_map/ppermute | solution.py:976
  343.7 15.8 %collective-permute-start.78 = (bf16[128,1024]{1,0:T(8,128)(2,1)S(1)}, bf16[128,1024]{1,0:T(8,128)(2,1)S(1)}, u32[]{:S(2)}, u32[]{:S(2)}) collective-permute-start(bf16[128,1024]{1,0:T(8,128)(2,1)S(1)} %hold.52.refs_5_.refs_4_.refs_9_), channel_id=1, source_target_pairs={{0,8},{10,2},{8,16},{18,10},{16,24},{26,18},{24,28},{30,26},{28,20... | collective-permute-start | bytes 786440 | tf_op jit(solution)/shard_map/ppermute | solution.py:976
  345.0 14.5 %collective-permute-start.77 = (bf16[128,1024]{1,0:T(8,128)(2,1)S(1)}, bf16[128,1024]{1,0:T(8,128)(2,1)S(1)}, u32[]{:S(2)}, u32[]{:S(2)}) collective-permute-start(bf16[128,1024]{1,0:T(8,128)(2,1)S(1)} %hold.51.refs_4_.refs_3_.refs_1_), channel_id=1, source_target_pairs={{0,8},{10,2},{8,16},{18,10},{16,24},{26,18},{24,28},{30,26},{28,20... | collective-permute-start | bytes 786440 | tf_op jit(solution)/shard_map/ppermute | solution.py:976
  346.9 11.4 %collective-permute-start.76 = (bf16[256,512]{1,0:T(8,128)(2,1)S(1)}, bf16[256,512]{1,0:T(8,128)(2,1)S(1)}, u32[]{:S(2)}, u32[]{:S(2)}) collective-permute-start(bf16[256,512]{1,0:T(8,128)(2,1)S(1)} %hold.50.refs_3_.refs_2_.refs_5_), channel_id=1, source_target_pairs={{0,8},{10,2},{8,16},{18,10},{16,24},{26,18},{24,28},{30,26},{28,20... | collective-permute-start | bytes 786440 | tf_op jit(solution)/shard_map/ppermute | solution.py:976
  349.9 11.3 %collective-permute-start.70 = (bf16[272,512]{1,0:T(8,128)(2,1)S(1)}, bf16[272,512]{1,0:T(8,128)(2,1)S(1)}, u32[]{:S(2)}, u32[]{:S(2)}) collective-permute-start(bf16[272,512]{1,0:T(8,128)(2,1)S(1)} %add.71.refs_6_.refs_5_), channel_id=1, source_target_pairs={{0,8},{10,2},{8,16},{18,10},{16,24},{26,18},{24,28},{30,26},{28,20... | collective-permute-start | bytes 835592 | tf_op jit(solution)/shard_map/ppermute | solution.py:976
  364.8 22.1 %collective-permute-start.84 = (bf16[8,256,512]{2,1,0:T(8,128)(2,1)S(1)}, bf16[8,256,512]{2,1,0:T(8,128)(2,1)S(1)}, u32[]{:S(2)}, u32[]{:S(2)}) collective-permute-start(bf16[8,256,512]{2,1,0:T(8,128)(2,1)S(1)} %pack.6.refs_1_), channel_id=1, source_target_pairs={{0,2},{2,0},{4,6},{6,4},{8,10},{10,8},{12,14},{14,12},{16,18},{18,... | collective-permute-start | bytes 6291464 | tf_op jit(solution)/shard_map/ppermute | solution.py:962
  408.8 17.0 %collective-permute-start.98 = (bf16[8,256,1024]{2,1,0:T(8,128)(2,1)S(1)}, bf16[8,256,1024]{2,1,0:T(8,128)(2,1)S(1)}, u32[]{:S(2)}, u32[]{:S(2)}) collective-permute-start(bf16[8,256,1024]{2,1,0:T(8,128)(2,1)S(1)} %pack.7.refs_1_), channel_id=1, source_target_pairs={{0,2},{2,0},{4,6},{6,4},{8,10},{10,8},{12,14},{14,12},{16,18},{18,... | collective-permute-start | bytes 12582920 | tf_op jit(solution)/shard_map/ppermute | solution.py:962
  415.6 15.5 %collective-permute-start.95 = (bf16[5,272,512]{2,1,0:T(8,128)(2,1)S(1)}, bf16[5,272,512]{2,1,0:T(8,128)(2,1)S(1)}, u32[]{:S(2)}, u32[]{:S(2)}) collective-permute-start(bf16[5,272,512]{2,1,0:T(8,128)(2,1)S(1)} %pack.8.refs_1_), channel_id=1, source_target_pairs={{0,2},{2,0},{4,6},{6,4},{8,10},{10,8},{12,14},{14,12},{16,18},{18,... | collective-permute-start | bytes 4177928 | tf_op jit(solution)/shard_map/ppermute | solution.py:962
  (110 other events, 1048.2 us)

commit v4 on v3

--- a/solution.py
+++ b/solution.py
@@ -175,7 +175,7 @@
     return jnp.concatenate([a, b], axis=1)
 
 
-def forward_attention(layer, part_index, length, swapped, head, tau, vectors, w_qkv, w_out, tables):
+def forward_attention(layer, part_index, length, swapped, head, tau, vectors, w_qkv, w_out, tables, after):
     first = layer == 0
     rows = sum(n for _, _, n in head) if first else head[0].shape[0]
     width = w_out.shape[2]
@@ -284,7 +284,7 @@
     ]
     scratch += [pltpu.VMEM((rows, local), bf16)] * 4
     scratch.append(pltpu.VMEM((head[0][2], width), bf16) if first else pltpu.VMEM((rows, width), f32))
-    return call(kernel, ins, outs, scratch, 4 * 10**9, "forward_attention")
+    return call(kernel, ins, outs, scratch, 4 * 10**9, "forward_attention", after=after)
 
 
 def forward_mlp(layer, swapped, x, own, got, vectors, w_up, w_down, after):
@@ -929,6 +929,7 @@
         self.extra = []
         self.cuts = [(0, 5), (5, 8)] if kind == "attention" and layer == 0 else [(0, 8)]
         self.packed = []
+        self.waits = not (kind == "attention" and layer == 0)
         self.lanes = LANES[kind][min(layer, 1)]
         self.core = lax.axis_index("dp") & 1
         self.p = links.ring_place()
@@ -950,19 +951,21 @@
         if self.steps == 14:
             for lane, v in zip(self.done, self.raw):
                 lane.append(v)
+            if self.waits:
+                return []
         if self.packed and len(self.packed[-1]) == 2 and not self.packed[-1][-1][1]:
             (_, peer), state = self.packed[-1][0], self.packed[-1][-1]
             state[1] = True
             out.append(self.write(peer, state[0], False, after))
-        if self.steps == 15:
+        if self.steps == 15 + self.waits:
             return out
         for low, high in self.cuts:
-            if self.steps == min(high + 7, 14):
+            if self.steps == min(high + 7, 14 + self.waits):
                 mine = pack([lane[low:high] for lane in self.done], after)
                 peer = lax.ppermute(mine, "dp", self.links.core_pairs)
                 out.append(self.write(mine, low, True, []))
                 self.packed.append(((mine, peer), [low, False]))
-        if self.steps == 14:
+        if self.steps >= 14:
             return out
         if self.steps == 0:
             now, self.blocks = merge([(self.blocks, self.raw)] + self.extra, self.lanes, after)
@@ -984,7 +987,7 @@
         return token
 
     def going(self):
-        return self.steps < 15
+        return self.steps < 15 + self.waits
 
 
 LANES = {"mlp": (2, 1), "attention": (1, 1)}
@@ -1042,8 +1045,7 @@
 
         heads = [group_rows(tokens, 0)]
         heads += [group_rows(tokens, m, [heads[-1][-1][0]]) for m in range(1, parts)]
-        gs = [group_rows(cotangent, m, [heads[-1][-1][0]]) for m in range(parts)]
-        arrived = [g[-1][0] for g in gs]
+        gs = []
         vectors = [norm_gain.reshape(2 * layers, width), norm_bias.reshape(2 * layers, width)]
         vectors += [time_weight, jnp.zeros((layers, width), f32)]
         vectors = jnp.concatenate(vectors)
@@ -1053,22 +1055,26 @@
             index = links.gather_tensor(time_index)
         onehot = (index[:, None] == jnp.arange(time_table.shape[0], dtype=jnp.int32)[None, :]).astype(f32)
         tau = jnp.dot(onehot, time_table, precision=lax.Precision.HIGHEST)
+        latest = []
         saved = [[None] * parts for _ in range(layers)]
         after = [[None] * parts for _ in range(layers)]
         for l in range(layers):
             for m in range(parts):
                 x_near, part, *out = forward_attention(
-                    l, m, length, paired, heads[m], tau, vectors, wq, w_out, tables
+                    l, m, length, paired, heads[m], tau, vectors, wq, w_out, tables, latest
                 )
+                latest = [part]
                 if l > 0:
                     after[l - 1][m] = out.pop()
                 saved[l][m] = out
                 heads[m] = (x_near, *links.start_sum(part))
             for m in range(parts):
-                x1, part, *out = forward_mlp(l, paired, *heads[m], vectors, w_up, w_down, arrived)
+                x1, part, *out = forward_mlp(l, paired, *heads[m], vectors, w_up, w_down, latest)
+                latest = [part]
                 heads[m] = (x1, part) if l == layers - 1 else (x1, *links.start_sum(part))
                 saved[l][m] += out
-                arrived = []
+                if l == layers - 1:
+                    gs.append(group_rows(cotangent, m, [part] + [g[-1][0] for g in gs]))
 
         kind = Stream if links.ring else Plain
         streams = []
@@ -1095,8 +1101,9 @@
             for m in range(parts):
                 g2s[m], gms[m], dus[m], part, s = backward_mlp(
                     l, l == layers - 1, m, length, paired, gs[m], after[l][m], tau, vectors, saved[l][m][9],
-                    w_up, w_down, step(),
+                    w_up, w_down, step(latest),
                 )
+                latest = []
                 ran(s)
                 if l < layers - 1:
                     small.append((l + 1, (0, 2), s))
@@ -1149,7 +1156,15 @@
             final.extra = [(kept, lax.ppermute(send, "dp", links.core_pairs))]
             final.steps -= 1
             while any(s.going() for s in streams):
-                last[:] = step()
+                moving = [s for s in streams if s.steps < 13]
+                ending = [s for s in streams if s.steps >= 13 and s.going()]
+                now = []
+                for s in moving:
+                    now += s.step(list(last))
+                rest = []
+                for s in ending:
+                    rest += s.step(now or list(last))
+                last[:] = now + rest
             ends = [pair for pair, _ in final.packed]
             begins = [low for low, _ in final.cuts]
             gains, biases, times, norms = small_outputs(ends, begins, layers, width, final.core, final.p)

time: 449 us -> 439 us (0.978)
  waiting for transfers between devices: 157 us -> 148 us
    ppermute x70, waiting for transfers between devices: 111 us -> 100 us  [step(): self.raw = [lax.ppermute(v, 'dp', self.links.ring_pairs) for v in now]]
    pallas_call x113, Pallas kernels: 176 us -> 172 us  [call(): pl.pallas_call(run, out_shape=[(pltpu.HBM if away else pltpu.VMEM)(s, d)...]
  transfers between devices with their start and end apart: 101 -> 101, of which waited for: 58 -> 57; matrix products, arithmetic and copies ran while one was open for 1% -> 1% of each run, Pallas kernels for 39% -> 39%
where the time goes in v4:
time: 439 us; the launch traced here: 434 us
  Pallas kernels  172 us (39%)
  waiting for transfers between devices  148 us (34%)
  starting transfers between devices  103 us (23%)
  local copies, waits for them, and re-layouts  6.37 us (1%)
    pallas_call x113, Pallas kernels, call(): pl.pallas_call(run, out_shape=[(pltpu.HBM if away else pltpu.VMEM)(s, d)...  172 us
    ppermute x70, waiting for transfers between devices, step(): self.raw = [lax.ppermute(v, 'dp', self.links.ring_pairs) for v in now]  100 us
    ppermute x70, starting transfers between devices, step(): self.raw = [lax.ppermute(v, 'dp', self.links.ring_pairs) for v in now]  83.6 us
    ppermute x21, waiting for transfers between devices, swap_tensor(): return lax.ppermute(v, 'tensor', [(0, 1), (1, 0)])  45.8 us
    ppermute x21, starting transfers between devices, swap_tensor(): return lax.ppermute(v, 'tensor', [(0, 1), (1, 0)])  17.9 us
  transfers between devices with their start and end apart: 101, of which 57 were waited for; matrix products, arithmetic and copies ran while one was open for 1% of the time, Pallas kernels for 39%

profile of v4, /device:TPU:0, one launch (start us, length us, event | category | flops | bytes accessed | tf_op | source)
XLA Modules:
  0.0 433.5 jit_solution(14127285338066799941)
XLA Ops:
  1.8 3.0 collective-permute-start.1
  8.4 2.8 collective-permute-done
  14.3 5.1 %forward_attention.4 = (f32[256,1024]{1,0:T(8,128)S(1)}, bf16[256,1024]{1,0:T(8,128)(2,1)S(1)}, f32[256,1024]{1,0:T(8,128)}, bf16[256,1024]{1,0:T(8,128)(2,1)}, ...) custom-call(bf16[256,1024]{1,0:T(8,128)(2,1)} %refs_0_.5, ...), custom_call_target="tpu_custom_call" | custom-call | flops 80000000000 | bytes 1048576 | tf_op jit(solution)/shard_map/forward_attention/pallas_call | solution.py:124
  19.9 5.1 %forward_attention.5 = (f32[256,1024]{1,0:T(8,128)S(1)}, bf16[256,1024]{1,0:T(8,128)(2,1)S(1)}, f32[256,1024]{1,0:T(8,128)}, bf16[256,1024]{1,0:T(8,128)(2,1)}, ...) custom-call(bf16[256,1024]{1,0:T(8,128)(2,1)} %refs_0_.5, ...), custom_call_target="tpu_custom_call" | custom-call | flops 80000000000 | bytes 1048576 | tf_op jit(solution)/shard_map/forward_attention/pallas_call | solution.py:124
  26.6 7.7 %collective-permute-done.2.refs_2_ = bf16[256,1024]{1,0:T(8,128)(2,1)S(1)} collective-permute-done((bf16[256,1024]{1,0:T(8,128)(2,1)S(1)}, bf16[256,1024]{1,0:T(8,128)(2,1)S(1)}, u32[]{:S(2)}, u32[]{:S(2)}) %collective-permute-start.2) | collective-permute-done | bytes 524320 | tf_op jit(solution)/shard_map/ppermute | solution.py:625
  34.3 6.4 %forward_mlp.4 = (f32[256,1024]{1,0:T(8,128)S(1)}, bf16[256,1024]{1,0:T(8,128)(2,1)S(1)}, f32[256,1024]{1,0:T(8,128)}, bf16[256,1024]{1,0:T(8,128)(2,1)}, bf16[2...) custom-call(f32[256,1024]{1,0:T(8,128)S(1)} %get-tuple-element.171.refs_0_, ...), custom_call_target="tpu_custom_call" | custom-call | flops 120000004096 | bytes 1048576 | tf_op jit(solution)/shard_map/forward_mlp/pallas_call | solution.py:124
  41.0 4.5 %collective-permute-done.5.refs_2_ = bf16[256,1024]{1,0:T(8,128)(2,1)S(1)} collective-permute-done((bf16[256,1024]{1,0:T(8,128)(2,1)S(1)}, bf16[256,1024]{1,0:T(8,128)(2,1)S(1)}, u32[]{:S(2)}, u32[]{:S(2)}) %collective-permute-start.5) | collective-permute-done | bytes 524320 | tf_op jit(solution)/shard_map/ppermute | solution.py:625
  45.5 6.4 %forward_mlp.5 = (f32[256,1024]{1,0:T(8,128)S(1)}, bf16[256,1024]{1,0:T(8,128)(2,1)S(1)}, f32[256,1024]{1,0:T(8,128)}, bf16[256,1024]{1,0:T(8,128)(2,1)}, bf16[2...) custom-call(f32[256,1024]{1,0:T(8,128)S(1)} %get-tuple-element.176.refs_0_, ...), custom_call_target="tpu_custom_call" | custom-call | flops 120000004096 | bytes 1048576 | tf_op jit(solution)/shard_map/forward_mlp/pallas_call | solution.py:124
  52.3 4.4 %collective-permute-done.4.refs_2_ = bf16[256,1024]{1,0:T(8,128)(2,1)S(1)} collective-permute-done((bf16[256,1024]{1,0:T(8,128)(2,1)S(1)}, bf16[256,1024]{1,0:T(8,128)(2,1)S(1)}, u32[]{:S(2)}, u32[]{:S(2)}) %collective-permute-start.4) | collective-permute-done | bytes 524320 | tf_op jit(solution)/shard_map/ppermute | solution.py:625
  56.7 5.4 %forward_attention.6 = (f32[256,1024]{1,0:T(8,128)S(1)}, bf16[256,1024]{1,0:T(8,128)(2,1)S(1)}, f32[256,1024]{1,0:T(8,128)}, bf16[256,1024]{1,0:T(8,128)(2,1)}, ...) custom-call(f32[256,1024]{1,0:T(8,128)S(1)} %get-tuple-element.174.r, ...), custom_call_target="tpu_custom_call" | custom-call | flops 80000000000 | bytes 1048576 | tf_op jit(solution)/shard_map/forward_attention/pallas_call | solution.py:124
  62.4 5.5 %collective-permute-done.7.refs_2_ = bf16[256,1024]{1,0:T(8,128)(2,1)S(1)} collective-permute-done((bf16[256,1024]{1,0:T(8,128)(2,1)S(1)}, bf16[256,1024]{1,0:T(8,128)(2,1)S(1)}, u32[]{:S(2)}, u32[]{:S(2)}) %collective-permute-start.7) | collective-permute-done | bytes 524320 | tf_op jit(solution)/shard_map/ppermute | solution.py:625
  68.0 5.3 %forward_attention.7 = (f32[256,1024]{1,0:T(8,128)S(1)}, bf16[256,1024]{1,0:T(8,128)(2,1)S(1)}, f32[256,1024]{1,0:T(8,128)}, bf16[256,1024]{1,0:T(8,128)(2,1)}, ...) custom-call(f32[256,1024]{1,0:T(8,128)S(1)} %get-tuple-element.180.r, ...), custom_call_target="tpu_custom_call" | custom-call | flops 80000000000 | bytes 1048576 | tf_op jit(solution)/shard_map/forward_attention/pallas_call | solution.py:124
  73.7 5.5 %collective-permute-done.6.refs_2_ = bf16[256,1024]{1,0:T(8,128)(2,1)S(1)} collective-permute-done((bf16[256,1024]{1,0:T(8,128)(2,1)S(1)}, bf16[256,1024]{1,0:T(8,128)(2,1)S(1)}, u32[]{:S(2)}, u32[]{:S(2)}) %collective-permute-start.6) | collective-permute-done | bytes 524320 | tf_op jit(solution)/shard_map/ppermute | solution.py:625
  79.2 6.4 %forward_mlp.6 = (f32[256,1024]{1,0:T(8,128)S(1)}, bf16[256,1024]{1,0:T(8,128)(2,1)S(1)}, f32[256,1024]{1,0:T(8,128)}, bf16[256,1024]{1,0:T(8,128)(2,1)}, bf16[2...) custom-call(f32[256,1024]{1,0:T(8,128)S(1)} %get-tuple-element.178.refs_0_, ...), custom_call_target="tpu_custom_call" | custom-call | flops 120000004096 | bytes 1048576 | tf_op jit(solution)/shard_map/forward_mlp/pallas_call | solution.py:124
  86.0 4.4 %collective-permute-done.9.refs_2_ = bf16[256,1024]{1,0:T(8,128)(2,1)S(1)} collective-permute-done((bf16[256,1024]{1,0:T(8,128)(2,1)S(1)}, bf16[256,1024]{1,0:T(8,128)(2,1)S(1)}, u32[]{:S(2)}, u32[]{:S(2)}) %collective-permute-start.9) | collective-permute-done | bytes 524320 | tf_op jit(solution)/shard_map/ppermute | solution.py:625
  90.4 6.4 %forward_mlp.7 = (f32[256,1024]{1,0:T(8,128)S(1)}, bf16[256,1024]{1,0:T(8,128)(2,1)S(1)}, f32[256,1024]{1,0:T(8,128)}, bf16[256,1024]{1,0:T(8,128)(2,1)}, bf16[2...) custom-call(f32[256,1024]{1,0:T(8,128)S(1)} %get-tuple-element.187.refs_0_, ...), custom_call_target="tpu_custom_call" | custom-call | flops 120000004096 | bytes 1048576 | tf_op jit(solution)/shard_map/forward_mlp/pallas_call | solution.py:124
  98.5 6.1 %backward_mlp.4 = (f32[256,1024]{1,0:T(8,128)S(1)}, bf16[256,1024]{1,0:T(8,128)(2,1)S(1)}, bf16[256,2048]{1,0:T(8,128)(2,1)S(1)}, bf16[256,1024]{1,0:T(8,128)(2,1)S(1)}, f32[24,1024]{1,0:T(8,128)}) custom-call(bf16[256,1024]{1,0:T(8,128)(2,1)S(1)} %copy-done.6, bf16[128,1024]{1,0:T(8,128)(2,1)S(1)} %collective-permute-done.8.refs_1_.refs_2_.refs_6_, ...), custom_call_target="tpu_custom_call" | custom-call | flops 120000004096 | bytes 1048576 | tf_op jit(solution)/shard_map/backward_mlp/pallas_call | solution.py:124
  105.3 7.0 %backward_mlp.5 = (f32[256,1024]{1,0:T(8,128)S(1)}, bf16[256,1024]{1,0:T(8,128)(2,1)S(1)}, bf16[256,2048]{1,0:T(8,128)(2,1)S(1)}, bf16[256,1024]{1,0:T(8,128)(2,1)}, f32[24,1024]{1,0:T(8,128)}) custom-call(bf16[256,1024]{1,0:T(8,128)(2,1)S(1)} %copy-done.6, bf16[128,1024]{1,0:T(8,128)(2,1)S(1)} %collective-permute-done.12.refs_1_.refs_11_, ...), custom_call_target="tpu_custom_call" | custom-call | flops 120000004096 | bytes 1048576 | tf_op jit(solution)/shard_map/backward_mlp/pallas_call | solution.py:124
  113.9 4.2 collective-permute-done.10.refs_3_.refs_9_
  118.3 5.8 %mlp_gradients.2 = (bf16[8,256,1024]{2,1,0:T(8,128)(2,1)}, bf16[8,256,1024]{2,1,0:T(8,128)(2,1)S(1)}) custom-call(s32[2]{0:T(128)S(1)} %pad_add_fusion.1.refs_0_, bf16[256,2048]{1,0:T(8,128)(2,1)S(1)} %copy-done.54, bf16[256,2048]{1,0:T(8,128)(2,1)S(1)} %copy-done.55, bf16[256,1024]{1,0:T(8,128)(2,1)S(1)} %get-tuple-element.202.refs_3_, ...), custom_call_target="tpu_custom_call" | custom-call | flops 179999997952 | bytes 1048576 | tf_op jit(solution)/shard_map/mlp_gradients/pallas_call | solution.py:124
  124.2 6.4 %backward_attention.4 = (f32[256,1024]{1,0:T(8,128)S(1)}, bf16[256,1024]{1,0:T(8,128)(2,1)S(1)}, bf16[256,512]{1,0:T(8,128)(2,1)S(1)}, bf16[256,512]{1,0:T(8,128...) custom-call(f32[256,1024]{1,0:T(8,128)S(1)} %get-tuple-element.189.refs_0_, ...), custom_call_target="tpu_custom_call" | custom-call | flops 140000002048 | bytes 1048576 | tf_op jit(solution)/shard_map/backward_attention/pallas_call | solution.py:124
  132.6 2.1 collective-permute-start.14
  134.7 8.4 %backward_attention.5 = (f32[256,1024]{1,0:T(8,128)S(1)}, bf16[256,1024]{1,0:T(8,128)(2,1)S(1)}, bf16[256,512]{1,0:T(8,128)(2,1)S(1)}, bf16[256,512]{1,0:T(8,128...) custom-call(f32[256,1024]{1,0:T(8,128)S(1)} %get-tuple-element.214.refs_0_, ...), custom_call_target="tpu_custom_call" | custom-call | flops 140000002048 | bytes 1048576 | tf_op jit(solution)/shard_map/backward_attention/pallas_call | solution.py:124
  146.2 2.9 attention_gradients.2
  149.3 4.5 %collective-permute-done.16.refs_0_ = bf16[256,1024]{1,0:T(8,128)(2,1)S(1)} collective-permute-done((bf16[256,1024]{1,0:T(8,128)(2,1)S(1)}, bf16[256,1024]{1,0:T(8,128)(2,1)S(1)}, u32[]{:S(2)}, u32[]{:S(2)}) %collective-permute-start.16) | collective-permute-done | bytes 524320 | tf_op jit(solution)/shard_map/ppermute | solution.py:979
  155.5 6.1 %backward_mlp.6 = (f32[256,1024]{1,0:T(8,128)S(1)}, bf16[256,1024]{1,0:T(8,128)(2,1)S(1)}, bf16[256,2048]{1,0:T(8,128)(2,1)S(1)}, bf16[256,1024]{1,0:T(8,128)(2,1)S(1)}, f32[24,1024]{1,0:T(8,128)S(1)}) custom-call(f32[256,1024]{1,0:T(8,128)S(1)} %get-tuple-element.195.refs_0_, f32[256,1024]{1,0:T(8,128)S(1)} %copy-done.40, ...), custom_call_target="tpu_custom_call" | custom-call | flops 120000004096 | bytes 1048576 | tf_op jit(solution)/shard_map/backward_mlp/pallas_call | solution.py:124
  163.3 2.0 collective-permute-start.19
  167.5 8.1 %backward_mlp.7 = (f32[256,1024]{1,0:T(8,128)S(1)}, bf16[256,1024]{1,0:T(8,128)(2,1)S(1)}, bf16[256,2048]{1,0:T(8,128)(2,1)S(1)}, bf16[256,1024]{1,0:T(8,128)(2,1)}, f32[24,1024]{1,0:T(8,128)S(1)}) custom-call(f32[256,1024]{1,0:T(8,128)S(1)} %get-tuple-element.241.refs_0_, f32[256,1024]{1,0:T(8,128)S(1)} %copy-done.38, ...), custom_call_target="tpu_custom_call" | custom-call | flops 120000004096 | bytes 1048576 | tf_op jit(solution)/shard_map/backward_mlp/pallas_call | solution.py:124
  179.5 7.2 %backward_attention.6 = (f32[256,1024]{1,0:T(8,128)S(1)}, bf16[256,1024]{1,0:T(8,128)(2,1)S(1)}, bf16[256,512]{1,0:T(8,128)(2,1)S(1)}, bf16[256,512]{1,0:T(8,128...) custom-call(f32[256,1024]{1,0:T(8,128)S(1)} %get-tuple-element.234.refs_0_, ...), custom_call_target="tpu_custom_call" | custom-call | flops 140000002048 | bytes 1048576 | tf_op jit(solution)/shard_map/backward_attention/pallas_call | solution.py:124
  192.3 5.9 %mlp_gradients.3 = (bf16[8,256,1024]{2,1,0:T(8,128)(2,1)}, bf16[8,256,1024]{2,1,0:T(8,128)(2,1)S(1)}) custom-call(s32[2]{0:T(128)S(1)} %copy-done.14, bf16[256,2048]{1,0:T(8,128)(2,1)S(1)} %copy-done.49, bf16[256,2048]{1,0:T(8,128)(2,1)S(1)} %copy-done.50, bf16[256,1024]{1,0:T(8,128)(2,1)S(1)} %get-tuple-element.260.refs_3_, ...), custom_call_target="tpu_custom_call" | custom-call | flops 179999997952 | bytes 1048576 | tf_op jit(solution)/shard_map/mlp_gradients/pallas_call | solution.py:124
  203.9 7.6 %backward_attention.7 = (f32[256,1024]{1,0:T(8,128)S(1)}, bf16[256,1024]{1,0:T(8,128)(2,1)S(1)}, bf16[256,512]{1,0:T(8,128)(2,1)S(1)}, bf16[256,512]{1,0:T(8,128...) custom-call(f32[256,1024]{1,0:T(8,128)S(1)} %get-tuple-element.251.refs_0_, ...), custom_call_target="tpu_custom_call" | custom-call | flops 140000002048 | bytes 1048576 | tf_op jit(solution)/shard_map/backward_attention/pallas_call | solution.py:124
  214.3 3.2 merge.6
  218.8 2.9 attention_gradients.3
  227.3 1.9 collective-permute-done.36.refs_0_
  229.4 2.7 collective-permute-done.42.refs_0_
  233.8 3.5 input_gradient.1
  237.3 3.2 collective-permute-done.44.refs_0_
  241.4 1.9 collective-permute-done.43.refs_0_
  245.7 6.3 %collective-permute-done.32.refs_4_ = bf16[256,1024]{1,0:T(8,128)(2,1)S(1)} collective-permute-done((bf16[256,1024]{1,0:T(8,128)(2,1)S(1)}, bf16[256,1024]{1,0:T(8,128)(2,1)S(1)}, u32[]{:S(2)}, u32[]{:S(2)}) %collective-permute-start.32) | collective-permute-done | bytes 524320 | tf_op jit(solution)/shard_map/ppermute | solution.py:625
  257.9 3.6 collective-permute-done.46.refs_0_
  265.0 2.0 collective-permute-done.54.refs_0_
  272.5 3.0 collective-permute-done.51.refs_0_
  288.3 4.3 collective-permute-done.56.refs_0_
  305.3 7.2 %collective-permute-done.55.refs_0_ = bf16[272,512]{1,0:T(8,128)(2,1)S(1)} collective-permute-done((bf16[272,512]{1,0:T(8,128)(2,1)S(1)}, bf16[272,512]{1,0:T(8,128)(2,1)S(1)}, u32[]{:S(2)}, u32[]{:S(2)}) %collective-permute-start.55) | collective-permute-done | bytes 278560 | tf_op jit(solution)/shard_map/ppermute | solution.py:979
  325.4 7.0 %collective-permute-done.72.refs_0_ = bf16[128,1024]{1,0:T(8,128)(2,1)S(1)} collective-permute-done((bf16[128,1024]{1,0:T(8,128)(2,1)S(1)}, bf16[128,1024]{1,0:T(8,128)(2,1)S(1)}, u32[]{:S(2)}, u32[]{:S(2)}) %collective-permute-start.72) | collective-permute-done | bytes 262176 | tf_op jit(solution)/shard_map/ppermute | solution.py:979
  332.4 2.8 collective-permute-done.71.refs_0_
  335.2 2.8 collective-permute-done.70.refs_0_
  338.0 3.0 collective-permute-done.65.refs_0_
  344.9 3.9 spread.10
  357.9 4.0 spread.11
  363.6 4.3 collective-permute-done.74.refs_0_
  370.7 2.8 collective-permute-done.83.refs_0_
  373.5 3.0 collective-permute-done.79.refs_0_
  379.7 2.9 spread.12
  384.5 4.4 %collective-permute-done.82.refs_0_ = bf16[272,512]{1,0:T(8,128)(2,1)S(1)} collective-permute-done((bf16[272,512]{1,0:T(8,128)(2,1)S(1)}, bf16[272,512]{1,0:T(8,128)(2,1)S(1)}, u32[]{:S(2)}, u32[]{:S(2)}) %collective-permute-start.82) | collective-permute-done | bytes 278560 | tf_op jit(solution)/shard_map/ppermute | solution.py:979
  391.5 2.9 spread.13
  399.8 2.4 collective-permute-done.90.refs_0_
  403.7 2.4 spread.14
  406.0 4.8 %collective-permute-done.94.refs_0_ = bf16[272,512]{1,0:T(8,128)(2,1)S(1)} collective-permute-done((bf16[272,512]{1,0:T(8,128)(2,1)S(1)}, bf16[272,512]{1,0:T(8,128)(2,1)S(1)}, u32[]{:S(2)}, u32[]{:S(2)}) %collective-permute-start.94) | collective-permute-done | bytes 278560 | tf_op jit(solution)/shard_map/ppermute | solution.py:979
  413.3 3.9 spread.15
  420.3 2.4 spread.16
  422.7 4.0 spread.17
  427.0 1.8 spread.18
  430.6 2.4 spread.19
  (417 shorter events, 148.1 us)
Async XLA Ops:
  19.3 14.9 %collective-permute-start.2 = (bf16[256,1024]{1,0:T(8,128)(2,1)S(1)}, bf16[256,1024]{1,0:T(8,128)(2,1)S(1)}, u32[]{:S(2)}, u32[]{:S(2)}) collective-permute-start(bf16[256,1024]{1,0:T(8,128)(2,1)S(1)} %get-tuple-element.172.refs_7_.refs_1_), channel_id=1, source_target_pairs={{0,1},{1,0},{2,3},{3,2},{4,5},{5,4},{6,7},{7,6},{8,9},{9,8},{10,11... | collective-permute-start | bytes 1572872 | tf_op jit(solution)/shard_map/ppermute | solution.py:625
  25.0 20.5 %collective-permute-start.5 = (bf16[256,1024]{1,0:T(8,128)(2,1)S(1)}, bf16[256,1024]{1,0:T(8,128)(2,1)S(1)}, u32[]{:S(2)}, u32[]{:S(2)}) collective-permute-start(bf16[256,1024]{1,0:T(8,128)(2,1)S(1)} %get-tuple-element.173.refs_6_.refs_1_), channel_id=1, source_target_pairs={{0,1},{1,0},{2,3},{3,2},{4,5},{5,4},{6,7},{7,6},{8,9},{9,8},{10,11... | collective-permute-start | bytes 1572872 | tf_op jit(solution)/shard_map/ppermute | solution.py:625
  40.6 16.1 %collective-permute-start.4 = (bf16[256,1024]{1,0:T(8,128)(2,1)S(1)}, bf16[256,1024]{1,0:T(8,128)(2,1)S(1)}, u32[]{:S(2)}, u32[]{:S(2)}) collective-permute-start(bf16[256,1024]{1,0:T(8,128)(2,1)S(1)} %get-tuple-element.175.refs_6_.refs_1_), channel_id=1, source_target_pairs={{0,1},{1,0},{2,3},{3,2},{4,5},{5,4},{6,7},{7,6},{8,9},{9,8},{10,11... | collective-permute-start | bytes 1572872 | tf_op jit(solution)/shard_map/ppermute | solution.py:625
  51.9 16.0 %collective-permute-start.7 = (bf16[256,1024]{1,0:T(8,128)(2,1)S(1)}, bf16[256,1024]{1,0:T(8,128)(2,1)S(1)}, u32[]{:S(2)}, u32[]{:S(2)}) collective-permute-start(bf16[256,1024]{1,0:T(8,128)(2,1)S(1)} %get-tuple-element.177.refs_9_.refs_1_), channel_id=1, source_target_pairs={{0,1},{1,0},{2,3},{3,2},{4,5},{5,4},{6,7},{7,6},{8,9},{9,8},{10,11... | collective-permute-start | bytes 1572872 | tf_op jit(solution)/shard_map/ppermute | solution.py:625
  62.1 17.1 %collective-permute-start.6 = (bf16[256,1024]{1,0:T(8,128)(2,1)S(1)}, bf16[256,1024]{1,0:T(8,128)(2,1)S(1)}, u32[]{:S(2)}, u32[]{:S(2)}) collective-permute-start(bf16[256,1024]{1,0:T(8,128)(2,1)S(1)} %get-tuple-element.179.refs_9_.refs_1_), channel_id=1, source_target_pairs={{0,1},{1,0},{2,3},{3,2},{4,5},{5,4},{6,7},{7,6},{8,9},{9,8},{10,11... | collective-permute-start | bytes 1572872 | tf_op jit(solution)/shard_map/ppermute | solution.py:625
  73.3 17.1 %collective-permute-start.9 = (bf16[256,1024]{1,0:T(8,128)(2,1)S(1)}, bf16[256,1024]{1,0:T(8,128)(2,1)S(1)}, u32[]{:S(2)}, u32[]{:S(2)}) collective-permute-start(bf16[256,1024]{1,0:T(8,128)(2,1)S(1)} %get-tuple-element.181.refs_6_.refs_1_), channel_id=1, source_target_pairs={{0,1},{1,0},{2,3},{3,2},{4,5},{5,4},{6,7},{7,6},{8,9},{9,8},{10,11... | collective-permute-start | bytes 1572872 | tf_op jit(solution)/shard_map/ppermute | solution.py:625
  104.7 13.5 %collective-permute-start.10 = (bf16[256,1024]{1,0:T(8,128)(2,1)S(1)}, bf16[256,1024]{1,0:T(8,128)(2,1)S(1)}, u32[]{:S(2)}, u32[]{:S(2)}) collective-permute-start(bf16[256,1024]{1,0:T(8,128)(2,1)S(1)} %get-tuple-element.191.refs_2_), channel_id=1, source_target_pairs={{0,1},{1,0},{2,3},{3,2},{4,5},{5,4},{6,7},{7,6},{8,9},{9,8},{10,11... | collective-permute-start | bytes 1572872 | tf_op jit(solution)/shard_map/ppermute | solution.py:625
  112.4 22.3 %collective-permute-start.15 = (bf16[256,1024]{1,0:T(8,128)(2,1)}, bf16[256,1024]{1,0:T(8,128)(2,1)}, u32[]{:S(2)}, u32[]{:S(2)}) collective-permute-start(bf16[256,1024]{1,0:T(8,128)(2,1)} %get-tuple-element.216.refs_2_), channel_id=1, source_target_pairs={{0,1},{1,0},{2,3},{3,2},{4,5},{5,4},{6,7},{7,6},{8,9},{9,8},{10,11... | collective-permute-start | bytes 1572872 | tf_op jit(solution)/shard_map/ppermute | solution.py:625
  130.7 15.5 %collective-permute-start.11 = (bf16[256,1024]{1,0:T(8,128)(2,1)S(1)}, bf16[256,1024]{1,0:T(8,128)(2,1)S(1)}, u32[]{:S(2)}, u32[]{:S(2)}) collective-permute-start(bf16[256,1024]{1,0:T(8,128)(2,1)S(1)} %get-tuple-element.197.refs_2_), channel_id=1, source_target_pairs={{0,1},{1,0},{2,3},{3,2},{4,5},{5,4},{6,7},{7,6},{8,9},{9,8},{10,11... | collective-permute-start | bytes 1572872 | tf_op jit(solution)/shard_map/ppermute | solution.py:625
  132.6 11.8 %collective-permute-start.14 = (bf16[256,1024]{1,0:T(8,128)(2,1)S(1)}, bf16[256,1024]{1,0:T(8,128)(2,1)S(1)}, u32[]{:S(2)}, u32[]{:S(2)}) collective-permute-start(bf16[256,1024]{1,0:T(8,128)(2,1)S(1)} %get-tuple-element.212.refs_12_), channel_id=1, source_target_pairs={{0,8},{10,2},{8,16},{18,10},{16,24},{26,18},{24,28},{30,26},{28,20... | collective-permute-start | bytes 1572872 | tf_op jit(solution)/shard_map/ppermute | solution.py:979
  143.1 24.3 %collective-permute-start.20 = (bf16[256,1024]{1,0:T(8,128)(2,1)}, bf16[256,1024]{1,0:T(8,128)(2,1)}, u32[]{:S(2)}, u32[]{:S(2)}) collective-permute-start(bf16[256,1024]{1,0:T(8,128)(2,1)} %get-tuple-element.243.refs_2_), channel_id=1, source_target_pairs={{0,1},{1,0},{2,3},{3,2},{4,5},{5,4},{6,7},{7,6},{8,9},{9,8},{10,11... | collective-permute-start | bytes 1572872 | tf_op jit(solution)/shard_map/ppermute | solution.py:625
  149.2 16.1 %collective-permute-start.21 = (bf16[8,256,512]{2,1,0:T(8,128)(2,1)S(1)}, bf16[8,256,512]{2,1,0:T(8,128)(2,1)S(1)}, u32[]{:S(2)}, u32[]{:S(2)}) collective-permute-start(bf16[8,256,512]{2,1,0:T(8,128)(2,1)S(1)} %get-tuple-element.246), channel_id=1, source_target_pairs={{0,2},{2,0},{4,6},{6,4},{8,10},{10,8},{12,14},{14,12},{16,18},{18,... | collective-permute-start | bytes 6291464 | tf_op jit(solution)/shard_map/ppermute | solution.py:942
  161.7 17.7 %collective-permute-start.17 = (bf16[256,1024]{1,0:T(8,128)(2,1)S(1)}, bf16[256,1024]{1,0:T(8,128)(2,1)S(1)}, u32[]{:S(2)}, u32[]{:S(2)}) collective-permute-start(bf16[256,1024]{1,0:T(8,128)(2,1)S(1)} %get-tuple-element.236.refs_2_), channel_id=1, source_target_pairs={{0,1},{1,0},{2,3},{3,2},{4,5},{5,4},{6,7},{7,6},{8,9},{9,8},{10,11... | collective-permute-start | bytes 1572872 | tf_op jit(solution)/shard_map/ppermute | solution.py:625
  163.3 12.4 %collective-permute-start.19 = (bf16[256,1024]{1,0:T(8,128)(2,1)S(1)}, bf16[256,1024]{1,0:T(8,128)(2,1)S(1)}, u32[]{:S(2)}, u32[]{:S(2)}) collective-permute-start(bf16[256,1024]{1,0:T(8,128)(2,1)S(1)} %add.41.refs_10_), channel_id=1, source_target_pairs={{0,8},{10,2},{8,16},{18,10},{16,24},{26,18},{24,28},{30,26},{28,20... | collective-permute-start | bytes 1572872 | tf_op jit(solution)/shard_map/ppermute | solution.py:979
  165.8 12.3 %collective-permute-start.22 = (bf16[256,512]{1,0:T(8,128)(2,1)S(1)}, bf16[256,512]{1,0:T(8,128)(2,1)S(1)}, u32[]{:S(2)}, u32[]{:S(2)}) collective-permute-start(bf16[256,512]{1,0:T(8,128)(2,1)S(1)} %get-tuple-element.247.refs_11_), channel_id=1, source_target_pairs={{0,8},{10,2},{8,16},{18,10},{16,24},{26,18},{24,28},{30,26},{28,20... | collective-permute-start | bytes 786440 | tf_op jit(solution)/shard_map/ppermute | solution.py:979
  175.8 14.4 %collective-permute-start.24 = (bf16[256,1024]{1,0:T(8,128)(2,1)S(1)}, bf16[256,1024]{1,0:T(8,128)(2,1)S(1)}, u32[]{:S(2)}, u32[]{:S(2)}) collective-permute-start(bf16[256,1024]{1,0:T(8,128)(2,1)S(1)} %add.42.refs_12_), channel_id=1, source_target_pairs={{0,8},{10,2},{8,16},{18,10},{16,24},{26,18},{24,28},{30,26},{28,20... | collective-permute-start | bytes 1572872 | tf_op jit(solution)/shard_map/ppermute | solution.py:979
  177.4 14.9 %collective-permute-start.23 = (bf16[256,1024]{1,0:T(8,128)(2,1)}, bf16[256,1024]{1,0:T(8,128)(2,1)}, u32[]{:S(2)}, u32[]{:S(2)}) collective-permute-start(bf16[256,1024]{1,0:T(8,128)(2,1)} %get-tuple-element.253.refs_2_), channel_id=1, source_target_pairs={{0,1},{1,0},{2,3},{3,2},{4,5},{5,4},{6,7},{7,6},{8,9},{9,8},{10,11... | collective-permute-start | bytes 1572872 | tf_op jit(solution)/shard_map/ppermute | solution.py:625
  186.7 31.3 %collective-permute-start.28 = (bf16[256,1024]{1,0:T(8,128)(2,1)}, bf16[256,1024]{1,0:T(8,128)(2,1)}, u32[]{:S(2)}, u32[]{:S(2)}) collective-permute-start(bf16[256,1024]{1,0:T(8,128)(2,1)} %get-tuple-element.276.refs_3_), channel_id=1, source_target_pairs={{0,1},{1,0},{2,3},{3,2},{4,5},{5,4},{6,7},{7,6},{8,9},{9,8},{10,11... | collective-permute-start | bytes 1572872 | tf_op jit(solution)/shard_map/ppermute | solution.py:625
  198.3 16.0 %collective-permute-start.31 = (bf16[8,256,1024]{2,1,0:T(8,128)(2,1)}, bf16[8,256,1024]{2,1,0:T(8,128)(2,1)}, u32[]{:S(2)}, u32[]{:S(2)}) collective-permute-start(bf16[8,256,1024]{2,1,0:T(8,128)(2,1)} %get-tuple-element.278), channel_id=1, source_target_pairs={{0,2},{2,0},{4,6},{6,4},{8,10},{10,8},{12,14},{14,12},{16,18},{18,... | collective-permute-start | bytes 12582920 | tf_op jit(solution)/shard_map/ppermute | solution.py:942
  199.6 12.0 %collective-permute-start.30 = (bf16[256,512]{1,0:T(8,128)(2,1)S(1)}, bf16[256,512]{1,0:T(8,128)(2,1)S(1)}, u32[]{:S(2)}, u32[]{:S(2)}) collective-permute-start(bf16[256,512]{1,0:T(8,128)(2,1)S(1)} %add.47.refs_13_), channel_id=1, source_target_pairs={{0,8},{10,2},{8,16},{18,10},{16,24},{26,18},{24,28},{30,26},{28,20... | collective-permute-start | bytes 786440 | tf_op jit(solution)/shard_map/ppermute | solution.py:979
  202.3 11.3 %collective-permute-start.29 = (bf16[256,1024]{1,0:T(8,128)(2,1)S(1)}, bf16[256,1024]{1,0:T(8,128)(2,1)S(1)}, u32[]{:S(2)}, u32[]{:S(2)}) collective-permute-start(bf16[256,1024]{1,0:T(8,128)(2,1)S(1)} %add.46.refs_12_), channel_id=1, source_target_pairs={{0,8},{10,2},{8,16},{18,10},{16,24},{26,18},{24,28},{30,26},{28,20... | collective-permute-start | bytes 1572872 | tf_op jit(solution)/shard_map/ppermute | solution.py:979
  212.8 20.5 %collective-permute-start.38 = (bf16[256,1024]{1,0:T(8,128)(2,1)S(1)}, bf16[256,1024]{1,0:T(8,128)(2,1)S(1)}, u32[]{:S(2)}, u32[]{:S(2)}) collective-permute-start(bf16[256,1024]{1,0:T(8,128)(2,1)S(1)} %get-tuple-element.289.refs_7_), channel_id=1, source_target_pairs={{0,1},{1,0},{2,3},{3,2},{4,5},{5,4},{6,7},{7,6},{8,9},{9,8},{10,11... | collective-permute-start | bytes 1572872 | tf_op jit(solution)/shard_map/ppermute | solution.py:625
  218.0 11.3 %collective-permute-start.36 = (bf16[128,1024]{1,0:T(8,128)(2,1)S(1)}, bf16[128,1024]{1,0:T(8,128)(2,1)S(1)}, u32[]{:S(2)}, u32[]{:S(2)}) collective-permute-start(bf16[128,1024]{1,0:T(8,128)(2,1)S(1)} %get-tuple-element.279.refs_16_), channel_id=1, source_target_pairs={{0,8},{10,2},{8,16},{18,10},{16,24},{26,18},{24,28},{30,26},{28,20... | collective-permute-start | bytes 786440 | tf_op jit(solution)/shard_map/ppermute | solution.py:979
  224.3 20.3 %collective-permute-start.41 = (bf16[256,1024]{1,0:T(8,128)(2,1)S(1)}, bf16[256,1024]{1,0:T(8,128)(2,1)S(1)}, u32[]{:S(2)}, u32[]{:S(2)}) collective-permute-start(bf16[256,1024]{1,0:T(8,128)(2,1)S(1)} %hold.40.refs_9_.refs_12_.refs_11_.refs_1_.refs_2_), channel_id=1, source_target_pairs={{0,8},{10,2},{8,16},{18,10},{16,24},{26,18},{24,28},{30,26},{28,20... | collective-permute-start | bytes 1572872 | tf_op jit(solution)/shard_map/ppermute | solution.py:979
  226.5 18.7 %collective-permute-start.33 = (bf16[256,1024]{1,0:T(8,128)(2,1)S(1)}, bf16[256,1024]{1,0:T(8,128)(2,1)S(1)}, u32[]{:S(2)}, u32[]{:S(2)}) collective-permute-start(bf16[256,1024]{1,0:T(8,128)(2,1)S(1)} %hold.39), channel_id=1, source_target_pairs={{0,1},{1,0},{2,3},{3,2},{4,5},{5,4},{6,7},{7,6},{8,9},{9,8},{10,11... | collective-permute-start | bytes 1572872 | tf_op jit(solution)/shard_map/ppermute | solution.py:625
  229.3 34.7 %collective-permute-start.39 = (bf16[8,256,512]{2,1,0:T(8,128)(2,1)S(1)}, bf16[8,256,512]{2,1,0:T(8,128)(2,1)S(1)}, u32[]{:S(2)}, u32[]{:S(2)}) collective-permute-start(bf16[8,256,512]{2,1,0:T(8,128)(2,1)S(1)} %get-tuple-element.293), channel_id=1, source_target_pairs={{0,2},{2,0},{4,6},{6,4},{8,10},{10,8},{12,14},{14,12},{16,18},{18,... | collective-permute-start | bytes 6291464 | tf_op jit(solution)/shard_map/ppermute | solution.py:942
  240.5 11.5 %collective-permute-start.32 = (bf16[256,1024]{1,0:T(8,128)(2,1)S(1)}, bf16[256,1024]{1,0:T(8,128)(2,1)S(1)}, u32[]{:S(2)}, u32[]{:S(2)}) collective-permute-start(bf16[256,1024]{1,0:T(8,128)(2,1)S(1)} %hold.38), channel_id=1, source_target_pairs={{0,1},{1,0},{2,3},{3,2},{4,5},{5,4},{6,7},{7,6},{8,9},{9,8},{10,11... | collective-permute-start | bytes 1572872 | tf_op jit(solution)/shard_map/ppermute | solution.py:625
  243.3 12.6 %collective-permute-start.47 = (bf16[256,512]{1,0:T(8,128)(2,1)S(1)}, bf16[256,512]{1,0:T(8,128)(2,1)S(1)}, u32[]{:S(2)}, u32[]{:S(2)}) collective-permute-start(bf16[256,512]{1,0:T(8,128)(2,1)S(1)} %add.53.refs_5_.refs_2_.refs_3_), channel_id=1, source_target_pairs={{0,8},{10,2},{8,16},{18,10},{16,24},{26,18},{24,28},{30,26},{28,20... | collective-permute-start | bytes 786440 | tf_op jit(solution)/shard_map/ppermute | solution.py:979
  244.6 11.5 %collective-permute-start.49 = (bf16[128,1024]{1,0:T(8,128)(2,1)S(1)}, bf16[128,1024]{1,0:T(8,128)(2,1)S(1)}, u32[]{:S(2)}, u32[]{:S(2)}) collective-permute-start(bf16[128,1024]{1,0:T(8,128)(2,1)S(1)} %add.55.refs_7_.refs_4_.refs_5_), channel_id=1, source_target_pairs={{0,8},{10,2},{8,16},{18,10},{16,24},{26,18},{24,28},{30,26},{28,20... | collective-permute-start | bytes 786440 | tf_op jit(solution)/shard_map/ppermute | solution.py:979
  245.2 12.1 %collective-permute-start.48 = (bf16[128,1024]{1,0:T(8,128)(2,1)S(1)}, bf16[128,1024]{1,0:T(8,128)(2,1)S(1)}, u32[]{:S(2)}, u32[]{:S(2)}) collective-permute-start(bf16[128,1024]{1,0:T(8,128)(2,1)S(1)} %add.54.refs_6_.refs_3_.refs_4_), channel_id=1, source_target_pairs={{0,8},{10,2},{8,16},{18,10},{16,24},{26,18},{24,28},{30,26},{28,20... | collective-permute-start | bytes 786440 | tf_op jit(solution)/shard_map/ppermute | solution.py:979
  256.1 15.2 %collective-permute-start.52 = (bf16[256,512]{1,0:T(8,128)(2,1)S(1)}, bf16[256,512]{1,0:T(8,128)(2,1)S(1)}, u32[]{:S(2)}, u32[]{:S(2)}) collective-permute-start(bf16[256,512]{1,0:T(8,128)(2,1)S(1)} %add.56.refs_3_.refs_2_.refs_0_), channel_id=1, source_target_pairs={{0,8},{10,2},{8,16},{18,10},{16,24},{26,18},{24,28},{30,26},{28,20... | collective-permute-start | bytes 786440 | tf_op jit(solution)/shard_map/ppermute | solution.py:979
  262.8 12.7 %collective-permute-start.51 = (bf16[256,1024]{1,0:T(8,128)(2,1)S(1)}, bf16[256,1024]{1,0:T(8,128)(2,1)S(1)}, u32[]{:S(2)}, u32[]{:S(2)}) collective-permute-start(bf16[256,1024]{1,0:T(8,128)(2,1)S(1)} %hold.42.refs_2_.refs_1_.refs_3_), channel_id=1, source_target_pairs={{0,8},{10,2},{8,16},{18,10},{16,24},{26,18},{24,28},{30,26},{28,20... | collective-permute-start | bytes 1572872 | tf_op jit(solution)/shard_map/ppermute | solution.py:979
  264.5 14.0 %collective-permute-start.45 = (bf16[272,512]{1,0:T(8,128)(2,1)S(1)}, bf16[272,512]{1,0:T(8,128)(2,1)S(1)}, u32[]{:S(2)}, u32[]{:S(2)}) collective-permute-start(bf16[272,512]{1,0:T(8,128)(2,1)S(1)} %get-tuple-element.297.refs_6_.refs_5_), channel_id=1, source_target_pairs={{0,8},{10,2},{8,16},{18,10},{16,24},{26,18},{24,28},{30,26},{28,20... | collective-permute-start | bytes 835592 | tf_op jit(solution)/shard_map/ppermute | solution.py:979
  267.2 14.2 %collective-permute-start.59 = (bf16[128,1024]{1,0:T(8,128)(2,1)S(1)}, bf16[128,1024]{1,0:T(8,128)(2,1)S(1)}, u32[]{:S(2)}, u32[]{:S(2)}) collective-permute-start(bf16[128,1024]{1,0:T(8,128)(2,1)S(1)} %add.61.refs_5_.refs_4_), channel_id=1, source_target_pairs={{0,8},{10,2},{8,16},{18,10},{16,24},{26,18},{24,28},{30,26},{28,20... | collective-permute-start | bytes 786440 | tf_op jit(solution)/shard_map/ppermute | solution.py:979
  270.0 14.2 %collective-permute-start.58 = (bf16[128,1024]{1,0:T(8,128)(2,1)S(1)}, bf16[128,1024]{1,0:T(8,128)(2,1)S(1)}, u32[]{:S(2)}, u32[]{:S(2)}) collective-permute-start(bf16[128,1024]{1,0:T(8,128)(2,1)S(1)} %add.60.refs_4_.refs_3_), channel_id=1, source_target_pairs={{0,8},{10,2},{8,16},{18,10},{16,24},{26,18},{24,28},{30,26},{28,20... | collective-permute-start | bytes 786440 | tf_op jit(solution)/shard_map/ppermute | solution.py:979
  271.3 15.6 %collective-permute-start.57 = (bf16[256,512]{1,0:T(8,128)(2,1)S(1)}, bf16[256,512]{1,0:T(8,128)(2,1)S(1)}, u32[]{:S(2)}, u32[]{:S(2)}) collective-permute-start(bf16[256,512]{1,0:T(8,128)(2,1)S(1)} %hold.44.refs_3_.refs_2_.refs_1_), channel_id=1, source_target_pairs={{0,8},{10,2},{8,16},{18,10},{16,24},{26,18},{24,28},{30,26},{28,20... | collective-permute-start | bytes 786440 | tf_op jit(solution)/shard_map/ppermute | solution.py:979
  275.6 17.0 %collective-permute-start.56 = (bf16[256,1024]{1,0:T(8,128)(2,1)S(1)}, bf16[256,1024]{1,0:T(8,128)(2,1)S(1)}, u32[]{:S(2)}, u32[]{:S(2)}) collective-permute-start(bf16[256,1024]{1,0:T(8,128)(2,1)S(1)} %hold.43.refs_2_.refs_1_.refs_4_), channel_id=1, source_target_pairs={{0,8},{10,2},{8,16},{18,10},{16,24},{26,18},{24,28},{30,26},{28,20... | collective-permute-start | bytes 1572872 | tf_op jit(solution)/shard_map/ppermute | solution.py:979
  278.6 17.0 %collective-permute-start.50 = (bf16[272,512]{1,0:T(8,128)(2,1)S(1)}, bf16[272,512]{1,0:T(8,128)(2,1)S(1)}, u32[]{:S(2)}, u32[]{:S(2)}) collective-permute-start(bf16[272,512]{1,0:T(8,128)(2,1)S(1)} %add.59.refs_6_.refs_5_), channel_id=1, source_target_pairs={{0,8},{10,2},{8,16},{18,10},{16,24},{26,18},{24,28},{30,26},{28,20... | collective-permute-start | bytes 835592 | tf_op jit(solution)/shard_map/ppermute | solution.py:979
  281.4 17.0 %collective-permute-start.64 = (bf16[128,1024]{1,0:T(8,128)(2,1)S(1)}, bf16[128,1024]{1,0:T(8,128)(2,1)S(1)}, u32[]{:S(2)}, u32[]{:S(2)}) collective-permute-start(bf16[128,1024]{1,0:T(8,128)(2,1)S(1)} %add.64.refs_5_.refs_4_), channel_id=1, source_target_pairs={{0,8},{10,2},{8,16},{18,10},{16,24},{26,18},{24,28},{30,26},{28,20... | collective-permute-start | bytes 786440 | tf_op jit(solution)/shard_map/ppermute | solution.py:979
  284.2 17.0 %collective-permute-start.63 = (bf16[128,1024]{1,0:T(8,128)(2,1)S(1)}, bf16[128,1024]{1,0:T(8,128)(2,1)S(1)}, u32[]{:S(2)}, u32[]{:S(2)}) collective-permute-start(bf16[128,1024]{1,0:T(8,128)(2,1)S(1)} %add.63.refs_4_.refs_3_), channel_id=1, source_target_pairs={{0,8},{10,2},{8,16},{18,10},{16,24},{26,18},{24,28},{30,26},{28,20... | collective-permute-start | bytes 786440 | tf_op jit(solution)/shard_map/ppermute | solution.py:979
  286.9 17.0 %collective-permute-start.62 = (bf16[256,512]{1,0:T(8,128)(2,1)S(1)}, bf16[256,512]{1,0:T(8,128)(2,1)S(1)}, u32[]{:S(2)}, u32[]{:S(2)}) collective-permute-start(bf16[256,512]{1,0:T(8,128)(2,1)S(1)} %hold.46.refs_3_.refs_2_), channel_id=1, source_target_pairs={{0,8},{10,2},{8,16},{18,10},{16,24},{26,18},{24,28},{30,26},{28,20... | collective-permute-start | bytes 786440 | tf_op jit(solution)/shard_map/ppermute | solution.py:979
  292.6 21.4 %collective-permute-start.61 = (bf16[256,1024]{1,0:T(8,128)(2,1)S(1)}, bf16[256,1024]{1,0:T(8,128)(2,1)S(1)}, u32[]{:S(2)}, u32[]{:S(2)}) collective-permute-start(bf16[256,1024]{1,0:T(8,128)(2,1)S(1)} %hold.45.refs_2_.refs_1_.refs_5_), channel_id=1, source_target_pairs={{0,8},{10,2},{8,16},{18,10},{16,24},{26,18},{24,28},{30,26},{28,20... | collective-permute-start | bytes 1572872 | tf_op jit(solution)/shard_map/ppermute | solution.py:979
  295.6 17.0 %collective-permute-start.55 = (bf16[272,512]{1,0:T(8,128)(2,1)S(1)}, bf16[272,512]{1,0:T(8,128)(2,1)S(1)}, u32[]{:S(2)}, u32[]{:S(2)}) collective-permute-start(bf16[272,512]{1,0:T(8,128)(2,1)S(1)} %add.62.refs_6_.refs_5_), channel_id=1, source_target_pairs={{0,8},{10,2},{8,16},{18,10},{16,24},{26,18},{24,28},{30,26},{28,20... | collective-permute-start | bytes 835592 | tf_op jit(solution)/shard_map/ppermute | solution.py:979
  298.4 17.0 %collective-permute-start.68 = (bf16[128,1024]{1,0:T(8,128)(2,1)S(1)}, bf16[128,1024]{1,0:T(8,128)(2,1)S(1)}, u32[]{:S(2)}, u32[]{:S(2)}) collective-permute-start(bf16[128,1024]{1,0:T(8,128)(2,1)S(1)} %add.67.refs_5_.refs_4_), channel_id=1, source_target_pairs={{0,8},{10,2},{8,16},{18,10},{16,24},{26,18},{24,28},{30,26},{28,20... | collective-permute-start | bytes 786440 | tf_op jit(solution)/shard_map/ppermute | solution.py:979
  301.2 17.0 %collective-permute-start.67 = (bf16[128,1024]{1,0:T(8,128)(2,1)S(1)}, bf16[128,1024]{1,0:T(8,128)(2,1)S(1)}, u32[]{:S(2)}, u32[]{:S(2)}) collective-permute-start(bf16[128,1024]{1,0:T(8,128)(2,1)S(1)} %add.66.refs_4_.refs_3_), channel_id=1, source_target_pairs={{0,8},{10,2},{8,16},{18,10},{16,24},{26,18},{24,28},{30,26},{28,20... | collective-permute-start | bytes 786440 | tf_op jit(solution)/shard_map/ppermute | solution.py:979
  304.0 17.0 %collective-permute-start.66 = (bf16[256,512]{1,0:T(8,128)(2,1)S(1)}, bf16[256,512]{1,0:T(8,128)(2,1)S(1)}, u32[]{:S(2)}, u32[]{:S(2)}) collective-permute-start(bf16[256,512]{1,0:T(8,128)(2,1)S(1)} %hold.48.refs_3_.refs_2_), channel_id=1, source_target_pairs={{0,8},{10,2},{8,16},{18,10},{16,24},{26,18},{24,28},{30,26},{28,20... | collective-permute-start | bytes 786440 | tf_op jit(solution)/shard_map/ppermute | solution.py:979
  312.6 11.3 %collective-permute-start.60 = (bf16[272,512]{1,0:T(8,128)(2,1)S(1)}, bf16[272,512]{1,0:T(8,128)(2,1)S(1)}, u32[]{:S(2)}, u32[]{:S(2)}) collective-permute-start(bf16[272,512]{1,0:T(8,128)(2,1)S(1)} %add.65.refs_6_.refs_5_), channel_id=1, source_target_pairs={{0,8},{10,2},{8,16},{18,10},{16,24},{26,18},{24,28},{30,26},{28,20... | collective-permute-start | bytes 835592 | tf_op jit(solution)/shard_map/ppermute | solution.py:979
  314.0 27.1 %collective-permute-start.73 = (bf16[256,1024]{1,0:T(8,128)(2,1)S(1)}, bf16[256,1024]{1,0:T(8,128)(2,1)S(1)}, u32[]{:S(2)}, u32[]{:S(2)}) collective-permute-start(bf16[256,1024]{1,0:T(8,128)(2,1)S(1)} %hold.47.refs_2_.refs_1_.refs_6_), channel_id=1, source_target_pairs={{0,8},{10,2},{8,16},{18,10},{16,24},{26,18},{24,28},{30,26},{28,20... | collective-permute-start | bytes 1572872 | tf_op jit(solution)/shard_map/ppermute | solution.py:979
  315.4 17.0 %collective-permute-start.72 = (bf16[128,1024]{1,0:T(8,128)(2,1)S(1)}, bf16[128,1024]{1,0:T(8,128)(2,1)S(1)}, u32[]{:S(2)}, u32[]{:S(2)}) collective-permute-start(bf16[128,1024]{1,0:T(8,128)(2,1)S(1)} %add.70.refs_4_.refs_3_.refs_8_), channel_id=1, source_target_pairs={{0,8},{10,2},{8,16},{18,10},{16,24},{26,18},{24,28},{30,26},{28,20... | collective-permute-start | bytes 786440 | tf_op jit(solution)/shard_map/ppermute | solution.py:979
  318.2 17.0 %collective-permute-start.71 = (bf16[128,1024]{1,0:T(8,128)(2,1)S(1)}, bf16[128,1024]{1,0:T(8,128)(2,1)S(1)}, u32[]{:S(2)}, u32[]{:S(2)}) collective-permute-start(bf16[128,1024]{1,0:T(8,128)(2,1)S(1)} %add.69.refs_3_.refs_2_.refs_0_), channel_id=1, source_target_pairs={{0,8},{10,2},{8,16},{18,10},{16,24},{26,18},{24,28},{30,26},{28,20... | collective-permute-start | bytes 786440 | tf_op jit(solution)/shard_map/ppermute | solution.py:979
  321.0 17.0 %collective-permute-start.70 = (bf16[256,512]{1,0:T(8,128)(2,1)S(1)}, bf16[256,512]{1,0:T(8,128)(2,1)S(1)}, u32[]{:S(2)}, u32[]{:S(2)}) collective-permute-start(bf16[256,512]{1,0:T(8,128)(2,1)S(1)} %hold.49.refs_2_.refs_1_.refs_4_), channel_id=1, source_target_pairs={{0,8},{10,2},{8,16},{18,10},{16,24},{26,18},{24,28},{30,26},{28,20... | collective-permute-start | bytes 786440 | tf_op jit(solution)/shard_map/ppermute | solution.py:979
  324.0 17.0 %collective-permute-start.65 = (bf16[272,512]{1,0:T(8,128)(2,1)S(1)}, bf16[272,512]{1,0:T(8,128)(2,1)S(1)}, u32[]{:S(2)}, u32[]{:S(2)}) collective-permute-start(bf16[272,512]{1,0:T(8,128)(2,1)S(1)} %add.68.refs_5_.refs_4_), channel_id=1, source_target_pairs={{0,8},{10,2},{8,16},{18,10},{16,24},{26,18},{24,28},{30,26},{28,20... | collective-permute-start | bytes 835592 | tf_op jit(solution)/shard_map/ppermute | solution.py:979
  341.4 16.5 %collective-permute-start.78 = (bf16[8,256,1024]{2,1,0:T(8,128)(2,1)S(1)}, bf16[8,256,1024]{2,1,0:T(8,128)(2,1)S(1)}, u32[]{:S(2)}, u32[]{:S(2)}) collective-permute-start(bf16[8,256,1024]{2,1,0:T(8,128)(2,1)S(1)} %pack.5.refs_1_), channel_id=1, source_target_pairs={{0,2},{2,0},{4,6},{6,4},{8,10},{10,8},{12,14},{14,12},{16,18},{18,... | collective-permute-start | bytes 12582920 | tf_op jit(solution)/shard_map/ppermute | solution.py:965
  344.4 12.1 %collective-permute-start.69 = (bf16[272,512]{1,0:T(8,128)(2,1)S(1)}, bf16[272,512]{1,0:T(8,128)(2,1)S(1)}, u32[]{:S(2)}, u32[]{:S(2)}) collective-permute-start(bf16[272,512]{1,0:T(8,128)(2,1)S(1)} %add.71.refs_11_.refs_5_.refs_4_), channel_id=1, source_target_pairs={{0,8},{10,2},{8,16},{18,10},{16,24},{26,18},{24,28},{30,26},{28,20... | collective-permute-start | bytes 835592 | tf_op jit(solution)/shard_map/ppermute | solution.py:979
  348.9 13.0 %collective-permute-start.81 = (bf16[128,1024]{1,0:T(8,128)(2,1)S(1)}, bf16[128,1024]{1,0:T(8,128)(2,1)S(1)}, u32[]{:S(2)}, u32[]{:S(2)}) collective-permute-start(bf16[128,1024]{1,0:T(8,128)(2,1)S(1)} %hold.55.refs_6_.refs_4_.refs_3_.refs_10_), channel_id=1, source_target_pairs={{0,8},{10,2},{8,16},{18,10},{16,24},{26,18},{24,28},{30,26},{28,20... | collective-permute-start | bytes 786440 | tf_op jit(solution)/shard_map/ppermute | solution.py:979
  350.7 12.4 %collective-permute-start.80 = (bf16[128,1024]{1,0:T(8,128)(2,1)S(1)}, bf16[128,1024]{1,0:T(8,128)(2,1)S(1)}, u32[]{:S(2)}, u32[]{:S(2)}) collective-permute-start(bf16[128,1024]{1,0:T(8,128)(2,1)S(1)} %hold.54.refs_5_.refs_3_.refs_2_), channel_id=1, source_target_pairs={{0,8},{10,2},{8,16},{18,10},{16,24},{26,18},{24,28},{30,26},{28,20... | collective-permute-start | bytes 786440 | tf_op jit(solution)/shard_map/ppermute | solution.py:979
  353.5 23.0 %collective-permute-start.85 = (bf16[256,512]{1,0:T(8,128)(2,1)S(1)}, bf16[256,512]{1,0:T(8,128)(2,1)S(1)}, u32[]{:S(2)}, u32[]{:S(2)}) collective-permute-start(bf16[256,512]{1,0:T(8,128)(2,1)S(1)} %hold.53.refs_4_.refs_2_.refs_1_.refs_6_), channel_id=1, source_target_pairs={{0,8},{10,2},{8,16},{18,10},{16,24},{26,18},{24,28},{30,26},{28,20... | collective-permute-start | bytes 786440 | tf_op jit(solution)/shard_map/ppermute | solution.py:979
  356.5 11.3 %collective-permute-start.74 = (bf16[272,512]{1,0:T(8,128)(2,1)S(1)}, bf16[272,512]{1,0:T(8,128)(2,1)S(1)}, u32[]{:S(2)}, u32[]{:S(2)}) collective-permute-start(bf16[272,512]{1,0:T(8,128)(2,1)S(1)} %add.72.refs_7_.refs_5_.refs_4_), channel_id=1, source_target_pairs={{0,8},{10,2},{8,16},{18,10},{16,24},{26,18},{24,28},{30,26},{28,20... | collective-permute-start | bytes 835592 | tf_op jit(solution)/shard_map/ppermute | solution.py:979
  376.7 14.9 %collective-permute-start.89 = (bf16[8,256,512]{2,1,0:T(8,128)(2,1)S(1)}, bf16[8,256,512]{2,1,0:T(8,128)(2,1)S(1)}, u32[]{:S(2)}, u32[]{:S(2)}) collective-permute-start(bf16[8,256,512]{2,1,0:T(8,128)(2,1)S(1)} %pack.6.refs_1_), channel_id=1, source_target_pairs={{0,2},{2,0},{4,6},{6,4},{8,10},{10,8},{12,14},{14,12},{16,18},{18,... | collective-permute-start | bytes 6291464 | tf_op jit(solution)/shard_map/ppermute | solution.py:965
  378.1 12.2 %collective-permute-start.87 = (bf16[128,1024]{1,0:T(8,128)(2,1)S(1)}, bf16[128,1024]{1,0:T(8,128)(2,1)S(1)}, u32[]{:S(2)}, u32[]{:S(2)}) collective-permute-start(bf16[128,1024]{1,0:T(8,128)(2,1)S(1)} %hold.59.refs_8_.refs_1_.refs_4_), channel_id=1, source_target_pairs={{0,8},{10,2},{8,16},{18,10},{16,24},{26,18},{24,28},{30,26},{28,20... | collective-permute-start | bytes 786440 | tf_op jit(solution)/shard_map/ppermute | solution.py:979
  383.2 13.8 %collective-permute-start.92 = (bf16[128,1024]{1,0:T(8,128)(2,1)S(1)}, bf16[128,1024]{1,0:T(8,128)(2,1)S(1)}, u32[]{:S(2)}, u32[]{:S(2)}) collective-permute-start(bf16[128,1024]{1,0:T(8,128)(2,1)S(1)} %hold.63.refs_5_.refs_2_.refs_13_), channel_id=1, source_target_pairs={{0,8},{10,2},{8,16},{18,10},{16,24},{26,18},{24,28},{30,26},{28,20... | collective-permute-start | bytes 786440 | tf_op jit(solution)/shard_map/ppermute | solution.py:979
  397.0 13.9 %collective-permute-start.97 = (bf16[128,1024]{1,0:T(8,128)(2,1)S(1)}, bf16[128,1024]{1,0:T(8,128)(2,1)S(1)}, u32[]{:S(2)}, u32[]{:S(2)}) collective-permute-start(bf16[128,1024]{1,0:T(8,128)(2,1)S(1)} %hold.66.refs_2_.refs_14_), channel_id=1, source_target_pairs={{0,8},{10,2},{8,16},{18,10},{16,24},{26,18},{24,28},{30,26},{28,20... | collective-permute-start | bytes 786440 | tf_op jit(solution)/shard_map/ppermute | solution.py:979
  398.4 12.4 %collective-permute-start.96 = (bf16[128,1024]{1,0:T(8,128)(2,1)S(1)}, bf16[128,1024]{1,0:T(8,128)(2,1)S(1)}, u32[]{:S(2)}, u32[]{:S(2)}) collective-permute-start(bf16[128,1024]{1,0:T(8,128)(2,1)S(1)} %hold.65.refs_1_.refs_6_), channel_id=1, source_target_pairs={{0,8},{10,2},{8,16},{18,10},{16,24},{26,18},{24,28},{30,26},{28,20... | collective-permute-start | bytes 786440 | tf_op jit(solution)/shard_map/ppermute | solution.py:979
  411.1 11.6 %collective-permute-start.99 = (bf16[8,256,1024]{2,1,0:T(8,128)(2,1)S(1)}, bf16[8,256,1024]{2,1,0:T(8,128)(2,1)S(1)}, u32[]{:S(2)}, u32[]{:S(2)}) collective-permute-start(bf16[8,256,1024]{2,1,0:T(8,128)(2,1)S(1)} %pack.8.refs_1_), channel_id=1, source_target_pairs={{0,2},{2,0},{4,6},{6,4},{8,10},{10,8},{12,14},{14,12},{16,18},{18,... | collective-permute-start | bytes 12582920 | tf_op jit(solution)/shard_map/ppermute | solution.py:965
  (115 other events, 1052.7 us)

commit v5 on v4

--- a/solution.py
+++ b/solution.py
@@ -1049,12 +1049,17 @@
         vectors = [norm_gain.reshape(2 * layers, width), norm_bias.reshape(2 * layers, width)]
         vectors += [time_weight, jnp.zeros((layers, width), f32)]
         vectors = jnp.concatenate(vectors)
-        if paired:
-            index = jnp.concatenate([time_index, links.swap_tensor(time_index)])
-        else:
-            index = links.gather_tensor(time_index)
-        onehot = (index[:, None] == jnp.arange(time_table.shape[0], dtype=jnp.int32)[None, :]).astype(f32)
-        tau = jnp.dot(onehot, time_table, precision=lax.Precision.HIGHEST)
+        def times(after):
+            if paired:
+                held = hold(time_index.astype(f32)[None, :], after)
+                index = jnp.concatenate([held, links.swap_tensor(held)], axis=1)[0].astype(jnp.int32)
+            else:
+                index = links.gather_tensor(time_index)
+            rows_of = jnp.arange(time_table.shape[0], dtype=jnp.int32)
+            onehot = (index[:, None] == rows_of[None, :]).astype(f32)
+            return jnp.dot(onehot, time_table, precision=lax.Precision.HIGHEST)
+
+        tau = None
         latest = []
         saved = [[None] * parts for _ in range(layers)]
         after = [[None] * parts for _ in range(layers)]
@@ -1066,6 +1071,8 @@
                 latest = [part]
                 if l > 0:
                     after[l - 1][m] = out.pop()
+                if tau is None and m == parts - 1:
+                    tau = times(latest)
                 saved[l][m] = out
                 heads[m] = (x_near, *links.start_sum(part))
             for m in range(parts):

time: 439 us -> 447 us (1.018)
  starting transfers between devices: 103 us -> 109 us
    ppermute x21, starting transfers between devices: 17.9 us -> 24.7 us  [swap_tensor(): return lax.ppermute(v, 'tensor', [(0, 1), (1, 0)])]
    pallas_call x113 -> x114, Pallas kernels: 172 us -> 172 us  [call(): pl.pallas_call(run, out_shape=[(pltpu.HBM if away else pltpu.VMEM)(s, d)...]
  transfers between devices with their start and end apart: 101 -> 101, of which waited for: 57 -> 55; matrix products, arithmetic and copies ran while one was open for 1% -> 1% of each run, Pallas kernels for 39% -> 38%
where the time goes in v5:
time: 447 us; the launch traced here: 441 us
  Pallas kernels  172 us (38%)
  waiting for transfers between devices  150 us (34%)
  starting transfers between devices  109 us (24%)
  local copies, waits for them, and re-layouts  5.42 us (1%)
    pallas_call x114, Pallas kernels, call(): pl.pallas_call(run, out_shape=[(pltpu.HBM if away else pltpu.VMEM)(s, d)...  172 us
    ppermute x70, waiting for transfers between devices, step(): self.raw = [lax.ppermute(v, 'dp', self.links.ring_pairs) for v in now]  99.5 us
    ppermute x70, starting transfers between devices, step(): self.raw = [lax.ppermute(v, 'dp', self.links.ring_pairs) for v in now]  82.8 us
    ppermute x21, waiting for transfers between devices, swap_tensor(): return lax.ppermute(v, 'tensor', [(0, 1), (1, 0)])  49.9 us
    ppermute x21, starting transfers between devices, swap_tensor(): return lax.ppermute(v, 'tensor', [(0, 1), (1, 0)])  24.7 us
  transfers between devices with their start and end apart: 101, of which 55 were waited for; matrix products, arithmetic and copies ran while one was open for 1% of the time, Pallas kernels for 38%

profile of v5, /device:TPU:0, one launch (start us, length us, event | category | flops | bytes accessed | tf_op | source)
XLA Modules:
  0.0 441.1 jit_solution(13148258333893783023)
XLA Ops:
  1.8 3.0 collective-permute-start
  9.0 2.2 collective-permute-done.refs_1_
  11.2 1.8 collective-permute-start.1
  13.0 5.1 %forward_attention.4 = (f32[256,1024]{1,0:T(8,128)S(1)}, bf16[256,1024]{1,0:T(8,128)(2,1)S(1)}, f32[256,1024]{1,0:T(8,128)}, bf16[256,1024]{1,0:T(8,128)(2,1)}, ...) custom-call(bf16[256,1024]{1,0:T(8,128)(2,1)} %refs_0_.5, ...), custom_call_target="tpu_custom_call" | custom-call | flops 80000000000 | bytes 1048576 | tf_op jit(solution)/shard_map/forward_attention/pallas_call | solution.py:124
  18.7 5.1 %forward_attention.5 = (f32[256,1024]{1,0:T(8,128)S(1)}, bf16[256,1024]{1,0:T(8,128)(2,1)S(1)}, f32[256,1024]{1,0:T(8,128)}, bf16[256,1024]{1,0:T(8,128)(2,1)}, ...) custom-call(bf16[256,1024]{1,0:T(8,128)(2,1)} %refs_0_.5, ...), custom_call_target="tpu_custom_call" | custom-call | flops 80000000000 | bytes 1048576 | tf_op jit(solution)/shard_map/forward_attention/pallas_call | solution.py:124
  25.9 16.0 %collective-permute-done.2 = f32[1,2]{1,0:T(1,128)S(1)} collective-permute-done((f32[1,2]{1,0:T(1,128)S(1)}, f32[1,2]{1,0:T(1,128)S(1)}, u32[]{:S(2)}, u32[]{:S(2)}) %collective-permute-start.2) | collective-permute-done | bytes 40 | tf_op jit(solution)/shard_map/ppermute | solution.py:625
  42.5 6.4 %forward_mlp.4 = (f32[256,1024]{1,0:T(8,128)S(1)}, bf16[256,1024]{1,0:T(8,128)(2,1)S(1)}, f32[256,1024]{1,0:T(8,128)}, bf16[256,1024]{1,0:T(8,128)(2,1)}, bf16[2...) custom-call(f32[256,1024]{1,0:T(8,128)S(1)} %get-tuple-element.173.refs_0_, ...), custom_call_target="tpu_custom_call" | custom-call | flops 120000004096 | bytes 1048576 | tf_op jit(solution)/shard_map/forward_mlp/pallas_call | solution.py:124
  49.7 6.4 %forward_mlp.5 = (f32[256,1024]{1,0:T(8,128)S(1)}, bf16[256,1024]{1,0:T(8,128)(2,1)S(1)}, f32[256,1024]{1,0:T(8,128)}, bf16[256,1024]{1,0:T(8,128)(2,1)}, bf16[2...) custom-call(f32[256,1024]{1,0:T(8,128)S(1)} %get-tuple-element.176.refs_0_, ...), custom_call_target="tpu_custom_call" | custom-call | flops 120000004096 | bytes 1048576 | tf_op jit(solution)/shard_map/forward_mlp/pallas_call | solution.py:124
  57.5 6.3 %collective-permute-done.4.refs_2_ = bf16[256,1024]{1,0:T(8,128)(2,1)S(1)} collective-permute-done((bf16[256,1024]{1,0:T(8,128)(2,1)S(1)}, bf16[256,1024]{1,0:T(8,128)(2,1)S(1)}, u32[]{:S(2)}, u32[]{:S(2)}) %collective-permute-start.4) | collective-permute-done | bytes 524320 | tf_op jit(solution)/shard_map/ppermute | solution.py:625
  63.8 5.4 %forward_attention.6 = (f32[256,1024]{1,0:T(8,128)S(1)}, bf16[256,1024]{1,0:T(8,128)(2,1)S(1)}, f32[256,1024]{1,0:T(8,128)}, bf16[256,1024]{1,0:T(8,128)(2,1)}, ...) custom-call(f32[256,1024]{1,0:T(8,128)S(1)} %get-tuple-element.174.r, ...), custom_call_target="tpu_custom_call" | custom-call | flops 80000000000 | bytes 1048576 | tf_op jit(solution)/shard_map/forward_attention/pallas_call | solution.py:124
  70.0 5.1 %collective-permute-done.7.refs_2_ = bf16[256,1024]{1,0:T(8,128)(2,1)S(1)} collective-permute-done((bf16[256,1024]{1,0:T(8,128)(2,1)S(1)}, bf16[256,1024]{1,0:T(8,128)(2,1)S(1)}, u32[]{:S(2)}, u32[]{:S(2)}) %collective-permute-start.7) | collective-permute-done | bytes 524320 | tf_op jit(solution)/shard_map/ppermute | solution.py:625
  75.0 5.3 %forward_attention.7 = (f32[256,1024]{1,0:T(8,128)S(1)}, bf16[256,1024]{1,0:T(8,128)(2,1)S(1)}, f32[256,1024]{1,0:T(8,128)}, bf16[256,1024]{1,0:T(8,128)(2,1)}, ...) custom-call(f32[256,1024]{1,0:T(8,128)S(1)} %get-tuple-element.180.r, ...), custom_call_target="tpu_custom_call" | custom-call | flops 80000000000 | bytes 1048576 | tf_op jit(solution)/shard_map/forward_attention/pallas_call | solution.py:124
  81.2 5.1 %collective-permute-done.6.refs_2_ = bf16[256,1024]{1,0:T(8,128)(2,1)S(1)} collective-permute-done((bf16[256,1024]{1,0:T(8,128)(2,1)S(1)}, bf16[256,1024]{1,0:T(8,128)(2,1)S(1)}, u32[]{:S(2)}, u32[]{:S(2)}) %collective-permute-start.6) | collective-permute-done | bytes 524320 | tf_op jit(solution)/shard_map/ppermute | solution.py:625
  86.3 6.4 %forward_mlp.6 = (f32[256,1024]{1,0:T(8,128)S(1)}, bf16[256,1024]{1,0:T(8,128)(2,1)S(1)}, f32[256,1024]{1,0:T(8,128)}, bf16[256,1024]{1,0:T(8,128)(2,1)}, bf16[2...) custom-call(f32[256,1024]{1,0:T(8,128)S(1)} %get-tuple-element.178.refs_0_, ...), custom_call_target="tpu_custom_call" | custom-call | flops 120000004096 | bytes 1048576 | tf_op jit(solution)/shard_map/forward_mlp/pallas_call | solution.py:124
  93.5 3.4 collective-permute-done.9.refs_2_
  97.0 6.4 %forward_mlp.7 = (f32[256,1024]{1,0:T(8,128)S(1)}, bf16[256,1024]{1,0:T(8,128)(2,1)S(1)}, f32[256,1024]{1,0:T(8,128)}, bf16[256,1024]{1,0:T(8,128)(2,1)}, bf16[2...) custom-call(f32[256,1024]{1,0:T(8,128)S(1)} %get-tuple-element.187.refs_0_, ...), custom_call_target="tpu_custom_call" | custom-call | flops 120000004096 | bytes 1048576 | tf_op jit(solution)/shard_map/forward_mlp/pallas_call | solution.py:124
  105.1 6.1 %backward_mlp.4 = (f32[256,1024]{1,0:T(8,128)S(1)}, bf16[256,1024]{1,0:T(8,128)(2,1)S(1)}, bf16[256,2048]{1,0:T(8,128)(2,1)S(1)}, bf16[256,1024]{1,0:T(8,128)(2,1)S(1)}, f32[24,1024]{1,0:T(8,128)}) custom-call(bf16[256,1024]{1,0:T(8,128)(2,1)S(1)} %copy-done.6, bf16[128,1024]{1,0:T(8,128)(2,1)S(1)} %collective-permute-done.8.refs_1_.refs_2_.refs_6_, ...), custom_call_target="tpu_custom_call" | custom-call | flops 120000004096 | bytes 1048576 | tf_op jit(solution)/shard_map/backward_mlp/pallas_call | solution.py:124
  112.6 7.0 %backward_mlp.5 = (f32[256,1024]{1,0:T(8,128)S(1)}, bf16[256,1024]{1,0:T(8,128)(2,1)S(1)}, bf16[256,2048]{1,0:T(8,128)(2,1)S(1)}, bf16[256,1024]{1,0:T(8,128)(2,1)}, f32[24,1024]{1,0:T(8,128)}) custom-call(bf16[256,1024]{1,0:T(8,128)(2,1)S(1)} %copy-done.6, bf16[128,1024]{1,0:T(8,128)(2,1)S(1)} %collective-permute-done.12.refs_1_.refs_11_, ...), custom_call_target="tpu_custom_call" | custom-call | flops 120000004096 | bytes 1048576 | tf_op jit(solution)/shard_map/backward_mlp/pallas_call | solution.py:124
  120.5 5.1 %collective-permute-done.10.refs_3_.refs_9_ = bf16[256,1024]{1,0:T(8,128)(2,1)S(1)} collective-permute-done((bf16[256,1024]{1,0:T(8,128)(2,1)S(1)}, bf16[256,1024]{1,0:T(8,128)(2,1)S(1)}, u32[]{:S(2)}, u32[]{:S(2)}) %collective-permute-start.10) | collective-permute-done | bytes 524320 | tf_op jit(solution)/shard_map/ppermute | solution.py:625
  125.7 5.8 %mlp_gradients.2 = (bf16[8,256,1024]{2,1,0:T(8,128)(2,1)}, bf16[8,256,1024]{2,1,0:T(8,128)(2,1)S(1)}) custom-call(s32[2]{0:T(128)S(1)} %pad_add_fusion.refs_0_, bf16[256,2048]{1,0:T(8,128)(2,1)S(1)} %copy-done.53, bf16[256,2048]{1,0:T(8,128)(2,1)S(1)} %copy-done.54, bf16[256,1024]{1,0:T(8,128)(2,1)S(1)} %get-tuple-element.202.refs_3_, ...), custom_call_target="tpu_custom_call" | custom-call | flops 179999997952 | bytes 1048576 | tf_op jit(solution)/shard_map/mlp_gradients/pallas_call | solution.py:124
  131.6 6.4 %backward_attention.4 = (f32[256,1024]{1,0:T(8,128)S(1)}, bf16[256,1024]{1,0:T(8,128)(2,1)S(1)}, bf16[256,512]{1,0:T(8,128)(2,1)S(1)}, bf16[256,512]{1,0:T(8,128...) custom-call(f32[256,1024]{1,0:T(8,128)S(1)} %get-tuple-element.189.refs_0_, ...), custom_call_target="tpu_custom_call" | custom-call | flops 140000002048 | bytes 1048576 | tf_op jit(solution)/shard_map/backward_attention/pallas_call | solution.py:124
  138.0 1.9 collective-permute-start.11
  142.6 8.4 %backward_attention.5 = (f32[256,1024]{1,0:T(8,128)S(1)}, bf16[256,1024]{1,0:T(8,128)(2,1)S(1)}, bf16[256,512]{1,0:T(8,128)(2,1)S(1)}, bf16[256,512]{1,0:T(8,128...) custom-call(f32[256,1024]{1,0:T(8,128)S(1)} %get-tuple-element.214.refs_0_, ...), custom_call_target="tpu_custom_call" | custom-call | flops 140000002048 | bytes 1048576 | tf_op jit(solution)/shard_map/backward_attention/pallas_call | solution.py:124
  153.8 2.9 attention_gradients.2
  156.9 4.5 %collective-permute-done.16.refs_0_ = bf16[256,1024]{1,0:T(8,128)(2,1)S(1)} collective-permute-done((bf16[256,1024]{1,0:T(8,128)(2,1)S(1)}, bf16[256,1024]{1,0:T(8,128)(2,1)S(1)}, u32[]{:S(2)}, u32[]{:S(2)}) %collective-permute-start.16) | collective-permute-done | bytes 524320 | tf_op jit(solution)/shard_map/ppermute | solution.py:979
  163.2 6.1 %backward_mlp.6 = (f32[256,1024]{1,0:T(8,128)S(1)}, bf16[256,1024]{1,0:T(8,128)(2,1)S(1)}, bf16[256,2048]{1,0:T(8,128)(2,1)S(1)}, bf16[256,1024]{1,0:T(8,128)(2,1)S(1)}, f32[24,1024]{1,0:T(8,128)S(1)}) custom-call(f32[256,1024]{1,0:T(8,128)S(1)} %get-tuple-element.195.refs_0_, f32[256,1024]{1,0:T(8,128)S(1)} %copy-done.39, ...), custom_call_target="tpu_custom_call" | custom-call | flops 120000004096 | bytes 1048576 | tf_op jit(solution)/shard_map/backward_mlp/pallas_call | solution.py:124
  170.9 2.0 collective-permute-start.19
  175.1 8.1 %backward_mlp.7 = (f32[256,1024]{1,0:T(8,128)S(1)}, bf16[256,1024]{1,0:T(8,128)(2,1)S(1)}, bf16[256,2048]{1,0:T(8,128)(2,1)S(1)}, bf16[256,1024]{1,0:T(8,128)(2,1)}, f32[24,1024]{1,0:T(8,128)S(1)}) custom-call(f32[256,1024]{1,0:T(8,128)S(1)} %get-tuple-element.241.refs_0_, f32[256,1024]{1,0:T(8,128)S(1)} %copy-done.37, ...), custom_call_target="tpu_custom_call" | custom-call | flops 120000004096 | bytes 1048576 | tf_op jit(solution)/shard_map/backward_mlp/pallas_call | solution.py:124
  187.4 7.3 %backward_attention.6 = (f32[256,1024]{1,0:T(8,128)S(1)}, bf16[256,1024]{1,0:T(8,128)(2,1)S(1)}, bf16[256,512]{1,0:T(8,128)(2,1)S(1)}, bf16[256,512]{1,0:T(8,128...) custom-call(f32[256,1024]{1,0:T(8,128)S(1)} %get-tuple-element.234.refs_0_, ...), custom_call_target="tpu_custom_call" | custom-call | flops 140000002048 | bytes 1048576 | tf_op jit(solution)/shard_map/backward_attention/pallas_call | solution.py:124
  199.9 5.9 %mlp_gradients.3 = (bf16[8,256,1024]{2,1,0:T(8,128)(2,1)}, bf16[8,256,1024]{2,1,0:T(8,128)(2,1)S(1)}) custom-call(s32[2]{0:T(128)S(1)} %copy-done.14, bf16[256,2048]{1,0:T(8,128)(2,1)S(1)} %copy-done.48, bf16[256,2048]{1,0:T(8,128)(2,1)S(1)} %copy-done.49, bf16[256,1024]{1,0:T(8,128)(2,1)S(1)} %get-tuple-element.260.refs_3_, ...), custom_call_target="tpu_custom_call" | custom-call | flops 179999997952 | bytes 1048576 | tf_op jit(solution)/shard_map/mlp_gradients/pallas_call | solution.py:124
  211.6 7.6 %backward_attention.7 = (f32[256,1024]{1,0:T(8,128)S(1)}, bf16[256,1024]{1,0:T(8,128)(2,1)S(1)}, bf16[256,512]{1,0:T(8,128)(2,1)S(1)}, bf16[256,512]{1,0:T(8,128...) custom-call(f32[256,1024]{1,0:T(8,128)S(1)} %get-tuple-element.251.refs_0_, ...), custom_call_target="tpu_custom_call" | custom-call | flops 140000002048 | bytes 1048576 | tf_op jit(solution)/shard_map/backward_attention/pallas_call | solution.py:124
  222.2 3.2 merge.6
  226.7 2.9 attention_gradients.3
  235.3 1.6 collective-permute-done.36.refs_0_
  237.0 2.7 collective-permute-done.42.refs_0_
  241.4 3.5 input_gradient.1
  244.9 3.2 collective-permute-done.44.refs_0_
  249.3 1.6 collective-permute-done.43.refs_0_
  253.3 6.3 %collective-permute-done.32.refs_4_ = bf16[256,1024]{1,0:T(8,128)(2,1)S(1)} collective-permute-done((bf16[256,1024]{1,0:T(8,128)(2,1)S(1)}, bf16[256,1024]{1,0:T(8,128)(2,1)S(1)}, u32[]{:S(2)}, u32[]{:S(2)}) %collective-permute-start.32) | collective-permute-done | bytes 524320 | tf_op jit(solution)/shard_map/ppermute | solution.py:625
  265.5 3.6 collective-permute-done.46.refs_0_
  272.6 2.0 collective-permute-done.54.refs_0_
  280.1 3.0 collective-permute-done.51.refs_0_
  295.9 4.3 collective-permute-done.56.refs_0_
  312.9 7.2 %collective-permute-done.55.refs_0_ = bf16[272,512]{1,0:T(8,128)(2,1)S(1)} collective-permute-done((bf16[272,512]{1,0:T(8,128)(2,1)S(1)}, bf16[272,512]{1,0:T(8,128)(2,1)S(1)}, u32[]{:S(2)}, u32[]{:S(2)}) %collective-permute-start.55) | collective-permute-done | bytes 278560 | tf_op jit(solution)/shard_map/ppermute | solution.py:979
  333.0 7.0 %collective-permute-done.72.refs_0_ = bf16[128,1024]{1,0:T(8,128)(2,1)S(1)} collective-permute-done((bf16[128,1024]{1,0:T(8,128)(2,1)S(1)}, bf16[128,1024]{1,0:T(8,128)(2,1)S(1)}, u32[]{:S(2)}, u32[]{:S(2)}) %collective-permute-start.72) | collective-permute-done | bytes 262176 | tf_op jit(solution)/shard_map/ppermute | solution.py:979
  340.0 2.8 collective-permute-done.71.refs_0_
  342.8 2.8 collective-permute-done.70.refs_0_
  345.6 3.0 collective-permute-done.65.refs_0_
  352.5 3.9 spread.10
  365.5 4.0 spread.11
  371.2 4.3 collective-permute-done.74.refs_0_
  378.3 2.8 collective-permute-done.83.refs_0_
  381.1 3.0 collective-permute-done.79.refs_0_
  387.3 2.9 spread.12
  392.1 4.4 %collective-permute-done.82.refs_0_ = bf16[272,512]{1,0:T(8,128)(2,1)S(1)} collective-permute-done((bf16[272,512]{1,0:T(8,128)(2,1)S(1)}, bf16[272,512]{1,0:T(8,128)(2,1)S(1)}, u32[]{:S(2)}, u32[]{:S(2)}) %collective-permute-start.82) | collective-permute-done | bytes 278560 | tf_op jit(solution)/shard_map/ppermute | solution.py:979
  399.1 2.9 spread.13
  407.3 2.5 collective-permute-done.90.refs_0_
  411.2 2.4 spread.14
  413.6 4.8 %collective-permute-done.94.refs_0_ = bf16[272,512]{1,0:T(8,128)(2,1)S(1)} collective-permute-done((bf16[272,512]{1,0:T(8,128)(2,1)S(1)}, bf16[272,512]{1,0:T(8,128)(2,1)S(1)}, u32[]{:S(2)}, u32[]{:S(2)}) %collective-permute-start.94) | collective-permute-done | bytes 278560 | tf_op jit(solution)/shard_map/ppermute | solution.py:979
  420.9 3.9 spread.15
  427.9 2.4 spread.16
  430.3 4.0 spread.17
  434.6 1.8 spread.18
  438.2 2.4 spread.19
  (417 shorter events, 150.6 us)
Async XLA Ops:
  18.1 24.4 %collective-permute-start.3 = (bf16[256,1024]{1,0:T(8,128)(2,1)S(1)}, bf16[256,1024]{1,0:T(8,128)(2,1)S(1)}, u32[]{:S(2)}, u32[]{:S(2)}) collective-permute-start(bf16[256,1024]{1,0:T(8,128)(2,1)S(1)} %get-tuple-element.171.refs_7_.refs_1_), channel_id=1, source_target_pairs={{0,1},{1,0},{2,3},{3,2},{4,5},{5,4},{6,7},{7,6},{8,9},{9,8},{10,11... | collective-permute-start | bytes 1572872 | tf_op jit(solution)/shard_map/ppermute | solution.py:625
  23.8 25.9 %collective-permute-start.5 = (bf16[256,1024]{1,0:T(8,128)(2,1)S(1)}, bf16[256,1024]{1,0:T(8,128)(2,1)S(1)}, u32[]{:S(2)}, u32[]{:S(2)}) collective-permute-start(bf16[256,1024]{1,0:T(8,128)(2,1)S(1)} %get-tuple-element.172.refs_1_.refs_6_), channel_id=1, source_target_pairs={{0,1},{1,0},{2,3},{3,2},{4,5},{5,4},{6,7},{7,6},{8,9},{9,8},{10,11... | collective-permute-start | bytes 1572872 | tf_op jit(solution)/shard_map/ppermute | solution.py:625
  25.4 16.6 %collective-permute-start.2 = (f32[1,2]{1,0:T(1,128)S(1)}, f32[1,2]{1,0:T(1,128)S(1)}, u32[]{:S(2)}, u32[]{:S(2)}) collective-permute-start(f32[1,2]{1,0:T(1,128)S(1)} %hold.37), channel_id=1, source_target_pairs={{0,1},{1,0},{2,3},{3,2},{4,5},{5,4},{6,7},{7,6},{8,9},{9,8},{10,11... | collective-permute-start | bytes 32 | tf_op jit(solution)/shard_map/ppermute | solution.py:625
  48.9 14.9 %collective-permute-start.4 = (bf16[256,1024]{1,0:T(8,128)(2,1)S(1)}, bf16[256,1024]{1,0:T(8,128)(2,1)S(1)}, u32[]{:S(2)}, u32[]{:S(2)}) collective-permute-start(bf16[256,1024]{1,0:T(8,128)(2,1)S(1)} %get-tuple-element.175.refs_6_.refs_1_), channel_id=1, source_target_pairs={{0,1},{1,0},{2,3},{3,2},{4,5},{5,4},{6,7},{7,6},{8,9},{9,8},{10,11... | collective-permute-start | bytes 1572872 | tf_op jit(solution)/shard_map/ppermute | solution.py:625
  56.1 18.9 %collective-permute-start.7 = (bf16[256,1024]{1,0:T(8,128)(2,1)S(1)}, bf16[256,1024]{1,0:T(8,128)(2,1)S(1)}, u32[]{:S(2)}, u32[]{:S(2)}) collective-permute-start(bf16[256,1024]{1,0:T(8,128)(2,1)S(1)} %get-tuple-element.177.refs_9_.refs_1_), channel_id=1, source_target_pairs={{0,1},{1,0},{2,3},{3,2},{4,5},{5,4},{6,7},{7,6},{8,9},{9,8},{10,11... | collective-permute-start | bytes 1572872 | tf_op jit(solution)/shard_map/ppermute | solution.py:625
  69.2 17.1 %collective-permute-start.6 = (bf16[256,1024]{1,0:T(8,128)(2,1)S(1)}, bf16[256,1024]{1,0:T(8,128)(2,1)S(1)}, u32[]{:S(2)}, u32[]{:S(2)}) collective-permute-start(bf16[256,1024]{1,0:T(8,128)(2,1)S(1)} %get-tuple-element.179.refs_9_.refs_1_), channel_id=1, source_target_pairs={{0,1},{1,0},{2,3},{3,2},{4,5},{5,4},{6,7},{7,6},{8,9},{9,8},{10,11... | collective-permute-start | bytes 1572872 | tf_op jit(solution)/shard_map/ppermute | solution.py:625
  80.4 16.6 %collective-permute-start.9 = (bf16[256,1024]{1,0:T(8,128)(2,1)S(1)}, bf16[256,1024]{1,0:T(8,128)(2,1)S(1)}, u32[]{:S(2)}, u32[]{:S(2)}) collective-permute-start(bf16[256,1024]{1,0:T(8,128)(2,1)S(1)} %get-tuple-element.181.refs_6_.refs_1_), channel_id=1, source_target_pairs={{0,1},{1,0},{2,3},{3,2},{4,5},{5,4},{6,7},{7,6},{8,9},{9,8},{10,11... | collective-permute-start | bytes 1572872 | tf_op jit(solution)/shard_map/ppermute | solution.py:625
  111.2 14.3 %collective-permute-start.10 = (bf16[256,1024]{1,0:T(8,128)(2,1)S(1)}, bf16[256,1024]{1,0:T(8,128)(2,1)S(1)}, u32[]{:S(2)}, u32[]{:S(2)}) collective-permute-start(bf16[256,1024]{1,0:T(8,128)(2,1)S(1)} %get-tuple-element.191.refs_2_), channel_id=1, source_target_pairs={{0,1},{1,0},{2,3},{3,2},{4,5},{5,4},{6,7},{7,6},{8,9},{9,8},{10,11... | collective-permute-start | bytes 1572872 | tf_op jit(solution)/shard_map/ppermute | solution.py:625
  119.6 23.0 %collective-permute-start.15 = (bf16[256,1024]{1,0:T(8,128)(2,1)}, bf16[256,1024]{1,0:T(8,128)(2,1)}, u32[]{:S(2)}, u32[]{:S(2)}) collective-permute-start(bf16[256,1024]{1,0:T(8,128)(2,1)} %get-tuple-element.216.refs_2_), channel_id=1, source_target_pairs={{0,1},{1,0},{2,3},{3,2},{4,5},{5,4},{6,7},{7,6},{8,9},{9,8},{10,11... | collective-permute-start | bytes 1572872 | tf_op jit(solution)/shard_map/ppermute | solution.py:625
  138.0 15.8 %collective-permute-start.11 = (bf16[256,1024]{1,0:T(8,128)(2,1)S(1)}, bf16[256,1024]{1,0:T(8,128)(2,1)S(1)}, u32[]{:S(2)}, u32[]{:S(2)}) collective-permute-start(bf16[256,1024]{1,0:T(8,128)(2,1)S(1)} %get-tuple-element.197.refs_2_), channel_id=1, source_target_pairs={{0,1},{1,0},{2,3},{3,2},{4,5},{5,4},{6,7},{7,6},{8,9},{9,8},{10,11... | collective-permute-start | bytes 1572872 | tf_op jit(solution)/shard_map/ppermute | solution.py:625
  151.1 24.0 %collective-permute-start.20 = (bf16[256,1024]{1,0:T(8,128)(2,1)}, bf16[256,1024]{1,0:T(8,128)(2,1)}, u32[]{:S(2)}, u32[]{:S(2)}) collective-permute-start(bf16[256,1024]{1,0:T(8,128)(2,1)} %get-tuple-element.243.refs_2_), channel_id=1, source_target_pairs={{0,1},{1,0},{2,3},{3,2},{4,5},{5,4},{6,7},{7,6},{8,9},{9,8},{10,11... | collective-permute-start | bytes 1572872 | tf_op jit(solution)/shard_map/ppermute | solution.py:625
  156.8 16.1 %collective-permute-start.21 = (bf16[8,256,512]{2,1,0:T(8,128)(2,1)S(1)}, bf16[8,256,512]{2,1,0:T(8,128)(2,1)S(1)}, u32[]{:S(2)}, u32[]{:S(2)}) collective-permute-start(bf16[8,256,512]{2,1,0:T(8,128)(2,1)S(1)} %get-tuple-element.246), channel_id=1, source_target_pairs={{0,2},{2,0},{4,6},{6,4},{8,10},{10,8},{12,14},{14,12},{16,18},{18,... | collective-permute-start | bytes 6291464 | tf_op jit(solution)/shard_map/ppermute | solution.py:942
  169.3 18.1 %collective-permute-start.17 = (bf16[256,1024]{1,0:T(8,128)(2,1)S(1)}, bf16[256,1024]{1,0:T(8,128)(2,1)S(1)}, u32[]{:S(2)}, u32[]{:S(2)}) collective-permute-start(bf16[256,1024]{1,0:T(8,128)(2,1)S(1)} %get-tuple-element.236.refs_2_), channel_id=1, source_target_pairs={{0,1},{1,0},{2,3},{3,2},{4,5},{5,4},{6,7},{7,6},{8,9},{9,8},{10,11... | collective-permute-start | bytes 1572872 | tf_op jit(solution)/shard_map/ppermute | solution.py:625
  170.9 12.4 %collective-permute-start.19 = (bf16[256,1024]{1,0:T(8,128)(2,1)S(1)}, bf16[256,1024]{1,0:T(8,128)(2,1)S(1)}, u32[]{:S(2)}, u32[]{:S(2)}) collective-permute-start(bf16[256,1024]{1,0:T(8,128)(2,1)S(1)} %add.39.refs_10_), channel_id=1, source_target_pairs={{0,8},{10,2},{8,16},{18,10},{16,24},{26,18},{24,28},{30,26},{28,20... | collective-permute-start | bytes 1572872 | tf_op jit(solution)/shard_map/ppermute | solution.py:979
  173.5 12.6 %collective-permute-start.22 = (bf16[256,512]{1,0:T(8,128)(2,1)S(1)}, bf16[256,512]{1,0:T(8,128)(2,1)S(1)}, u32[]{:S(2)}, u32[]{:S(2)}) collective-permute-start(bf16[256,512]{1,0:T(8,128)(2,1)S(1)} %get-tuple-element.247.refs_11_), channel_id=1, source_target_pairs={{0,8},{10,2},{8,16},{18,10},{16,24},{26,18},{24,28},{30,26},{28,20... | collective-permute-start | bytes 786440 | tf_op jit(solution)/shard_map/ppermute | solution.py:979
  183.4 14.4 %collective-permute-start.24 = (bf16[256,1024]{1,0:T(8,128)(2,1)S(1)}, bf16[256,1024]{1,0:T(8,128)(2,1)S(1)}, u32[]{:S(2)}, u32[]{:S(2)}) collective-permute-start(bf16[256,1024]{1,0:T(8,128)(2,1)S(1)} %add.40.refs_12_), channel_id=1, source_target_pairs={{0,8},{10,2},{8,16},{18,10},{16,24},{26,18},{24,28},{30,26},{28,20... | collective-permute-start | bytes 1572872 | tf_op jit(solution)/shard_map/ppermute | solution.py:979
  185.0 14.9 %collective-permute-start.23 = (bf16[256,1024]{1,0:T(8,128)(2,1)}, bf16[256,1024]{1,0:T(8,128)(2,1)}, u32[]{:S(2)}, u32[]{:S(2)}) collective-permute-start(bf16[256,1024]{1,0:T(8,128)(2,1)} %get-tuple-element.253.refs_2_), channel_id=1, source_target_pairs={{0,1},{1,0},{2,3},{3,2},{4,5},{5,4},{6,7},{7,6},{8,9},{9,8},{10,11... | collective-permute-start | bytes 1572872 | tf_op jit(solution)/shard_map/ppermute | solution.py:625
  194.7 31.2 %collective-permute-start.28 = (bf16[256,1024]{1,0:T(8,128)(2,1)}, bf16[256,1024]{1,0:T(8,128)(2,1)}, u32[]{:S(2)}, u32[]{:S(2)}) collective-permute-start(bf16[256,1024]{1,0:T(8,128)(2,1)} %get-tuple-element.276.refs_3_), channel_id=1, source_target_pairs={{0,1},{1,0},{2,3},{3,2},{4,5},{5,4},{6,7},{7,6},{8,9},{9,8},{10,11... | collective-permute-start | bytes 1572872 | tf_op jit(solution)/shard_map/ppermute | solution.py:625
  205.9 16.3 %collective-permute-start.31 = (bf16[8,256,1024]{2,1,0:T(8,128)(2,1)}, bf16[8,256,1024]{2,1,0:T(8,128)(2,1)}, u32[]{:S(2)}, u32[]{:S(2)}) collective-permute-start(bf16[8,256,1024]{2,1,0:T(8,128)(2,1)} %get-tuple-element.278), channel_id=1, source_target_pairs={{0,2},{2,0},{4,6},{6,4},{8,10},{10,8},{12,14},{14,12},{16,18},{18,... | collective-permute-start | bytes 12582920 | tf_op jit(solution)/shard_map/ppermute | solution.py:942
  207.2 12.0 %collective-permute-start.30 = (bf16[256,512]{1,0:T(8,128)(2,1)S(1)}, bf16[256,512]{1,0:T(8,128)(2,1)S(1)}, u32[]{:S(2)}, u32[]{:S(2)}) collective-permute-start(bf16[256,512]{1,0:T(8,128)(2,1)S(1)} %add.45.refs_13_), channel_id=1, source_target_pairs={{0,8},{10,2},{8,16},{18,10},{16,24},{26,18},{24,28},{30,26},{28,20... | collective-permute-start | bytes 786440 | tf_op jit(solution)/shard_map/ppermute | solution.py:979
  210.0 11.6 %collective-permute-start.29 = (bf16[256,1024]{1,0:T(8,128)(2,1)S(1)}, bf16[256,1024]{1,0:T(8,128)(2,1)S(1)}, u32[]{:S(2)}, u32[]{:S(2)}) collective-permute-start(bf16[256,1024]{1,0:T(8,128)(2,1)S(1)} %add.44.refs_12_), channel_id=1, source_target_pairs={{0,8},{10,2},{8,16},{18,10},{16,24},{26,18},{24,28},{30,26},{28,20... | collective-permute-start | bytes 1572872 | tf_op jit(solution)/shard_map/ppermute | solution.py:979
  219.2 11.4 %collective-permute-start.35 = (bf16[256,512]{1,0:T(8,128)(2,1)S(1)}, bf16[256,512]{1,0:T(8,128)(2,1)S(1)}, u32[]{:S(2)}, u32[]{:S(2)}) collective-permute-start(bf16[256,512]{1,0:T(8,128)(2,1)S(1)} %add.47.refs_15_), channel_id=1, source_target_pairs={{0,8},{10,2},{8,16},{18,10},{16,24},{26,18},{24,28},{30,26},{28,20... | collective-permute-start | bytes 786440 | tf_op jit(solution)/shard_map/ppermute | solution.py:979
  220.4 20.5 %collective-permute-start.38 = (bf16[256,1024]{1,0:T(8,128)(2,1)S(1)}, bf16[256,1024]{1,0:T(8,128)(2,1)S(1)}, u32[]{:S(2)}, u32[]{:S(2)}) collective-permute-start(bf16[256,1024]{1,0:T(8,128)(2,1)S(1)} %get-tuple-element.289.refs_7_), channel_id=1, source_target_pairs={{0,1},{1,0},{2,3},{3,2},{4,5},{5,4},{6,7},{7,6},{8,9},{9,8},{10,11... | collective-permute-start | bytes 1572872 | tf_op jit(solution)/shard_map/ppermute | solution.py:625
  232.2 20.0 %collective-permute-start.41 = (bf16[256,1024]{1,0:T(8,128)(2,1)S(1)}, bf16[256,1024]{1,0:T(8,128)(2,1)S(1)}, u32[]{:S(2)}, u32[]{:S(2)}) collective-permute-start(bf16[256,1024]{1,0:T(8,128)(2,1)S(1)} %hold.42.refs_9_.refs_12_.refs_11_.refs_1_.refs_2_), channel_id=1, source_target_pairs={{0,8},{10,2},{8,16},{18,10},{16,24},{26,18},{24,28},{30,26},{28,20... | collective-permute-start | bytes 1572872 | tf_op jit(solution)/shard_map/ppermute | solution.py:979
  234.1 18.7 %collective-permute-start.33 = (bf16[256,1024]{1,0:T(8,128)(2,1)S(1)}, bf16[256,1024]{1,0:T(8,128)(2,1)S(1)}, u32[]{:S(2)}, u32[]{:S(2)}) collective-permute-start(bf16[256,1024]{1,0:T(8,128)(2,1)S(1)} %hold.41), channel_id=1, source_target_pairs={{0,1},{1,0},{2,3},{3,2},{4,5},{5,4},{6,7},{7,6},{8,9},{9,8},{10,11... | collective-permute-start | bytes 1572872 | tf_op jit(solution)/shard_map/ppermute | solution.py:625
  236.9 34.7 %collective-permute-start.39 = (bf16[8,256,512]{2,1,0:T(8,128)(2,1)S(1)}, bf16[8,256,512]{2,1,0:T(8,128)(2,1)S(1)}, u32[]{:S(2)}, u32[]{:S(2)}) collective-permute-start(bf16[8,256,512]{2,1,0:T(8,128)(2,1)S(1)} %get-tuple-element.293), channel_id=1, source_target_pairs={{0,2},{2,0},{4,6},{6,4},{8,10},{10,8},{12,14},{14,12},{16,18},{18,... | collective-permute-start | bytes 6291464 | tf_op jit(solution)/shard_map/ppermute | solution.py:942
  248.1 11.5 %collective-permute-start.32 = (bf16[256,1024]{1,0:T(8,128)(2,1)S(1)}, bf16[256,1024]{1,0:T(8,128)(2,1)S(1)}, u32[]{:S(2)}, u32[]{:S(2)}) collective-permute-start(bf16[256,1024]{1,0:T(8,128)(2,1)S(1)} %hold.40), channel_id=1, source_target_pairs={{0,1},{1,0},{2,3},{3,2},{4,5},{5,4},{6,7},{7,6},{8,9},{9,8},{10,11... | collective-permute-start | bytes 1572872 | tf_op jit(solution)/shard_map/ppermute | solution.py:625
  251.0 12.5 %collective-permute-start.47 = (bf16[256,512]{1,0:T(8,128)(2,1)S(1)}, bf16[256,512]{1,0:T(8,128)(2,1)S(1)}, u32[]{:S(2)}, u32[]{:S(2)}) collective-permute-start(bf16[256,512]{1,0:T(8,128)(2,1)S(1)} %add.51.refs_5_.refs_2_.refs_3_), channel_id=1, source_target_pairs={{0,8},{10,2},{8,16},{18,10},{16,24},{26,18},{24,28},{30,26},{28,20... | collective-permute-start | bytes 786440 | tf_op jit(solution)/shard_map/ppermute | solution.py:979
  252.2 11.4 %collective-permute-start.49 = (bf16[128,1024]{1,0:T(8,128)(2,1)S(1)}, bf16[128,1024]{1,0:T(8,128)(2,1)S(1)}, u32[]{:S(2)}, u32[]{:S(2)}) collective-permute-start(bf16[128,1024]{1,0:T(8,128)(2,1)S(1)} %add.53.refs_7_.refs_4_.refs_5_), channel_id=1, source_target_pairs={{0,8},{10,2},{8,16},{18,10},{16,24},{26,18},{24,28},{30,26},{28,20... | collective-permute-start | bytes 786440 | tf_op jit(solution)/shard_map/ppermute | solution.py:979
  252.8 12.1 %collective-permute-start.48 = (bf16[128,1024]{1,0:T(8,128)(2,1)S(1)}, bf16[128,1024]{1,0:T(8,128)(2,1)S(1)}, u32[]{:S(2)}, u32[]{:S(2)}) collective-permute-start(bf16[128,1024]{1,0:T(8,128)(2,1)S(1)} %add.52.refs_6_.refs_3_.refs_4_), channel_id=1, source_target_pairs={{0,8},{10,2},{8,16},{18,10},{16,24},{26,18},{24,28},{30,26},{28,20... | collective-permute-start | bytes 786440 | tf_op jit(solution)/shard_map/ppermute | solution.py:979
  263.7 15.2 %collective-permute-start.52 = (bf16[256,512]{1,0:T(8,128)(2,1)S(1)}, bf16[256,512]{1,0:T(8,128)(2,1)S(1)}, u32[]{:S(2)}, u32[]{:S(2)}) collective-permute-start(bf16[256,512]{1,0:T(8,128)(2,1)S(1)} %add.54.refs_3_.refs_2_.refs_0_), channel_id=1, source_target_pairs={{0,8},{10,2},{8,16},{18,10},{16,24},{26,18},{24,28},{30,26},{28,20... | collective-permute-start | bytes 786440 | tf_op jit(solution)/shard_map/ppermute | solution.py:979
  270.4 12.7 %collective-permute-start.51 = (bf16[256,1024]{1,0:T(8,128)(2,1)S(1)}, bf16[256,1024]{1,0:T(8,128)(2,1)S(1)}, u32[]{:S(2)}, u32[]{:S(2)}) collective-permute-start(bf16[256,1024]{1,0:T(8,128)(2,1)S(1)} %hold.44.refs_2_.refs_1_.refs_3_), channel_id=1, source_target_pairs={{0,8},{10,2},{8,16},{18,10},{16,24},{26,18},{24,28},{30,26},{28,20... | collective-permute-start | bytes 1572872 | tf_op jit(solution)/shard_map/ppermute | solution.py:979
  272.1 14.0 %collective-permute-start.45 = (bf16[272,512]{1,0:T(8,128)(2,1)S(1)}, bf16[272,512]{1,0:T(8,128)(2,1)S(1)}, u32[]{:S(2)}, u32[]{:S(2)}) collective-permute-start(bf16[272,512]{1,0:T(8,128)(2,1)S(1)} %get-tuple-element.297.refs_6_.refs_5_), channel_id=1, source_target_pairs={{0,8},{10,2},{8,16},{18,10},{16,24},{26,18},{24,28},{30,26},{28,20... | collective-permute-start | bytes 835592 | tf_op jit(solution)/shard_map/ppermute | solution.py:979
  274.8 14.2 %collective-permute-start.59 = (bf16[128,1024]{1,0:T(8,128)(2,1)S(1)}, bf16[128,1024]{1,0:T(8,128)(2,1)S(1)}, u32[]{:S(2)}, u32[]{:S(2)}) collective-permute-start(bf16[128,1024]{1,0:T(8,128)(2,1)S(1)} %add.59.refs_5_.refs_4_), channel_id=1, source_target_pairs={{0,8},{10,2},{8,16},{18,10},{16,24},{26,18},{24,28},{30,26},{28,20... | collective-permute-start | bytes 786440 | tf_op jit(solution)/shard_map/ppermute | solution.py:979
  277.6 14.2 %collective-permute-start.58 = (bf16[128,1024]{1,0:T(8,128)(2,1)S(1)}, bf16[128,1024]{1,0:T(8,128)(2,1)S(1)}, u32[]{:S(2)}, u32[]{:S(2)}) collective-permute-start(bf16[128,1024]{1,0:T(8,128)(2,1)S(1)} %add.58.refs_4_.refs_3_), channel_id=1, source_target_pairs={{0,8},{10,2},{8,16},{18,10},{16,24},{26,18},{24,28},{30,26},{28,20... | collective-permute-start | bytes 786440 | tf_op jit(solution)/shard_map/ppermute | solution.py:979
  278.9 15.6 %collective-permute-start.57 = (bf16[256,512]{1,0:T(8,128)(2,1)S(1)}, bf16[256,512]{1,0:T(8,128)(2,1)S(1)}, u32[]{:S(2)}, u32[]{:S(2)}) collective-permute-start(bf16[256,512]{1,0:T(8,128)(2,1)S(1)} %hold.46.refs_3_.refs_2_.refs_1_), channel_id=1, source_target_pairs={{0,8},{10,2},{8,16},{18,10},{16,24},{26,18},{24,28},{30,26},{28,20... | collective-permute-start | bytes 786440 | tf_op jit(solution)/shard_map/ppermute | solution.py:979
  283.2 17.0 %collective-permute-start.56 = (bf16[256,1024]{1,0:T(8,128)(2,1)S(1)}, bf16[256,1024]{1,0:T(8,128)(2,1)S(1)}, u32[]{:S(2)}, u32[]{:S(2)}) collective-permute-start(bf16[256,1024]{1,0:T(8,128)(2,1)S(1)} %hold.45.refs_2_.refs_1_.refs_4_), channel_id=1, source_target_pairs={{0,8},{10,2},{8,16},{18,10},{16,24},{26,18},{24,28},{30,26},{28,20... | collective-permute-start | bytes 1572872 | tf_op jit(solution)/shard_map/ppermute | solution.py:979
  286.2 17.0 %collective-permute-start.50 = (bf16[272,512]{1,0:T(8,128)(2,1)S(1)}, bf16[272,512]{1,0:T(8,128)(2,1)S(1)}, u32[]{:S(2)}, u32[]{:S(2)}) collective-permute-start(bf16[272,512]{1,0:T(8,128)(2,1)S(1)} %add.57.refs_6_.refs_5_), channel_id=1, source_target_pairs={{0,8},{10,2},{8,16},{18,10},{16,24},{26,18},{24,28},{30,26},{28,20... | collective-permute-start | bytes 835592 | tf_op jit(solution)/shard_map/ppermute | solution.py:979
  289.0 17.0 %collective-permute-start.64 = (bf16[128,1024]{1,0:T(8,128)(2,1)S(1)}, bf16[128,1024]{1,0:T(8,128)(2,1)S(1)}, u32[]{:S(2)}, u32[]{:S(2)}) collective-permute-start(bf16[128,1024]{1,0:T(8,128)(2,1)S(1)} %add.62.refs_5_.refs_4_), channel_id=1, source_target_pairs={{0,8},{10,2},{8,16},{18,10},{16,24},{26,18},{24,28},{30,26},{28,20... | collective-permute-start | bytes 786440 | tf_op jit(solution)/shard_map/ppermute | solution.py:979
  291.8 17.0 %collective-permute-start.63 = (bf16[128,1024]{1,0:T(8,128)(2,1)S(1)}, bf16[128,1024]{1,0:T(8,128)(2,1)S(1)}, u32[]{:S(2)}, u32[]{:S(2)}) collective-permute-start(bf16[128,1024]{1,0:T(8,128)(2,1)S(1)} %add.61.refs_4_.refs_3_), channel_id=1, source_target_pairs={{0,8},{10,2},{8,16},{18,10},{16,24},{26,18},{24,28},{30,26},{28,20... | collective-permute-start | bytes 786440 | tf_op jit(solution)/shard_map/ppermute | solution.py:979
  294.5 17.0 %collective-permute-start.62 = (bf16[256,512]{1,0:T(8,128)(2,1)S(1)}, bf16[256,512]{1,0:T(8,128)(2,1)S(1)}, u32[]{:S(2)}, u32[]{:S(2)}) collective-permute-start(bf16[256,512]{1,0:T(8,128)(2,1)S(1)} %hold.48.refs_3_.refs_2_), channel_id=1, source_target_pairs={{0,8},{10,2},{8,16},{18,10},{16,24},{26,18},{24,28},{30,26},{28,20... | collective-permute-start | bytes 786440 | tf_op jit(solution)/shard_map/ppermute | solution.py:979
  300.2 21.4 %collective-permute-start.61 = (bf16[256,1024]{1,0:T(8,128)(2,1)S(1)}, bf16[256,1024]{1,0:T(8,128)(2,1)S(1)}, u32[]{:S(2)}, u32[]{:S(2)}) collective-permute-start(bf16[256,1024]{1,0:T(8,128)(2,1)S(1)} %hold.47.refs_2_.refs_1_.refs_5_), channel_id=1, source_target_pairs={{0,8},{10,2},{8,16},{18,10},{16,24},{26,18},{24,28},{30,26},{28,20... | collective-permute-start | bytes 1572872 | tf_op jit(solution)/shard_map/ppermute | solution.py:979
  303.2 17.0 %collective-permute-start.55 = (bf16[272,512]{1,0:T(8,128)(2,1)S(1)}, bf16[272,512]{1,0:T(8,128)(2,1)S(1)}, u32[]{:S(2)}, u32[]{:S(2)}) collective-permute-start(bf16[272,512]{1,0:T(8,128)(2,1)S(1)} %add.60.refs_6_.refs_5_), channel_id=1, source_target_pairs={{0,8},{10,2},{8,16},{18,10},{16,24},{26,18},{24,28},{30,26},{28,20... | collective-permute-start | bytes 835592 | tf_op jit(solution)/shard_map/ppermute | solution.py:979
  306.0 17.0 %collective-permute-start.68 = (bf16[128,1024]{1,0:T(8,128)(2,1)S(1)}, bf16[128,1024]{1,0:T(8,128)(2,1)S(1)}, u32[]{:S(2)}, u32[]{:S(2)}) collective-permute-start(bf16[128,1024]{1,0:T(8,128)(2,1)S(1)} %add.65.refs_5_.refs_4_), channel_id=1, source_target_pairs={{0,8},{10,2},{8,16},{18,10},{16,24},{26,18},{24,28},{30,26},{28,20... | collective-permute-start | bytes 786440 | tf_op jit(solution)/shard_map/ppermute | solution.py:979
  308.8 17.0 %collective-permute-start.67 = (bf16[128,1024]{1,0:T(8,128)(2,1)S(1)}, bf16[128,1024]{1,0:T(8,128)(2,1)S(1)}, u32[]{:S(2)}, u32[]{:S(2)}) collective-permute-start(bf16[128,1024]{1,0:T(8,128)(2,1)S(1)} %add.64.refs_4_.refs_3_), channel_id=1, source_target_pairs={{0,8},{10,2},{8,16},{18,10},{16,24},{26,18},{24,28},{30,26},{28,20... | collective-permute-start | bytes 786440 | tf_op jit(solution)/shard_map/ppermute | solution.py:979
  311.6 17.0 %collective-permute-start.66 = (bf16[256,512]{1,0:T(8,128)(2,1)S(1)}, bf16[256,512]{1,0:T(8,128)(2,1)S(1)}, u32[]{:S(2)}, u32[]{:S(2)}) collective-permute-start(bf16[256,512]{1,0:T(8,128)(2,1)S(1)} %hold.50.refs_3_.refs_2_), channel_id=1, source_target_pairs={{0,8},{10,2},{8,16},{18,10},{16,24},{26,18},{24,28},{30,26},{28,20... | collective-permute-start | bytes 786440 | tf_op jit(solution)/shard_map/ppermute | solution.py:979
  320.2 11.3 %collective-permute-start.60 = (bf16[272,512]{1,0:T(8,128)(2,1)S(1)}, bf16[272,512]{1,0:T(8,128)(2,1)S(1)}, u32[]{:S(2)}, u32[]{:S(2)}) collective-permute-start(bf16[272,512]{1,0:T(8,128)(2,1)S(1)} %add.63.refs_6_.refs_5_), channel_id=1, source_target_pairs={{0,8},{10,2},{8,16},{18,10},{16,24},{26,18},{24,28},{30,26},{28,20... | collective-permute-start | bytes 835592 | tf_op jit(solution)/shard_map/ppermute | solution.py:979
  321.6 27.1 %collective-permute-start.73 = (bf16[256,1024]{1,0:T(8,128)(2,1)S(1)}, bf16[256,1024]{1,0:T(8,128)(2,1)S(1)}, u32[]{:S(2)}, u32[]{:S(2)}) collective-permute-start(bf16[256,1024]{1,0:T(8,128)(2,1)S(1)} %hold.49.refs_2_.refs_1_.refs_6_), channel_id=1, source_target_pairs={{0,8},{10,2},{8,16},{18,10},{16,24},{26,18},{24,28},{30,26},{28,20... | collective-permute-start | bytes 1572872 | tf_op jit(solution)/shard_map/ppermute | solution.py:979
  323.0 17.0 %collective-permute-start.72 = (bf16[128,1024]{1,0:T(8,128)(2,1)S(1)}, bf16[128,1024]{1,0:T(8,128)(2,1)S(1)}, u32[]{:S(2)}, u32[]{:S(2)}) collective-permute-start(bf16[128,1024]{1,0:T(8,128)(2,1)S(1)} %add.68.refs_4_.refs_3_.refs_8_), channel_id=1, source_target_pairs={{0,8},{10,2},{8,16},{18,10},{16,24},{26,18},{24,28},{30,26},{28,20... | collective-permute-start | bytes 786440 | tf_op jit(solution)/shard_map/ppermute | solution.py:979
  325.8 17.0 %collective-permute-start.71 = (bf16[128,1024]{1,0:T(8,128)(2,1)S(1)}, bf16[128,1024]{1,0:T(8,128)(2,1)S(1)}, u32[]{:S(2)}, u32[]{:S(2)}) collective-permute-start(bf16[128,1024]{1,0:T(8,128)(2,1)S(1)} %add.67.refs_3_.refs_2_.refs_0_), channel_id=1, source_target_pairs={{0,8},{10,2},{8,16},{18,10},{16,24},{26,18},{24,28},{30,26},{28,20... | collective-permute-start | bytes 786440 | tf_op jit(solution)/shard_map/ppermute | solution.py:979
  328.6 17.0 %collective-permute-start.70 = (bf16[256,512]{1,0:T(8,128)(2,1)S(1)}, bf16[256,512]{1,0:T(8,128)(2,1)S(1)}, u32[]{:S(2)}, u32[]{:S(2)}) collective-permute-start(bf16[256,512]{1,0:T(8,128)(2,1)S(1)} %hold.51.refs_2_.refs_1_.refs_4_), channel_id=1, source_target_pairs={{0,8},{10,2},{8,16},{18,10},{16,24},{26,18},{24,28},{30,26},{28,20... | collective-permute-start | bytes 786440 | tf_op jit(solution)/shard_map/ppermute | solution.py:979
  331.6 17.0 %collective-permute-start.65 = (bf16[272,512]{1,0:T(8,128)(2,1)S(1)}, bf16[272,512]{1,0:T(8,128)(2,1)S(1)}, u32[]{:S(2)}, u32[]{:S(2)}) collective-permute-start(bf16[272,512]{1,0:T(8,128)(2,1)S(1)} %add.66.refs_5_.refs_4_), channel_id=1, source_target_pairs={{0,8},{10,2},{8,16},{18,10},{16,24},{26,18},{24,28},{30,26},{28,20... | collective-permute-start | bytes 835592 | tf_op jit(solution)/shard_map/ppermute | solution.py:979
  349.0 16.5 %collective-permute-start.78 = (bf16[8,256,1024]{2,1,0:T(8,128)(2,1)S(1)}, bf16[8,256,1024]{2,1,0:T(8,128)(2,1)S(1)}, u32[]{:S(2)}, u32[]{:S(2)}) collective-permute-start(bf16[8,256,1024]{2,1,0:T(8,128)(2,1)S(1)} %pack.5.refs_1_), channel_id=1, source_target_pairs={{0,2},{2,0},{4,6},{6,4},{8,10},{10,8},{12,14},{14,12},{16,18},{18,... | collective-permute-start | bytes 12582920 | tf_op jit(solution)/shard_map/ppermute | solution.py:965
  352.0 12.1 %collective-permute-start.69 = (bf16[272,512]{1,0:T(8,128)(2,1)S(1)}, bf16[272,512]{1,0:T(8,128)(2,1)S(1)}, u32[]{:S(2)}, u32[]{:S(2)}) collective-permute-start(bf16[272,512]{1,0:T(8,128)(2,1)S(1)} %add.69.refs_11_.refs_5_.refs_4_), channel_id=1, source_target_pairs={{0,8},{10,2},{8,16},{18,10},{16,24},{26,18},{24,28},{30,26},{28,20... | collective-permute-start | bytes 835592 | tf_op jit(solution)/shard_map/ppermute | solution.py:979
  356.5 12.9 %collective-permute-start.81 = (bf16[128,1024]{1,0:T(8,128)(2,1)S(1)}, bf16[128,1024]{1,0:T(8,128)(2,1)S(1)}, u32[]{:S(2)}, u32[]{:S(2)}) collective-permute-start(bf16[128,1024]{1,0:T(8,128)(2,1)S(1)} %hold.57.refs_6_.refs_4_.refs_3_.refs_10_), channel_id=1, source_target_pairs={{0,8},{10,2},{8,16},{18,10},{16,24},{26,18},{24,28},{30,26},{28,20... | collective-permute-start | bytes 786440 | tf_op jit(solution)/shard_map/ppermute | solution.py:979
  358.3 12.4 %collective-permute-start.80 = (bf16[128,1024]{1,0:T(8,128)(2,1)S(1)}, bf16[128,1024]{1,0:T(8,128)(2,1)S(1)}, u32[]{:S(2)}, u32[]{:S(2)}) collective-permute-start(bf16[128,1024]{1,0:T(8,128)(2,1)S(1)} %hold.56.refs_5_.refs_3_.refs_2_), channel_id=1, source_target_pairs={{0,8},{10,2},{8,16},{18,10},{16,24},{26,18},{24,28},{30,26},{28,20... | collective-permute-start | bytes 786440 | tf_op jit(solution)/shard_map/ppermute | solution.py:979
  361.1 23.0 %collective-permute-start.85 = (bf16[256,512]{1,0:T(8,128)(2,1)S(1)}, bf16[256,512]{1,0:T(8,128)(2,1)S(1)}, u32[]{:S(2)}, u32[]{:S(2)}) collective-permute-start(bf16[256,512]{1,0:T(8,128)(2,1)S(1)} %hold.55.refs_4_.refs_2_.refs_1_.refs_6_), channel_id=1, source_target_pairs={{0,8},{10,2},{8,16},{18,10},{16,24},{26,18},{24,28},{30,26},{28,20... | collective-permute-start | bytes 786440 | tf_op jit(solution)/shard_map/ppermute | solution.py:979
  364.1 11.3 %collective-permute-start.74 = (bf16[272,512]{1,0:T(8,128)(2,1)S(1)}, bf16[272,512]{1,0:T(8,128)(2,1)S(1)}, u32[]{:S(2)}, u32[]{:S(2)}) collective-permute-start(bf16[272,512]{1,0:T(8,128)(2,1)S(1)} %add.70.refs_7_.refs_5_.refs_4_), channel_id=1, source_target_pairs={{0,8},{10,2},{8,16},{18,10},{16,24},{26,18},{24,28},{30,26},{28,20... | collective-permute-start | bytes 835592 | tf_op jit(solution)/shard_map/ppermute | solution.py:979
  384.3 14.9 %collective-permute-start.89 = (bf16[8,256,512]{2,1,0:T(8,128)(2,1)S(1)}, bf16[8,256,512]{2,1,0:T(8,128)(2,1)S(1)}, u32[]{:S(2)}, u32[]{:S(2)}) collective-permute-start(bf16[8,256,512]{2,1,0:T(8,128)(2,1)S(1)} %pack.6.refs_1_), channel_id=1, source_target_pairs={{0,2},{2,0},{4,6},{6,4},{8,10},{10,8},{12,14},{14,12},{16,18},{18,... | collective-permute-start | bytes 6291464 | tf_op jit(solution)/shard_map/ppermute | solution.py:965
  385.7 12.2 %collective-permute-start.87 = (bf16[128,1024]{1,0:T(8,128)(2,1)S(1)}, bf16[128,1024]{1,0:T(8,128)(2,1)S(1)}, u32[]{:S(2)}, u32[]{:S(2)}) collective-permute-start(bf16[128,1024]{1,0:T(8,128)(2,1)S(1)} %hold.61.refs_8_.refs_1_.refs_4_), channel_id=1, source_target_pairs={{0,8},{10,2},{8,16},{18,10},{16,24},{26,18},{24,28},{30,26},{28,20... | collective-permute-start | bytes 786440 | tf_op jit(solution)/shard_map/ppermute | solution.py:979
  390.8 13.8 %collective-permute-start.92 = (bf16[128,1024]{1,0:T(8,128)(2,1)S(1)}, bf16[128,1024]{1,0:T(8,128)(2,1)S(1)}, u32[]{:S(2)}, u32[]{:S(2)}) collective-permute-start(bf16[128,1024]{1,0:T(8,128)(2,1)S(1)} %hold.65.refs_5_.refs_2_.refs_13_), channel_id=1, source_target_pairs={{0,8},{10,2},{8,16},{18,10},{16,24},{26,18},{24,28},{30,26},{28,20... | collective-permute-start | bytes 786440 | tf_op jit(solution)/shard_map/ppermute | solution.py:979
  404.6 13.9 %collective-permute-start.97 = (bf16[128,1024]{1,0:T(8,128)(2,1)S(1)}, bf16[128,1024]{1,0:T(8,128)(2,1)S(1)}, u32[]{:S(2)}, u32[]{:S(2)}) collective-permute-start(bf16[128,1024]{1,0:T(8,128)(2,1)S(1)} %hold.68.refs_2_.refs_14_), channel_id=1, source_target_pairs={{0,8},{10,2},{8,16},{18,10},{16,24},{26,18},{24,28},{30,26},{28,20... | collective-permute-start | bytes 786440 | tf_op jit(solution)/shard_map/ppermute | solution.py:979
  406.0 12.4 %collective-permute-start.96 = (bf16[128,1024]{1,0:T(8,128)(2,1)S(1)}, bf16[128,1024]{1,0:T(8,128)(2,1)S(1)}, u32[]{:S(2)}, u32[]{:S(2)}) collective-permute-start(bf16[128,1024]{1,0:T(8,128)(2,1)S(1)} %hold.67.refs_1_.refs_6_), channel_id=1, source_target_pairs={{0,8},{10,2},{8,16},{18,10},{16,24},{26,18},{24,28},{30,26},{28,20... | collective-permute-start | bytes 786440 | tf_op jit(solution)/shard_map/ppermute | solution.py:979
  418.7 11.6 %collective-permute-start.99 = (bf16[8,256,1024]{2,1,0:T(8,128)(2,1)S(1)}, bf16[8,256,1024]{2,1,0:T(8,128)(2,1)S(1)}, u32[]{:S(2)}, u32[]{:S(2)}) collective-permute-start(bf16[8,256,1024]{2,1,0:T(8,128)(2,1)S(1)} %pack.8.refs_1_), channel_id=1, source_target_pairs={{0,2},{2,0},{4,6},{6,4},{8,10},{10,8},{12,14},{14,12},{16,18},{18,... | collective-permute-start | bytes 12582920 | tf_op jit(solution)/shard_map/ppermute | solution.py:965
  (114 other events, 1113.6 us)
